TPU v7x, 32 devices: a whole 2x2x4 slice. The times are simulated.
32 devices in a mesh: lon: 4 (over z), lat: 4 (over x, core), rep: 2 (over y).
Axes of the slice: x: 2, y: 2, z: 4, core: 2. Of those that a mesh axis runs over, the one named last changes fastest.
Arguments:
- inputs: float32 [2, 64, 128, 256], P('rep', 'lat', 'lon'), may hold values from -6 to 6
- cotangent: float32 [2, 64, 128, 256], P('rep', 'lat', 'lon'), may hold values from -6 to 6
- first_weight: float32 [2304, 256], replicated, may hold values from -0.125 to 0.125
- second_weight: float32 [2304, 256], replicated, may hold values from -0.125 to 0.125
Outputs:
- output: float32 [2, 64, 128, 256], P('rep', 'lat', 'lon')
- input_grad: float32 [2, 64, 128, 256], P('rep', 'lat', 'lon')
- first_grad: float32 [2304, 256], P('lon', ('lat', 'rep'))
- second_grad: float32 [2304, 256], P('lon', ('lat', 'rep'))
All inputs are finite; a program needn't handle non-finite values.
Results may differ from a plain program's by a relative error of at most 0.00012.
Values sent between devices are 32-bit elements; how exact they have to be, the bound alone decides.
No kernel may reach another device: no remote copies, remote signals or barrier semaphores. Data moves between devices by JAX's collectives and lax.ppermute only.
A program may use at most 128 MiB of HBM per device.

v0:
```python
import math

import jax
import jax.numpy as jnp
from jax import lax
from jax.experimental import pallas as pl
from jax.experimental.pallas import tpu as pltpu
from jax.sharding import PartitionSpec as P

F32 = jnp.float32
BF16 = jnp.bfloat16
VMEM = pl.BlockSpec(memory_space=pltpu.VMEM)
LINE = 24
EDGE = 8


def call(body, outs, ins, flops=0, scratch=(), limit=32):
    size = sum(math.prod(a.shape) * a.dtype.itemsize for a in ins)
    return pl.pallas_call(
        body,
        out_shape=[jax.ShapeDtypeStruct(shape, dtype) for shape, dtype in outs],
        in_specs=[VMEM] * len(ins),
        out_specs=[VMEM] * len(outs),
        scratch_shapes=[pltpu.VMEM(shape, dtype) for shape, dtype in scratch],
        compiler_params=pltpu.CompilerParams(vmem_limit_bytes=limit * 1024 * 1024),
        cost_estimate=pl.CostEstimate(flops=flops, bytes_accessed=size, transcendentals=0),
    )(*ins)


def split(value):
    high = value.astype(BF16)
    return high, (value - high.astype(F32)).astype(BF16)


def dot(a, b):
    return jnp.dot(a, b, preferred_element_type=F32)


def silu(value):
    return value / (1.0 + jnp.exp(-value))


def slope(value):
    sigma = 1.0 / (1.0 + jnp.exp(-value))
    return sigma * (1.0 + value * (1.0 - sigma))


def relative_blocks(flip):
    lat, y = lax.axis_index("lat"), lax.axis_index("rep")
    x, core = lat // 2, lat % 2
    order = []
    for r_core in range(2):
        c = core + r_core - 2 * core * r_core
        y_first = c == (1 if flip else 0)
        for r_first in range(2):
            for r_second in range(2):
                move_y = jnp.where(y_first, r_first, r_second)
                move_x = jnp.where(y_first, r_second, r_first)
                there_y = y + move_y - 2 * y * move_y
                there_x = x + move_x - 2 * x * move_x
                order.append(there_x * 4 + c * 2 + there_y)
    return order


def pack_rows(here, grad, one, two):
    rows = here.shape[0]
    even = lax.axis_index("lat") % 2 == 0
    for f, field in enumerate((here, grad)):
        low, high = field[0:2], field[rows - 2 : rows]
        one[f] = jnp.where(even, high, low)
        two[f] = jnp.where(even, low, high)


def pack_cols(here, grad, one, two, first, second):
    rows, cols = here.shape[:2]
    even_lat = lax.axis_index("lat") % 2 == 0
    even = lax.axis_index("lon") % 2 == 0
    for f, field in enumerate((here, grad)):
        low = jnp.where(even_lat, two[f], one[f])
        high = jnp.where(even_lat, one[f], two[f])
        for c in range(2):
            edges = []
            for col in (c, cols - 2 + c):
                edges.append(
                    jnp.concatenate(
                        [
                            low[:, col],
                            field[:, col],
                            high[:, col],
                            jnp.zeros((LINE - rows - 4, field.shape[2]), F32),
                        ],
                        axis=0,
                    )
                )
            first[f, c] = jnp.where(even, edges[1], edges[0])
            second[f, c] = jnp.where(even, edges[0], edges[1])


def pair_swap(one, two, axis, periodic):
    count = lax.axis_size(axis)
    pairs = [(i, i + 1) for i in range(0, count - 1, 2)]
    mates = [(i, i + 1) for i in range(1, count - 1, 2)]
    if periodic:
        mates.append((count - 1, 0))
    return tuple(
        lax.ppermute(block, axis, who + [(b, a) for a, b in who])
        for block, who in ((one, pairs), (two, mates))
    )


def prepare(weights, high, low):
    high[...], low[...] = split(weights[...])


def prepare_back(weights, high, low):
    size = weights.shape[1]
    for tap in range(9):
        there = 8 - tap
        block = weights[there * size : (there + 1) * size, :].T
        high[tap * size : (tap + 1) * size, :], low[tap * size : (tap + 1) * size, :] = split(block)


def turn(flip, value, high, low, scratch):
    channels = value.shape[1]
    each = channels // 8
    scratch[...] = value.T
    for i, block in enumerate(relative_blocks(flip)):
        part = scratch[pl.ds(pl.multiple_of(block * each, each), each), :]
        high[i * each : (i + 1) * each, :], low[i * each : (i + 1) * each, :] = split(part)


def turn_grad(grad, high, low, scratch):
    cells = grad.shape[0] * grad.shape[1]
    turn(False, grad[...].reshape(cells, grad.shape[2]), high, low, scratch)


def lay_taps(wide, x_high, x_low):
    rows, padded, channels = wide.shape
    cols = padded - 2 * EDGE
    for b in range(3):
        part = wide[:, EDGE - 1 + b : EDGE - 1 + b + cols, :].reshape(rows * cols, channels)
        high, low = split(part)
        x_high[:, b * channels : (b + 1) * channels] = high
        x_low[:, b * channels : (b + 1) * channels] = low


def convolve(x_high, x_low, first_row, rows, cols, w_high, w_low):
    channels = w_high.shape[1]
    total = None
    for a in range(3):
        cells = slice((first_row + a) * cols, (first_row + a + rows) * cols)
        taps = slice(a * 3 * channels, (a + 1) * 3 * channels)
        for x, w in ((x_high, w_high), (x_high, w_low), (x_low, w_high)):
            part = dot(x[cells, :], w[taps, :])
            total = part if total is None else total + part
    return total


def side_columns(mine_one, mine_two, got_one, got_two, f):
    even = lax.axis_index("lon") % 2 == 0

    def either(a, b):
        return jnp.where(even, a, b)

    left = [either(got_two[f, c], got_one[f, c]) for c in range(2)]
    left.append(either(mine_two[f, 0], mine_one[f, 0]))
    right = [either(mine_one[f, 1], mine_two[f, 1])]
    right += [either(got_one[f, c], got_two[f, c]) for c in range(2)]
    return left, right


def ring(left, right, w_high, w_low, r_high, r_low):
    channels = w_high.shape[1]
    for s, columns in enumerate((left, right)):
        for a in range(3):
            for b in range(3):
                high, low = split(columns[b])
                value = columns[b]
                if a:
                    value = jnp.concatenate(
                        [value[a:], jnp.zeros((a, value.shape[1]), F32)], axis=0
                    )
                place = (
                    slice(s * LINE, (s + 1) * LINE),
                    slice((a * 3 + b) * channels, (a * 3 + b + 1) * channels),
                )
                r_high[place], r_low[place] = split(value)
    return (
        dot(r_high[...], w_high[...])
        + dot(r_high[...], w_low[...])
        + dot(r_low[...], w_high[...])
    )


def spread(value, function, got_rows, columns, f, wide):
    rows, cols, channels = value.shape
    even_lat = lax.axis_index("lat") % 2 == 0
    one, two = got_rows
    wide[2 : rows + 2, EDGE : EDGE + cols, :] = function(value[...])
    wide[0:2, EDGE : EDGE + cols, :] = function(jnp.where(even_lat, two[f], one[f]))
    wide[rows + 2 : rows + 4, EDGE : EDGE + cols, :] = function(
        jnp.where(even_lat, one[f], two[f])
    )
    left, right = columns
    wide[:, EDGE - 1 : EDGE, :] = left[1][: rows + 4].reshape(rows + 4, 1, channels)
    wide[:, EDGE + cols : EDGE + cols + 1, :] = right[1][: rows + 4].reshape(rows + 4, 1, channels)


def inside(rows):
    row = lax.axis_index("lat") * rows - 1 + lax.broadcasted_iota(jnp.int32, (rows + 2, 1, 1), 0)
    return (row >= 0) & (row < rows * lax.axis_size("lat"))


def inside_line(rows):
    row = lax.axis_index("lat") * rows - 1 + lax.broadcasted_iota(jnp.int32, (LINE, 1), 0)
    return (row >= 0) & (row < rows * lax.axis_size("lat"))


def spread_ext(main, side, wide):
    tall, cols, channels = main.shape
    wide[:, EDGE : EDGE + cols, :] = main
    wide[:, EDGE - 1 : EDGE, :] = side[:tall].reshape(tall, 1, channels)
    wide[:, EDGE + cols : EDGE + cols + 1, :] = side[LINE : LINE + tall].reshape(tall, 1, channels)


def products(t_high, t_low, x_high, x_low, first_row, cells, cols, scale, away, keep):
    half = t_high.shape[0] // 2
    width = x_high.shape[1]
    for a in range(3):
        rows = slice((first_row + a) * cols, (first_row + a) * cols + cells)
        total = (
            dot(t_high[...], x_high[rows, :])
            + dot(t_high[...], x_low[rows, :])
            + dot(t_low[...], x_high[rows, :])
        ) * scale
        away[:, a * width : (a + 1) * width] = total[half:]
        keep[:, a * width : (a + 1) * width] = total[:half]


def hidden_kernel(
    scale, here, r1, r2, m1, m2, q1, q2, w_high, w_low, t_high, t_low,
    hidden, side, x1_high, x1_low, x2_high, x2_low, away, keep,
    wide, wide2, r_high, r_low,
):
    rows, cols, channels = here.shape
    left, right = side_columns(m1, m2, q1, q2, 0)
    left, right = [silu(v) for v in left], [silu(v) for v in right]
    spread(here, silu, (r1, r2), (left, right), 0, wide)
    lay_taps(wide, x1_high, x1_low)
    main = convolve(x1_high, x1_low, 0, rows + 2, cols, w_high, w_low)
    around = ring(left, right, w_high, w_low, r_high, r_low)
    hidden[...] = main
    side[...] = around
    act = jnp.where(inside(rows), silu(main).reshape(rows + 2, cols, channels), 0.0)
    line = inside_line(rows)
    around = jnp.where(jnp.concatenate([line, line], axis=0), silu(around), 0.0)
    spread_ext(act, around, wide2)
    lay_taps(wide2, x2_high, x2_low)
    products(t_high, t_low, x2_high, x2_low, 0, rows * cols, cols, scale, away, keep)


def inner_kernel(
    scale, grad, r1, r2, m1, m2, q1, q2, w_high, w_low, hidden, side, x1_high, x1_low,
    x3_high, x3_low, away, keep,
    wide, xc_high, xc_low, wide2, r_high, r_low, turned, t_high, t_low,
):
    rows, cols, channels = grad.shape
    columns = side_columns(m1, m2, q1, q2, 1)
    spread(grad, lambda v: v, (r1, r2), columns, 1, wide)
    lay_taps(wide, xc_high, xc_low)
    main = convolve(xc_high, xc_low, 0, rows + 2, cols, w_high, w_low) * slope(hidden[...])
    around = ring(*columns, w_high, w_low, r_high, r_low) * slope(side[...])
    main = jnp.where(inside(rows), main.reshape(rows + 2, cols, channels), 0.0)
    line = inside_line(rows)
    around = jnp.where(jnp.concatenate([line, line], axis=0), around, 0.0)
    turn(True, main[1 : rows + 1].reshape(rows * cols, channels), t_high, t_low, turned)
    products(t_high, t_low, x1_high, x1_low, 1, rows * cols, cols, scale, away, keep)
    spread_ext(main, around, wide2)
    lay_taps(wide2, x3_high, x3_low)


def output_kernel(here, x_high, x_low, w_high, w_low, out):
    rows, cols, channels = here.shape
    total = convolve(x_high, x_low, 0, rows, cols, w_high, w_low)
    out[...] = here[...] + total.reshape(rows, cols, channels)


def input_grad_kernel(here, grad, x_high, x_low, w_high, w_low, out):
    rows, cols, channels = here.shape
    total = convolve(x_high, x_low, 0, rows, cols, w_high, w_low)
    out[...] = grad[...] + total.reshape(rows, cols, channels) * slope(here[...])


def plane_perm(count, even, odd):
    return [(i, i ^ (odd if (i // 2) % 2 else even)) for i in range(count)]


def scatter_sum(away, keep, flip):
    half, taps = keep.shape
    lon, lat, rep = lax.axis_size("lon"), lax.axis_size("lat"), lax.axis_size("rep")
    plane = lat * rep
    axes = ("lat", "rep")
    one, two = (4, 1) if flip else (1, 4)
    held = keep + lax.ppermute(away, axes, plane_perm(plane, 2, 2))
    held = held[: half // 2] + lax.ppermute(held[half // 2 :], axes, plane_perm(plane, one, two))
    each = half // 4
    tail = held[:each] + lax.ppermute(held[each:], axes, plane_perm(plane, two, one))
    if lon != 4:
        return lax.psum_scatter(tail, "lon", scatter_dimension=1, tiled=True).T
    blocks = jnp.swapaxes(tail.reshape(each, lon, taps // lon), 0, 1)
    z = lax.axis_index("lon")
    total = lax.dynamic_index_in_dim(blocks, z, 0, keepdims=False)
    for step in range(1, lon):
        block = lax.dynamic_index_in_dim(blocks, z ^ step, 0, keepdims=False)
        total = total + lax.ppermute(block, "lon", [(i, i ^ step) for i in range(lon)])
    return total.T


def local(inputs, cotangent, first_weight, second_weight):
    here, grad = inputs[0], cotangent[0]
    rows, cols, channels = here.shape
    cells, tall = rows * cols, rows + 2
    width = 3 * channels
    scale = 1.0 / math.sqrt(
        cells * lax.axis_size("rep") * lax.axis_size("lat") * lax.axis_size("lon")
    )
    edge = ((2, 2, cols, channels), F32)
    one, two = call(pack_rows, [edge] * 2, [here, grad])
    r1, r2 = pair_swap(one, two, "lat", False)
    pair = [((9 * channels, channels), BF16)] * 2
    w1_high, w1_low = call(prepare, pair, [first_weight])
    t_high, t_low = call(
        turn_grad, [((channels, cells), BF16)] * 2, [grad], scratch=[((channels, cells), F32)]
    )
    line = ((2, 2, LINE, channels), F32)
    m1, m2 = call(pack_cols, [line] * 2, [here, grad, r1, r2])
    q1, q2 = pair_swap(m1, m2, "lon", True)
    b2_high, b2_low = call(prepare_back, pair, [second_weight])
    conv_flops = 2 * 3 * 9 * tall * cols * channels * channels
    grad_flops = 2 * 3 * 9 * cells * channels * channels
    lines = ((2 * LINE, channels), F32)
    wide = ((rows + 4, cols + 2 * EDGE, channels), F32)
    wide2 = ((tall, cols + 2 * EDGE, channels), F32)
    taps_1 = [(((rows + 4) * cols, width), BF16)] * 2
    taps_2 = [((tall * cols, width), BF16)] * 2
    around = [((2 * LINE, 3 * width), BF16)] * 2
    halves = [((channels // 2, 9 * channels), F32)] * 2
    hidden, side, x1_high, x1_low, x2_high, x2_low, away, keep = call(
        lambda *refs: hidden_kernel(scale, *refs),
        [((tall * cols, channels), F32), lines] + taps_1 + taps_2 + halves,
        [here, r1, r2, m1, m2, q1, q2, w1_high, w1_low, t_high, t_low],
        conv_flops + grad_flops,
        scratch=[wide, wide2] + around,
    )
    second_grad = scatter_sum(away, keep, False)
    x3_high, x3_low, away, keep = call(
        lambda *refs: inner_kernel(scale, *refs),
        taps_2 + halves,
        [grad, r1, r2, m1, m2, q1, q2, b2_high, b2_low, hidden, side, x1_high, x1_low],
        conv_flops + grad_flops,
        scratch=[wide] + taps_1 + [wide2] + around + [((channels, cells), F32)]
        + [((channels, cells), BF16)] * 2,
    )
    first_grad = scatter_sum(away, keep, True)
    w2_high, w2_low = call(prepare, pair, [second_weight])
    b1_high, b1_low = call(prepare_back, pair, [first_weight])
    shape = ((rows, cols, channels), F32)
    (output,) = call(
        output_kernel, [shape], [here, x2_high, x2_low, w2_high, w2_low], grad_flops
    )
    (input_grad,) = call(
        input_grad_kernel, [shape], [here, grad, x3_high, x3_low, b1_high, b1_low], grad_flops
    )
    return (output[None], input_grad[None], first_grad, second_grad)


def solution(mesh):
    in_specs = (P("rep", "lat", "lon", None), P("rep", "lat", "lon", None), P(), P())
    out_specs = (
        P("rep", "lat", "lon", None),
        P("rep", "lat", "lon", None),
        P("lon", ("lat", "rep")),
        P("lon", ("lat", "rep")),
    )
    return jax.shard_map(local, mesh=mesh, in_specs=in_specs, out_specs=out_specs, check_vma=False)
```

profile of v0, /device:TPU:0, one launch (start us, length us, event | category | flops | bytes accessed | tf_op | source)
XLA Modules:
  0.0 94.2 jit_solution(18283197870394587599)
XLA Ops:
  0.6 0.0 copy-start.2
  0.6 1.0 %copy-done.2 = f32[1,16,32,256]{3,2,1,0:T(8,128)S(1)} copy-done((f32[1,16,32,256]{3,2,1,0:T(8,128)S(1)}, f32[1,16,32,256]{3,2,1,0:T(8,128)}, u32[]{:S(2)}) %copy-start.2) | copy-done | bytes 524312
  1.7 1.0 %copy-done.5 = f32[1,16,32,256]{3,2,1,0:T(8,128)S(1)} copy-done((f32[1,16,32,256]{3,2,1,0:T(8,128)S(1)}, f32[1,16,32,256]{3,2,1,0:T(8,128)}, u32[]{:S(2)}) %copy-start.5) | copy-done | bytes 524312
  2.8 0.5 collective-permute-start
  3.3 0.8 collective-permute-start.1
  4.1 0.2 collective-permute-done.one.refs_1_
  4.3 0.0 collective-permute-done.1.two.refs_2_
  4.3 0.1 shard_map.76
  4.3 3.0 %collective-permute-start.2 = (f32[2,2,24,256]{3,2,1,0:T(8,128)S(1)}, f32[2,2,24,256]{3,2,1,0:T(8,128)S(1)}, u32[]{:S(2)}, u32[]{:S(2)}) collective-permute-start(f32[2,2,24,256]{3,2,1,0:T(8,128)S(1)} %get-tuple-element.32.refs_3_), channel_id=1, source_target_pairs={{0,8},{16,24},{8,0},{24,16},{1,9},{17,25},{9,1},{25,17},{2,10},{18... | collective-permute-start | bytes 294920 | tf_op jit(solution)/shard_map/ppermute | solution.py:106
  7.3 2.5 %collective-permute-start.3 = (f32[2,2,24,256]{3,2,1,0:T(8,128)S(1)}, f32[2,2,24,256]{3,2,1,0:T(8,128)S(1)}, u32[]{:S(2)}, u32[]{:S(2)}) collective-permute-start(f32[2,2,24,256]{3,2,1,0:T(8,128)S(1)} %get-tuple-element.33.refs_4_), channel_id=1, source_target_pairs={{8,16},{24,0},{16,8},{0,24},{9,17},{25,1},{17,9},{1,25},{10,18},{2... | collective-permute-start | bytes 294920 | tf_op jit(solution)/shard_map/ppermute | solution.py:106
  9.8 1.0 %copy-done.3 = f32[1,16,32,256]{3,2,1,0:T(8,128)S(1)} copy-done((f32[1,16,32,256]{3,2,1,0:T(8,128)S(1)}, f32[1,16,32,256]{3,2,1,0:T(8,128)}, u32[]{:S(2)}) %copy-start.3) | copy-done | bytes 524312
  10.9 0.3 shard_map.78
  11.1 0.0 copy-start.6
  11.2 0.3 shard_map.77
  11.5 2.2 %collective-permute-done.3.refs_6_ = f32[2,2,24,256]{3,2,1,0:T(8,128)S(1)} collective-permute-done((f32[2,2,24,256]{3,2,1,0:T(8,128)S(1)}, f32[2,2,24,256]{3,2,1,0:T(8,128)S(1)}, u32[]{:S(2)}, u32[]{:S(2)}) %collective-permute-start.3) | collective-permute-done | bytes 98336 | tf_op jit(solution)/shard_map/ppermute | solution.py:106
  13.8 8.2 %shard_map.79 = (f32[576,256]{1,0:T(8,128)S(1)}, f32[48,256]{1,0:T(8,128)S(1)}, bf16[640,768]{1,0:T(8,128)(2,1)S(1)}, bf16[640,768]{1,0:T(8,128)(2,1)S(1)}, bf16...) custom-call(f32[16,32,256]{2,1,0:T(8,128)S(1)} %bitcast.49, ...), custom_call_target="tpu_custom_call" | custom-call | flops 3850371072 | bytes 4063232 | tf_op jit(solution)/shard_map/pallas_call | solution.py:19
  22.0 0.0 copy-start.4
  22.0 4.4 %collective-permute-start.10 = (f32[128,2304]{1,0:T(8,128)S(1)}, f32[128,2304]{1,0:T(8,128)S(1)}, u32[]{:S(2)}, u32[]{:S(2)}) collective-permute-start(f32[128,2304]{1,0:T(8,128)S(1)} %get-tuple-element.55), channel_id=1, source_target_pairs={{0,2},{1,3},{2,0},{3,1},{4,6},{5,7},{6,4},{7,5},{8,10},{9,11},{10,... | collective-permute-start | bytes 3538952 | tf_op jit(solution)/shard_map/ppermute | solution.py:304
  26.4 0.7 shard_map.82
  27.1 9.3 %shard_map.83 = (bf16[576,768]{1,0:T(8,128)(2,1)S(1)}, bf16[576,768]{1,0:T(8,128)(2,1)S(1)}, f32[128,2304]{1,0:T(8,128)}, f32[128,2304]{1,0:T(8,128)S(1)}) custom-call(f32[16,32,256]{2,1,0:T(8,128)S(1)} %bitcast.45, f32[2,2,32,256]{3,2,1,0:T(8,128)S(1)} %collective-permute-done.one.refs_1_, f32[2,2,32,256]{3,2,1,0:T(8,128)S(1)} %collective-permute-done.1.two.refs_2_, ...), custom_call_target="tpu_custom_call" | custom-call | flops 3850371072 | bytes 6144000 | tf_op jit(solution)/shard_map/pallas_call | solution.py:19
  36.4 0.6 collective-permute-start.4
  37.0 0.0 collective-permute-done.10
  37.0 0.1 add.63
  37.2 0.2 copy-done.13
  37.4 0.3 copy-done.15
  37.7 0.9 slice.37
  38.6 1.5 %collective-permute-start.11 = (f32[64,2304]{1,0:T(8,128)}, f32[64,2304]{1,0:T(8,128)}, u32[]{:S(2)}, u32[]{:S(2)}) collective-permute-start(f32[64,2304]{1,0:T(8,128)} %slice.37), channel_id=1, source_target_pairs={{0,1},{1,0},{2,6},{3,7},{4,5},{5,4},{6,2},{7,3},{8,9},{9,8},{10,14... | collective-permute-start | bytes 1769480 | tf_op jit(solution)/shard_map/ppermute | solution.py:305
  40.1 0.3 shard_map.80
  40.5 1.0 %copy-done.9 = bf16[2304,256]{1,0:T(8,128)(2,1)} copy-done((bf16[2304,256]{1,0:T(8,128)(2,1)}, bf16[2304,256]{1,0:T(8,128)(2,1)S(1)}, u32[]{:S(2)}) %copy-start.9) | copy-done | bytes 1179672
  41.5 0.7 shard_map.84
  42.2 0.3 copy-done.11
  42.5 1.0 %copy-done.7 = bf16[2304,256]{1,0:T(8,128)(2,1)} copy-done((bf16[2304,256]{1,0:T(8,128)(2,1)}, bf16[2304,256]{1,0:T(8,128)(2,1)S(1)}, u32[]{:S(2)}) %copy-start.7) | copy-done | bytes 1179672
  43.6 1.3 %copy-done.10 = bf16[2304,256]{1,0:T(8,128)(2,1)S(1)} copy-done((bf16[2304,256]{1,0:T(8,128)(2,1)S(1)}, bf16[2304,256]{1,0:T(8,128)(2,1)}, u32[]{:S(2)}) %copy-start.10) | copy-done | bytes 1179672
  44.8 1.3 %copy-done.12 = bf16[2304,256]{1,0:T(8,128)(2,1)S(1)} copy-done((bf16[2304,256]{1,0:T(8,128)(2,1)S(1)}, bf16[2304,256]{1,0:T(8,128)(2,1)}, u32[]{:S(2)}) %copy-start.12) | copy-done | bytes 1179672
  46.1 1.2 %copy-done.18 = bf16[576,768]{1,0:T(8,128)(2,1)S(1)} copy-done((bf16[576,768]{1,0:T(8,128)(2,1)S(1)}, bf16[576,768]{1,0:T(8,128)(2,1)}, u32[]{:S(2)}) %copy-start.18) | copy-done | bytes 884760
  47.3 1.2 %copy-done.20 = bf16[576,768]{1,0:T(8,128)(2,1)S(1)} copy-done((bf16[576,768]{1,0:T(8,128)(2,1)S(1)}, bf16[576,768]{1,0:T(8,128)(2,1)}, u32[]{:S(2)}) %copy-start.20) | copy-done | bytes 884760
  48.4 2.8 %shard_map.81 = f32[16,32,256]{2,1,0:T(8,128)} custom-call(f32[16,32,256]{2,1,0:T(8,128)S(1)} %bitcast.50, bf16[576,768]{1,0:T(8,128)(2,1)S(1)} %copy-done.18, bf16[576,768]{1,0:T(8,128)(2,1)S(1)} %copy-done.20, bf16[2304,256]{1,0:T(8,128)(2,1)S(1)} %copy-done.10, bf16[2304,256]{1,0:T(8,128)(2,1)S(1)} %copy-done.12), custom_call_target="tpu_custom_call" | custom-call | flops 1811939328 | bytes 4653056 | tf_op jit(solution)/shard_map/pallas_call | solution.py:19
  51.2 0.0 collective-permute-done.4
  51.2 1.4 %add.53 = f32[128,2304]{1,0:T(8,128)S(1)} add(f32[128,2304]{1,0:T(8,128)S(1)} %get-tuple-element.52, f32[128,2304]{1,0:T(8,128)} %collective-permute-done.4) | non-fusion elementwise | flops 294912 | bytes 3538944 | tf_op jit(solution)/shard_map/add | solution.py:304
  52.7 3.0 %collective-permute-start.5 = (f32[64,2304]{1,0:T(8,128)S(1)}, f32[64,2304]{1,0:T(8,128)S(1)}, u32[]{:S(2)}, u32[]{:S(2)}) collective-permute-start(f32[64,2304]{1,0:T(8,128)S(1)} %slice.33), channel_id=1, source_target_pairs={{0,4},{1,5},{2,3},{3,2},{4,0},{5,1},{6,7},{7,6},{8,12},{9,13},{10,... | collective-permute-start | bytes 1769480 | tf_op jit(solution)/shard_map/ppermute | solution.py:305
  55.6 0.0 collective-permute-done.11
  55.7 1.1 %slice_add_fusion = f32[64,2304]{1,0:T(8,128)S(1)} fusion(f32[64,2304]{1,0:T(8,128)} %collective-permute-done.11, f32[128,2304]{1,0:T(8,128)S(1)} %copy-done.22), kind=kLoop, calls=%fused_computation | loop fusion | flops 147456 | bytes 1769472 | tf_op jit(solution)/shard_map/add | solution.py:305
  56.8 1.2 %collective-permute-start.12 = (f32[32,2304]{1,0:T(8,128)S(1)}, f32[32,2304]{1,0:T(8,128)S(1)}, u32[]{:S(2)}, u32[]{:S(2)}) collective-permute-start(f32[32,2304]{1,0:T(8,128)S(1)} %slice.39), channel_id=1, source_target_pairs={{0,4},{1,5},{2,3},{3,2},{4,0},{5,1},{6,7},{7,6},{8,12},{9,13},{10,... | collective-permute-start | bytes 884744 | tf_op jit(solution)/shard_map/ppermute | solution.py:307
  58.0 5.5 %collective-permute-done.5 = f32[64,2304]{1,0:T(8,128)S(1)} collective-permute-done((f32[64,2304]{1,0:T(8,128)S(1)}, f32[64,2304]{1,0:T(8,128)S(1)}, u32[]{:S(2)}, u32[]{:S(2)}) %collective-permute-start.5) | collective-permute-done | bytes 589856 | tf_op jit(solution)/shard_map/ppermute | solution.py:305
  63.5 0.1 slice_add_fusion.1
  63.6 0.8 slice.35
  64.3 0.5 collective-permute-start.6
  64.8 3.4 %collective-permute-done.12 = f32[32,2304]{1,0:T(8,128)S(1)} collective-permute-done((f32[32,2304]{1,0:T(8,128)S(1)}, f32[32,2304]{1,0:T(8,128)S(1)}, u32[]{:S(2)}, u32[]{:S(2)}) %collective-permute-start.12) | collective-permute-done | bytes 294944 | tf_op jit(solution)/shard_map/ppermute | solution.py:307
  68.2 1.0 %reshape.31 = f32[32,4,576]{2,1,0:T(4,128)} reshape(f32[32,2304]{1,0:T(8,128)S(1)} %slice_add_fusion.2) | data formatting | bytes 589824 | tf_op jit(solution)/shard_map/reshape | solution.py:310
  69.2 2.1 %collective-permute-done.6 = f32[32,2304]{1,0:T(8,128)S(1)} collective-permute-done((f32[32,2304]{1,0:T(8,128)}, f32[32,2304]{1,0:T(8,128)S(1)}, u32[]{:S(2)}, u32[]{:S(2)}) %collective-permute-start.6) | collective-permute-done | bytes 294944 | tf_op jit(solution)/shard_map/ppermute | solution.py:307
  71.3 0.7 slice_add_fusion.3
  72.0 2.1 %reshape.30 = f32[32,4,576]{2,1,0:T(4,128)} reshape(f32[32,2304]{1,0:T(8,128)} %slice_add_fusion.3) | data formatting | bytes 589824 | tf_op jit(solution)/shard_map/reshape | solution.py:310
  74.1 2.6 %constant_dynamic-slice_fusion.3 = (f32[32,1,576]{2,1,0:T(1,128)S(1)}, f32[32,1,576]{2,1,0:T(1,128)S(1)}, f32[32,1,576]{2,1,0:T(1,128)S(1)}, f32[32,1,576]{2,1,0...) fusion(f32[32,4,576]{2,1,0:T(4,128)} %reshape.31, ...), kind=kLoop, calls=%fused_computation.21 | loop fusion | bytes 1179664 | tf_op jit(solution)/shard_map/dynamic-slice.4
  76.7 2.6 %collective-permute-start.9 = (f32[32,576]{1,0:T(8,128)S(1)}, f32[32,576]{1,0:T(8,128)S(1)}, u32[]{:S(2)}, u32[]{:S(2)}) collective-permute-start(f32[32,576]{1,0:T(8,128)S(1)} %bitcast.53), channel_id=1, source_target_pairs={{0,24},{8,16},{16,8},{24,0},{1,25},{9,17},{17,9},{25,1},{2,26},{10... | collective-permute-start | bytes 221192 | tf_op jit(solution)/shard_map/ppermute | solution.py:315
  79.3 1.8 %collective-permute-start.7 = (f32[32,576]{1,0:T(8,128)S(1)}, f32[32,576]{1,0:T(8,128)S(1)}, u32[]{:S(2)}, u32[]{:S(2)}) collective-permute-start(f32[32,576]{1,0:T(8,128)S(1)} %bitcast.54), channel_id=1, source_target_pairs={{0,8},{8,0},{16,24},{24,16},{1,9},{9,1},{17,25},{25,17},{2,10},{10... | collective-permute-start | bytes 221192 | tf_op jit(solution)/shard_map/ppermute | solution.py:315
  81.1 1.2 %copy-done.16 = bf16[576,768]{1,0:T(8,128)(2,1)S(1)} copy-done((bf16[576,768]{1,0:T(8,128)(2,1)S(1)}, bf16[576,768]{1,0:T(8,128)(2,1)}, u32[]{:S(2)}) %copy-start.16) | copy-done | bytes 884760
  82.3 2.8 %shard_map.85 = f32[16,32,256]{2,1,0:T(8,128)} custom-call(f32[16,32,256]{2,1,0:T(8,128)S(1)} %bitcast.51, f32[16,32,256]{2,1,0:T(8,128)S(1)} %bitcast.46, bf16[576,768]{1,0:T(8,128)(2,1)S(1)} %copy-done.14, bf16[576,768]{1,0:T(8,128)(2,1)S(1)} %copy-done.16, bf16[2304,256]{1,0:T(8,128)(2,1)S(1)} %get-tuple-element.50.w_high, bf16[2304,256]{1,0:T(8,128)(2,1)S(1)} %copy-done.8), custom_call_target="tpu_custom_call" | custom-call | flops 1811939328 | bytes 5177344 | tf_op jit(solution)/shard_map/pallas_call | solution.py:19
  85.1 2.6 %collective-permute-start.15 = (f32[32,576]{1,0:T(8,128)S(1)}, f32[32,576]{1,0:T(8,128)S(1)}, u32[]{:S(2)}, u32[]{:S(2)}) collective-permute-start(f32[32,576]{1,0:T(8,128)S(1)} %bitcast.55), channel_id=1, source_target_pairs={{0,24},{8,16},{16,8},{24,0},{1,25},{9,17},{17,9},{25,1},{2,26},{10... | collective-permute-start | bytes 221192 | tf_op jit(solution)/shard_map/ppermute | solution.py:315
  87.7 0.0 collective-permute-done.9
  87.7 1.9 %collective-permute-start.13 = (f32[32,576]{1,0:T(8,128)S(1)}, f32[32,576]{1,0:T(8,128)S(1)}, u32[]{:S(2)}, u32[]{:S(2)}) collective-permute-start(f32[32,576]{1,0:T(8,128)S(1)} %bitcast.57), channel_id=1, source_target_pairs={{0,8},{8,0},{16,24},{24,16},{1,9},{9,1},{17,25},{25,17},{2,10},{10... | collective-permute-start | bytes 221192 | tf_op jit(solution)/shard_map/ppermute | solution.py:315
  89.6 0.7 fusion.5
  90.2 1.6 %collective-permute-done.15 = f32[32,576]{1,0:T(8,128)S(1)} collective-permute-done((f32[32,576]{1,0:T(8,128)S(1)}, f32[32,576]{1,0:T(8,128)S(1)}, u32[]{:S(2)}, u32[]{:S(2)}) %collective-permute-start.15) | collective-permute-done | bytes 73760 | tf_op jit(solution)/shard_map/ppermute | solution.py:315
  91.9 1.6 %collective-permute-done.14 = f32[32,576]{1,0:T(8,128)S(1)} collective-permute-done((f32[32,576]{1,0:T(8,128)S(1)}, f32[32,576]{1,0:T(8,128)S(1)}, u32[]{:S(2)}, u32[]{:S(2)}) %collective-permute-start.14) | collective-permute-done | bytes 73760 | tf_op jit(solution)/shard_map/ppermute | solution.py:315
  93.5 0.7 fusion.2
  (46 shorter events, 0.2 us)
Async XLA Ops:
  0.6 1.0 %copy-start.2 = (f32[1,16,32,256]{3,2,1,0:T(8,128)S(1)}, f32[1,16,32,256]{3,2,1,0:T(8,128)}, u32[]{:S(2)}) copy-start(f32[1,16,32,256]{3,2,1,0:T(8,128)} %param.5) | copy-start | bytes 1572868
  1.7 1.0 %copy-start.5 = (f32[1,16,32,256]{3,2,1,0:T(8,128)S(1)}, f32[1,16,32,256]{3,2,1,0:T(8,128)}, u32[]{:S(2)}) copy-start(f32[1,16,32,256]{3,2,1,0:T(8,128)} %param.4) | copy-start | bytes 1572868
  2.7 8.4 %copy-start.1 = (f32[2304,256]{1,0:T(8,128)S(1)}, f32[2304,256]{1,0:T(8,128)}, u32[]{:S(2)}) copy-start(f32[2304,256]{1,0:T(8,128)} %weights.7) | copy-start | bytes 7077892
  2.8 1.5 %collective-permute-start = (f32[2,2,32,256]{3,2,1,0:T(8,128)S(1)}, f32[2,2,32,256]{3,2,1,0:T(8,128)S(1)}, u32[]{:S(2)}, u32[]{:S(2)}) collective-permute-start(f32[2,2,32,256]{3,2,1,0:T(8,128)S(1)} %get-tuple-element.30), channel_id=1, source_target_pairs={{0,2},{4,6},{2,0},{6,4},{1,3},{5,7},{3,1},{7,5},{8,10},{12,14},{10... | collective-permute-start | bytes 393224 | tf_op jit(solution)/shard_map/ppermute | solution.py:106
  3.3 1.0 %collective-permute-start.1 = (f32[2,2,32,256]{3,2,1,0:T(8,128)S(1)}, f32[2,2,32,256]{3,2,1,0:T(8,128)S(1)}, u32[]{:S(2)}, u32[]{:S(2)}) collective-permute-start(f32[2,2,32,256]{3,2,1,0:T(8,128)S(1)} %get-tuple-element.31), channel_id=1, source_target_pairs={{2,4},{4,2},{3,5},{5,3},{10,12},{12,10},{11,13},{13,11},{18,20},{2... | collective-permute-start | bytes 393224 | tf_op jit(solution)/shard_map/ppermute | solution.py:106
  4.3 7.2 %collective-permute-start.2 = (f32[2,2,24,256]{3,2,1,0:T(8,128)S(1)}, f32[2,2,24,256]{3,2,1,0:T(8,128)S(1)}, u32[]{:S(2)}, u32[]{:S(2)}) collective-permute-start(f32[2,2,24,256]{3,2,1,0:T(8,128)S(1)} %get-tuple-element.32.refs_3_), channel_id=1, source_target_pairs={{0,8},{16,24},{8,0},{24,16},{1,9},{17,25},{9,1},{25,17},{2,10},{18... | collective-permute-start | bytes 294920 | tf_op jit(solution)/shard_map/ppermute | solution.py:106
  7.3 6.4 %collective-permute-start.3 = (f32[2,2,24,256]{3,2,1,0:T(8,128)S(1)}, f32[2,2,24,256]{3,2,1,0:T(8,128)S(1)}, u32[]{:S(2)}, u32[]{:S(2)}) collective-permute-start(f32[2,2,24,256]{3,2,1,0:T(8,128)S(1)} %get-tuple-element.33.refs_4_), channel_id=1, source_target_pairs={{8,16},{24,0},{16,8},{0,24},{9,17},{25,1},{17,9},{1,25},{10,18},{2... | collective-permute-start | bytes 294920 | tf_op jit(solution)/shard_map/ppermute | solution.py:106
  9.8 1.0 %copy-start.3 = (f32[1,16,32,256]{3,2,1,0:T(8,128)S(1)}, f32[1,16,32,256]{3,2,1,0:T(8,128)}, u32[]{:S(2)}) copy-start(f32[1,16,32,256]{3,2,1,0:T(8,128)} %param.5) | copy-start | bytes 1572868
  11.1 2.6 %copy-start.6 = (f32[1,16,32,256]{3,2,1,0:T(8,128)S(1)}, f32[1,16,32,256]{3,2,1,0:T(8,128)}, u32[]{:S(2)}) copy-start(f32[1,16,32,256]{3,2,1,0:T(8,128)} %param.4) | copy-start | bytes 1572868
  13.8 12.6 %copy-start = (f32[2304,256]{1,0:T(8,128)S(1)}, f32[2304,256]{1,0:T(8,128)}, u32[]{:S(2)}) copy-start(f32[2304,256]{1,0:T(8,128)} %weights.6) | copy-start | bytes 7077892
  22.0 5.1 %copy-start.17 = (bf16[576,768]{1,0:T(8,128)(2,1)}, bf16[576,768]{1,0:T(8,128)(2,1)S(1)}, u32[]{:S(2)}) copy-start(bf16[576,768]{1,0:T(8,128)(2,1)S(1)} %get-tuple-element.38.x_high) | copy-start | bytes 2654212
  22.0 5.1 %copy-start.19 = (bf16[576,768]{1,0:T(8,128)(2,1)}, bf16[576,768]{1,0:T(8,128)(2,1)S(1)}, u32[]{:S(2)}) copy-start(bf16[576,768]{1,0:T(8,128)(2,1)S(1)} %get-tuple-element.39.x_low) | copy-start | bytes 2654212
  22.0 5.1 %copy-start.4 = (f32[1,16,32,256]{3,2,1,0:T(8,128)S(1)}, f32[1,16,32,256]{3,2,1,0:T(8,128)}, u32[]{:S(2)}) copy-start(f32[1,16,32,256]{3,2,1,0:T(8,128)} %param.5) | copy-start | bytes 1572868
  22.0 15.0 %collective-permute-start.10 = (f32[128,2304]{1,0:T(8,128)S(1)}, f32[128,2304]{1,0:T(8,128)S(1)}, u32[]{:S(2)}, u32[]{:S(2)}) collective-permute-start(f32[128,2304]{1,0:T(8,128)S(1)} %get-tuple-element.55), channel_id=1, source_target_pairs={{0,2},{1,3},{2,0},{3,1},{4,6},{5,7},{6,4},{7,5},{8,10},{9,11},{10,... | collective-permute-start | bytes 3538952 | tf_op jit(solution)/shard_map/ppermute | solution.py:304
  36.4 1.0 %copy-start.13 = (bf16[576,768]{1,0:T(8,128)(2,1)}, bf16[576,768]{1,0:T(8,128)(2,1)S(1)}, u32[]{:S(2)}) copy-start(bf16[576,768]{1,0:T(8,128)(2,1)S(1)} %get-tuple-element.48.x_high) | copy-start | bytes 2654212
  36.4 1.3 %copy-start.15 = (bf16[576,768]{1,0:T(8,128)(2,1)}, bf16[576,768]{1,0:T(8,128)(2,1)S(1)}, u32[]{:S(2)}) copy-start(bf16[576,768]{1,0:T(8,128)(2,1)S(1)} %get-tuple-element.49.x_low) | copy-start | bytes 2654212
  36.4 14.8 %collective-permute-start.4 = (f32[128,2304]{1,0:T(8,128)}, f32[128,2304]{1,0:T(8,128)}, u32[]{:S(2)}, u32[]{:S(2)}) collective-permute-start(f32[128,2304]{1,0:T(8,128)} %get-tuple-element.53), channel_id=1, source_target_pairs={{0,2},{1,3},{2,0},{3,1},{4,6},{5,7},{6,4},{7,5},{8,10},{9,11},{10,... | collective-permute-start | bytes 3538952 | tf_op jit(solution)/shard_map/ppermute | solution.py:304
  37.7 2.8 %copy-start.21 = (f32[128,2304]{1,0:T(8,128)}, f32[128,2304]{1,0:T(8,128)S(1)}, u32[]{:S(2)}) copy-start(f32[128,2304]{1,0:T(8,128)S(1)} %add.63) | copy-start | bytes 3538948
  38.6 17.1 %collective-permute-start.11 = (f32[64,2304]{1,0:T(8,128)}, f32[64,2304]{1,0:T(8,128)}, u32[]{:S(2)}, u32[]{:S(2)}) collective-permute-start(f32[64,2304]{1,0:T(8,128)} %slice.37), channel_id=1, source_target_pairs={{0,1},{1,0},{2,6},{3,7},{4,5},{5,4},{6,2},{7,3},{8,9},{9,8},{10,14... | collective-permute-start | bytes 1769480 | tf_op jit(solution)/shard_map/ppermute | solution.py:305
  40.5 1.0 %copy-start.9 = (bf16[2304,256]{1,0:T(8,128)(2,1)}, bf16[2304,256]{1,0:T(8,128)(2,1)S(1)}, u32[]{:S(2)}) copy-start(bf16[2304,256]{1,0:T(8,128)(2,1)S(1)} %get-tuple-element.40.w_high) | copy-start | bytes 3538948
  41.5 1.0 %copy-start.11 = (bf16[2304,256]{1,0:T(8,128)(2,1)}, bf16[2304,256]{1,0:T(8,128)(2,1)S(1)}, u32[]{:S(2)}) copy-start(bf16[2304,256]{1,0:T(8,128)(2,1)S(1)} %get-tuple-element.41.w_low) | copy-start | bytes 3538948
  42.5 1.0 %copy-start.7 = (bf16[2304,256]{1,0:T(8,128)(2,1)}, bf16[2304,256]{1,0:T(8,128)(2,1)S(1)}, u32[]{:S(2)}) copy-start(bf16[2304,256]{1,0:T(8,128)(2,1)S(1)} %get-tuple-element.51.w_low) | copy-start | bytes 3538948
  43.5 1.3 %copy-start.10 = (bf16[2304,256]{1,0:T(8,128)(2,1)S(1)}, bf16[2304,256]{1,0:T(8,128)(2,1)}, u32[]{:S(2)}) copy-start(bf16[2304,256]{1,0:T(8,128)(2,1)} %copy-done.9) | copy-start | bytes 3538948
  44.8 1.3 %copy-start.12 = (bf16[2304,256]{1,0:T(8,128)(2,1)S(1)}, bf16[2304,256]{1,0:T(8,128)(2,1)}, u32[]{:S(2)}) copy-start(bf16[2304,256]{1,0:T(8,128)(2,1)} %copy-done.11) | copy-start | bytes 3538948
  46.1 1.2 %copy-start.18 = (bf16[576,768]{1,0:T(8,128)(2,1)S(1)}, bf16[576,768]{1,0:T(8,128)(2,1)}, u32[]{:S(2)}) copy-start(bf16[576,768]{1,0:T(8,128)(2,1)} %copy-done.17) | copy-start | bytes 2654212
  47.3 1.2 %copy-start.20 = (bf16[576,768]{1,0:T(8,128)(2,1)S(1)}, bf16[576,768]{1,0:T(8,128)(2,1)}, u32[]{:S(2)}) copy-start(bf16[576,768]{1,0:T(8,128)(2,1)} %copy-done.19) | copy-start | bytes 2654212
  52.6 3.0 %copy-start.22 = (f32[128,2304]{1,0:T(8,128)S(1)}, f32[128,2304]{1,0:T(8,128)}, u32[]{:S(2)}) copy-start(f32[128,2304]{1,0:T(8,128)} %copy-done.21) | copy-start | bytes 3538948
  52.7 10.8 %collective-permute-start.5 = (f32[64,2304]{1,0:T(8,128)S(1)}, f32[64,2304]{1,0:T(8,128)S(1)}, u32[]{:S(2)}, u32[]{:S(2)}) collective-permute-start(f32[64,2304]{1,0:T(8,128)S(1)} %slice.33), channel_id=1, source_target_pairs={{0,4},{1,5},{2,3},{3,2},{4,0},{5,1},{6,7},{7,6},{8,12},{9,13},{10,... | collective-permute-start | bytes 1769480 | tf_op jit(solution)/shard_map/ppermute | solution.py:305
  56.8 11.4 %collective-permute-start.12 = (f32[32,2304]{1,0:T(8,128)S(1)}, f32[32,2304]{1,0:T(8,128)S(1)}, u32[]{:S(2)}, u32[]{:S(2)}) collective-permute-start(f32[32,2304]{1,0:T(8,128)S(1)} %slice.39), channel_id=1, source_target_pairs={{0,4},{1,5},{2,3},{3,2},{4,0},{5,1},{6,7},{7,6},{8,12},{9,13},{10,... | collective-permute-start | bytes 884744 | tf_op jit(solution)/shard_map/ppermute | solution.py:307
  64.3 6.9 %collective-permute-start.6 = (f32[32,2304]{1,0:T(8,128)}, f32[32,2304]{1,0:T(8,128)S(1)}, u32[]{:S(2)}, u32[]{:S(2)}) collective-permute-start(f32[32,2304]{1,0:T(8,128)} %slice.35), channel_id=1, source_target_pairs={{0,1},{1,0},{2,6},{3,7},{4,5},{5,4},{6,2},{7,3},{8,9},{9,8},{10,14... | collective-permute-start | bytes 884744 | tf_op jit(solution)/shard_map/ppermute | solution.py:307
  72.0 9.1 %copy-start.8 = (bf16[2304,256]{1,0:T(8,128)(2,1)S(1)}, bf16[2304,256]{1,0:T(8,128)(2,1)}, u32[]{:S(2)}) copy-start(bf16[2304,256]{1,0:T(8,128)(2,1)} %copy-done.7) | copy-start | bytes 3538948
  74.1 7.1 %copy-start.14 = (bf16[576,768]{1,0:T(8,128)(2,1)S(1)}, bf16[576,768]{1,0:T(8,128)(2,1)}, u32[]{:S(2)}) copy-start(bf16[576,768]{1,0:T(8,128)(2,1)} %copy-done.13) | copy-start | bytes 2654212
  76.7 11.0 %collective-permute-start.9 = (f32[32,576]{1,0:T(8,128)S(1)}, f32[32,576]{1,0:T(8,128)S(1)}, u32[]{:S(2)}, u32[]{:S(2)}) collective-permute-start(f32[32,576]{1,0:T(8,128)S(1)} %bitcast.53), channel_id=1, source_target_pairs={{0,24},{8,16},{16,8},{24,0},{1,25},{9,17},{17,9},{25,1},{2,26},{10... | collective-permute-start | bytes 221192 | tf_op jit(solution)/shard_map/ppermute | solution.py:315
  79.3 10.3 %collective-permute-start.8 = (f32[32,576]{1,0:T(8,128)S(1)}, f32[32,576]{1,0:T(8,128)S(1)}, u32[]{:S(2)}, u32[]{:S(2)}) collective-permute-start(f32[32,576]{1,0:T(8,128)S(1)} %bitcast.52), channel_id=1, source_target_pairs={{0,16},{8,24},{16,0},{24,8},{1,17},{9,25},{17,1},{25,9},{2,18},{10... | collective-permute-start | bytes 221192 | tf_op jit(solution)/shard_map/ppermute | solution.py:315
  79.3 10.2 %collective-permute-start.7 = (f32[32,576]{1,0:T(8,128)S(1)}, f32[32,576]{1,0:T(8,128)S(1)}, u32[]{:S(2)}, u32[]{:S(2)}) collective-permute-start(f32[32,576]{1,0:T(8,128)S(1)} %bitcast.54), channel_id=1, source_target_pairs={{0,8},{8,0},{16,24},{24,16},{1,9},{9,1},{17,25},{25,17},{2,10},{10... | collective-permute-start | bytes 221192 | tf_op jit(solution)/shard_map/ppermute | solution.py:315
  81.1 1.2 %copy-start.16 = (bf16[576,768]{1,0:T(8,128)(2,1)S(1)}, bf16[576,768]{1,0:T(8,128)(2,1)}, u32[]{:S(2)}) copy-start(bf16[576,768]{1,0:T(8,128)(2,1)} %copy-done.15) | copy-start | bytes 2654212
  85.1 6.8 %collective-permute-start.15 = (f32[32,576]{1,0:T(8,128)S(1)}, f32[32,576]{1,0:T(8,128)S(1)}, u32[]{:S(2)}, u32[]{:S(2)}) collective-permute-start(f32[32,576]{1,0:T(8,128)S(1)} %bitcast.55), channel_id=1, source_target_pairs={{0,24},{8,16},{16,8},{24,0},{1,25},{9,17},{17,9},{25,1},{2,26},{10... | collective-permute-start | bytes 221192 | tf_op jit(solution)/shard_map/ppermute | solution.py:315
  87.7 5.8 %collective-permute-start.14 = (f32[32,576]{1,0:T(8,128)S(1)}, f32[32,576]{1,0:T(8,128)S(1)}, u32[]{:S(2)}, u32[]{:S(2)}) collective-permute-start(f32[32,576]{1,0:T(8,128)S(1)} %bitcast.56), channel_id=1, source_target_pairs={{0,16},{8,24},{16,0},{24,8},{1,17},{9,25},{17,1},{25,9},{2,18},{10... | collective-permute-start | bytes 221192 | tf_op jit(solution)/shard_map/ppermute | solution.py:315
  87.7 5.8 %collective-permute-start.13 = (f32[32,576]{1,0:T(8,128)S(1)}, f32[32,576]{1,0:T(8,128)S(1)}, u32[]{:S(2)}, u32[]{:S(2)}) collective-permute-start(f32[32,576]{1,0:T(8,128)S(1)} %bitcast.57), channel_id=1, source_target_pairs={{0,8},{8,0},{16,24},{24,16},{1,9},{9,1},{17,25},{25,17},{2,10},{10... | collective-permute-start | bytes 221192 | tf_op jit(solution)/shard_map/ppermute | solution.py:315
where the time goes:
time: 94.8 us; the launch traced here: 94.2 us
  starting transfers between devices  26.9 us (28%)
  Pallas kernels  25.5 us (27%)
  local copies, waits for them, and re-layouts  19.5 us (21%)
  waiting for transfers between devices  16.6 us (18%)
  other arithmetic  4.79 us (5%)
    pallas_call x11, Pallas kernels, call(): pl.pallas_call(body, out_shape=[jax.ShapeDtypeStruct(shape, dtype) for sh...  25.5 us
    unnamed x52, local copies, waits for them, and re-layouts  12.2 us
    ppermute x6, starting transfers between devices, scatter_sum(): lax.ppermute(block, 'lon', [(i, i ^ step) for i in range(lon)])  8.87 us
    ppermute x4, starting transfers between devices, pair_swap(): lax.ppermute(block, axis, who + [(b, a) for a, b in who])  6.78 us
    ppermute x2, waiting for transfers between devices, scatter_sum(): lax.ppermute(held[half // 2:], axes, plane_perm(plane, one, two))  5.5 us
    ppermute x2, waiting for transfers between devices, scatter_sum(): lax.ppermute(held[each:], axes, plane_perm(plane, two, one))  5.41 us
    ppermute x2, starting transfers between devices, scatter_sum(): held = keep + lax.ppermute(away, axes, plane_perm(plane, 2, 2))  5 us
    ppermute x2, starting transfers between devices, scatter_sum(): lax.ppermute(held[half // 2:], axes, plane_perm(plane, one, two))  4.5 us
  transfers between devices with their start and end apart: 16, of which 7 were waited for; matrix products, arithmetic and copies ran while one was open for 7% of the time, Pallas kernels for 18%

commit v1 on v0

--- a/solution.py
+++ b/solution.py
@@ -14,12 +14,18 @@
 EDGE = 8
 
 
-def call(body, outs, ins, flops=0, scratch=(), limit=32):
+def call(body, outs, ins, flops=0, scratch=(), limit=16, after=()):
     size = sum(math.prod(a.shape) * a.dtype.itemsize for a in ins)
+    used, skip = len(ins), len(after)
+
+    def kernel(*refs):
+        body(*refs[:used], *refs[used + skip :])
+
+    ins = list(ins) + list(after)
     return pl.pallas_call(
-        body,
+        kernel,
         out_shape=[jax.ShapeDtypeStruct(shape, dtype) for shape, dtype in outs],
-        in_specs=[VMEM] * len(ins),
+        in_specs=[VMEM] * used + [pl.BlockSpec(memory_space=pl.ANY)] * skip,
         out_specs=[VMEM] * len(outs),
         scratch_shapes=[pltpu.VMEM(shape, dtype) for shape, dtype in scratch],
         compiler_params=pltpu.CompilerParams(vmem_limit_bytes=limit * 1024 * 1024),
@@ -62,13 +68,28 @@
     return order
 
 
-def pack_rows(here, grad, one, two):
-    rows = here.shape[0]
+def pack_rows(low_here, high_here, low_grad, high_grad, one, two):
     even = lax.axis_index("lat") % 2 == 0
-    for f, field in enumerate((here, grad)):
-        low, high = field[0:2], field[rows - 2 : rows]
-        one[f] = jnp.where(even, high, low)
-        two[f] = jnp.where(even, low, high)
+    for f, (low, high) in enumerate(((low_here, high_here), (low_grad, high_grad))):
+        one[f] = jnp.where(even, high[...], low[...])
+        two[f] = jnp.where(even, low[...], high[...])
+
+
+def rows_messages(here, grad):
+    rows, cols, channels = here.shape
+    block = (2, cols, channels)
+    low = pl.BlockSpec(block, lambda i: (0, 0, 0))
+    high = pl.BlockSpec(block, lambda i: (rows // 2 - 1, 0, 0))
+    shape = (2, *block)
+    whole = pl.BlockSpec(shape, lambda i: (0, 0, 0, 0))
+    return pl.pallas_call(
+        pack_rows,
+        grid=(1,),
+        out_shape=[jax.ShapeDtypeStruct(shape, F32)] * 2,
+        in_specs=[low, high] * 2,
+        out_specs=[VMEM] * 2,
+        compiler_params=pltpu.CompilerParams(vmem_limit_bytes=4 * 1024 * 1024),
+    )(here, here, grad, grad)
 
 
 def pack_cols(here, grad, one, two, first, second):
@@ -260,9 +281,9 @@
 
 
 def inner_kernel(
-    scale, grad, r1, r2, m1, m2, q1, q2, w_high, w_low, hidden, side, x1_high, x1_low,
-    x3_high, x3_low, away, keep,
-    wide, xc_high, xc_low, wide2, r_high, r_low, turned, t_high, t_low,
+    grad, r1, r2, m1, m2, q1, q2, w_high, w_low, hidden, side,
+    x3_high, x3_low, t_high, t_low,
+    wide, xc_high, xc_low, wide2, r_high, r_low, turned,
 ):
     rows, cols, channels = grad.shape
     columns = side_columns(m1, m2, q1, q2, 1)
@@ -274,9 +295,12 @@
     line = inside_line(rows)
     around = jnp.where(jnp.concatenate([line, line], axis=0), around, 0.0)
     turn(True, main[1 : rows + 1].reshape(rows * cols, channels), t_high, t_low, turned)
-    products(t_high, t_low, x1_high, x1_low, 1, rows * cols, cols, scale, away, keep)
     spread_ext(main, around, wide2)
     lay_taps(wide2, x3_high, x3_low)
+
+
+def inner_products(scale, cols, t_high, t_low, x1_high, x1_low, away, keep):
+    products(t_high, t_low, x1_high, x1_low, 1, t_high.shape[1], cols, scale, away, keep)
 
 
 def output_kernel(here, x_high, x_low, w_high, w_low, out):
@@ -295,24 +319,50 @@
     return [(i, i ^ (odd if (i // 2) % 2 else even)) for i in range(count)]
 
 
-def scatter_sum(away, keep, flip):
-    half, taps = keep.shape
-    lon, lat, rep = lax.axis_size("lon"), lax.axis_size("lat"), lax.axis_size("rep")
-    plane = lat * rep
-    axes = ("lat", "rep")
-    one, two = (4, 1) if flip else (1, 4)
-    held = keep + lax.ppermute(away, axes, plane_perm(plane, 2, 2))
-    held = held[: half // 2] + lax.ppermute(held[half // 2 :], axes, plane_perm(plane, one, two))
-    each = half // 4
-    tail = held[:each] + lax.ppermute(held[each:], axes, plane_perm(plane, two, one))
+def plane_swap(away, flip, second):
+    count = lax.axis_size("lat") * lax.axis_size("rep")
+    one, two = (1, 4) if flip == second else (4, 1)
+    return lax.ppermute(away, ("lat", "rep"), plane_perm(count, one, two))
+
+
+def core_swap(away):
+    count = lax.axis_size("lat") * lax.axis_size("rep")
+    return lax.ppermute(away, ("lat", "rep"), plane_perm(count, 2, 2))
+
+
+def add_halves(keep, got, next_keep, next_away):
+    half = keep.shape[0] // 2
+    next_keep[...] = keep[:half] + got[:half]
+    next_away[...] = keep[half:] + got[half:]
+
+
+def add_both(keep_1, got_1, keep_2, got_2, *outs):
+    add_halves(keep_1, got_1, *outs[:2])
+    add_halves(keep_2, got_2, *outs[2:])
+
+
+def cut_blocks(keep, got, *blocks):
+    total = keep[...] + got[...]
+    count = len(blocks)
+    size = total.shape[1] // count
+    parts = [total[:, i * size : (i + 1) * size] for i in range(count)]
+    z = lax.axis_index("lon")
+    for step, block in enumerate(blocks):
+        value = parts[step]
+        for place in range(1, count):
+            value = jnp.where(z == place, parts[place ^ step], value)
+        block[...] = value
+
+
+def last_sum(keep, got, after=()):
+    each, taps = keep.shape
+    lon = lax.axis_size("lon")
     if lon != 4:
-        return lax.psum_scatter(tail, "lon", scatter_dimension=1, tiled=True).T
-    blocks = jnp.swapaxes(tail.reshape(each, lon, taps // lon), 0, 1)
-    z = lax.axis_index("lon")
-    total = lax.dynamic_index_in_dim(blocks, z, 0, keepdims=False)
+        return lax.psum_scatter(keep + got, "lon", scatter_dimension=1, tiled=True).T
+    blocks = call(cut_blocks, [((each, taps // lon), F32)] * lon, [keep, got], after=after)
+    total = blocks[0]
     for step in range(1, lon):
-        block = lax.dynamic_index_in_dim(blocks, z ^ step, 0, keepdims=False)
-        total = total + lax.ppermute(block, "lon", [(i, i ^ step) for i in range(lon)])
+        total = total + lax.ppermute(blocks[step], "lon", [(i, i ^ step) for i in range(lon)])
     return total.T
 
 
@@ -324,8 +374,7 @@
     scale = 1.0 / math.sqrt(
         cells * lax.axis_size("rep") * lax.axis_size("lat") * lax.axis_size("lon")
     )
-    edge = ((2, 2, cols, channels), F32)
-    one, two = call(pack_rows, [edge] * 2, [here, grad])
+    one, two = rows_messages(here, grad)
     r1, r2 = pair_swap(one, two, "lat", False)
     pair = [((9 * channels, channels), BF16)] * 2
     w1_high, w1_low = call(prepare, pair, [first_weight])
@@ -352,25 +401,54 @@
         conv_flops + grad_flops,
         scratch=[wide, wide2] + around,
     )
-    second_grad = scatter_sum(away, keep, False)
-    x3_high, x3_low, away, keep = call(
-        lambda *refs: inner_kernel(scale, *refs),
-        taps_2 + halves,
-        [grad, r1, r2, m1, m2, q1, q2, b2_high, b2_low, hidden, side, x1_high, x1_low],
-        conv_flops + grad_flops,
-        scratch=[wide] + taps_1 + [wide2] + around + [((channels, cells), F32)]
-        + [((channels, cells), BF16)] * 2,
-    )
-    first_grad = scatter_sum(away, keep, True)
+    got_2 = core_swap(away)
+    keep_2 = keep
+    x3_high, x3_low, t_high, t_low = call(
+        inner_kernel,
+        taps_2 + [((channels, cells), BF16)] * 2,
+        [grad, r1, r2, m1, m2, q1, q2, b2_high, b2_low, hidden, side],
+        conv_flops,
+        scratch=[wide] + taps_1 + [wide2] + around + [((channels, cells), F32)],
+    )
+
+    def halves_of(count):
+        return [((count, 9 * channels), F32)] * 2
+
+    keep_2, away_2 = call(add_halves, halves_of(channels // 4), [keep_2, got_2], after=[t_low])
+    got_2 = plane_swap(away_2, False, False)
+    away, keep_1 = call(
+        lambda *refs: inner_products(scale, cols, *refs),
+        halves,
+        [t_high, t_low, x1_high, x1_low],
+        grad_flops,
+        after=[keep_2],
+    )
+    got_1 = core_swap(away)
     w2_high, w2_low = call(prepare, pair, [second_weight])
     b1_high, b1_low = call(prepare_back, pair, [first_weight])
     shape = ((rows, cols, channels), F32)
     (output,) = call(
-        output_kernel, [shape], [here, x2_high, x2_low, w2_high, w2_low], grad_flops
-    )
+        output_kernel, [shape], [here, x2_high, x2_low, w2_high, w2_low], grad_flops, after=[keep_1]
+    )
+    keep_1, away_1, keep_2, away_2 = call(
+        add_both,
+        halves_of(channels // 4) + halves_of(channels // 8),
+        [keep_1, got_1, keep_2, got_2],
+        after=[output],
+    )
+    got_1 = plane_swap(away_1, True, False)
+    got_2 = plane_swap(away_2, False, True)
     (input_grad,) = call(
-        input_grad_kernel, [shape], [here, grad, x3_high, x3_low, b1_high, b1_low], grad_flops
-    )
+        input_grad_kernel,
+        [shape],
+        [here, grad, x3_high, x3_low, b1_high, b1_low],
+        grad_flops,
+        after=[keep_2],
+    )
+    second_grad = last_sum(keep_2, got_2, after=[input_grad])
+    keep_1, away_1 = call(add_halves, halves_of(channels // 8), [keep_1, got_1])
+    got_1 = plane_swap(away_1, True, True)
+    first_grad = last_sum(keep_1, got_1)
     return (output[None], input_grad[None], first_grad, second_grad)
 
 

time: 94.8 us -> 80 us (0.84)
  local copies, waits for them, and re-layouts: 19.5 us -> 6.26 us
  waiting for transfers between devices: 16.6 us -> 22.9 us
  other arithmetic: 4.79 us -> 1.31 us
  Pallas kernels: 25.5 us -> 23 us
  starting transfers between devices: 26.9 us -> 25.2 us
    unnamed x52 -> x20, local copies, waits for them, and re-layouts: 12.2 us -> 6.26 us
    ppermute x12, waiting for transfers between devices: 14.2 us -> 19.4 us  [the longest x4 12.8 us: plane_swap(): return lax.ppermute(away, ('lat', 'rep'), plane_perm(count, one, two))]
    add x6 -> x0, other arithmetic: 3.48 us -> none  [the longest x2 1.51 us: scatter_sum(): held = keep + lax.ppermute(away, axes, plane_perm(plane, 2, 2))]
    reshape x2 -> x0, local copies, waits for them, and re-layouts: 3.03 us -> none  [scatter_sum(): blocks = jnp.swapaxes(tail.reshape(each, lon, taps // lon), 0, 1)]
    another operation x1 -> x0, local copies, waits for them, and re-layouts: 2.57 us -> none
    pallas_call x11 -> x17, Pallas kernels: 25.5 us -> 23 us  [the longest x16 23 us: call(): pl.pallas_call(kernel, out_shape=[jax.ShapeDtypeStruct(shape, dtype) for...]
    slice x4 -> x0, local copies, waits for them, and re-layouts: 1.73 us -> none  [the longest x2 0.95 us: scatter_sum(): held[half // 2:]]
    ppermute x12, starting transfers between devices: 20.1 us -> 18.4 us  [the longest x6 8 us: last_sum(): lax.ppermute(blocks[step], 'lon', [(i, i ^ step) for i in range(lon)])]
  transfers between devices with their start and end apart: 16 -> 16, of which waited for: 7 -> 6; matrix products, arithmetic and copies ran while one was open for 7% -> 1% of each run, Pallas kernels for 18% -> 16%
where the time goes in v1:
time: 80 us; the launch traced here: 79.5 us
  starting transfers between devices  25.2 us (32%)
  Pallas kernels  23 us (29%)
  waiting for transfers between devices  22.9 us (29%)
  local copies, waits for them, and re-layouts  6.26 us (8%)
  other arithmetic  1.31 us (2%)
  between operations  0.8 us (1%)
    pallas_call x16, Pallas kernels, call(): pl.pallas_call(kernel, out_shape=[jax.ShapeDtypeStruct(shape, dtype) for...  23 us
    ppermute x4, waiting for transfers between devices, plane_swap(): return lax.ppermute(away, ('lat', 'rep'), plane_perm(count, one, two))  12.8 us
    ppermute x6, starting transfers between devices, last_sum(): lax.ppermute(blocks[step], 'lon', [(i, i ^ step) for i in range(lon)])  8 us
    ppermute x4, starting transfers between devices, pair_swap(): lax.ppermute(block, axis, who + [(b, a) for a, b in who])  6.78 us
    ppermute x6, waiting for transfers between devices, last_sum(): lax.ppermute(blocks[step], 'lon', [(i, i ^ step) for i in range(lon)])  6.58 us
    unnamed x20, local copies, waits for them, and re-layouts  6.26 us
    ppermute x4, starting transfers between devices, plane_swap(): return lax.ppermute(away, ('lat', 'rep'), plane_perm(count, one, two))  6.2 us
    ppermute x2, starting transfers between devices, core_swap(): return lax.ppermute(away, ('lat', 'rep'), plane_perm(count, 2, 2))  4.24 us
  transfers between devices with their start and end apart: 16, of which 6 were waited for; matrix products, arithmetic and copies ran while one was open for 1% of the time, Pallas kernels for 16%

profile of v1, /device:TPU:0, one launch (start us, length us, event | category | flops | bytes accessed | tf_op | source)
XLA Modules:
  0.0 79.5 jit_solution(14990055105956110032)
XLA Ops:
  0.6 0.0 copy-start.2
  0.6 1.0 %copy-done.2 = f32[1,16,32,256]{3,2,1,0:T(8,128)S(1)} copy-done((f32[1,16,32,256]{3,2,1,0:T(8,128)S(1)}, f32[1,16,32,256]{3,2,1,0:T(8,128)}, u32[]{:S(2)}) %copy-start.2) | copy-done | bytes 524312
  1.7 1.0 %copy-done.5 = f32[1,16,32,256]{3,2,1,0:T(8,128)S(1)} copy-done((f32[1,16,32,256]{3,2,1,0:T(8,128)S(1)}, f32[1,16,32,256]{3,2,1,0:T(8,128)}, u32[]{:S(2)}) %copy-start.5) | copy-done | bytes 524312
  2.7 0.0 copy-start.1
  2.8 0.5 collective-permute-start
  3.3 0.8 collective-permute-start.1
  4.1 0.2 collective-permute-done.refs_2_.refs_1_
  4.3 0.0 collective-permute-done.1.refs_3_.refs_2_
  4.3 0.0 copy-start.3
  4.3 1.0 %copy-done.3 = f32[1,16,32,256]{3,2,1,0:T(8,128)S(1)} copy-done((f32[1,16,32,256]{3,2,1,0:T(8,128)S(1)}, f32[1,16,32,256]{3,2,1,0:T(8,128)}, u32[]{:S(2)}) %copy-start.3) | copy-done | bytes 524312
  5.3 0.0 copy-start.6
  5.3 1.0 %copy-done.6 = f32[1,16,32,256]{3,2,1,0:T(8,128)S(1)} copy-done((f32[1,16,32,256]{3,2,1,0:T(8,128)S(1)}, f32[1,16,32,256]{3,2,1,0:T(8,128)}, u32[]{:S(2)}) %copy-start.6) | copy-done | bytes 524312
  6.4 0.1 shard_map.76
  6.4 3.0 %collective-permute-start.2 = (f32[2,2,24,256]{3,2,1,0:T(8,128)S(1)}, f32[2,2,24,256]{3,2,1,0:T(8,128)S(1)}, u32[]{:S(2)}, u32[]{:S(2)}) collective-permute-start(f32[2,2,24,256]{3,2,1,0:T(8,128)S(1)} %get-tuple-element.50.refs_3_), channel_id=1, source_target_pairs={{0,8},{16,24},{8,0},{24,16},{1,9},{17,25},{9,1},{25,17},{2,10},{18... | collective-permute-start | bytes 294920 | tf_op jit(solution)/shard_map/ppermute | solution.py:127
  9.4 2.5 %collective-permute-start.3 = (f32[2,2,24,256]{3,2,1,0:T(8,128)S(1)}, f32[2,2,24,256]{3,2,1,0:T(8,128)S(1)}, u32[]{:S(2)}, u32[]{:S(2)}) collective-permute-start(f32[2,2,24,256]{3,2,1,0:T(8,128)S(1)} %get-tuple-element.51.refs_4_), channel_id=1, source_target_pairs={{8,16},{24,0},{16,8},{0,24},{9,17},{25,1},{17,9},{1,25},{10,18},{2... | collective-permute-start | bytes 294920 | tf_op jit(solution)/shard_map/ppermute | solution.py:127
  11.9 0.0 copy-done.4
  11.9 0.3 shard_map.78
  12.2 0.0 copy-done.1
  12.2 0.3 shard_map.77
  12.5 0.0 collective-permute-done.2.refs_5_
  12.6 3.3 %collective-permute-done.3.refs_6_ = f32[2,2,24,256]{3,2,1,0:T(8,128)S(1)} collective-permute-done((f32[2,2,24,256]{3,2,1,0:T(8,128)S(1)}, f32[2,2,24,256]{3,2,1,0:T(8,128)S(1)}, u32[]{:S(2)}, u32[]{:S(2)}) %collective-permute-start.3) | collective-permute-done | bytes 98336 | tf_op jit(solution)/shard_map/ppermute | solution.py:127
  15.9 8.2 %shard_map.79 = (f32[576,256]{1,0:T(8,128)S(1)}, f32[48,256]{1,0:T(8,128)S(1)}, bf16[640,768]{1,0:T(8,128)(2,1)S(1)}, bf16[640,768]{1,0:T(8,128)(2,1)S(1)}, bf16...) custom-call(f32[16,32,256]{2,1,0:T(8,128)S(1)} %bitcast.17, ...), custom_call_target="tpu_custom_call" | custom-call | flops 3850371072 | bytes 4063232 | tf_op jit(solution)/shard_map/pallas_call | solution.py:25
  24.1 4.2 %collective-permute-start.4 = (f32[128,2304]{1,0:T(8,128)S(1)}, f32[128,2304]{1,0:T(8,128)S(1)}, u32[]{:S(2)}, u32[]{:S(2)}) collective-permute-start(f32[128,2304]{1,0:T(8,128)S(1)} %get-tuple-element.69), channel_id=1, source_target_pairs={{0,2},{1,3},{2,0},{3,1},{4,6},{5,7},{6,4},{7,5},{8,10},{9,11},{10,... | collective-permute-start | bytes 3538952 | tf_op jit(solution)/shard_map/ppermute | solution.py:330
  28.2 0.0 copy-done
  28.2 0.7 shard_map.81
  28.9 3.3 %shard_map.82 = (bf16[576,768]{1,0:T(8,128)(2,1)S(1)}, bf16[576,768]{1,0:T(8,128)(2,1)S(1)}, bf16[256,512]{1,0:T(8,128)(2,1)S(1)}, bf16[256,512]{1,0:T(8,128)(2,1)S(1)}) custom-call(f32[16,32,256]{2,1,0:T(8,128)S(1)} %bitcast.12, f32[2,2,32,256]{3,2,1,0:T(8,128)S(1)} %collective-permute-done.refs_2_.refs_1_, ...), custom_call_target="tpu_custom_call" | custom-call | flops 2038431744 | bytes 4177920 | tf_op jit(solution)/shard_map/pallas_call | solution.py:25
  32.2 0.0 collective-permute-done.4.refs_1_
  32.2 0.1 shard_map.83
  32.4 2.0 %shard_map.84 = (f32[128,2304]{1,0:T(8,128)S(1)}, f32[128,2304]{1,0:T(8,128)S(1)}) custom-call(bf16[256,512]{1,0:T(8,128)(2,1)S(1)} %get-tuple-element.64.refs_0_, bf16[256,512]{1,0:T(8,128)(2,1)S(1)} %get-tuple-element.65.refs_2_.refs_1_, bf16[640,768]{1,0:T(8,128)(2,1)S(1)} %get-tuple-element.66.refs_2_, bf16[640,768]{1,0:T(8,128)(2,1)S(1)} %get-tuple-element.67.refs_3_, ...), custom_call_target="tpu_custom_call" | custom-call | flops 1811939328 | bytes 2490368 | tf_op jit(solution)/shard_map/pallas_call | solution.py:25
  34.4 0.1 collective-permute-start.5
  34.5 1.6 %collective-permute-start.6 = (f32[64,2304]{1,0:T(8,128)S(1)}, f32[64,2304]{1,0:T(8,128)S(1)}, u32[]{:S(2)}, u32[]{:S(2)}) collective-permute-start(f32[64,2304]{1,0:T(8,128)S(1)} %get-tuple-element.77), channel_id=1, source_target_pairs={{0,1},{1,0},{2,6},{3,7},{4,5},{5,4},{6,2},{7,3},{8,9},{9,8},{10,14... | collective-permute-start | bytes 1769480 | tf_op jit(solution)/shard_map/ppermute | solution.py:325
  36.0 0.3 shard_map.80
  36.4 0.0 copy-done.7
  36.4 3.0 %shard_map.85.refs_4_ = f32[16,32,256]{2,1,0:T(8,128)} custom-call(f32[16,32,256]{2,1,0:T(8,128)S(1)} %bitcast.18, bf16[576,768]{1,0:T(8,128)(2,1)S(1)} %get-tuple-element.56.refs_1_, bf16[576,768]{1,0:T(8,128)(2,1)S(1)} %get-tuple-element.57.refs_2_, bf16[2304,256]{1,0:T(8,128)(2,1)S(1)} %get-tuple-element.58.refs_3_, ...), custom_call_target="tpu_custom_call" | custom-call | flops 1811939328 | bytes 4653056 | tf_op jit(solution)/shard_map/pallas_call | solution.py:25
  39.4 5.0 %collective-permute-done.6.refs_3_ = f32[64,2304]{1,0:T(8,128)S(1)} collective-permute-done((f32[64,2304]{1,0:T(8,128)S(1)}, f32[64,2304]{1,0:T(8,128)S(1)}, u32[]{:S(2)}, u32[]{:S(2)}) %collective-permute-start.6) | collective-permute-done | bytes 589856 | tf_op jit(solution)/shard_map/ppermute | solution.py:325
  44.4 0.0 collective-permute-done.5.refs_1_
  44.4 1.0 %copy-done.9 = f32[16,32,256]{2,1,0:T(8,128)S(1)} copy-done((f32[16,32,256]{2,1,0:T(8,128)S(1)}, f32[16,32,256]{2,1,0:T(8,128)}, u32[]{:S(2)}) %copy-start.9) | copy-done | bytes 524312
  45.5 0.2 shard_map.87
  45.6 3.0 %collective-permute-start.7 = (f32[64,2304]{1,0:T(8,128)S(1)}, f32[64,2304]{1,0:T(8,128)S(1)}, u32[]{:S(2)}, u32[]{:S(2)}) collective-permute-start(f32[64,2304]{1,0:T(8,128)S(1)} %get-tuple-element.80), channel_id=1, source_target_pairs={{0,4},{1,5},{2,3},{3,2},{4,0},{5,1},{6,7},{7,6},{8,12},{9,13},{10,... | collective-permute-start | bytes 1769480 | tf_op jit(solution)/shard_map/ppermute | solution.py:325
  48.6 0.1 collective-permute-start.12
  48.7 7.8 %collective-permute-done.7.refs_1_ = f32[64,2304]{1,0:T(8,128)S(1)} collective-permute-done((f32[64,2304]{1,0:T(8,128)S(1)}, f32[64,2304]{1,0:T(8,128)S(1)}, u32[]{:S(2)}, u32[]{:S(2)}) %collective-permute-start.7) | collective-permute-done | bytes 589856 | tf_op jit(solution)/shard_map/ppermute | solution.py:325
  56.5 0.1 shard_map.89
  56.5 1.6 %collective-permute-start.8 = (f32[32,2304]{1,0:T(8,128)S(1)}, f32[32,2304]{1,0:T(8,128)S(1)}, u32[]{:S(2)}, u32[]{:S(2)}) collective-permute-start(f32[32,2304]{1,0:T(8,128)S(1)} %get-tuple-element.82), channel_id=1, source_target_pairs={{0,1},{1,0},{2,6},{3,7},{4,5},{5,4},{6,2},{7,3},{8,9},{9,8},{10,14... | collective-permute-start | bytes 884744 | tf_op jit(solution)/shard_map/ppermute | solution.py:325
  58.1 0.7 shard_map.86
  58.8 2.8 %shard_map.88.refs_2_ = f32[16,32,256]{2,1,0:T(8,128)} custom-call(f32[16,32,256]{2,1,0:T(8,128)S(1)} %bitcast.19, f32[16,32,256]{2,1,0:T(8,128)S(1)} %bitcast.13, bf16[576,768]{1,0:T(8,128)(2,1)S(1)} %get-tuple-element.72.refs_2_, bf16[576,768]{1,0:T(8,128)(2,1)S(1)} %get-tuple-element.73.refs_3_, bf16[2304,256]{1,0:T(8,128)(2,1)S(1)} %get-tuple-element.74.refs_4_, ...), custom_call_target="tpu_custom_call" | custom-call | flops 1811939328 | bytes 5177344 | tf_op jit(solution)/shard_map/pallas_call | solution.py:25
  61.6 0.0 collective-permute-done.12.refs_1_
  61.6 1.0 %copy-done.8 = f32[16,32,256]{2,1,0:T(8,128)S(1)} copy-done((f32[16,32,256]{2,1,0:T(8,128)S(1)}, f32[16,32,256]{2,1,0:T(8,128)}, u32[]{:S(2)}) %copy-start.8) | copy-done | bytes 524312
  62.6 0.5 shard_map.91
  63.1 0.1 collective-permute-start.13
  63.2 3.1 %collective-permute-start.14 = (f32[32,576]{1,0:T(8,128)S(1)}, f32[32,576]{1,0:T(8,128)S(1)}, u32[]{:S(2)}, u32[]{:S(2)}) collective-permute-start(f32[32,576]{1,0:T(8,128)S(1)} %get-tuple-element.90), channel_id=1, source_target_pairs={{0,16},{8,24},{16,0},{24,8},{1,17},{9,25},{17,1},{25,9},{2,18},{10... | collective-permute-start | bytes 221192 | tf_op jit(solution)/shard_map/ppermute | solution.py:365
  66.3 1.2 %collective-permute-start.15 = (f32[32,576]{1,0:T(8,128)S(1)}, f32[32,576]{1,0:T(8,128)S(1)}, u32[]{:S(2)}, u32[]{:S(2)}) collective-permute-start(f32[32,576]{1,0:T(8,128)S(1)} %get-tuple-element.91), channel_id=1, source_target_pairs={{0,24},{8,16},{16,8},{24,0},{1,25},{9,17},{17,9},{25,1},{2,26},{10... | collective-permute-start | bytes 221192 | tf_op jit(solution)/shard_map/ppermute | solution.py:365
  67.6 0.0 collective-permute-done.8.refs_1_
  67.6 0.5 shard_map.90
  68.1 1.0 %collective-permute-start.10 = (f32[32,576]{1,0:T(8,128)S(1)}, f32[32,576]{1,0:T(8,128)S(1)}, u32[]{:S(2)}, u32[]{:S(2)}) collective-permute-start(f32[32,576]{1,0:T(8,128)S(1)} %get-tuple-element.85), channel_id=1, source_target_pairs={{0,16},{8,24},{16,0},{24,8},{1,17},{9,25},{17,1},{25,9},{2,18},{10... | collective-permute-start | bytes 221192 | tf_op jit(solution)/shard_map/ppermute | solution.py:365
  69.1 1.7 %collective-permute-start.11 = (f32[32,576]{1,0:T(8,128)S(1)}, f32[32,576]{1,0:T(8,128)S(1)}, u32[]{:S(2)}, u32[]{:S(2)}) collective-permute-start(f32[32,576]{1,0:T(8,128)S(1)} %get-tuple-element.86), channel_id=1, source_target_pairs={{0,24},{8,16},{16,8},{24,0},{1,25},{9,17},{17,9},{25,1},{2,26},{10... | collective-permute-start | bytes 221192 | tf_op jit(solution)/shard_map/ppermute | solution.py:365
  70.8 0.0 collective-permute-done.13
  70.8 0.8 %collective-permute-start.9 = (f32[32,576]{1,0:T(8,128)S(1)}, f32[32,576]{1,0:T(8,128)S(1)}, u32[]{:S(2)}, u32[]{:S(2)}) collective-permute-start(f32[32,576]{1,0:T(8,128)S(1)} %get-tuple-element.84), channel_id=1, source_target_pairs={{0,8},{8,0},{16,24},{24,16},{1,9},{9,1},{17,25},{25,17},{2,10},{10... | collective-permute-start | bytes 221192 | tf_op jit(solution)/shard_map/ppermute | solution.py:365
  71.7 2.4 %collective-permute-done.14 = f32[32,576]{1,0:T(8,128)S(1)} collective-permute-done((f32[32,576]{1,0:T(8,128)S(1)}, f32[32,576]{1,0:T(8,128)S(1)}, u32[]{:S(2)}, u32[]{:S(2)}) %collective-permute-start.14) | collective-permute-done | bytes 73760 | tf_op jit(solution)/shard_map/ppermute | solution.py:365
  74.1 0.0 collective-permute-done.15
  74.1 0.7 add_bitcast_fusion
  74.7 4.1 %collective-permute-done.10 = f32[32,576]{1,0:T(8,128)S(1)} collective-permute-done((f32[32,576]{1,0:T(8,128)S(1)}, f32[32,576]{1,0:T(8,128)S(1)}, u32[]{:S(2)}, u32[]{:S(2)}) %collective-permute-start.10) | collective-permute-done | bytes 73760 | tf_op jit(solution)/shard_map/ppermute | solution.py:365
  78.9 0.0 collective-permute-done.11
  78.9 0.0 collective-permute-done.9
  78.9 0.7 add_bitcast_fusion.1
  (7 shorter events, 0.0 us)
Async XLA Ops:
  0.6 1.0 %copy-start.2 = (f32[1,16,32,256]{3,2,1,0:T(8,128)S(1)}, f32[1,16,32,256]{3,2,1,0:T(8,128)}, u32[]{:S(2)}) copy-start(f32[1,16,32,256]{3,2,1,0:T(8,128)} %param.5) | copy-start | bytes 1572868
  1.7 1.0 %copy-start.5 = (f32[1,16,32,256]{3,2,1,0:T(8,128)S(1)}, f32[1,16,32,256]{3,2,1,0:T(8,128)}, u32[]{:S(2)}) copy-start(f32[1,16,32,256]{3,2,1,0:T(8,128)} %param.4) | copy-start | bytes 1572868
  2.7 9.5 %copy-start.1 = (f32[2304,256]{1,0:T(8,128)S(1)}, f32[2304,256]{1,0:T(8,128)}, u32[]{:S(2)}) copy-start(f32[2304,256]{1,0:T(8,128)} %refs_0_.7) | copy-start | bytes 7077892
  2.8 1.5 %collective-permute-start = (f32[2,2,32,256]{3,2,1,0:T(8,128)S(1)}, f32[2,2,32,256]{3,2,1,0:T(8,128)S(1)}, u32[]{:S(2)}, u32[]{:S(2)}) collective-permute-start(f32[2,2,32,256]{3,2,1,0:T(8,128)S(1)} %get-tuple-element.48), channel_id=1, source_target_pairs={{0,2},{4,6},{2,0},{6,4},{1,3},{5,7},{3,1},{7,5},{8,10},{12,14},{10... | collective-permute-start | bytes 393224 | tf_op jit(solution)/shard_map/ppermute | solution.py:127
  3.3 1.0 %collective-permute-start.1 = (f32[2,2,32,256]{3,2,1,0:T(8,128)S(1)}, f32[2,2,32,256]{3,2,1,0:T(8,128)S(1)}, u32[]{:S(2)}, u32[]{:S(2)}) collective-permute-start(f32[2,2,32,256]{3,2,1,0:T(8,128)S(1)} %get-tuple-element.49), channel_id=1, source_target_pairs={{2,4},{4,2},{3,5},{5,3},{10,12},{12,10},{11,13},{13,11},{18,20},{2... | collective-permute-start | bytes 393224 | tf_op jit(solution)/shard_map/ppermute | solution.py:127
  4.3 1.0 %copy-start.3 = (f32[1,16,32,256]{3,2,1,0:T(8,128)S(1)}, f32[1,16,32,256]{3,2,1,0:T(8,128)}, u32[]{:S(2)}) copy-start(f32[1,16,32,256]{3,2,1,0:T(8,128)} %param.5) | copy-start | bytes 1572868
  5.3 1.0 %copy-start.6 = (f32[1,16,32,256]{3,2,1,0:T(8,128)S(1)}, f32[1,16,32,256]{3,2,1,0:T(8,128)}, u32[]{:S(2)}) copy-start(f32[1,16,32,256]{3,2,1,0:T(8,128)} %param.4) | copy-start | bytes 1572868
  6.3 5.6 %copy-start.4 = (f32[1,16,32,256]{3,2,1,0:T(8,128)S(1)}, f32[1,16,32,256]{3,2,1,0:T(8,128)}, u32[]{:S(2)}) copy-start(f32[1,16,32,256]{3,2,1,0:T(8,128)} %param.5) | copy-start | bytes 1572868
  6.4 6.1 %collective-permute-start.2 = (f32[2,2,24,256]{3,2,1,0:T(8,128)S(1)}, f32[2,2,24,256]{3,2,1,0:T(8,128)S(1)}, u32[]{:S(2)}, u32[]{:S(2)}) collective-permute-start(f32[2,2,24,256]{3,2,1,0:T(8,128)S(1)} %get-tuple-element.50.refs_3_), channel_id=1, source_target_pairs={{0,8},{16,24},{8,0},{24,16},{1,9},{17,25},{9,1},{25,17},{2,10},{18... | collective-permute-start | bytes 294920 | tf_op jit(solution)/shard_map/ppermute | solution.py:127
  9.4 6.4 %collective-permute-start.3 = (f32[2,2,24,256]{3,2,1,0:T(8,128)S(1)}, f32[2,2,24,256]{3,2,1,0:T(8,128)S(1)}, u32[]{:S(2)}, u32[]{:S(2)}) collective-permute-start(f32[2,2,24,256]{3,2,1,0:T(8,128)S(1)} %get-tuple-element.51.refs_4_), channel_id=1, source_target_pairs={{8,16},{24,0},{16,8},{0,24},{9,17},{25,1},{17,9},{1,25},{10,18},{2... | collective-permute-start | bytes 294920 | tf_op jit(solution)/shard_map/ppermute | solution.py:127
  15.9 12.4 %copy-start = (f32[2304,256]{1,0:T(8,128)S(1)}, f32[2304,256]{1,0:T(8,128)}, u32[]{:S(2)}) copy-start(f32[2304,256]{1,0:T(8,128)} %refs_0_.6) | copy-start | bytes 7077892
  24.1 8.2 %collective-permute-start.4 = (f32[128,2304]{1,0:T(8,128)S(1)}, f32[128,2304]{1,0:T(8,128)S(1)}, u32[]{:S(2)}, u32[]{:S(2)}) collective-permute-start(f32[128,2304]{1,0:T(8,128)S(1)} %get-tuple-element.69), channel_id=1, source_target_pairs={{0,2},{1,3},{2,0},{3,1},{4,6},{5,7},{6,4},{7,5},{8,10},{9,11},{10,... | collective-permute-start | bytes 3538952 | tf_op jit(solution)/shard_map/ppermute | solution.py:330
  34.4 10.0 %collective-permute-start.5 = (f32[128,2304]{1,0:T(8,128)S(1)}, f32[128,2304]{1,0:T(8,128)S(1)}, u32[]{:S(2)}, u32[]{:S(2)}) collective-permute-start(f32[128,2304]{1,0:T(8,128)S(1)} %get-tuple-element.76), channel_id=1, source_target_pairs={{0,2},{1,3},{2,0},{3,1},{4,6},{5,7},{6,4},{7,5},{8,10},{9,11},{10,... | collective-permute-start | bytes 3538952 | tf_op jit(solution)/shard_map/ppermute | solution.py:330
  34.5 1.9 %copy-start.7 = (f32[1,16,32,256]{3,2,1,0:T(8,128)S(1)}, f32[1,16,32,256]{3,2,1,0:T(8,128)}, u32[]{:S(2)}) copy-start(f32[1,16,32,256]{3,2,1,0:T(8,128)} %param.4) | copy-start | bytes 1572868
  34.5 9.9 %collective-permute-start.6 = (f32[64,2304]{1,0:T(8,128)S(1)}, f32[64,2304]{1,0:T(8,128)S(1)}, u32[]{:S(2)}, u32[]{:S(2)}) collective-permute-start(f32[64,2304]{1,0:T(8,128)S(1)} %get-tuple-element.77), channel_id=1, source_target_pairs={{0,1},{1,0},{2,6},{3,7},{4,5},{5,4},{6,2},{7,3},{8,9},{9,8},{10,14... | collective-permute-start | bytes 1769480 | tf_op jit(solution)/shard_map/ppermute | solution.py:325
  44.4 1.0 %copy-start.9 = (f32[16,32,256]{2,1,0:T(8,128)S(1)}, f32[16,32,256]{2,1,0:T(8,128)}, u32[]{:S(2)}) copy-start(f32[16,32,256]{2,1,0:T(8,128)} %shard_map.85.refs_4_) | copy-start | bytes 1572868
  45.6 10.8 %collective-permute-start.7 = (f32[64,2304]{1,0:T(8,128)S(1)}, f32[64,2304]{1,0:T(8,128)S(1)}, u32[]{:S(2)}, u32[]{:S(2)}) collective-permute-start(f32[64,2304]{1,0:T(8,128)S(1)} %get-tuple-element.80), channel_id=1, source_target_pairs={{0,4},{1,5},{2,3},{3,2},{4,0},{5,1},{6,7},{7,6},{8,12},{9,13},{10,... | collective-permute-start | bytes 1769480 | tf_op jit(solution)/shard_map/ppermute | solution.py:325
  48.6 13.0 %collective-permute-start.12 = (f32[32,2304]{1,0:T(8,128)S(1)}, f32[32,2304]{1,0:T(8,128)S(1)}, u32[]{:S(2)}, u32[]{:S(2)}) collective-permute-start(f32[32,2304]{1,0:T(8,128)S(1)} %get-tuple-element.87), channel_id=1, source_target_pairs={{0,4},{1,5},{2,3},{3,2},{4,0},{5,1},{6,7},{7,6},{8,12},{9,13},{10,... | collective-permute-start | bytes 884744 | tf_op jit(solution)/shard_map/ppermute | solution.py:325
  56.5 11.1 %collective-permute-start.8 = (f32[32,2304]{1,0:T(8,128)S(1)}, f32[32,2304]{1,0:T(8,128)S(1)}, u32[]{:S(2)}, u32[]{:S(2)}) collective-permute-start(f32[32,2304]{1,0:T(8,128)S(1)} %get-tuple-element.82), channel_id=1, source_target_pairs={{0,1},{1,0},{2,6},{3,7},{4,5},{5,4},{6,2},{7,3},{8,9},{9,8},{10,14... | collective-permute-start | bytes 884744 | tf_op jit(solution)/shard_map/ppermute | solution.py:325
  61.6 1.0 %copy-start.8 = (f32[16,32,256]{2,1,0:T(8,128)S(1)}, f32[16,32,256]{2,1,0:T(8,128)}, u32[]{:S(2)}) copy-start(f32[16,32,256]{2,1,0:T(8,128)} %shard_map.88.refs_2_) | copy-start | bytes 1572868
  63.1 7.7 %collective-permute-start.13 = (f32[32,576]{1,0:T(8,128)S(1)}, f32[32,576]{1,0:T(8,128)S(1)}, u32[]{:S(2)}, u32[]{:S(2)}) collective-permute-start(f32[32,576]{1,0:T(8,128)S(1)} %get-tuple-element.89), channel_id=1, source_target_pairs={{0,8},{8,0},{16,24},{24,16},{1,9},{9,1},{17,25},{25,17},{2,10},{10... | collective-permute-start | bytes 221192 | tf_op jit(solution)/shard_map/ppermute | solution.py:365
  63.2 10.9 %collective-permute-start.14 = (f32[32,576]{1,0:T(8,128)S(1)}, f32[32,576]{1,0:T(8,128)S(1)}, u32[]{:S(2)}, u32[]{:S(2)}) collective-permute-start(f32[32,576]{1,0:T(8,128)S(1)} %get-tuple-element.90), channel_id=1, source_target_pairs={{0,16},{8,24},{16,0},{24,8},{1,17},{9,25},{17,1},{25,9},{2,18},{10... | collective-permute-start | bytes 221192 | tf_op jit(solution)/shard_map/ppermute | solution.py:365
  66.3 7.7 %collective-permute-start.15 = (f32[32,576]{1,0:T(8,128)S(1)}, f32[32,576]{1,0:T(8,128)S(1)}, u32[]{:S(2)}, u32[]{:S(2)}) collective-permute-start(f32[32,576]{1,0:T(8,128)S(1)} %get-tuple-element.91), channel_id=1, source_target_pairs={{0,24},{8,16},{16,8},{24,0},{1,25},{9,17},{17,9},{25,1},{2,26},{10... | collective-permute-start | bytes 221192 | tf_op jit(solution)/shard_map/ppermute | solution.py:365
  68.1 10.8 %collective-permute-start.10 = (f32[32,576]{1,0:T(8,128)S(1)}, f32[32,576]{1,0:T(8,128)S(1)}, u32[]{:S(2)}, u32[]{:S(2)}) collective-permute-start(f32[32,576]{1,0:T(8,128)S(1)} %get-tuple-element.85), channel_id=1, source_target_pairs={{0,16},{8,24},{16,0},{24,8},{1,17},{9,25},{17,1},{25,9},{2,18},{10... | collective-permute-start | bytes 221192 | tf_op jit(solution)/shard_map/ppermute | solution.py:365
  69.1 9.8 %collective-permute-start.11 = (f32[32,576]{1,0:T(8,128)S(1)}, f32[32,576]{1,0:T(8,128)S(1)}, u32[]{:S(2)}, u32[]{:S(2)}) collective-permute-start(f32[32,576]{1,0:T(8,128)S(1)} %get-tuple-element.86), channel_id=1, source_target_pairs={{0,24},{8,16},{16,8},{24,0},{1,25},{9,17},{17,9},{25,1},{2,26},{10... | collective-permute-start | bytes 221192 | tf_op jit(solution)/shard_map/ppermute | solution.py:365
  70.8 8.1 %collective-permute-start.9 = (f32[32,576]{1,0:T(8,128)S(1)}, f32[32,576]{1,0:T(8,128)S(1)}, u32[]{:S(2)}, u32[]{:S(2)}) collective-permute-start(f32[32,576]{1,0:T(8,128)S(1)} %get-tuple-element.84), channel_id=1, source_target_pairs={{0,8},{8,0},{16,24},{24,16},{1,9},{9,1},{17,25},{25,17},{2,10},{10... | collective-permute-start | bytes 221192 | tf_op jit(solution)/shard_map/ppermute | solution.py:365

commit v2 on v1

--- a/solution.py
+++ b/solution.py
@@ -14,8 +14,7 @@
 EDGE = 8
 
 
-def call(body, outs, ins, flops=0, scratch=(), limit=16, after=()):
-    size = sum(math.prod(a.shape) * a.dtype.itemsize for a in ins)
+def call(body, outs, ins, scratch=(), limit=16, after=()):
     used, skip = len(ins), len(after)
 
     def kernel(*refs):
@@ -29,7 +28,7 @@
         out_specs=[VMEM] * len(outs),
         scratch_shapes=[pltpu.VMEM(shape, dtype) for shape, dtype in scratch],
         compiler_params=pltpu.CompilerParams(vmem_limit_bytes=limit * 1024 * 1024),
-        cost_estimate=pl.CostEstimate(flops=flops, bytes_accessed=size, transcendentals=0),
+        cost_estimate=pl.CostEstimate(flops=0, bytes_accessed=0, transcendentals=0),
     )(*ins)
 
 
@@ -42,22 +41,26 @@
     return jnp.dot(a, b, preferred_element_type=F32)
 
 
+def sigmoid(value):
+    return 0.5 * jnp.tanh(0.5 * value) + 0.5
+
+
 def silu(value):
-    return value / (1.0 + jnp.exp(-value))
+    return value * sigmoid(value)
 
 
 def slope(value):
-    sigma = 1.0 / (1.0 + jnp.exp(-value))
+    sigma = sigmoid(value)
     return sigma * (1.0 + value * (1.0 - sigma))
 
 
-def relative_blocks(flip):
+def relative_blocks():
     lat, y = lax.axis_index("lat"), lax.axis_index("rep")
     x, core = lat // 2, lat % 2
     order = []
     for r_core in range(2):
         c = core + r_core - 2 * core * r_core
-        y_first = c == (1 if flip else 0)
+        y_first = c == 0
         for r_first in range(2):
             for r_second in range(2):
                 move_y = jnp.where(y_first, r_first, r_second)
@@ -73,23 +76,6 @@
     for f, (low, high) in enumerate(((low_here, high_here), (low_grad, high_grad))):
         one[f] = jnp.where(even, high[...], low[...])
         two[f] = jnp.where(even, low[...], high[...])
-
-
-def rows_messages(here, grad):
-    rows, cols, channels = here.shape
-    block = (2, cols, channels)
-    low = pl.BlockSpec(block, lambda i: (0, 0, 0))
-    high = pl.BlockSpec(block, lambda i: (rows // 2 - 1, 0, 0))
-    shape = (2, *block)
-    whole = pl.BlockSpec(shape, lambda i: (0, 0, 0, 0))
-    return pl.pallas_call(
-        pack_rows,
-        grid=(1,),
-        out_shape=[jax.ShapeDtypeStruct(shape, F32)] * 2,
-        in_specs=[low, high] * 2,
-        out_specs=[VMEM] * 2,
-        compiler_params=pltpu.CompilerParams(vmem_limit_bytes=4 * 1024 * 1024),
-    )(here, here, grad, grad)
 
 
 def pack_cols(here, grad, one, two, first, second):
@@ -141,18 +127,18 @@
         high[tap * size : (tap + 1) * size, :], low[tap * size : (tap + 1) * size, :] = split(block)
 
 
-def turn(flip, value, high, low, scratch):
+def turn(value, high, low, scratch):
     channels = value.shape[1]
     each = channels // 8
     scratch[...] = value.T
-    for i, block in enumerate(relative_blocks(flip)):
+    for i, block in enumerate(relative_blocks()):
         part = scratch[pl.ds(pl.multiple_of(block * each, each), each), :]
         high[i * each : (i + 1) * each, :], low[i * each : (i + 1) * each, :] = split(part)
 
 
 def turn_grad(grad, high, low, scratch):
     cells = grad.shape[0] * grad.shape[1]
-    turn(False, grad[...].reshape(cells, grad.shape[2]), high, low, scratch)
+    turn(grad[...].reshape(cells, grad.shape[2]), high, low, scratch)
 
 
 def lay_taps(wide, x_high, x_low):
@@ -294,7 +280,7 @@
     main = jnp.where(inside(rows), main.reshape(rows + 2, cols, channels), 0.0)
     line = inside_line(rows)
     around = jnp.where(jnp.concatenate([line, line], axis=0), around, 0.0)
-    turn(True, main[1 : rows + 1].reshape(rows * cols, channels), t_high, t_low, turned)
+    turn(main[1 : rows + 1].reshape(rows * cols, channels), t_high, t_low, turned)
     spread_ext(main, around, wide2)
     lay_taps(wide2, x3_high, x3_low)
 
@@ -303,13 +289,15 @@
     products(t_high, t_low, x1_high, x1_low, 1, t_high.shape[1], cols, scale, away, keep)
 
 
-def output_kernel(here, x_high, x_low, w_high, w_low, out):
+def output_kernel(here, x_high, x_low, w_high, w_low, out, token):
+    token[...] = jnp.zeros(token.shape, F32)
     rows, cols, channels = here.shape
     total = convolve(x_high, x_low, 0, rows, cols, w_high, w_low)
     out[...] = here[...] + total.reshape(rows, cols, channels)
 
 
-def input_grad_kernel(here, grad, x_high, x_low, w_high, w_low, out):
+def input_grad_kernel(here, grad, x_high, x_low, w_high, w_low, out, token):
+    token[...] = jnp.zeros(token.shape, F32)
     rows, cols, channels = here.shape
     total = convolve(x_high, x_low, 0, rows, cols, w_high, w_low)
     out[...] = grad[...] + total.reshape(rows, cols, channels) * slope(here[...])
@@ -319,9 +307,9 @@
     return [(i, i ^ (odd if (i // 2) % 2 else even)) for i in range(count)]
 
 
-def plane_swap(away, flip, second):
+def plane_swap(away, second):
     count = lax.axis_size("lat") * lax.axis_size("rep")
-    one, two = (1, 4) if flip == second else (4, 1)
+    one, two = (4, 1) if second else (1, 4)
     return lax.ppermute(away, ("lat", "rep"), plane_perm(count, one, two))
 
 
@@ -334,11 +322,6 @@
     half = keep.shape[0] // 2
     next_keep[...] = keep[:half] + got[:half]
     next_away[...] = keep[half:] + got[half:]
-
-
-def add_both(keep_1, got_1, keep_2, got_2, *outs):
-    add_halves(keep_1, got_1, *outs[:2])
-    add_halves(keep_2, got_2, *outs[2:])
 
 
 def cut_blocks(keep, got, *blocks):
@@ -374,7 +357,9 @@
     scale = 1.0 / math.sqrt(
         cells * lax.axis_size("rep") * lax.axis_size("lat") * lax.axis_size("lon")
     )
-    one, two = rows_messages(here, grad)
+    edge = ((2, 2, cols, channels), F32)
+    edges = [here[:2], here[rows - 2 :], grad[:2], grad[rows - 2 :]]
+    one, two = call(pack_rows, [edge] * 2, edges)
     r1, r2 = pair_swap(one, two, "lat", False)
     pair = [((9 * channels, channels), BF16)] * 2
     w1_high, w1_low = call(prepare, pair, [first_weight])
@@ -385,8 +370,6 @@
     m1, m2 = call(pack_cols, [line] * 2, [here, grad, r1, r2])
     q1, q2 = pair_swap(m1, m2, "lon", True)
     b2_high, b2_low = call(prepare_back, pair, [second_weight])
-    conv_flops = 2 * 3 * 9 * tall * cols * channels * channels
-    grad_flops = 2 * 3 * 9 * cells * channels * channels
     lines = ((2 * LINE, channels), F32)
     wide = ((rows + 4, cols + 2 * EDGE, channels), F32)
     wide2 = ((tall, cols + 2 * EDGE, channels), F32)
@@ -398,7 +381,6 @@
         lambda *refs: hidden_kernel(scale, *refs),
         [((tall * cols, channels), F32), lines] + taps_1 + taps_2 + halves,
         [here, r1, r2, m1, m2, q1, q2, w1_high, w1_low, t_high, t_low],
-        conv_flops + grad_flops,
         scratch=[wide, wide2] + around,
     )
     got_2 = core_swap(away)
@@ -407,7 +389,6 @@
         inner_kernel,
         taps_2 + [((channels, cells), BF16)] * 2,
         [grad, r1, r2, m1, m2, q1, q2, b2_high, b2_low, hidden, side],
-        conv_flops,
         scratch=[wide] + taps_1 + [wide2] + around + [((channels, cells), F32)],
     )
 
@@ -415,39 +396,33 @@
         return [((count, 9 * channels), F32)] * 2
 
     keep_2, away_2 = call(add_halves, halves_of(channels // 4), [keep_2, got_2], after=[t_low])
-    got_2 = plane_swap(away_2, False, False)
+    got_2 = plane_swap(away_2, False)
     away, keep_1 = call(
         lambda *refs: inner_products(scale, cols, *refs),
         halves,
         [t_high, t_low, x1_high, x1_low],
-        grad_flops,
         after=[keep_2],
     )
     got_1 = core_swap(away)
+    keep_1, away_1 = call(add_halves, halves_of(channels // 4), [keep_1, got_1])
+    got_1 = plane_swap(away_1, False)
     w2_high, w2_low = call(prepare, pair, [second_weight])
     b1_high, b1_low = call(prepare_back, pair, [first_weight])
-    shape = ((rows, cols, channels), F32)
-    (output,) = call(
-        output_kernel, [shape], [here, x2_high, x2_low, w2_high, w2_low], grad_flops, after=[keep_1]
-    )
-    keep_1, away_1, keep_2, away_2 = call(
-        add_both,
-        halves_of(channels // 4) + halves_of(channels // 8),
-        [keep_1, got_1, keep_2, got_2],
-        after=[output],
-    )
-    got_1 = plane_swap(away_1, True, False)
-    got_2 = plane_swap(away_2, False, True)
-    (input_grad,) = call(
+    outs = [((rows, cols, channels), F32), ((8, 128), F32)]
+    output, token = call(
+        output_kernel, outs, [here, x2_high, x2_low, w2_high, w2_low], after=[keep_1]
+    )
+    keep_2, away_2 = call(add_halves, halves_of(channels // 8), [keep_2, got_2], after=[token])
+    got_2 = plane_swap(away_2, True)
+    input_grad, token = call(
         input_grad_kernel,
-        [shape],
+        outs,
         [here, grad, x3_high, x3_low, b1_high, b1_low],
-        grad_flops,
         after=[keep_2],
     )
-    second_grad = last_sum(keep_2, got_2, after=[input_grad])
-    keep_1, away_1 = call(add_halves, halves_of(channels // 8), [keep_1, got_1])
-    got_1 = plane_swap(away_1, True, True)
+    keep_1, away_1 = call(add_halves, halves_of(channels // 8), [keep_1, got_1], after=[token])
+    got_1 = plane_swap(away_1, True)
+    second_grad = last_sum(keep_2, got_2, after=[keep_1])
     first_grad = last_sum(keep_1, got_1)
     return (output[None], input_grad[None], first_grad, second_grad)
 

time: 80 us -> 72.2 us (0.903)
  waiting for transfers between devices: 22.9 us -> 14.2 us
  starting transfers between devices: 25.2 us -> 27.8 us
  local copies, waits for them, and re-layouts: 6.26 us -> 4.78 us
    ppermute x4, waiting for transfers between devices: 12.8 us -> 5.12 us  [plane_swap(): return lax.ppermute(away, ('lat', 'rep'), plane_perm(count, one, two))]
    ppermute x4, starting transfers between devices: 6.2 us -> 8.93 us  [plane_swap(): return lax.ppermute(away, ('lat', 'rep'), plane_perm(count, one, two))]
    unnamed x20 -> x14, local copies, waits for them, and re-layouts: 6.26 us -> 3.76 us
    ppermute x4, waiting for transfers between devices: 3.5 us -> 1.98 us  [pair_swap(): lax.ppermute(block, axis, who + [(b, a) for a, b in who])]
    ppermute x2, waiting for transfers between devices: 0.01 us -> 1.25 us  [core_swap(): return lax.ppermute(away, ('lat', 'rep'), plane_perm(count, 2, 2))]
    slice x0 -> x1, local copies, waits for them, and re-layouts: none -> 1.01 us  [local(): edges = [here[:2], here[rows - 2:], grad[:2], grad[rows - 2:]]]
    pallas_call x16 -> x18, Pallas kernels: 23 us -> 23 us  [call(): pl.pallas_call(kernel, out_shape=[jax.ShapeDtypeStruct(shape, dtype) for...]
  transfers between devices with their start and end apart: 16 -> 16, of which waited for: 6 -> 7; matrix products, arithmetic and copies ran while one was open for 1% -> 1% of each run, Pallas kernels for 16% -> 18%
where the time goes in v2:
time: 72.2 us; the launch traced here: 71.9 us
  starting transfers between devices  27.8 us (39%)
  Pallas kernels  23 us (32%)
  waiting for transfers between devices  14.2 us (20%)
  local copies, waits for them, and re-layouts  4.78 us (7%)
  other arithmetic  1.31 us (2%)
  between operations  0.8 us (1%)
    pallas_call x18, Pallas kernels, call(): pl.pallas_call(kernel, out_shape=[jax.ShapeDtypeStruct(shape, dtype) for...  23 us
    ppermute x4, starting transfers between devices, plane_swap(): return lax.ppermute(away, ('lat', 'rep'), plane_perm(count, one, two))  8.93 us
    ppermute x6, starting transfers between devices, last_sum(): lax.ppermute(blocks[step], 'lon', [(i, i ^ step) for i in range(lon)])  8.01 us
    ppermute x4, starting transfers between devices, pair_swap(): lax.ppermute(block, axis, who + [(b, a) for a, b in who])  6.65 us
    ppermute x6, waiting for transfers between devices, last_sum(): lax.ppermute(blocks[step], 'lon', [(i, i ^ step) for i in range(lon)])  5.84 us
    ppermute x4, waiting for transfers between devices, plane_swap(): return lax.ppermute(away, ('lat', 'rep'), plane_perm(count, one, two))  5.12 us
    ppermute x2, starting transfers between devices, core_swap(): return lax.ppermute(away, ('lat', 'rep'), plane_perm(count, 2, 2))  4.25 us
    unnamed x14, local copies, waits for them, and re-layouts  3.76 us
  transfers between devices with their start and end apart: 16, of which 7 were waited for; matrix products, arithmetic and copies ran while one was open for 1% of the time, Pallas kernels for 18%

profile of v2, /device:TPU:0, one launch (start us, length us, event | category | flops | bytes accessed | tf_op | source)
XLA Modules:
  0.0 71.9 jit_solution(8192949762729769459)
XLA Ops:
  0.6 0.0 copy-start.3
  0.6 1.0 %slice_bitcast_fusion = (f32[2,32,256]{2,1,0:T(8,128)S(1)}, f32[2,32,256]{2,1,0:T(8,128)S(1)}, f32[2,32,256]{2,1,0:T(8,128)S(1)}, f32[2,32,256]{2,1,0:T(8,128)S(1)}) fusion(f32[1,16,32,256]{3,2,1,0:T(8,128)} %param.5, f32[1,16,32,256]{3,2,1,0:T(8,128)} %param.4), kind=kLoop, calls=%fused_computation.2 | loop fusion | bytes 524288 | tf_op jit(solution)/shard_map/slice | solution.py:361
  1.7 0.5 collective-permute-start
  2.2 0.7 collective-permute-start.1
  2.9 0.3 collective-permute-done.refs_2_.refs_1_
  3.2 0.0 collective-permute-done.1.refs_3_.refs_2_
  3.2 0.0 copy-start
  3.2 1.0 %copy-done = f32[1,16,32,256]{3,2,1,0:T(8,128)S(1)} copy-done((f32[1,16,32,256]{3,2,1,0:T(8,128)S(1)}, f32[1,16,32,256]{3,2,1,0:T(8,128)}, u32[]{:S(2)}) %copy-start) | copy-done | bytes 524312
  4.3 0.0 copy-start.2
  4.3 1.0 %copy-done.2 = f32[1,16,32,256]{3,2,1,0:T(8,128)S(1)} copy-done((f32[1,16,32,256]{3,2,1,0:T(8,128)S(1)}, f32[1,16,32,256]{3,2,1,0:T(8,128)}, u32[]{:S(2)}) %copy-start.2) | copy-done | bytes 524312
  5.3 0.1 shard_map.76
  5.4 3.0 %collective-permute-start.2 = (f32[2,2,24,256]{3,2,1,0:T(8,128)S(1)}, f32[2,2,24,256]{3,2,1,0:T(8,128)S(1)}, u32[]{:S(2)}, u32[]{:S(2)}) collective-permute-start(f32[2,2,24,256]{3,2,1,0:T(8,128)S(1)} %get-tuple-element.54.refs_3_), channel_id=1, source_target_pairs={{0,8},{16,24},{8,0},{24,16},{1,9},{17,25},{9,1},{25,17},{2,10},{18... | collective-permute-start | bytes 294920 | tf_op jit(solution)/shard_map/ppermute | solution.py:113
  8.4 2.5 %collective-permute-start.3 = (f32[2,2,24,256]{3,2,1,0:T(8,128)S(1)}, f32[2,2,24,256]{3,2,1,0:T(8,128)S(1)}, u32[]{:S(2)}, u32[]{:S(2)}) collective-permute-start(f32[2,2,24,256]{3,2,1,0:T(8,128)S(1)} %get-tuple-element.55.refs_4_), channel_id=1, source_target_pairs={{8,16},{24,0},{16,8},{0,24},{9,17},{25,1},{17,9},{1,25},{10,18},{2... | collective-permute-start | bytes 294920 | tf_op jit(solution)/shard_map/ppermute | solution.py:113
  10.8 0.0 copy-done.3
  10.9 0.3 shard_map.78
  11.1 0.0 copy-start.5
  11.1 1.7 %copy-done.5 = f32[2304,256]{1,0:T(8,128)S(1)} copy-done((f32[2304,256]{1,0:T(8,128)S(1)}, f32[2304,256]{1,0:T(8,128)}, u32[]{:S(2)}) %copy-start.5) | copy-done | bytes 2359320
  12.8 0.3 shard_map.77
  13.1 0.0 collective-permute-done.2.refs_5_
  13.2 1.6 %collective-permute-done.3.refs_6_ = f32[2,2,24,256]{3,2,1,0:T(8,128)S(1)} collective-permute-done((f32[2,2,24,256]{3,2,1,0:T(8,128)S(1)}, f32[2,2,24,256]{3,2,1,0:T(8,128)S(1)}, u32[]{:S(2)}, u32[]{:S(2)}) %collective-permute-start.3) | collective-permute-done | bytes 98336 | tf_op jit(solution)/shard_map/ppermute | solution.py:113
  14.8 0.0 copy-done.1
  14.8 8.1 %shard_map.79 = (f32[576,256]{1,0:T(8,128)S(1)}, f32[48,256]{1,0:T(8,128)S(1)}, bf16[640,768]{1,0:T(8,128)(2,1)S(1)}, bf16[640,768]{1,0:T(8,128)(2,1)S(1)}, bf16...) custom-call(f32[16,32,256]{2,1,0:T(8,128)S(1)} %bitcast.17, ...), custom_call_target="tpu_custom_call" | custom-call | tf_op jit(solution)/shard_map/pallas_call | solution.py:24
  23.0 4.2 %collective-permute-start.4 = (f32[128,2304]{1,0:T(8,128)S(1)}, f32[128,2304]{1,0:T(8,128)S(1)}, u32[]{:S(2)}, u32[]{:S(2)}) collective-permute-start(f32[128,2304]{1,0:T(8,128)S(1)} %get-tuple-element.73), channel_id=1, source_target_pairs={{0,2},{1,3},{2,0},{3,1},{4,6},{5,7},{6,4},{7,5},{8,10},{9,11},{10,... | collective-permute-start | bytes 3538952 | tf_op jit(solution)/shard_map/ppermute | solution.py:318
  27.1 0.0 copy-done.4
  27.1 0.7 shard_map.81
  27.8 3.3 %shard_map.82 = (bf16[576,768]{1,0:T(8,128)(2,1)S(1)}, bf16[576,768]{1,0:T(8,128)(2,1)S(1)}, bf16[256,512]{1,0:T(8,128)(2,1)S(1)}, bf16[256,512]{1,0:T(8,128)(2,1)S(1)}) custom-call(f32[16,32,256]{2,1,0:T(8,128)S(1)} %bitcast.22, f32[2,2,32,256]{3,2,1,0:T(8,128)S(1)} %collective-permute-done.refs_2_.refs_1_, ...), custom_call_target="tpu_custom_call" | custom-call | tf_op jit(solution)/shard_map/pallas_call | solution.py:24
  31.1 0.0 collective-permute-done.4.refs_1_
  31.1 0.1 shard_map.83
  31.3 2.0 %shard_map.84 = (f32[128,2304]{1,0:T(8,128)S(1)}, f32[128,2304]{1,0:T(8,128)S(1)}) custom-call(bf16[256,512]{1,0:T(8,128)(2,1)S(1)} %get-tuple-element.68.refs_0_, bf16[256,512]{1,0:T(8,128)(2,1)S(1)} %get-tuple-element.69.refs_2_.refs_1_, bf16[640,768]{1,0:T(8,128)(2,1)S(1)} %get-tuple-element.70.refs_2_, bf16[640,768]{1,0:T(8,128)(2,1)S(1)} %get-tuple-element.71.refs_3_, ...), custom_call_target="tpu_custom_call" | custom-call | tf_op jit(solution)/shard_map/pallas_call | solution.py:24
  33.3 0.1 collective-permute-start.5
  33.3 1.6 %collective-permute-start.6 = (f32[64,2304]{1,0:T(8,128)S(1)}, f32[64,2304]{1,0:T(8,128)S(1)}, u32[]{:S(2)}, u32[]{:S(2)}) collective-permute-start(f32[64,2304]{1,0:T(8,128)S(1)} %get-tuple-element.83), channel_id=1, source_target_pairs={{0,1},{1,0},{2,6},{3,7},{4,5},{5,4},{6,2},{7,3},{8,9},{9,8},{10,14... | collective-permute-start | bytes 1769480 | tf_op jit(solution)/shard_map/ppermute | solution.py:313
  34.9 1.2 %collective-permute-done.5.refs_1_ = f32[128,2304]{1,0:T(8,128)S(1)} collective-permute-done((f32[128,2304]{1,0:T(8,128)S(1)}, f32[128,2304]{1,0:T(8,128)S(1)}, u32[]{:S(2)}, u32[]{:S(2)}) %collective-permute-start.5) | collective-permute-done | bytes 1179680 | tf_op jit(solution)/shard_map/ppermute | solution.py:318
  36.2 0.1 shard_map.85
  36.3 1.6 %collective-permute-start.7 = (f32[64,2304]{1,0:T(8,128)S(1)}, f32[64,2304]{1,0:T(8,128)S(1)}, u32[]{:S(2)}, u32[]{:S(2)}) collective-permute-start(f32[64,2304]{1,0:T(8,128)S(1)} %get-tuple-element.87), channel_id=1, source_target_pairs={{0,1},{1,0},{2,6},{3,7},{4,5},{5,4},{6,2},{7,3},{8,9},{9,8},{10,14... | collective-permute-start | bytes 1769480 | tf_op jit(solution)/shard_map/ppermute | solution.py:313
  37.9 0.3 shard_map.80
  38.2 0.0 copy-start.6
  38.2 3.0 %shard_map.86 = (f32[16,32,256]{2,1,0:T(8,128)}, f32[8,128]{1,0:T(8,128)S(1)}) custom-call(f32[16,32,256]{2,1,0:T(8,128)S(1)} %bitcast.18, bf16[576,768]{1,0:T(8,128)(2,1)S(1)} %get-tuple-element.60.refs_1_, bf16[576,768]{1,0:T(8,128)(2,1)S(1)} %get-tuple-element.61.refs_2_, bf16[2304,256]{1,0:T(8,128)(2,1)S(1)} %get-tuple-element.62.refs_3_, ...), custom_call_target="tpu_custom_call" | custom-call | tf_op jit(solution)/shard_map/pallas_call | solution.py:24
  41.2 2.1 %collective-permute-done.6.refs_1_ = f32[64,2304]{1,0:T(8,128)S(1)} collective-permute-done((f32[64,2304]{1,0:T(8,128)S(1)}, f32[64,2304]{1,0:T(8,128)S(1)}, u32[]{:S(2)}, u32[]{:S(2)}) %collective-permute-start.6) | collective-permute-done | bytes 589856 | tf_op jit(solution)/shard_map/ppermute | solution.py:313
  43.3 0.1 shard_map.88
  43.4 2.9 %collective-permute-start.12 = (f32[32,2304]{1,0:T(8,128)S(1)}, f32[32,2304]{1,0:T(8,128)S(1)}, u32[]{:S(2)}, u32[]{:S(2)}) collective-permute-start(f32[32,2304]{1,0:T(8,128)S(1)} %get-tuple-element.95), channel_id=1, source_target_pairs={{0,4},{1,5},{2,3},{3,2},{4,0},{5,1},{6,7},{7,6},{8,12},{9,13},{10,... | collective-permute-start | bytes 884744 | tf_op jit(solution)/shard_map/ppermute | solution.py:313
  46.2 0.0 copy-done.6
  46.2 0.7 shard_map.87
  46.9 2.8 %shard_map.89 = (f32[16,32,256]{2,1,0:T(8,128)}, f32[8,128]{1,0:T(8,128)S(1)}) custom-call(f32[16,32,256]{2,1,0:T(8,128)S(1)} %bitcast.19, f32[16,32,256]{2,1,0:T(8,128)S(1)} %bitcast.23, bf16[576,768]{1,0:T(8,128)(2,1)S(1)} %get-tuple-element.79.refs_2_, bf16[576,768]{1,0:T(8,128)(2,1)S(1)} %get-tuple-element.80.refs_3_, ...), custom_call_target="tpu_custom_call" | custom-call | tf_op jit(solution)/shard_map/pallas_call | solution.py:24
  49.7 3.0 %collective-permute-done.7.refs_1_ = f32[64,2304]{1,0:T(8,128)S(1)} collective-permute-done((f32[64,2304]{1,0:T(8,128)S(1)}, f32[64,2304]{1,0:T(8,128)S(1)}, u32[]{:S(2)}, u32[]{:S(2)}) %collective-permute-start.7) | collective-permute-done | bytes 589856 | tf_op jit(solution)/shard_map/ppermute | solution.py:313
  52.8 0.1 shard_map.90
  52.8 2.9 %collective-permute-start.8 = (f32[32,2304]{1,0:T(8,128)S(1)}, f32[32,2304]{1,0:T(8,128)S(1)}, u32[]{:S(2)}, u32[]{:S(2)}) collective-permute-start(f32[32,2304]{1,0:T(8,128)S(1)} %get-tuple-element.90), channel_id=1, source_target_pairs={{0,4},{1,5},{2,3},{3,2},{4,0},{5,1},{6,7},{7,6},{8,12},{9,13},{10,... | collective-permute-start | bytes 884744 | tf_op jit(solution)/shard_map/ppermute | solution.py:313
  55.7 0.0 collective-permute-done.12.refs_1_
  55.7 0.5 shard_map.92
  56.2 0.1 collective-permute-start.13
  56.3 3.1 %collective-permute-start.14 = (f32[32,576]{1,0:T(8,128)S(1)}, f32[32,576]{1,0:T(8,128)S(1)}, u32[]{:S(2)}, u32[]{:S(2)}) collective-permute-start(f32[32,576]{1,0:T(8,128)S(1)} %get-tuple-element.98), channel_id=1, source_target_pairs={{0,16},{8,24},{16,0},{24,8},{1,17},{9,25},{17,1},{25,9},{2,18},{10... | collective-permute-start | bytes 221192 | tf_op jit(solution)/shard_map/ppermute | solution.py:348
  59.4 1.3 %collective-permute-start.15 = (f32[32,576]{1,0:T(8,128)S(1)}, f32[32,576]{1,0:T(8,128)S(1)}, u32[]{:S(2)}, u32[]{:S(2)}) collective-permute-start(f32[32,576]{1,0:T(8,128)S(1)} %get-tuple-element.99), channel_id=1, source_target_pairs={{0,24},{8,16},{16,8},{24,0},{1,25},{9,17},{17,9},{25,1},{2,26},{10... | collective-permute-start | bytes 221192 | tf_op jit(solution)/shard_map/ppermute | solution.py:348
  60.7 0.0 collective-permute-done.8.refs_1_
  60.7 0.5 shard_map.91
  61.2 1.6 %collective-permute-start.10 = (f32[32,576]{1,0:T(8,128)S(1)}, f32[32,576]{1,0:T(8,128)S(1)}, u32[]{:S(2)}, u32[]{:S(2)}) collective-permute-start(f32[32,576]{1,0:T(8,128)S(1)} %get-tuple-element.93), channel_id=1, source_target_pairs={{0,16},{8,24},{16,0},{24,8},{1,17},{9,25},{17,1},{25,9},{2,18},{10... | collective-permute-start | bytes 221192 | tf_op jit(solution)/shard_map/ppermute | solution.py:348
  62.8 1.0 %collective-permute-start.11 = (f32[32,576]{1,0:T(8,128)S(1)}, f32[32,576]{1,0:T(8,128)S(1)}, u32[]{:S(2)}, u32[]{:S(2)}) collective-permute-start(f32[32,576]{1,0:T(8,128)S(1)} %get-tuple-element.94), channel_id=1, source_target_pairs={{0,24},{8,16},{16,8},{24,0},{1,25},{9,17},{17,9},{25,1},{2,26},{10... | collective-permute-start | bytes 221192 | tf_op jit(solution)/shard_map/ppermute | solution.py:348
  63.9 0.0 collective-permute-done.13
  63.9 0.9 %collective-permute-start.9 = (f32[32,576]{1,0:T(8,128)S(1)}, f32[32,576]{1,0:T(8,128)S(1)}, u32[]{:S(2)}, u32[]{:S(2)}) collective-permute-start(f32[32,576]{1,0:T(8,128)S(1)} %get-tuple-element.92), channel_id=1, source_target_pairs={{0,8},{8,0},{16,24},{24,16},{1,9},{9,1},{17,25},{25,17},{2,10},{10... | collective-permute-start | bytes 221192 | tf_op jit(solution)/shard_map/ppermute | solution.py:348
  64.8 1.7 %collective-permute-done.14 = f32[32,576]{1,0:T(8,128)S(1)} collective-permute-done((f32[32,576]{1,0:T(8,128)S(1)}, f32[32,576]{1,0:T(8,128)S(1)}, u32[]{:S(2)}, u32[]{:S(2)}) %collective-permute-start.14) | collective-permute-done | bytes 73760 | tf_op jit(solution)/shard_map/ppermute | solution.py:348
  66.5 0.0 collective-permute-done.15
  66.5 0.7 add_bitcast_fusion
  67.1 4.2 %collective-permute-done.10 = f32[32,576]{1,0:T(8,128)S(1)} collective-permute-done((f32[32,576]{1,0:T(8,128)S(1)}, f32[32,576]{1,0:T(8,128)S(1)}, u32[]{:S(2)}, u32[]{:S(2)}) %collective-permute-start.10) | collective-permute-done | bytes 73760 | tf_op jit(solution)/shard_map/ppermute | solution.py:348
  71.3 0.0 collective-permute-done.11
  71.3 0.0 collective-permute-done.9
  71.3 0.7 add_bitcast_fusion.1
  (3 shorter events, 0.0 us)
Async XLA Ops:
  0.6 10.2 %copy-start.3 = (f32[1,16,32,256]{3,2,1,0:T(8,128)S(1)}, f32[1,16,32,256]{3,2,1,0:T(8,128)}, u32[]{:S(2)}) copy-start(f32[1,16,32,256]{3,2,1,0:T(8,128)} %param.5) | copy-start | bytes 1572868
  1.7 1.5 %collective-permute-start = (f32[2,2,32,256]{3,2,1,0:T(8,128)S(1)}, f32[2,2,32,256]{3,2,1,0:T(8,128)S(1)}, u32[]{:S(2)}, u32[]{:S(2)}) collective-permute-start(f32[2,2,32,256]{3,2,1,0:T(8,128)S(1)} %get-tuple-element.52), channel_id=1, source_target_pairs={{0,2},{4,6},{2,0},{6,4},{1,3},{5,7},{3,1},{7,5},{8,10},{12,14},{10... | collective-permute-start | bytes 393224 | tf_op jit(solution)/shard_map/ppermute | solution.py:113
  2.2 1.0 %collective-permute-start.1 = (f32[2,2,32,256]{3,2,1,0:T(8,128)S(1)}, f32[2,2,32,256]{3,2,1,0:T(8,128)S(1)}, u32[]{:S(2)}, u32[]{:S(2)}) collective-permute-start(f32[2,2,32,256]{3,2,1,0:T(8,128)S(1)} %get-tuple-element.53), channel_id=1, source_target_pairs={{2,4},{4,2},{3,5},{5,3},{10,12},{12,10},{11,13},{13,11},{18,20},{2... | collective-permute-start | bytes 393224 | tf_op jit(solution)/shard_map/ppermute | solution.py:113
  3.2 1.0 %copy-start = (f32[1,16,32,256]{3,2,1,0:T(8,128)S(1)}, f32[1,16,32,256]{3,2,1,0:T(8,128)}, u32[]{:S(2)}) copy-start(f32[1,16,32,256]{3,2,1,0:T(8,128)} %param.4) | copy-start | bytes 1572868
  4.3 1.0 %copy-start.2 = (f32[1,16,32,256]{3,2,1,0:T(8,128)S(1)}, f32[1,16,32,256]{3,2,1,0:T(8,128)}, u32[]{:S(2)}) copy-start(f32[1,16,32,256]{3,2,1,0:T(8,128)} %param.5) | copy-start | bytes 1572868
  5.4 7.8 %collective-permute-start.2 = (f32[2,2,24,256]{3,2,1,0:T(8,128)S(1)}, f32[2,2,24,256]{3,2,1,0:T(8,128)S(1)}, u32[]{:S(2)}, u32[]{:S(2)}) collective-permute-start(f32[2,2,24,256]{3,2,1,0:T(8,128)S(1)} %get-tuple-element.54.refs_3_), channel_id=1, source_target_pairs={{0,8},{16,24},{8,0},{24,16},{1,9},{17,25},{9,1},{25,17},{2,10},{18... | collective-permute-start | bytes 294920 | tf_op jit(solution)/shard_map/ppermute | solution.py:113
  8.4 6.4 %collective-permute-start.3 = (f32[2,2,24,256]{3,2,1,0:T(8,128)S(1)}, f32[2,2,24,256]{3,2,1,0:T(8,128)S(1)}, u32[]{:S(2)}, u32[]{:S(2)}) collective-permute-start(f32[2,2,24,256]{3,2,1,0:T(8,128)S(1)} %get-tuple-element.55.refs_4_), channel_id=1, source_target_pairs={{8,16},{24,0},{16,8},{0,24},{9,17},{25,1},{17,9},{1,25},{10,18},{2... | collective-permute-start | bytes 294920 | tf_op jit(solution)/shard_map/ppermute | solution.py:113
  11.1 1.7 %copy-start.5 = (f32[2304,256]{1,0:T(8,128)S(1)}, f32[2304,256]{1,0:T(8,128)}, u32[]{:S(2)}) copy-start(f32[2304,256]{1,0:T(8,128)} %refs_0_.7) | copy-start | bytes 7077892
  12.8 2.0 %copy-start.1 = (f32[1,16,32,256]{3,2,1,0:T(8,128)S(1)}, f32[1,16,32,256]{3,2,1,0:T(8,128)}, u32[]{:S(2)}) copy-start(f32[1,16,32,256]{3,2,1,0:T(8,128)} %param.4) | copy-start | bytes 1572868
  14.8 12.3 %copy-start.4 = (f32[2304,256]{1,0:T(8,128)S(1)}, f32[2304,256]{1,0:T(8,128)}, u32[]{:S(2)}) copy-start(f32[2304,256]{1,0:T(8,128)} %refs_0_.6) | copy-start | bytes 7077892
  23.0 8.2 %collective-permute-start.4 = (f32[128,2304]{1,0:T(8,128)S(1)}, f32[128,2304]{1,0:T(8,128)S(1)}, u32[]{:S(2)}, u32[]{:S(2)}) collective-permute-start(f32[128,2304]{1,0:T(8,128)S(1)} %get-tuple-element.73), channel_id=1, source_target_pairs={{0,2},{1,3},{2,0},{3,1},{4,6},{5,7},{6,4},{7,5},{8,10},{9,11},{10,... | collective-permute-start | bytes 3538952 | tf_op jit(solution)/shard_map/ppermute | solution.py:318
  33.3 2.9 %collective-permute-start.5 = (f32[128,2304]{1,0:T(8,128)S(1)}, f32[128,2304]{1,0:T(8,128)S(1)}, u32[]{:S(2)}, u32[]{:S(2)}) collective-permute-start(f32[128,2304]{1,0:T(8,128)S(1)} %get-tuple-element.76), channel_id=1, source_target_pairs={{0,2},{1,3},{2,0},{3,1},{4,6},{5,7},{6,4},{7,5},{8,10},{9,11},{10,... | collective-permute-start | bytes 3538952 | tf_op jit(solution)/shard_map/ppermute | solution.py:318
  33.3 9.9 %collective-permute-start.6 = (f32[64,2304]{1,0:T(8,128)S(1)}, f32[64,2304]{1,0:T(8,128)S(1)}, u32[]{:S(2)}, u32[]{:S(2)}) collective-permute-start(f32[64,2304]{1,0:T(8,128)S(1)} %get-tuple-element.83), channel_id=1, source_target_pairs={{0,1},{1,0},{2,6},{3,7},{4,5},{5,4},{6,2},{7,3},{8,9},{9,8},{10,14... | collective-permute-start | bytes 1769480 | tf_op jit(solution)/shard_map/ppermute | solution.py:313
  36.3 16.5 %collective-permute-start.7 = (f32[64,2304]{1,0:T(8,128)S(1)}, f32[64,2304]{1,0:T(8,128)S(1)}, u32[]{:S(2)}, u32[]{:S(2)}) collective-permute-start(f32[64,2304]{1,0:T(8,128)S(1)} %get-tuple-element.87), channel_id=1, source_target_pairs={{0,1},{1,0},{2,6},{3,7},{4,5},{5,4},{6,2},{7,3},{8,9},{9,8},{10,14... | collective-permute-start | bytes 1769480 | tf_op jit(solution)/shard_map/ppermute | solution.py:313
  38.2 8.0 %copy-start.6 = (f32[2304,256]{1,0:T(8,128)S(1)}, f32[2304,256]{1,0:T(8,128)}, u32[]{:S(2)}) copy-start(f32[2304,256]{1,0:T(8,128)} %refs_0_.7) | copy-start | bytes 7077892
  43.4 12.4 %collective-permute-start.12 = (f32[32,2304]{1,0:T(8,128)S(1)}, f32[32,2304]{1,0:T(8,128)S(1)}, u32[]{:S(2)}, u32[]{:S(2)}) collective-permute-start(f32[32,2304]{1,0:T(8,128)S(1)} %get-tuple-element.95), channel_id=1, source_target_pairs={{0,4},{1,5},{2,3},{3,2},{4,0},{5,1},{6,7},{7,6},{8,12},{9,13},{10,... | collective-permute-start | bytes 884744 | tf_op jit(solution)/shard_map/ppermute | solution.py:313
  52.8 7.9 %collective-permute-start.8 = (f32[32,2304]{1,0:T(8,128)S(1)}, f32[32,2304]{1,0:T(8,128)S(1)}, u32[]{:S(2)}, u32[]{:S(2)}) collective-permute-start(f32[32,2304]{1,0:T(8,128)S(1)} %get-tuple-element.90), channel_id=1, source_target_pairs={{0,4},{1,5},{2,3},{3,2},{4,0},{5,1},{6,7},{7,6},{8,12},{9,13},{10,... | collective-permute-start | bytes 884744 | tf_op jit(solution)/shard_map/ppermute | solution.py:313
  56.2 7.7 %collective-permute-start.13 = (f32[32,576]{1,0:T(8,128)S(1)}, f32[32,576]{1,0:T(8,128)S(1)}, u32[]{:S(2)}, u32[]{:S(2)}) collective-permute-start(f32[32,576]{1,0:T(8,128)S(1)} %get-tuple-element.97), channel_id=1, source_target_pairs={{0,8},{8,0},{16,24},{24,16},{1,9},{9,1},{17,25},{25,17},{2,10},{10... | collective-permute-start | bytes 221192 | tf_op jit(solution)/shard_map/ppermute | solution.py:348
  56.3 10.1 %collective-permute-start.14 = (f32[32,576]{1,0:T(8,128)S(1)}, f32[32,576]{1,0:T(8,128)S(1)}, u32[]{:S(2)}, u32[]{:S(2)}) collective-permute-start(f32[32,576]{1,0:T(8,128)S(1)} %get-tuple-element.98), channel_id=1, source_target_pairs={{0,16},{8,24},{16,0},{24,8},{1,17},{9,25},{17,1},{25,9},{2,18},{10... | collective-permute-start | bytes 221192 | tf_op jit(solution)/shard_map/ppermute | solution.py:348
  59.4 7.1 %collective-permute-start.15 = (f32[32,576]{1,0:T(8,128)S(1)}, f32[32,576]{1,0:T(8,128)S(1)}, u32[]{:S(2)}, u32[]{:S(2)}) collective-permute-start(f32[32,576]{1,0:T(8,128)S(1)} %get-tuple-element.99), channel_id=1, source_target_pairs={{0,24},{8,16},{16,8},{24,0},{1,25},{9,17},{17,9},{25,1},{2,26},{10... | collective-permute-start | bytes 221192 | tf_op jit(solution)/shard_map/ppermute | solution.py:348
  61.2 10.0 %collective-permute-start.10 = (f32[32,576]{1,0:T(8,128)S(1)}, f32[32,576]{1,0:T(8,128)S(1)}, u32[]{:S(2)}, u32[]{:S(2)}) collective-permute-start(f32[32,576]{1,0:T(8,128)S(1)} %get-tuple-element.93), channel_id=1, source_target_pairs={{0,16},{8,24},{16,0},{24,8},{1,17},{9,25},{17,1},{25,9},{2,18},{10... | collective-permute-start | bytes 221192 | tf_op jit(solution)/shard_map/ppermute | solution.py:348
  62.8 8.4 %collective-permute-start.11 = (f32[32,576]{1,0:T(8,128)S(1)}, f32[32,576]{1,0:T(8,128)S(1)}, u32[]{:S(2)}, u32[]{:S(2)}) collective-permute-start(f32[32,576]{1,0:T(8,128)S(1)} %get-tuple-element.94), channel_id=1, source_target_pairs={{0,24},{8,16},{16,8},{24,0},{1,25},{9,17},{17,9},{25,1},{2,26},{10... | collective-permute-start | bytes 221192 | tf_op jit(solution)/shard_map/ppermute | solution.py:348
  63.9 7.4 %collective-permute-start.9 = (f32[32,576]{1,0:T(8,128)S(1)}, f32[32,576]{1,0:T(8,128)S(1)}, u32[]{:S(2)}, u32[]{:S(2)}) collective-permute-start(f32[32,576]{1,0:T(8,128)S(1)} %get-tuple-element.92), channel_id=1, source_target_pairs={{0,8},{8,0},{16,24},{24,16},{1,9},{9,1},{17,25},{25,17},{2,10},{10... | collective-permute-start | bytes 221192 | tf_op jit(solution)/shard_map/ppermute | solution.py:348

commit v3 on v2

--- a/solution.py
+++ b/solution.py
@@ -10,6 +10,7 @@
 F32 = jnp.float32
 BF16 = jnp.bfloat16
 VMEM = pl.BlockSpec(memory_space=pltpu.VMEM)
+PIECES = 4
 LINE = 24
 EDGE = 8
 
@@ -136,8 +137,9 @@
         high[i * each : (i + 1) * each, :], low[i * each : (i + 1) * each, :] = split(part)
 
 
-def turn_grad(grad, high, low, scratch):
+def turn_grad(here, grad, act, high, low, scratch):
     cells = grad.shape[0] * grad.shape[1]
+    act[...] = silu(here[...])
     turn(grad[...].reshape(cells, grad.shape[2]), high, low, scratch)
 
 
@@ -203,7 +205,7 @@
     rows, cols, channels = value.shape
     even_lat = lax.axis_index("lat") % 2 == 0
     one, two = got_rows
-    wide[2 : rows + 2, EDGE : EDGE + cols, :] = function(value[...])
+    wide[2 : rows + 2, EDGE : EDGE + cols, :] = value[...]
     wide[0:2, EDGE : EDGE + cols, :] = function(jnp.where(even_lat, two[f], one[f]))
     wide[rows + 2 : rows + 4, EDGE : EDGE + cols, :] = function(
         jnp.where(even_lat, one[f], two[f])
@@ -230,7 +232,7 @@
     wide[:, EDGE + cols : EDGE + cols + 1, :] = side[LINE : LINE + tall].reshape(tall, 1, channels)
 
 
-def products(t_high, t_low, x_high, x_low, first_row, cells, cols, scale, away, keep):
+def products(t_high, t_low, x_high, x_low, first_row, cells, cols, scale, *outs):
     half = t_high.shape[0] // 2
     width = x_high.shape[1]
     for a in range(3):
@@ -240,30 +242,33 @@
             + dot(t_high[...], x_low[rows, :])
             + dot(t_low[...], x_high[rows, :])
         ) * scale
-        away[:, a * width : (a + 1) * width] = total[half:]
+        *aways, keep = outs
         keep[:, a * width : (a + 1) * width] = total[:half]
+        size = half // len(aways)
+        for i, away in enumerate(aways):
+            part = total[half + i * size : half + (i + 1) * size]
+            away[:, a * width : (a + 1) * width] = part
 
 
 def hidden_kernel(
-    scale, here, r1, r2, m1, m2, q1, q2, w_high, w_low, t_high, t_low,
-    hidden, side, x1_high, x1_low, x2_high, x2_low, away, keep,
+    act, r1, r2, m1, m2, q1, q2, w_high, w_low,
+    hidden, side, x1_high, x1_low, x2_high, x2_low,
     wide, wide2, r_high, r_low,
 ):
-    rows, cols, channels = here.shape
+    rows, cols, channels = act.shape
     left, right = side_columns(m1, m2, q1, q2, 0)
     left, right = [silu(v) for v in left], [silu(v) for v in right]
-    spread(here, silu, (r1, r2), (left, right), 0, wide)
+    spread(act, silu, (r1, r2), (left, right), 0, wide)
     lay_taps(wide, x1_high, x1_low)
     main = convolve(x1_high, x1_low, 0, rows + 2, cols, w_high, w_low)
     around = ring(left, right, w_high, w_low, r_high, r_low)
     hidden[...] = main
     side[...] = around
-    act = jnp.where(inside(rows), silu(main).reshape(rows + 2, cols, channels), 0.0)
+    after = jnp.where(inside(rows), silu(main).reshape(rows + 2, cols, channels), 0.0)
     line = inside_line(rows)
     around = jnp.where(jnp.concatenate([line, line], axis=0), silu(around), 0.0)
-    spread_ext(act, around, wide2)
+    spread_ext(after, around, wide2)
     lay_taps(wide2, x2_high, x2_low)
-    products(t_high, t_low, x2_high, x2_low, 0, rows * cols, cols, scale, away, keep)
 
 
 def inner_kernel(
@@ -285,8 +290,8 @@
     lay_taps(wide2, x3_high, x3_low)
 
 
-def inner_products(scale, cols, t_high, t_low, x1_high, x1_low, away, keep):
-    products(t_high, t_low, x1_high, x1_low, 1, t_high.shape[1], cols, scale, away, keep)
+def products_kernel(scale, cols, first_row, t_high, t_low, x_high, x_low, *outs):
+    products(t_high, t_low, x_high, x_low, first_row, t_high.shape[1], cols, scale, *outs)
 
 
 def output_kernel(here, x_high, x_low, w_high, w_low, out, token):
@@ -318,10 +323,22 @@
     return lax.ppermute(away, ("lat", "rep"), plane_perm(count, 2, 2))
 
 
-def add_halves(keep, got, next_keep, next_away):
+def add_halves(keep, got, next_keep, next_away, *token):
+    for ref in token:
+        ref[...] = jnp.zeros(ref.shape, F32)
     half = keep.shape[0] // 2
     next_keep[...] = keep[:half] + got[:half]
     next_away[...] = keep[half:] + got[half:]
+
+
+def add_pieces(keep, *refs):
+    *gots, next_keep, next_away = refs
+    size = gots[0].shape[0]
+    for i, got in enumerate(gots):
+        value = keep[i * size : (i + 1) * size] + got[...]
+        target = next_keep if i < len(gots) // 2 else next_away
+        place = i % (len(gots) // 2) * size
+        target[place : place + size] = value
 
 
 def cut_blocks(keep, got, *blocks):
@@ -337,14 +354,18 @@
         block[...] = value
 
 
+def wide_sum(keep, got):
+    return lax.psum_scatter(keep + got, "lon", scatter_dimension=1, tiled=True).T
+
+
 def last_sum(keep, got, after=()):
     each, taps = keep.shape
     lon = lax.axis_size("lon")
     if lon != 4:
-        return lax.psum_scatter(keep + got, "lon", scatter_dimension=1, tiled=True).T
+        return wide_sum(keep, got)
     blocks = call(cut_blocks, [((each, taps // lon), F32)] * lon, [keep, got], after=after)
     total = blocks[0]
-    for step in range(1, lon):
+    for step in (3, 2, 1):
         total = total + lax.ppermute(blocks[step], "lon", [(i, i ^ step) for i in range(lon)])
     return total.T
 
@@ -363,11 +384,14 @@
     r1, r2 = pair_swap(one, two, "lat", False)
     pair = [((9 * channels, channels), BF16)] * 2
     w1_high, w1_low = call(prepare, pair, [first_weight])
-    t_high, t_low = call(
-        turn_grad, [((channels, cells), BF16)] * 2, [grad], scratch=[((channels, cells), F32)]
+    act, t_high, t_low = call(
+        turn_grad,
+        [((rows, cols, channels), F32)] + [((channels, cells), BF16)] * 2,
+        [here, grad],
+        scratch=[((channels, cells), F32)],
     )
     line = ((2, 2, LINE, channels), F32)
-    m1, m2 = call(pack_cols, [line] * 2, [here, grad, r1, r2])
+    m1, m2 = call(pack_cols, [line] * 2, [here, grad, r1, r2], after=[t_low])
     q1, q2 = pair_swap(m1, m2, "lon", True)
     b2_high, b2_low = call(prepare_back, pair, [second_weight])
     lines = ((2 * LINE, channels), F32)
@@ -377,11 +401,16 @@
     taps_2 = [((tall * cols, width), BF16)] * 2
     around = [((2 * LINE, 3 * width), BF16)] * 2
     halves = [((channels // 2, 9 * channels), F32)] * 2
-    hidden, side, x1_high, x1_low, x2_high, x2_low, away, keep = call(
-        lambda *refs: hidden_kernel(scale, *refs),
-        [((tall * cols, channels), F32), lines] + taps_1 + taps_2 + halves,
-        [here, r1, r2, m1, m2, q1, q2, w1_high, w1_low, t_high, t_low],
+    hidden, side, x1_high, x1_low, x2_high, x2_low = call(
+        hidden_kernel,
+        [((tall * cols, channels), F32), lines] + taps_1 + taps_2,
+        [act, r1, r2, m1, m2, q1, q2, w1_high, w1_low],
         scratch=[wide, wide2] + around,
+    )
+    away, keep = call(
+        lambda *refs: products_kernel(scale, cols, 0, *refs),
+        halves,
+        [t_high, t_low, x2_high, x2_low],
     )
     got_2 = core_swap(away)
     keep_2 = keep
@@ -397,14 +426,14 @@
 
     keep_2, away_2 = call(add_halves, halves_of(channels // 4), [keep_2, got_2], after=[t_low])
     got_2 = plane_swap(away_2, False)
-    away, keep_1 = call(
-        lambda *refs: inner_products(scale, cols, *refs),
-        halves,
+    *aways, keep_1 = call(
+        lambda *refs: products_kernel(scale, cols, 1, *refs),
+        [((channels // 2 // PIECES, 9 * channels), F32)] * PIECES + halves[:1],
         [t_high, t_low, x1_high, x1_low],
         after=[keep_2],
     )
-    got_1 = core_swap(away)
-    keep_1, away_1 = call(add_halves, halves_of(channels // 4), [keep_1, got_1])
+    gots = [core_swap(away) for away in aways]
+    keep_1, away_1 = call(add_pieces, halves_of(channels // 4), [keep_1, *gots])
     got_1 = plane_swap(away_1, False)
     w2_high, w2_low = call(prepare, pair, [second_weight])
     b1_high, b1_low = call(prepare_back, pair, [first_weight])
@@ -420,7 +449,8 @@
         [here, grad, x3_high, x3_low, b1_high, b1_low],
         after=[keep_2],
     )
-    keep_1, away_1 = call(add_halves, halves_of(channels // 8), [keep_1, got_1], after=[token])
+    each = channels // 8
+    keep_1, away_1 = call(add_halves, halves_of(each), [keep_1, got_1], after=[token])
     got_1 = plane_swap(away_1, True)
     second_grad = last_sum(keep_2, got_2, after=[keep_1])
     first_grad = last_sum(keep_1, got_1)

time: 72.2 us -> 68.4 us (0.947)
  Pallas kernels: 23 us -> 20.2 us
  waiting for transfers between devices: 14.2 us -> 16 us
  local copies, waits for them, and re-layouts: 4.78 us -> 3.06 us
  starting transfers between devices: 27.8 us -> 26.7 us
    pallas_call x18 -> x19, Pallas kernels: 23 us -> 20.2 us  [call(): pl.pallas_call(kernel, out_shape=[jax.ShapeDtypeStruct(shape, dtype) for...]
    ppermute x4, waiting for transfers between devices: 1.98 us -> 3.69 us  [pair_swap(): lax.ppermute(block, axis, who + [(b, a) for a, b in who])]
    unnamed x14 -> x12, local copies, waits for them, and re-layouts: 3.76 us -> 2.1 us
    ppermute x4, waiting for transfers between devices: 5.12 us -> 6.58 us  [plane_swap(): return lax.ppermute(away, ('lat', 'rep'), plane_perm(count, one, two))]
    ppermute x4, starting transfers between devices: 8.93 us -> 7.83 us  [plane_swap(): return lax.ppermute(away, ('lat', 'rep'), plane_perm(count, one, two))]
    ppermute x2 -> x5, waiting for transfers between devices: 1.25 us -> 0.31 us  [core_swap(): return lax.ppermute(away, ('lat', 'rep'), plane_perm(count, 2, 2))]
    ppermute x6, starting transfers between devices: 8.01 us -> 8.91 us  [last_sum(): lax.ppermute(blocks[step], 'lon', [(i, i ^ step) for i in range(lon)])]
    ppermute x2 -> x5, starting transfers between devices: 4.25 us -> 3.66 us  [core_swap(): return lax.ppermute(away, ('lat', 'rep'), plane_perm(count, 2, 2))]
  transfers between devices with their start and end apart: 16 -> 19, of which waited for: 7 -> 6; matrix products, arithmetic and copies ran while one was open for 1% -> 1% of each run, Pallas kernels for 18% -> 19%
where the time goes in v3:
time: 68.4 us; the launch traced here: 68 us
  starting transfers between devices  26.7 us (39%)
  Pallas kernels  20.2 us (30%)
  waiting for transfers between devices  16 us (23%)
  local copies, waits for them, and re-layouts  3.06 us (4%)
  other arithmetic  1.31 us (2%)
  between operations  0.84 us (1%)
    pallas_call x19, Pallas kernels, call(): pl.pallas_call(kernel, out_shape=[jax.ShapeDtypeStruct(shape, dtype) for...  20.2 us
    ppermute x6, starting transfers between devices, last_sum(): lax.ppermute(blocks[step], 'lon', [(i, i ^ step) for i in range(lon)])  8.91 us
    ppermute x4, starting transfers between devices, plane_swap(): return lax.ppermute(away, ('lat', 'rep'), plane_perm(count, one, two))  7.83 us
    ppermute x4, waiting for transfers between devices, plane_swap(): return lax.ppermute(away, ('lat', 'rep'), plane_perm(count, one, two))  6.58 us
    ppermute x4, starting transfers between devices, pair_swap(): lax.ppermute(block, axis, who + [(b, a) for a, b in who])  6.31 us
    ppermute x6, waiting for transfers between devices, last_sum(): lax.ppermute(blocks[step], 'lon', [(i, i ^ step) for i in range(lon)])  5.36 us
    ppermute x4, waiting for transfers between devices, pair_swap(): lax.ppermute(block, axis, who + [(b, a) for a, b in who])  3.69 us
    ppermute x5, starting transfers between devices, core_swap(): return lax.ppermute(away, ('lat', 'rep'), plane_perm(count, 2, 2))  3.66 us
  transfers between devices with their start and end apart: 19, of which 6 were waited for; matrix products, arithmetic and copies ran while one was open for 1% of the time, Pallas kernels for 19%

profile of v3, /device:TPU:0, one launch (start us, length us, event | category | flops | bytes accessed | tf_op | source)
XLA Modules:
  0.0 68.0 jit_solution(776784467729780885)
XLA Ops:
  0.6 1.0 %slice_bitcast_fusion = (f32[2,32,256]{2,1,0:T(8,128)S(1)}, f32[2,32,256]{2,1,0:T(8,128)S(1)}, f32[2,32,256]{2,1,0:T(8,128)S(1)}, f32[2,32,256]{2,1,0:T(8,128)S(1)}) fusion(f32[1,16,32,256]{3,2,1,0:T(8,128)} %param.5, f32[1,16,32,256]{3,2,1,0:T(8,128)} %param.4), kind=kLoop, calls=%fused_computation.2 | loop fusion | bytes 524288 | tf_op jit(solution)/shard_map/slice | solution.py:382
  1.6 0.5 collective-permute-start
  2.2 0.7 collective-permute-start.1
  2.8 0.0 copy-start
  2.8 1.0 %copy-done = f32[1,16,32,256]{3,2,1,0:T(8,128)S(1)} copy-done((f32[1,16,32,256]{3,2,1,0:T(8,128)S(1)}, f32[1,16,32,256]{3,2,1,0:T(8,128)}, u32[]{:S(2)}) %copy-start) | copy-done | bytes 524312
  3.9 1.0 %copy-done.2 = f32[1,16,32,256]{3,2,1,0:T(8,128)S(1)} copy-done((f32[1,16,32,256]{3,2,1,0:T(8,128)S(1)}, f32[1,16,32,256]{3,2,1,0:T(8,128)}, u32[]{:S(2)}) %copy-start.2) | copy-done | bytes 524312
  4.9 0.4 shard_map.75
  5.3 0.0 collective-permute-done.refs_2_.refs_1_
  5.3 0.0 collective-permute-done.1.refs_3_.refs_2_
  5.3 0.1 shard_map.77
  5.4 2.7 %collective-permute-start.2 = (f32[2,2,24,256]{3,2,1,0:T(8,128)S(1)}, f32[2,2,24,256]{3,2,1,0:T(8,128)S(1)}, u32[]{:S(2)}, u32[]{:S(2)}) collective-permute-start(f32[2,2,24,256]{3,2,1,0:T(8,128)S(1)} %get-tuple-element.60.refs_3_), channel_id=1, source_target_pairs={{0,8},{16,24},{8,0},{24,16},{1,9},{17,25},{9,1},{25,17},{2,10},{18... | collective-permute-start | bytes 294920 | tf_op jit(solution)/shard_map/ppermute | solution.py:114
  8.0 2.5 %collective-permute-start.3 = (f32[2,2,24,256]{3,2,1,0:T(8,128)S(1)}, f32[2,2,24,256]{3,2,1,0:T(8,128)S(1)}, u32[]{:S(2)}, u32[]{:S(2)}) collective-permute-start(f32[2,2,24,256]{3,2,1,0:T(8,128)S(1)} %get-tuple-element.61.refs_4_), channel_id=1, source_target_pairs={{8,16},{24,0},{16,8},{0,24},{9,17},{25,1},{17,9},{1,25},{10,18},{2... | collective-permute-start | bytes 294920 | tf_op jit(solution)/shard_map/ppermute | solution.py:114
  10.5 0.3 shard_map.78
  10.9 0.0 collective-permute-done.2.refs_5_
  10.9 3.7 %collective-permute-done.3.refs_6_ = f32[2,2,24,256]{3,2,1,0:T(8,128)S(1)} collective-permute-done((f32[2,2,24,256]{3,2,1,0:T(8,128)S(1)}, f32[2,2,24,256]{3,2,1,0:T(8,128)S(1)}, u32[]{:S(2)}, u32[]{:S(2)}) %collective-permute-start.3) | collective-permute-done | bytes 98336 | tf_op jit(solution)/shard_map/ppermute | solution.py:114
  14.6 3.2 %shard_map.79 = (f32[576,256]{1,0:T(8,128)S(1)}, f32[48,256]{1,0:T(8,128)S(1)}, bf16[640,768]{1,0:T(8,128)(2,1)S(1)}, bf16[640,768]{1,0:T(8,128)(2,1)S(1)}, bf16...) custom-call(f32[16,32,256]{2,1,0:T(8,128)S(1)} %get-tuple-element.56.refs_0_, ...), custom_call_target="tpu_custom_call" | custom-call | tf_op jit(solution)/shard_map/pallas_call | solution.py:25
  17.8 2.0 %shard_map.83 = (f32[128,2304]{1,0:T(8,128)S(1)}, f32[128,2304]{1,0:T(8,128)S(1)}) custom-call(bf16[256,512]{1,0:T(8,128)(2,1)S(1)} %get-tuple-element.76.refs_0_, bf16[256,512]{1,0:T(8,128)(2,1)S(1)} %get-tuple-element.59.refs_4_.refs_1_, bf16[576,768]{1,0:T(8,128)(2,1)S(1)} %get-tuple-element.64.refs_2_.refs_1_, ...), custom_call_target="tpu_custom_call" | custom-call | tf_op jit(solution)/shard_map/pallas_call | solution.py:25
  19.8 0.0 copy-start.3
  19.8 2.6 %collective-permute-start.4 = (f32[128,2304]{1,0:T(8,128)S(1)}, f32[128,2304]{1,0:T(8,128)S(1)}, u32[]{:S(2)}, u32[]{:S(2)}) collective-permute-start(f32[128,2304]{1,0:T(8,128)S(1)} %get-tuple-element.78), channel_id=1, source_target_pairs={{0,2},{1,3},{2,0},{3,1},{4,6},{5,7},{6,4},{7,5},{8,10},{9,11},{10,... | collective-permute-start | bytes 3538952 | tf_op jit(solution)/shard_map/ppermute | solution.py:323
  22.4 0.7 shard_map.81
  23.1 3.3 %shard_map.82 = (bf16[576,768]{1,0:T(8,128)(2,1)S(1)}, bf16[576,768]{1,0:T(8,128)(2,1)S(1)}, bf16[256,512]{1,0:T(8,128)(2,1)S(1)}, bf16[256,512]{1,0:T(8,128)(2,1)S(1)}) custom-call(f32[16,32,256]{2,1,0:T(8,128)S(1)} %bitcast.22, f32[2,2,32,256]{3,2,1,0:T(8,128)S(1)} %collective-permute-done.refs_2_.refs_1_, ...), custom_call_target="tpu_custom_call" | custom-call | tf_op jit(solution)/shard_map/pallas_call | solution.py:25
  26.4 0.0 collective-permute-done.4.refs_1_
  26.4 0.1 shard_map.84
  26.5 2.0 %shard_map.85 = (f32[32,2304]{1,0:T(8,128)S(1)}, f32[32,2304]{1,0:T(8,128)S(1)}, f32[32,2304]{1,0:T(8,128)S(1)}, f32[32,2304]{1,0:T(8,128)S(1)}, f32[128,2304]{1,0:T(8,128)S(1)}) custom-call(bf16[256,512]{1,0:T(8,128)(2,1)S(1)} %get-tuple-element.72.refs_0_, bf16[256,512]{1,0:T(8,128)(2,1)S(1)} %get-tuple-element.73.refs_2_.refs_1_, ...), custom_call_target="tpu_custom_call" | custom-call | tf_op jit(solution)/shard_map/pallas_call | solution.py:25
  28.5 0.3 collective-permute-start.5
  28.9 0.2 collective-permute-start.6
  29.1 0.3 collective-permute-start.7
  29.4 0.2 collective-permute-start.8
  29.6 1.5 %collective-permute-start.9 = (f32[64,2304]{1,0:T(8,128)S(1)}, f32[64,2304]{1,0:T(8,128)S(1)}, u32[]{:S(2)}, u32[]{:S(2)}) collective-permute-start(f32[64,2304]{1,0:T(8,128)S(1)} %get-tuple-element.91), channel_id=1, source_target_pairs={{0,1},{1,0},{2,6},{3,7},{4,5},{5,4},{6,2},{7,3},{8,9},{9,8},{10,14... | collective-permute-start | bytes 1769480 | tf_op jit(solution)/shard_map/ppermute | solution.py:318
  31.1 0.0 collective-permute-done.5.refs_1_
  31.1 0.0 collective-permute-done.6.refs_2_
  31.1 0.0 collective-permute-done.7.refs_3_
  31.1 0.3 collective-permute-done.8.refs_4_
  31.4 0.1 shard_map.86
  31.6 0.0 copy-start.1
  31.6 1.6 %collective-permute-start.10 = (f32[64,2304]{1,0:T(8,128)S(1)}, f32[64,2304]{1,0:T(8,128)S(1)}, u32[]{:S(2)}, u32[]{:S(2)}) collective-permute-start(f32[64,2304]{1,0:T(8,128)S(1)} %get-tuple-element.95), channel_id=1, source_target_pairs={{0,1},{1,0},{2,6},{3,7},{4,5},{5,4},{6,2},{7,3},{8,9},{9,8},{10,14... | collective-permute-start | bytes 1769480 | tf_op jit(solution)/shard_map/ppermute | solution.py:318
  33.1 0.3 shard_map.80
  33.5 3.0 %shard_map.87 = (f32[16,32,256]{2,1,0:T(8,128)}, f32[8,128]{1,0:T(8,128)S(1)}) custom-call(f32[16,32,256]{2,1,0:T(8,128)S(1)} %bitcast.18, bf16[576,768]{1,0:T(8,128)(2,1)S(1)} %get-tuple-element.64.refs_2_.refs_1_, bf16[576,768]{1,0:T(8,128)(2,1)S(1)} %get-tuple-element.65.refs_3_.refs_2_, bf16[2304,256]{1,0:T(8,128)(2,1)S(1)} %get-tuple-element.66.refs_3_, ...), custom_call_target="tpu_custom_call" | custom-call | tf_op jit(solution)/shard_map/pallas_call | solution.py:25
  36.5 3.0 %collective-permute-done.9.refs_1_ = f32[64,2304]{1,0:T(8,128)S(1)} collective-permute-done((f32[64,2304]{1,0:T(8,128)S(1)}, f32[64,2304]{1,0:T(8,128)S(1)}, u32[]{:S(2)}, u32[]{:S(2)}) %collective-permute-start.9) | collective-permute-done | bytes 589856 | tf_op jit(solution)/shard_map/ppermute | solution.py:318
  39.5 0.1 shard_map.89
  39.6 2.4 %collective-permute-start.15 = (f32[32,2304]{1,0:T(8,128)S(1)}, f32[32,2304]{1,0:T(8,128)S(1)}, u32[]{:S(2)}, u32[]{:S(2)}) collective-permute-start(f32[32,2304]{1,0:T(8,128)S(1)} %get-tuple-element.103), channel_id=1, source_target_pairs={{0,4},{1,5},{2,3},{3,2},{4,0},{5,1},{6,7},{7,6},{8,12},{9,13},{10,... | collective-permute-start | bytes 884744 | tf_op jit(solution)/shard_map/ppermute | solution.py:318
  41.9 0.7 shard_map.88
  42.6 2.8 %shard_map.90 = (f32[16,32,256]{2,1,0:T(8,128)}, f32[8,128]{1,0:T(8,128)S(1)}) custom-call(f32[16,32,256]{2,1,0:T(8,128)S(1)} %bitcast.19, f32[16,32,256]{2,1,0:T(8,128)S(1)} %bitcast.23, bf16[576,768]{1,0:T(8,128)(2,1)S(1)} %get-tuple-element.87.refs_2_, bf16[576,768]{1,0:T(8,128)(2,1)S(1)} %get-tuple-element.88.refs_3_, ...), custom_call_target="tpu_custom_call" | custom-call | tf_op jit(solution)/shard_map/pallas_call | solution.py:25
  45.4 3.6 %collective-permute-done.10.refs_1_ = f32[64,2304]{1,0:T(8,128)S(1)} collective-permute-done((f32[64,2304]{1,0:T(8,128)S(1)}, f32[64,2304]{1,0:T(8,128)S(1)}, u32[]{:S(2)}, u32[]{:S(2)}) %collective-permute-start.10) | collective-permute-done | bytes 589856 | tf_op jit(solution)/shard_map/ppermute | solution.py:318
  49.0 0.1 shard_map.91
  49.0 2.4 %collective-permute-start.11 = (f32[32,2304]{1,0:T(8,128)S(1)}, f32[32,2304]{1,0:T(8,128)S(1)}, u32[]{:S(2)}, u32[]{:S(2)}) collective-permute-start(f32[32,2304]{1,0:T(8,128)S(1)} %get-tuple-element.98), channel_id=1, source_target_pairs={{0,4},{1,5},{2,3},{3,2},{4,0},{5,1},{6,7},{7,6},{8,12},{9,13},{10,... | collective-permute-start | bytes 884744 | tf_op jit(solution)/shard_map/ppermute | solution.py:318
  51.4 0.0 collective-permute-done.15.refs_1_
  51.4 0.5 shard_map.93
  51.9 2.7 %collective-permute-start.16 = (f32[32,576]{1,0:T(8,128)S(1)}, f32[32,576]{1,0:T(8,128)S(1)}, u32[]{:S(2)}, u32[]{:S(2)}) collective-permute-start(f32[32,576]{1,0:T(8,128)S(1)} %get-tuple-element.105), channel_id=1, source_target_pairs={{0,24},{8,16},{16,8},{24,0},{1,25},{9,17},{17,9},{25,1},{2,26},{10... | collective-permute-start | bytes 221192 | tf_op jit(solution)/shard_map/ppermute | solution.py:369
  54.6 0.0 collective-permute-start.17
  54.6 1.8 %collective-permute-start.18 = (f32[32,576]{1,0:T(8,128)S(1)}, f32[32,576]{1,0:T(8,128)S(1)}, u32[]{:S(2)}, u32[]{:S(2)}) collective-permute-start(f32[32,576]{1,0:T(8,128)S(1)} %get-tuple-element.107), channel_id=1, source_target_pairs={{0,8},{8,0},{16,24},{24,16},{1,9},{9,1},{17,25},{25,17},{2,10},{10... | collective-permute-start | bytes 221192 | tf_op jit(solution)/shard_map/ppermute | solution.py:369
  56.4 0.0 collective-permute-done.11.refs_1_
  56.4 0.5 shard_map.92
  56.9 2.7 %collective-permute-start.12 = (f32[32,576]{1,0:T(8,128)S(1)}, f32[32,576]{1,0:T(8,128)S(1)}, u32[]{:S(2)}, u32[]{:S(2)}) collective-permute-start(f32[32,576]{1,0:T(8,128)S(1)} %get-tuple-element.100), channel_id=1, source_target_pairs={{0,24},{8,16},{16,8},{24,0},{1,25},{9,17},{17,9},{25,1},{2,26},{10... | collective-permute-start | bytes 221192 | tf_op jit(solution)/shard_map/ppermute | solution.py:369
  59.5 0.0 collective-permute-start.13
  59.5 0.0 collective-permute-done.16
  59.6 1.8 %collective-permute-start.14 = (f32[32,576]{1,0:T(8,128)S(1)}, f32[32,576]{1,0:T(8,128)S(1)}, u32[]{:S(2)}, u32[]{:S(2)}) collective-permute-start(f32[32,576]{1,0:T(8,128)S(1)} %get-tuple-element.102), channel_id=1, source_target_pairs={{0,8},{8,0},{16,24},{24,16},{1,9},{9,1},{17,25},{25,17},{2,10},{10... | collective-permute-start | bytes 221192 | tf_op jit(solution)/shard_map/ppermute | solution.py:369
  61.4 2.2 %collective-permute-done.17 = f32[32,576]{1,0:T(8,128)S(1)} collective-permute-done((f32[32,576]{1,0:T(8,128)S(1)}, f32[32,576]{1,0:T(8,128)S(1)}, u32[]{:S(2)}, u32[]{:S(2)}) %collective-permute-start.17) | collective-permute-done | bytes 73760 | tf_op jit(solution)/shard_map/ppermute | solution.py:369
  63.5 0.0 collective-permute-done.18
  63.5 0.7 add_bitcast_fusion
  64.2 0.0 collective-permute-done.12
  64.2 3.2 %collective-permute-done.13 = f32[32,576]{1,0:T(8,128)S(1)} collective-permute-done((f32[32,576]{1,0:T(8,128)S(1)}, f32[32,576]{1,0:T(8,128)S(1)}, u32[]{:S(2)}, u32[]{:S(2)}) %collective-permute-start.13) | collective-permute-done | bytes 73760 | tf_op jit(solution)/shard_map/ppermute | solution.py:369
  67.4 0.0 collective-permute-done.14
  67.4 0.7 add_bitcast_fusion.1
  (8 shorter events, 0.0 us)
Async XLA Ops:
  1.6 3.6 %collective-permute-start = (f32[2,2,32,256]{3,2,1,0:T(8,128)S(1)}, f32[2,2,32,256]{3,2,1,0:T(8,128)S(1)}, u32[]{:S(2)}, u32[]{:S(2)}) collective-permute-start(f32[2,2,32,256]{3,2,1,0:T(8,128)S(1)} %get-tuple-element.57), channel_id=1, source_target_pairs={{0,2},{4,6},{2,0},{6,4},{1,3},{5,7},{3,1},{7,5},{8,10},{12,14},{10... | collective-permute-start | bytes 393224 | tf_op jit(solution)/shard_map/ppermute | solution.py:114
  2.2 3.1 %collective-permute-start.1 = (f32[2,2,32,256]{3,2,1,0:T(8,128)S(1)}, f32[2,2,32,256]{3,2,1,0:T(8,128)S(1)}, u32[]{:S(2)}, u32[]{:S(2)}) collective-permute-start(f32[2,2,32,256]{3,2,1,0:T(8,128)S(1)} %get-tuple-element.58), channel_id=1, source_target_pairs={{2,4},{4,2},{3,5},{5,3},{10,12},{12,10},{11,13},{13,11},{18,20},{2... | collective-permute-start | bytes 393224 | tf_op jit(solution)/shard_map/ppermute | solution.py:114
  2.8 1.0 %copy-start = (f32[1,16,32,256]{3,2,1,0:T(8,128)S(1)}, f32[1,16,32,256]{3,2,1,0:T(8,128)}, u32[]{:S(2)}) copy-start(f32[1,16,32,256]{3,2,1,0:T(8,128)} %param.4) | copy-start | bytes 1572868
  3.9 1.0 %copy-start.2 = (f32[1,16,32,256]{3,2,1,0:T(8,128)S(1)}, f32[1,16,32,256]{3,2,1,0:T(8,128)}, u32[]{:S(2)}) copy-start(f32[1,16,32,256]{3,2,1,0:T(8,128)} %param.5) | copy-start | bytes 1572868
  4.9 5.6 %copy-start.5 = (f32[2304,256]{1,0:T(8,128)S(1)}, f32[2304,256]{1,0:T(8,128)}, u32[]{:S(2)}) copy-start(f32[2304,256]{1,0:T(8,128)} %refs_0_.7) | copy-start | bytes 7077892
  5.4 5.5 %collective-permute-start.2 = (f32[2,2,24,256]{3,2,1,0:T(8,128)S(1)}, f32[2,2,24,256]{3,2,1,0:T(8,128)S(1)}, u32[]{:S(2)}, u32[]{:S(2)}) collective-permute-start(f32[2,2,24,256]{3,2,1,0:T(8,128)S(1)} %get-tuple-element.60.refs_3_), channel_id=1, source_target_pairs={{0,8},{16,24},{8,0},{24,16},{1,9},{17,25},{9,1},{25,17},{2,10},{18... | collective-permute-start | bytes 294920 | tf_op jit(solution)/shard_map/ppermute | solution.py:114
  8.0 6.5 %collective-permute-start.3 = (f32[2,2,24,256]{3,2,1,0:T(8,128)S(1)}, f32[2,2,24,256]{3,2,1,0:T(8,128)S(1)}, u32[]{:S(2)}, u32[]{:S(2)}) collective-permute-start(f32[2,2,24,256]{3,2,1,0:T(8,128)S(1)} %get-tuple-element.61.refs_4_), channel_id=1, source_target_pairs={{8,16},{24,0},{16,8},{0,24},{9,17},{25,1},{17,9},{1,25},{10,18},{2... | collective-permute-start | bytes 294920 | tf_op jit(solution)/shard_map/ppermute | solution.py:114
  14.6 7.8 %copy-start.4 = (f32[2304,256]{1,0:T(8,128)S(1)}, f32[2304,256]{1,0:T(8,128)}, u32[]{:S(2)}) copy-start(f32[2304,256]{1,0:T(8,128)} %refs_0_.6) | copy-start | bytes 7077892
  19.8 3.3 %copy-start.3 = (f32[1,16,32,256]{3,2,1,0:T(8,128)S(1)}, f32[1,16,32,256]{3,2,1,0:T(8,128)}, u32[]{:S(2)}) copy-start(f32[1,16,32,256]{3,2,1,0:T(8,128)} %param.5) | copy-start | bytes 1572868
  19.8 6.6 %collective-permute-start.4 = (f32[128,2304]{1,0:T(8,128)S(1)}, f32[128,2304]{1,0:T(8,128)S(1)}, u32[]{:S(2)}, u32[]{:S(2)}) collective-permute-start(f32[128,2304]{1,0:T(8,128)S(1)} %get-tuple-element.78), channel_id=1, source_target_pairs={{0,2},{1,3},{2,0},{3,1},{4,6},{5,7},{6,4},{7,5},{8,10},{9,11},{10,... | collective-permute-start | bytes 3538952 | tf_op jit(solution)/shard_map/ppermute | solution.py:323
  28.5 2.6 %collective-permute-start.5 = (f32[32,2304]{1,0:T(8,128)S(1)}, f32[32,2304]{1,0:T(8,128)S(1)}, u32[]{:S(2)}, u32[]{:S(2)}) collective-permute-start(f32[32,2304]{1,0:T(8,128)S(1)} %get-tuple-element.81), channel_id=1, source_target_pairs={{0,2},{1,3},{2,0},{3,1},{4,6},{5,7},{6,4},{7,5},{8,10},{9,11},{10,... | collective-permute-start | bytes 884744 | tf_op jit(solution)/shard_map/ppermute | solution.py:323
  28.9 2.3 %collective-permute-start.6 = (f32[32,2304]{1,0:T(8,128)S(1)}, f32[32,2304]{1,0:T(8,128)S(1)}, u32[]{:S(2)}, u32[]{:S(2)}) collective-permute-start(f32[32,2304]{1,0:T(8,128)S(1)} %get-tuple-element.82), channel_id=1, source_target_pairs={{0,2},{1,3},{2,0},{3,1},{4,6},{5,7},{6,4},{7,5},{8,10},{9,11},{10,... | collective-permute-start | bytes 884744 | tf_op jit(solution)/shard_map/ppermute | solution.py:323
  29.1 2.0 %collective-permute-start.7 = (f32[32,2304]{1,0:T(8,128)S(1)}, f32[32,2304]{1,0:T(8,128)S(1)}, u32[]{:S(2)}, u32[]{:S(2)}) collective-permute-start(f32[32,2304]{1,0:T(8,128)S(1)} %get-tuple-element.83), channel_id=1, source_target_pairs={{0,2},{1,3},{2,0},{3,1},{4,6},{5,7},{6,4},{7,5},{8,10},{9,11},{10,... | collective-permute-start | bytes 884744 | tf_op jit(solution)/shard_map/ppermute | solution.py:323
  29.4 2.1 %collective-permute-start.8 = (f32[32,2304]{1,0:T(8,128)S(1)}, f32[32,2304]{1,0:T(8,128)S(1)}, u32[]{:S(2)}, u32[]{:S(2)}) collective-permute-start(f32[32,2304]{1,0:T(8,128)S(1)} %get-tuple-element.84), channel_id=1, source_target_pairs={{0,2},{1,3},{2,0},{3,1},{4,6},{5,7},{6,4},{7,5},{8,10},{9,11},{10,... | collective-permute-start | bytes 884744 | tf_op jit(solution)/shard_map/ppermute | solution.py:323
  29.6 9.9 %collective-permute-start.9 = (f32[64,2304]{1,0:T(8,128)S(1)}, f32[64,2304]{1,0:T(8,128)S(1)}, u32[]{:S(2)}, u32[]{:S(2)}) collective-permute-start(f32[64,2304]{1,0:T(8,128)S(1)} %get-tuple-element.91), channel_id=1, source_target_pairs={{0,1},{1,0},{2,6},{3,7},{4,5},{5,4},{6,2},{7,3},{8,9},{9,8},{10,14... | collective-permute-start | bytes 1769480 | tf_op jit(solution)/shard_map/ppermute | solution.py:318
  31.6 1.9 %copy-start.1 = (f32[1,16,32,256]{3,2,1,0:T(8,128)S(1)}, f32[1,16,32,256]{3,2,1,0:T(8,128)}, u32[]{:S(2)}) copy-start(f32[1,16,32,256]{3,2,1,0:T(8,128)} %param.4) | copy-start | bytes 1572868
  31.6 17.4 %collective-permute-start.10 = (f32[64,2304]{1,0:T(8,128)S(1)}, f32[64,2304]{1,0:T(8,128)S(1)}, u32[]{:S(2)}, u32[]{:S(2)}) collective-permute-start(f32[64,2304]{1,0:T(8,128)S(1)} %get-tuple-element.95), channel_id=1, source_target_pairs={{0,1},{1,0},{2,6},{3,7},{4,5},{5,4},{6,2},{7,3},{8,9},{9,8},{10,14... | collective-permute-start | bytes 1769480 | tf_op jit(solution)/shard_map/ppermute | solution.py:318
  39.6 11.9 %collective-permute-start.15 = (f32[32,2304]{1,0:T(8,128)S(1)}, f32[32,2304]{1,0:T(8,128)S(1)}, u32[]{:S(2)}, u32[]{:S(2)}) collective-permute-start(f32[32,2304]{1,0:T(8,128)S(1)} %get-tuple-element.103), channel_id=1, source_target_pairs={{0,4},{1,5},{2,3},{3,2},{4,0},{5,1},{6,7},{7,6},{8,12},{9,13},{10,... | collective-permute-start | bytes 884744 | tf_op jit(solution)/shard_map/ppermute | solution.py:318
  49.0 7.3 %collective-permute-start.11 = (f32[32,2304]{1,0:T(8,128)S(1)}, f32[32,2304]{1,0:T(8,128)S(1)}, u32[]{:S(2)}, u32[]{:S(2)}) collective-permute-start(f32[32,2304]{1,0:T(8,128)S(1)} %get-tuple-element.98), channel_id=1, source_target_pairs={{0,4},{1,5},{2,3},{3,2},{4,0},{5,1},{6,7},{7,6},{8,12},{9,13},{10,... | collective-permute-start | bytes 884744 | tf_op jit(solution)/shard_map/ppermute | solution.py:318
  51.9 7.6 %collective-permute-start.16 = (f32[32,576]{1,0:T(8,128)S(1)}, f32[32,576]{1,0:T(8,128)S(1)}, u32[]{:S(2)}, u32[]{:S(2)}) collective-permute-start(f32[32,576]{1,0:T(8,128)S(1)} %get-tuple-element.105), channel_id=1, source_target_pairs={{0,24},{8,16},{16,8},{24,0},{1,25},{9,17},{17,9},{25,1},{2,26},{10... | collective-permute-start | bytes 221192 | tf_op jit(solution)/shard_map/ppermute | solution.py:369
  54.6 8.9 %collective-permute-start.17 = (f32[32,576]{1,0:T(8,128)S(1)}, f32[32,576]{1,0:T(8,128)S(1)}, u32[]{:S(2)}, u32[]{:S(2)}) collective-permute-start(f32[32,576]{1,0:T(8,128)S(1)} %get-tuple-element.106), channel_id=1, source_target_pairs={{0,16},{8,24},{16,0},{24,8},{1,17},{9,25},{17,1},{25,9},{2,18},{10... | collective-permute-start | bytes 221192 | tf_op jit(solution)/shard_map/ppermute | solution.py:369
  54.6 8.9 %collective-permute-start.18 = (f32[32,576]{1,0:T(8,128)S(1)}, f32[32,576]{1,0:T(8,128)S(1)}, u32[]{:S(2)}, u32[]{:S(2)}) collective-permute-start(f32[32,576]{1,0:T(8,128)S(1)} %get-tuple-element.107), channel_id=1, source_target_pairs={{0,8},{8,0},{16,24},{24,16},{1,9},{9,1},{17,25},{25,17},{2,10},{10... | collective-permute-start | bytes 221192 | tf_op jit(solution)/shard_map/ppermute | solution.py:369
  56.9 7.3 %collective-permute-start.12 = (f32[32,576]{1,0:T(8,128)S(1)}, f32[32,576]{1,0:T(8,128)S(1)}, u32[]{:S(2)}, u32[]{:S(2)}) collective-permute-start(f32[32,576]{1,0:T(8,128)S(1)} %get-tuple-element.100), channel_id=1, source_target_pairs={{0,24},{8,16},{16,8},{24,0},{1,25},{9,17},{17,9},{25,1},{2,26},{10... | collective-permute-start | bytes 221192 | tf_op jit(solution)/shard_map/ppermute | solution.py:369
  59.5 7.8 %collective-permute-start.13 = (f32[32,576]{1,0:T(8,128)S(1)}, f32[32,576]{1,0:T(8,128)S(1)}, u32[]{:S(2)}, u32[]{:S(2)}) collective-permute-start(f32[32,576]{1,0:T(8,128)S(1)} %get-tuple-element.101), channel_id=1, source_target_pairs={{0,16},{8,24},{16,0},{24,8},{1,17},{9,25},{17,1},{25,9},{2,18},{10... | collective-permute-start | bytes 221192 | tf_op jit(solution)/shard_map/ppermute | solution.py:369
  59.6 7.8 %collective-permute-start.14 = (f32[32,576]{1,0:T(8,128)S(1)}, f32[32,576]{1,0:T(8,128)S(1)}, u32[]{:S(2)}, u32[]{:S(2)}) collective-permute-start(f32[32,576]{1,0:T(8,128)S(1)} %get-tuple-element.102), channel_id=1, source_target_pairs={{0,8},{8,0},{16,24},{24,16},{1,9},{9,1},{17,25},{25,17},{2,10},{10... | collective-permute-start | bytes 221192 | tf_op jit(solution)/shard_map/ppermute | solution.py:369

commit v4 on v3

--- a/solution.py
+++ b/solution.py
@@ -10,12 +10,12 @@
 F32 = jnp.float32
 BF16 = jnp.bfloat16
 VMEM = pl.BlockSpec(memory_space=pltpu.VMEM)
-PIECES = 4
+LONG = 10**10
 LINE = 24
 EDGE = 8
 
 
-def call(body, outs, ins, scratch=(), limit=16, after=()):
+def call(body, outs, ins, scratch=(), limit=16, after=(), flops=0):
     used, skip = len(ins), len(after)
 
     def kernel(*refs):
@@ -29,7 +29,7 @@
         out_specs=[VMEM] * len(outs),
         scratch_shapes=[pltpu.VMEM(shape, dtype) for shape, dtype in scratch],
         compiler_params=pltpu.CompilerParams(vmem_limit_bytes=limit * 1024 * 1024),
-        cost_estimate=pl.CostEstimate(flops=0, bytes_accessed=0, transcendentals=0),
+        cost_estimate=pl.CostEstimate(flops=flops, bytes_accessed=0, transcendentals=0),
     )(*ins)
 
 
@@ -233,8 +233,8 @@
 
 
 def products(t_high, t_low, x_high, x_low, first_row, cells, cols, scale, *outs):
-    half = t_high.shape[0] // 2
     width = x_high.shape[1]
+    size = t_high.shape[0] // len(outs)
     for a in range(3):
         rows = slice((first_row + a) * cols, (first_row + a) * cols + cells)
         total = (
@@ -242,12 +242,8 @@
             + dot(t_high[...], x_low[rows, :])
             + dot(t_low[...], x_high[rows, :])
         ) * scale
-        *aways, keep = outs
-        keep[:, a * width : (a + 1) * width] = total[:half]
-        size = half // len(aways)
-        for i, away in enumerate(aways):
-            part = total[half + i * size : half + (i + 1) * size]
-            away[:, a * width : (a + 1) * width] = part
+        for i, out in enumerate(outs):
+            out[:, a * width : (a + 1) * width] = total[i * size : (i + 1) * size]
 
 
 def hidden_kernel(
@@ -331,17 +327,9 @@
     next_away[...] = keep[half:] + got[half:]
 
 
-def add_pieces(keep, *refs):
-    *gots, next_keep, next_away = refs
-    size = gots[0].shape[0]
-    for i, got in enumerate(gots):
-        value = keep[i * size : (i + 1) * size] + got[...]
-        target = next_keep if i < len(gots) // 2 else next_away
-        place = i % (len(gots) // 2) * size
-        target[place : place + size] = value
-
-
-def cut_blocks(keep, got, *blocks):
+def cut_blocks(keep, got, *outs):
+    *blocks, token = outs
+    token[...] = jnp.zeros(token.shape, F32)
     total = keep[...] + got[...]
     count = len(blocks)
     size = total.shape[1] // count
@@ -358,16 +346,20 @@
     return lax.psum_scatter(keep + got, "lon", scatter_dimension=1, tiled=True).T
 
 
-def last_sum(keep, got, after=()):
+def add_blocks(one, two, three, four, out):
+    out[...] = (one[...] + two[...] + three[...] + four[...]).T
+
+
+def send_blocks(keep, got, after=(), flops=0):
     each, taps = keep.shape
     lon = lax.axis_size("lon")
-    if lon != 4:
-        return wide_sum(keep, got)
-    blocks = call(cut_blocks, [((each, taps // lon), F32)] * lon, [keep, got], after=after)
-    total = blocks[0]
-    for step in (3, 2, 1):
-        total = total + lax.ppermute(blocks[step], "lon", [(i, i ^ step) for i in range(lon)])
-    return total.T
+    outs = [((each, taps // lon), F32)] * lon + [((8, 128), F32)]
+    *blocks, token = call(cut_blocks, outs, [keep, got], after=after, flops=flops)
+    gots = [
+        lax.ppermute(blocks[step], "lon", [(i, i ^ step) for i in range(lon)])
+        for step in (3, 2, 1)
+    ]
+    return [blocks[0], *gots], token
 
 
 def local(inputs, cotangent, first_weight, second_weight):
@@ -393,7 +385,6 @@
     line = ((2, 2, LINE, channels), F32)
     m1, m2 = call(pack_cols, [line] * 2, [here, grad, r1, r2], after=[t_low])
     q1, q2 = pair_swap(m1, m2, "lon", True)
-    b2_high, b2_low = call(prepare_back, pair, [second_weight])
     lines = ((2 * LINE, channels), F32)
     wide = ((rows + 4, cols + 2 * EDGE, channels), F32)
     wide2 = ((tall, cols + 2 * EDGE, channels), F32)
@@ -407,53 +398,74 @@
         [act, r1, r2, m1, m2, q1, q2, w1_high, w1_low],
         scratch=[wide, wide2] + around,
     )
-    away, keep = call(
-        lambda *refs: products_kernel(scale, cols, 0, *refs),
-        halves,
-        [t_high, t_low, x2_high, x2_low],
-    )
-    got_2 = core_swap(away)
-    keep_2 = keep
+    half = halves[0]
+    each = channels // 8
+
+    def halves_of(count):
+        return [((count, 9 * channels), F32)] * 2
+
+    def second_products(name, after):
+        part = slice(0, channels // 2) if name == "keep" else slice(channels // 2, channels)
+        return call(
+            lambda high, low, *refs: products_kernel(
+                scale, cols, 0, high.at[part], low.at[part], *refs
+            ),
+            [half],
+            [t_high, t_low, x2_high, x2_low],
+            after=after,
+        )[0]
+
+    away_2 = second_products("away", [])
+    got_2 = core_swap(away_2)
+    keep_2 = second_products("keep", [away_2])
+    b2_high, b2_low = call(prepare_back, pair, [second_weight], after=[away_2])
+    w2_high, w2_low = call(prepare, pair, [second_weight], after=[away_2])
+    b1_high, b1_low = call(prepare_back, pair, [first_weight], after=[away_2])
+    keep_2, away_2 = call(
+        add_halves, halves_of(2 * each), [keep_2, got_2], after=[b2_low]
+    )
+    got_2 = plane_swap(away_2, False)
     x3_high, x3_low, t_high, t_low = call(
         inner_kernel,
         taps_2 + [((channels, cells), BF16)] * 2,
         [grad, r1, r2, m1, m2, q1, q2, b2_high, b2_low, hidden, side],
         scratch=[wide] + taps_1 + [wide2] + around + [((channels, cells), F32)],
-    )
-
-    def halves_of(count):
-        return [((count, 9 * channels), F32)] * 2
-
-    keep_2, away_2 = call(add_halves, halves_of(channels // 4), [keep_2, got_2], after=[t_low])
-    got_2 = plane_swap(away_2, False)
-    *aways, keep_1 = call(
+        after=[keep_2],
+    )
+    keep_1, away_1 = call(
         lambda *refs: products_kernel(scale, cols, 1, *refs),
-        [((channels // 2 // PIECES, 9 * channels), F32)] * PIECES + halves[:1],
+        [half, half],
         [t_high, t_low, x1_high, x1_low],
-        after=[keep_2],
-    )
-    gots = [core_swap(away) for away in aways]
-    keep_1, away_1 = call(add_pieces, halves_of(channels // 4), [keep_1, *gots])
+    )
+    got_1 = core_swap(away_1)
+    keep_2, away_2 = call(add_halves, halves_of(each), [keep_2, got_2], flops=LONG)
+    got_2 = plane_swap(away_2, True)
+    keep_1, away_1 = call(add_halves, halves_of(2 * each), [keep_1, got_1], after=[keep_2])
     got_1 = plane_swap(away_1, False)
-    w2_high, w2_low = call(prepare, pair, [second_weight])
-    b1_high, b1_low = call(prepare_back, pair, [first_weight])
     outs = [((rows, cols, channels), F32), ((8, 128), F32)]
     output, token = call(
         output_kernel, outs, [here, x2_high, x2_low, w2_high, w2_low], after=[keep_1]
     )
-    keep_2, away_2 = call(add_halves, halves_of(channels // 8), [keep_2, got_2], after=[token])
-    got_2 = plane_swap(away_2, True)
+    direct = lax.axis_size("lon") == 4
+    if direct:
+        blocks, token = send_blocks(keep_2, got_2, [token], LONG)
+    else:
+        second_grad = wide_sum(keep_2, got_2)
+    keep_1, away_1 = call(add_halves, halves_of(each), [keep_1, got_1], after=[token])
+    got_1 = plane_swap(away_1, True)
     input_grad, token = call(
         input_grad_kernel,
         outs,
         [here, grad, x3_high, x3_low, b1_high, b1_low],
-        after=[keep_2],
-    )
-    each = channels // 8
-    keep_1, away_1 = call(add_halves, halves_of(each), [keep_1, got_1], after=[token])
-    got_1 = plane_swap(away_1, True)
-    second_grad = last_sum(keep_2, got_2, after=[keep_1])
-    first_grad = last_sum(keep_1, got_1)
+        after=[keep_1],
+    )
+    if direct:
+        shape = (blocks[0].shape[1], each)
+        (second_grad,) = call(add_blocks, [(shape, F32)], blocks, after=[token], flops=LONG)
+        blocks, _ = send_blocks(keep_1, got_1, [second_grad])
+        first_grad = sum(blocks[1:], blocks[0]).T
+    else:
+        first_grad = wide_sum(keep_1, got_1)
     return (output[None], input_grad[None], first_grad, second_grad)
 
 

time: 68.4 us -> 66.9 us (0.978)
  waiting for transfers between devices: 16 us -> 13.7 us
  Pallas kernels: 20.2 us -> 21 us
  local copies, waits for them, and re-layouts: 3.06 us -> 3.83 us
    ppermute x6, waiting for transfers between devices: 5.36 us -> 2.84 us  [send_blocks(): lax.ppermute(blocks[step], 'lon', [(i, i ^ step) for i in range(lon)])]
    pallas_call x19 -> x21, Pallas kernels: 20.2 us -> 21 us  [call(): pl.pallas_call(kernel, out_shape=[jax.ShapeDtypeStruct(shape, dtype) for...]
    unnamed x12 -> x13, local copies, waits for them, and re-layouts: 2.1 us -> 2.87 us
    ppermute x5 -> x2, starting transfers between devices: 3.66 us -> 3.4 us  [core_swap(): return lax.ppermute(away, ('lat', 'rep'), plane_perm(count, 2, 2))]
  transfers between devices with their start and end apart: 19 -> 16, of which waited for: 6 -> 7; matrix products, arithmetic and copies ran while one was open for 1% -> 1% of each run, Pallas kernels for 19% -> 23%
where the time goes in v4:
time: 66.9 us; the launch traced here: 66.5 us
  starting transfers between devices  26.5 us (40%)
  Pallas kernels  21 us (31%)
  waiting for transfers between devices  13.7 us (20%)
  local copies, waits for them, and re-layouts  3.83 us (6%)
  between operations  0.84 us (1%)
    pallas_call x21, Pallas kernels, call(): pl.pallas_call(kernel, out_shape=[jax.ShapeDtypeStruct(shape, dtype) for...  21 us
    ppermute x6, starting transfers between devices, send_blocks(): lax.ppermute(blocks[step], 'lon', [(i, i ^ step) for i in range(lon)])  8.84 us
    ppermute x4, starting transfers between devices, plane_swap(): return lax.ppermute(away, ('lat', 'rep'), plane_perm(count, one, two))  7.92 us
    ppermute x4, waiting for transfers between devices, plane_swap(): return lax.ppermute(away, ('lat', 'rep'), plane_perm(count, one, two))  6.48 us
    ppermute x4, starting transfers between devices, pair_swap(): lax.ppermute(block, axis, who + [(b, a) for a, b in who])  6.31 us
    ppermute x4, waiting for transfers between devices, pair_swap(): lax.ppermute(block, axis, who + [(b, a) for a, b in who])  3.69 us
    ppermute x2, starting transfers between devices, core_swap(): return lax.ppermute(away, ('lat', 'rep'), plane_perm(count, 2, 2))  3.4 us
    unnamed x13, local copies, waits for them, and re-layouts  2.87 us
  transfers between devices with their start and end apart: 16, of which 7 were waited for; matrix products, arithmetic and copies ran while one was open for 1% of the time, Pallas kernels for 23%

profile of v4, /device:TPU:0, one launch (start us, length us, event | category | flops | bytes accessed | tf_op | source)
XLA Modules:
  0.0 66.5 jit_solution(13181663676798016117)
XLA Ops:
  0.6 1.0 %slice_bitcast_fusion = (f32[2,32,256]{2,1,0:T(8,128)S(1)}, f32[2,32,256]{2,1,0:T(8,128)S(1)}, f32[2,32,256]{2,1,0:T(8,128)S(1)}, f32[2,32,256]{2,1,0:T(8,128)S(1)}) fusion(f32[1,16,32,256]{3,2,1,0:T(8,128)} %param.5, f32[1,16,32,256]{3,2,1,0:T(8,128)} %param.4), kind=kLoop, calls=%fused_computation.1 | loop fusion | bytes 524288 | tf_op jit(solution)/shard_map/slice | solution.py:374
  1.6 0.5 collective-permute-start
  2.2 0.7 collective-permute-start.1
  2.8 0.0 copy-start
  2.8 1.0 %copy-done = f32[1,16,32,256]{3,2,1,0:T(8,128)S(1)} copy-done((f32[1,16,32,256]{3,2,1,0:T(8,128)S(1)}, f32[1,16,32,256]{3,2,1,0:T(8,128)}, u32[]{:S(2)}) %copy-start) | copy-done | bytes 524312
  3.9 1.0 %copy-done.2 = f32[1,16,32,256]{3,2,1,0:T(8,128)S(1)} copy-done((f32[1,16,32,256]{3,2,1,0:T(8,128)S(1)}, f32[1,16,32,256]{3,2,1,0:T(8,128)}, u32[]{:S(2)}) %copy-start.2) | copy-done | bytes 524312
  4.9 0.4 shard_map.75
  5.3 0.0 collective-permute-done.refs_2_.refs_1_
  5.3 0.0 collective-permute-done.1.refs_3_.refs_2_
  5.3 0.1 shard_map.77
  5.4 2.7 %collective-permute-start.2 = (f32[2,2,24,256]{3,2,1,0:T(8,128)S(1)}, f32[2,2,24,256]{3,2,1,0:T(8,128)S(1)}, u32[]{:S(2)}, u32[]{:S(2)}) collective-permute-start(f32[2,2,24,256]{3,2,1,0:T(8,128)S(1)} %get-tuple-element.56.refs_3_), channel_id=1, source_target_pairs={{0,8},{16,24},{8,0},{24,16},{1,9},{17,25},{9,1},{25,17},{2,10},{18... | collective-permute-start | bytes 294920 | tf_op jit(solution)/shard_map/ppermute | solution.py:114
  8.0 2.5 %collective-permute-start.3 = (f32[2,2,24,256]{3,2,1,0:T(8,128)S(1)}, f32[2,2,24,256]{3,2,1,0:T(8,128)S(1)}, u32[]{:S(2)}, u32[]{:S(2)}) collective-permute-start(f32[2,2,24,256]{3,2,1,0:T(8,128)S(1)} %get-tuple-element.57.refs_4_), channel_id=1, source_target_pairs={{8,16},{24,0},{16,8},{0,24},{9,17},{25,1},{17,9},{1,25},{10,18},{2... | collective-permute-start | bytes 294920 | tf_op jit(solution)/shard_map/ppermute | solution.py:114
  10.5 0.0 copy-done.5
  10.5 0.3 shard_map.78
  10.9 0.0 collective-permute-done.2.refs_5_
  10.9 3.7 %collective-permute-done.3.refs_6_ = f32[2,2,24,256]{3,2,1,0:T(8,128)S(1)} collective-permute-done((f32[2,2,24,256]{3,2,1,0:T(8,128)S(1)}, f32[2,2,24,256]{3,2,1,0:T(8,128)S(1)}, u32[]{:S(2)}, u32[]{:S(2)}) %collective-permute-start.3) | collective-permute-done | bytes 98336 | tf_op jit(solution)/shard_map/ppermute | solution.py:114
  14.6 3.2 %shard_map.79 = (f32[576,256]{1,0:T(8,128)S(1)}, f32[48,256]{1,0:T(8,128)S(1)}, bf16[640,768]{1,0:T(8,128)(2,1)S(1)}, bf16[640,768]{1,0:T(8,128)(2,1)S(1)}, bf16...) custom-call(f32[16,32,256]{2,1,0:T(8,128)S(1)} %get-tuple-element.52.refs_0_, ...), custom_call_target="tpu_custom_call" | custom-call | tf_op jit(solution)/shard_map/pallas_call | solution.py:25
  17.8 1.1 %shard_map.80.refs_1_.refs_4_ = f32[128,2304]{1,0:T(8,128)S(1)} custom-call(bf16[256,512]{1,0:T(8,128)(2,1)S(1)} %get-tuple-element.62.refs_0_, bf16[256,512]{1,0:T(8,128)(2,1)S(1)} %get-tuple-element.55.refs_4_.refs_1_, bf16[576,768]{1,0:T(8,128)(2,1)S(1)} %get-tuple-element.60.refs_2_.refs_1_, bf16[576,768]{1,0:T(8,128)(2,1)S(1)} %get-tuple-element.61.refs_3_.refs_2_), custom_call_target="tpu_custom_call" | custom-call | tf_op jit(solution)/shard_map/pallas_call | solution.py:25
  18.9 0.0 copy-start.4
  18.9 2.6 %collective-permute-start.4 = (f32[128,2304]{1,0:T(8,128)S(1)}, f32[128,2304]{1,0:T(8,128)S(1)}, u32[]{:S(2)}, u32[]{:S(2)}) collective-permute-start(f32[128,2304]{1,0:T(8,128)S(1)} %shard_map.80.refs_1_.refs_4_), channel_id=1, source_target_pairs={{0,2},{1,3},{2,0},{3,1},{4,6},{5,7},{6,4},{7,5},{8,10},{9,11},{10,... | collective-permute-start | bytes 3538952 | tf_op jit(solution)/shard_map/ppermute | solution.py:319
  21.5 1.1 %shard_map.83.refs_0_ = f32[128,2304]{1,0:T(8,128)S(1)} custom-call(bf16[256,512]{1,0:T(8,128)(2,1)S(1)} %get-tuple-element.62.refs_0_, bf16[256,512]{1,0:T(8,128)(2,1)S(1)} %get-tuple-element.55.refs_4_.refs_1_, bf16[576,768]{1,0:T(8,128)(2,1)S(1)} %get-tuple-element.60.refs_2_.refs_1_, bf16[576,768]{1,0:T(8,128)(2,1)S(1)} %get-tuple-element.61.refs_3_.refs_2_, ...), custom_call_target="tpu_custom_call" | custom-call | tf_op jit(solution)/shard_map/pallas_call | solution.py:25
  22.6 0.0 copy-done.4
  22.6 0.7 %shard_map.82 = (bf16[2304,256]{1,0:T(8,128)(2,1)S(1)}, bf16[2304,256]{1,0:T(8,128)(2,1)S(1)}) custom-call(f32[2304,256]{1,0:T(8,128)S(1)} %copy-done.4, f32[128,2304]{1,0:T(8,128)S(1)} %shard_map.80.refs_1_.refs_4_), custom_call_target="tpu_custom_call" | custom-call | tf_op jit(solution)/shard_map/pallas_call | solution.py:25
  23.2 0.7 %collective-permute-done.4.refs_1_ = f32[128,2304]{1,0:T(8,128)S(1)} collective-permute-done((f32[128,2304]{1,0:T(8,128)S(1)}, f32[128,2304]{1,0:T(8,128)S(1)}, u32[]{:S(2)}, u32[]{:S(2)}) %collective-permute-start.4) | collective-permute-done | bytes 1179680 | tf_op jit(solution)/shard_map/ppermute | solution.py:319
  23.9 0.1 shard_map.84
  24.1 1.6 %collective-permute-start.6 = (f32[64,2304]{1,0:T(8,128)S(1)}, f32[64,2304]{1,0:T(8,128)S(1)}, u32[]{:S(2)}, u32[]{:S(2)}) collective-permute-start(f32[64,2304]{1,0:T(8,128)S(1)} %get-tuple-element.76), channel_id=1, source_target_pairs={{0,1},{1,0},{2,6},{3,7},{4,5},{5,4},{6,2},{7,3},{8,9},{9,8},{10,14... | collective-permute-start | bytes 1769480 | tf_op jit(solution)/shard_map/ppermute | solution.py:314
  25.6 0.0 copy-done.3
  25.6 3.3 %shard_map.85 = (bf16[576,768]{1,0:T(8,128)(2,1)S(1)}, bf16[576,768]{1,0:T(8,128)(2,1)S(1)}, bf16[256,512]{1,0:T(8,128)(2,1)S(1)}, bf16[256,512]{1,0:T(8,128)(2,1)S(1)}) custom-call(f32[16,32,256]{2,1,0:T(8,128)S(1)} %bitcast.20, f32[2,2,32,256]{3,2,1,0:T(8,128)S(1)} %collective-permute-done.refs_2_.refs_1_, ...), custom_call_target="tpu_custom_call" | custom-call | tf_op jit(solution)/shard_map/pallas_call | solution.py:25
  29.0 2.0 %shard_map.86 = (f32[128,2304]{1,0:T(8,128)S(1)}, f32[128,2304]{1,0:T(8,128)S(1)}) custom-call(bf16[256,512]{1,0:T(8,128)(2,1)S(1)} %get-tuple-element.70.refs_0_, bf16[256,512]{1,0:T(8,128)(2,1)S(1)} %get-tuple-element.71.refs_1_, bf16[640,768]{1,0:T(8,128)(2,1)S(1)} %get-tuple-element.72.refs_2_, bf16[640,768]{1,0:T(8,128)(2,1)S(1)} %get-tuple-element.73.refs_3_), custom_call_target="tpu_custom_call" | custom-call | tf_op jit(solution)/shard_map/pallas_call | solution.py:25
  31.0 0.8 %collective-permute-start.5 = (f32[128,2304]{1,0:T(8,128)S(1)}, f32[128,2304]{1,0:T(8,128)S(1)}, u32[]{:S(2)}, u32[]{:S(2)}) collective-permute-start(f32[128,2304]{1,0:T(8,128)S(1)} %get-tuple-element.75), channel_id=1, source_target_pairs={{0,2},{1,3},{2,0},{3,1},{4,6},{5,7},{6,4},{7,5},{8,10},{9,11},{10,... | collective-permute-start | bytes 3538952 | tf_op jit(solution)/shard_map/ppermute | solution.py:319
  31.8 2.2 %collective-permute-done.6.refs_1_ = f32[64,2304]{1,0:T(8,128)S(1)} collective-permute-done((f32[64,2304]{1,0:T(8,128)S(1)}, f32[64,2304]{1,0:T(8,128)S(1)}, u32[]{:S(2)}, u32[]{:S(2)}) %collective-permute-start.6) | collective-permute-done | bytes 589856 | tf_op jit(solution)/shard_map/ppermute | solution.py:314
  34.0 0.1 shard_map.87
  34.1 2.5 %collective-permute-start.8 = (f32[32,2304]{1,0:T(8,128)S(1)}, f32[32,2304]{1,0:T(8,128)S(1)}, u32[]{:S(2)}, u32[]{:S(2)}) collective-permute-start(f32[32,2304]{1,0:T(8,128)S(1)} %get-tuple-element.85), channel_id=1, source_target_pairs={{0,4},{1,5},{2,3},{3,2},{4,0},{5,1},{6,7},{7,6},{8,12},{9,13},{10,... | collective-permute-start | bytes 884744 | tf_op jit(solution)/shard_map/ppermute | solution.py:314
  36.6 0.3 shard_map.81
  36.9 0.0 collective-permute-done.5.refs_1_
  36.9 0.0 copy-start.1
  36.9 0.1 shard_map.88
  37.1 1.6 %collective-permute-start.7 = (f32[64,2304]{1,0:T(8,128)S(1)}, f32[64,2304]{1,0:T(8,128)S(1)}, u32[]{:S(2)}, u32[]{:S(2)}) collective-permute-start(f32[64,2304]{1,0:T(8,128)S(1)} %get-tuple-element.84), channel_id=1, source_target_pairs={{0,1},{1,0},{2,6},{3,7},{4,5},{5,4},{6,2},{7,3},{8,9},{9,8},{10,14... | collective-permute-start | bytes 1769480 | tf_op jit(solution)/shard_map/ppermute | solution.py:314
  38.6 0.0 copy-done.1
  38.6 3.0 %shard_map.89 = (f32[16,32,256]{2,1,0:T(8,128)}, f32[8,128]{1,0:T(8,128)S(1)}) custom-call(f32[16,32,256]{2,1,0:T(8,128)S(1)} %bitcast.16, bf16[576,768]{1,0:T(8,128)(2,1)S(1)} %get-tuple-element.60.refs_2_.refs_1_, bf16[576,768]{1,0:T(8,128)(2,1)S(1)} %get-tuple-element.61.refs_3_.refs_2_, bf16[2304,256]{1,0:T(8,128)(2,1)S(1)} %get-tuple-element.63.refs_3_, ...), custom_call_target="tpu_custom_call" | custom-call | tf_op jit(solution)/shard_map/pallas_call | solution.py:25
  41.6 2.5 %collective-permute-done.8.refs_1_ = f32[32,2304]{1,0:T(8,128)S(1)} collective-permute-done((f32[32,2304]{1,0:T(8,128)S(1)}, f32[32,2304]{1,0:T(8,128)S(1)}, u32[]{:S(2)}, u32[]{:S(2)}) %collective-permute-start.8) | collective-permute-done | bytes 294944 | tf_op jit(solution)/shard_map/ppermute | solution.py:314
  44.1 0.5 shard_map.91
  44.6 2.7 %collective-permute-start.10 = (f32[32,576]{1,0:T(8,128)S(1)}, f32[32,576]{1,0:T(8,128)S(1)}, u32[]{:S(2)}, u32[]{:S(2)}) collective-permute-start(f32[32,576]{1,0:T(8,128)S(1)} %get-tuple-element.92), channel_id=1, source_target_pairs={{0,24},{8,16},{16,8},{24,0},{1,25},{9,17},{17,9},{25,1},{2,26},{10... | collective-permute-start | bytes 221192 | tf_op jit(solution)/shard_map/ppermute | solution.py:359
  47.3 0.0 collective-permute-start.11
  47.3 1.8 %collective-permute-start.12 = (f32[32,576]{1,0:T(8,128)S(1)}, f32[32,576]{1,0:T(8,128)S(1)}, u32[]{:S(2)}, u32[]{:S(2)}) collective-permute-start(f32[32,576]{1,0:T(8,128)S(1)} %get-tuple-element.94), channel_id=1, source_target_pairs={{0,8},{8,0},{16,24},{24,16},{1,9},{9,1},{17,25},{25,17},{2,10},{10... | collective-permute-start | bytes 221192 | tf_op jit(solution)/shard_map/ppermute | solution.py:359
  49.1 0.7 %shard_map.90 = (bf16[2304,256]{1,0:T(8,128)(2,1)S(1)}, bf16[2304,256]{1,0:T(8,128)(2,1)S(1)}) custom-call(f32[2304,256]{1,0:T(8,128)S(1)} %copy-done.5, f32[128,2304]{1,0:T(8,128)S(1)} %shard_map.80.refs_1_.refs_4_), custom_call_target="tpu_custom_call" | custom-call | tf_op jit(solution)/shard_map/pallas_call | solution.py:25
  49.8 0.0 collective-permute-done.7.refs_1_
  49.8 0.1 shard_map.92
  49.9 2.3 %collective-permute-start.9 = (f32[32,2304]{1,0:T(8,128)S(1)}, f32[32,2304]{1,0:T(8,128)S(1)}, u32[]{:S(2)}, u32[]{:S(2)}) collective-permute-start(f32[32,2304]{1,0:T(8,128)S(1)} %get-tuple-element.90), channel_id=1, source_target_pairs={{0,4},{1,5},{2,3},{3,2},{4,0},{5,1},{6,7},{7,6},{8,12},{9,13},{10,... | collective-permute-start | bytes 884744 | tf_op jit(solution)/shard_map/ppermute | solution.py:314
  52.1 2.8 %shard_map.93 = (f32[16,32,256]{2,1,0:T(8,128)}, f32[8,128]{1,0:T(8,128)S(1)}) custom-call(f32[16,32,256]{2,1,0:T(8,128)S(1)} %bitcast.17, f32[16,32,256]{2,1,0:T(8,128)S(1)} %bitcast.21, bf16[576,768]{1,0:T(8,128)(2,1)S(1)} %get-tuple-element.80.refs_2_, bf16[576,768]{1,0:T(8,128)(2,1)S(1)} %get-tuple-element.81.refs_3_, ...), custom_call_target="tpu_custom_call" | custom-call | tf_op jit(solution)/shard_map/pallas_call | solution.py:25
  54.9 0.0 collective-permute-done.10.refs_1_
  54.9 0.0 collective-permute-done.11.refs_2_
  54.9 0.0 collective-permute-done.12.refs_3_
  54.9 0.1 shard_map.94.refs_2_
  55.1 1.8 %collective-permute-done.9.refs_1_ = f32[32,2304]{1,0:T(8,128)S(1)} collective-permute-done((f32[32,2304]{1,0:T(8,128)S(1)}, f32[32,2304]{1,0:T(8,128)S(1)}, u32[]{:S(2)}, u32[]{:S(2)}) %collective-permute-start.9) | collective-permute-done | bytes 294944 | tf_op jit(solution)/shard_map/ppermute | solution.py:314
  56.8 1.0 %shard_map.95 = (f32[32,576]{1,0:T(8,128)S(1)}, f32[32,576]{1,0:T(8,128)S(1)}, f32[32,576]{1,0:T(8,128)S(1)}, f32[32,576]{1,0:T(8,128)S(1)}, f32[8,128]{1,0:T(8,128)}) custom-call(f32[32,2304]{1,0:T(8,128)S(1)} %get-tuple-element.88.refs_6_.refs_0_, f32[32,2304]{1,0:T(8,128)S(1)} %collective-permute-done.9.refs_1_, f32[576,32]{1,0:T(8,128)S(1)} %shard_map.94.refs_2_), custom_call_target="tpu_custom_call" | custom-call | tf_op jit(solution)/shard_map/pallas_call | solution.py:25
  57.9 2.6 %collective-permute-start.13 = (f32[32,576]{1,0:T(8,128)S(1)}, f32[32,576]{1,0:T(8,128)S(1)}, u32[]{:S(2)}, u32[]{:S(2)}) collective-permute-start(f32[32,576]{1,0:T(8,128)S(1)} %get-tuple-element.97), channel_id=1, source_target_pairs={{0,24},{8,16},{16,8},{24,0},{1,25},{9,17},{17,9},{25,1},{2,26},{10... | collective-permute-start | bytes 221192 | tf_op jit(solution)/shard_map/ppermute | solution.py:359
  60.5 0.0 collective-permute-start.14
  60.5 1.8 %collective-permute-start.15 = (f32[32,576]{1,0:T(8,128)S(1)}, f32[32,576]{1,0:T(8,128)S(1)}, u32[]{:S(2)}, u32[]{:S(2)}) collective-permute-start(f32[32,576]{1,0:T(8,128)S(1)} %get-tuple-element.99), channel_id=1, source_target_pairs={{0,8},{8,0},{16,24},{24,16},{1,9},{9,1},{17,25},{25,17},{2,10},{10... | collective-permute-start | bytes 221192 | tf_op jit(solution)/shard_map/ppermute | solution.py:359
  62.2 0.8 %copy.8 = f32[576,32]{0,1:T(8,128)} copy(f32[576,32]{1,0:T(8,128)S(1)} %shard_map.94.refs_2_) | data formatting | bytes 147456
  63.0 1.1 %collective-permute-done.13 = f32[32,576]{1,0:T(8,128)S(1)} collective-permute-done((f32[32,576]{1,0:T(8,128)S(1)}, f32[32,576]{1,0:T(8,128)S(1)}, u32[]{:S(2)}, u32[]{:S(2)}) %collective-permute-start.13) | collective-permute-done | bytes 73760 | tf_op jit(solution)/shard_map/ppermute | solution.py:359
  64.1 1.8 %collective-permute-done.14 = f32[32,576]{1,0:T(8,128)S(1)} collective-permute-done((f32[32,576]{1,0:T(8,128)S(1)}, f32[32,576]{1,0:T(8,128)S(1)}, u32[]{:S(2)}, u32[]{:S(2)}) %collective-permute-start.14) | collective-permute-done | bytes 73760 | tf_op jit(solution)/shard_map/ppermute | solution.py:359
  65.9 0.0 collective-permute-done.15
  65.9 0.7 add_bitcast_fusion
  (4 shorter events, 0.0 us)
Async XLA Ops:
  1.6 3.6 %collective-permute-start = (f32[2,2,32,256]{3,2,1,0:T(8,128)S(1)}, f32[2,2,32,256]{3,2,1,0:T(8,128)S(1)}, u32[]{:S(2)}, u32[]{:S(2)}) collective-permute-start(f32[2,2,32,256]{3,2,1,0:T(8,128)S(1)} %get-tuple-element.53), channel_id=1, source_target_pairs={{0,2},{4,6},{2,0},{6,4},{1,3},{5,7},{3,1},{7,5},{8,10},{12,14},{10... | collective-permute-start | bytes 393224 | tf_op jit(solution)/shard_map/ppermute | solution.py:114
  2.2 3.1 %collective-permute-start.1 = (f32[2,2,32,256]{3,2,1,0:T(8,128)S(1)}, f32[2,2,32,256]{3,2,1,0:T(8,128)S(1)}, u32[]{:S(2)}, u32[]{:S(2)}) collective-permute-start(f32[2,2,32,256]{3,2,1,0:T(8,128)S(1)} %get-tuple-element.54), channel_id=1, source_target_pairs={{2,4},{4,2},{3,5},{5,3},{10,12},{12,10},{11,13},{13,11},{18,20},{2... | collective-permute-start | bytes 393224 | tf_op jit(solution)/shard_map/ppermute | solution.py:114
  2.8 1.0 %copy-start = (f32[1,16,32,256]{3,2,1,0:T(8,128)S(1)}, f32[1,16,32,256]{3,2,1,0:T(8,128)}, u32[]{:S(2)}) copy-start(f32[1,16,32,256]{3,2,1,0:T(8,128)} %param.4) | copy-start | bytes 1572868
  3.9 1.0 %copy-start.2 = (f32[1,16,32,256]{3,2,1,0:T(8,128)S(1)}, f32[1,16,32,256]{3,2,1,0:T(8,128)}, u32[]{:S(2)}) copy-start(f32[1,16,32,256]{3,2,1,0:T(8,128)} %param.5) | copy-start | bytes 1572868
  4.9 5.6 %copy-start.5 = (f32[2304,256]{1,0:T(8,128)S(1)}, f32[2304,256]{1,0:T(8,128)}, u32[]{:S(2)}) copy-start(f32[2304,256]{1,0:T(8,128)} %refs_0_.7) | copy-start | bytes 7077892
  5.4 5.5 %collective-permute-start.2 = (f32[2,2,24,256]{3,2,1,0:T(8,128)S(1)}, f32[2,2,24,256]{3,2,1,0:T(8,128)S(1)}, u32[]{:S(2)}, u32[]{:S(2)}) collective-permute-start(f32[2,2,24,256]{3,2,1,0:T(8,128)S(1)} %get-tuple-element.56.refs_3_), channel_id=1, source_target_pairs={{0,8},{16,24},{8,0},{24,16},{1,9},{17,25},{9,1},{25,17},{2,10},{18... | collective-permute-start | bytes 294920 | tf_op jit(solution)/shard_map/ppermute | solution.py:114
  8.0 6.5 %collective-permute-start.3 = (f32[2,2,24,256]{3,2,1,0:T(8,128)S(1)}, f32[2,2,24,256]{3,2,1,0:T(8,128)S(1)}, u32[]{:S(2)}, u32[]{:S(2)}) collective-permute-start(f32[2,2,24,256]{3,2,1,0:T(8,128)S(1)} %get-tuple-element.57.refs_4_), channel_id=1, source_target_pairs={{8,16},{24,0},{16,8},{0,24},{9,17},{25,1},{17,9},{1,25},{10,18},{2... | collective-permute-start | bytes 294920 | tf_op jit(solution)/shard_map/ppermute | solution.py:114
  18.9 3.7 %copy-start.4 = (f32[2304,256]{1,0:T(8,128)S(1)}, f32[2304,256]{1,0:T(8,128)}, u32[]{:S(2)}) copy-start(f32[2304,256]{1,0:T(8,128)} %refs_0_.6) | copy-start | bytes 7077892
  18.9 5.1 %collective-permute-start.4 = (f32[128,2304]{1,0:T(8,128)S(1)}, f32[128,2304]{1,0:T(8,128)S(1)}, u32[]{:S(2)}, u32[]{:S(2)}) collective-permute-start(f32[128,2304]{1,0:T(8,128)S(1)} %shard_map.80.refs_1_.refs_4_), channel_id=1, source_target_pairs={{0,2},{1,3},{2,0},{3,1},{4,6},{5,7},{6,4},{7,5},{8,10},{9,11},{10,... | collective-permute-start | bytes 3538952 | tf_op jit(solution)/shard_map/ppermute | solution.py:319
  23.9 1.7 %copy-start.3 = (f32[1,16,32,256]{3,2,1,0:T(8,128)S(1)}, f32[1,16,32,256]{3,2,1,0:T(8,128)}, u32[]{:S(2)}) copy-start(f32[1,16,32,256]{3,2,1,0:T(8,128)} %param.5) | copy-start | bytes 1572868
  24.1 9.9 %collective-permute-start.6 = (f32[64,2304]{1,0:T(8,128)S(1)}, f32[64,2304]{1,0:T(8,128)S(1)}, u32[]{:S(2)}, u32[]{:S(2)}) collective-permute-start(f32[64,2304]{1,0:T(8,128)S(1)} %get-tuple-element.76), channel_id=1, source_target_pairs={{0,1},{1,0},{2,6},{3,7},{4,5},{5,4},{6,2},{7,3},{8,9},{9,8},{10,14... | collective-permute-start | bytes 1769480 | tf_op jit(solution)/shard_map/ppermute | solution.py:314
  31.0 5.9 %collective-permute-start.5 = (f32[128,2304]{1,0:T(8,128)S(1)}, f32[128,2304]{1,0:T(8,128)S(1)}, u32[]{:S(2)}, u32[]{:S(2)}) collective-permute-start(f32[128,2304]{1,0:T(8,128)S(1)} %get-tuple-element.75), channel_id=1, source_target_pairs={{0,2},{1,3},{2,0},{3,1},{4,6},{5,7},{6,4},{7,5},{8,10},{9,11},{10,... | collective-permute-start | bytes 3538952 | tf_op jit(solution)/shard_map/ppermute | solution.py:319
  34.1 10.0 %collective-permute-start.8 = (f32[32,2304]{1,0:T(8,128)S(1)}, f32[32,2304]{1,0:T(8,128)S(1)}, u32[]{:S(2)}, u32[]{:S(2)}) collective-permute-start(f32[32,2304]{1,0:T(8,128)S(1)} %get-tuple-element.85), channel_id=1, source_target_pairs={{0,4},{1,5},{2,3},{3,2},{4,0},{5,1},{6,7},{7,6},{8,12},{9,13},{10,... | collective-permute-start | bytes 884744 | tf_op jit(solution)/shard_map/ppermute | solution.py:314
  36.9 1.7 %copy-start.1 = (f32[1,16,32,256]{3,2,1,0:T(8,128)S(1)}, f32[1,16,32,256]{3,2,1,0:T(8,128)}, u32[]{:S(2)}) copy-start(f32[1,16,32,256]{3,2,1,0:T(8,128)} %param.4) | copy-start | bytes 1572868
  37.1 12.7 %collective-permute-start.7 = (f32[64,2304]{1,0:T(8,128)S(1)}, f32[64,2304]{1,0:T(8,128)S(1)}, u32[]{:S(2)}, u32[]{:S(2)}) collective-permute-start(f32[64,2304]{1,0:T(8,128)S(1)} %get-tuple-element.84), channel_id=1, source_target_pairs={{0,1},{1,0},{2,6},{3,7},{4,5},{5,4},{6,2},{7,3},{8,9},{9,8},{10,14... | collective-permute-start | bytes 1769480 | tf_op jit(solution)/shard_map/ppermute | solution.py:314
  44.6 10.3 %collective-permute-start.10 = (f32[32,576]{1,0:T(8,128)S(1)}, f32[32,576]{1,0:T(8,128)S(1)}, u32[]{:S(2)}, u32[]{:S(2)}) collective-permute-start(f32[32,576]{1,0:T(8,128)S(1)} %get-tuple-element.92), channel_id=1, source_target_pairs={{0,24},{8,16},{16,8},{24,0},{1,25},{9,17},{17,9},{25,1},{2,26},{10... | collective-permute-start | bytes 221192 | tf_op jit(solution)/shard_map/ppermute | solution.py:359
  47.3 7.6 %collective-permute-start.11 = (f32[32,576]{1,0:T(8,128)S(1)}, f32[32,576]{1,0:T(8,128)S(1)}, u32[]{:S(2)}, u32[]{:S(2)}) collective-permute-start(f32[32,576]{1,0:T(8,128)S(1)} %get-tuple-element.93), channel_id=1, source_target_pairs={{0,16},{8,24},{16,0},{24,8},{1,17},{9,25},{17,1},{25,9},{2,18},{10... | collective-permute-start | bytes 221192 | tf_op jit(solution)/shard_map/ppermute | solution.py:359
  47.3 7.6 %collective-permute-start.12 = (f32[32,576]{1,0:T(8,128)S(1)}, f32[32,576]{1,0:T(8,128)S(1)}, u32[]{:S(2)}, u32[]{:S(2)}) collective-permute-start(f32[32,576]{1,0:T(8,128)S(1)} %get-tuple-element.94), channel_id=1, source_target_pairs={{0,8},{8,0},{16,24},{24,16},{1,9},{9,1},{17,25},{25,17},{2,10},{10... | collective-permute-start | bytes 221192 | tf_op jit(solution)/shard_map/ppermute | solution.py:359
  49.9 7.0 %collective-permute-start.9 = (f32[32,2304]{1,0:T(8,128)S(1)}, f32[32,2304]{1,0:T(8,128)S(1)}, u32[]{:S(2)}, u32[]{:S(2)}) collective-permute-start(f32[32,2304]{1,0:T(8,128)S(1)} %get-tuple-element.90), channel_id=1, source_target_pairs={{0,4},{1,5},{2,3},{3,2},{4,0},{5,1},{6,7},{7,6},{8,12},{9,13},{10,... | collective-permute-start | bytes 884744 | tf_op jit(solution)/shard_map/ppermute | solution.py:314
  57.9 6.2 %collective-permute-start.13 = (f32[32,576]{1,0:T(8,128)S(1)}, f32[32,576]{1,0:T(8,128)S(1)}, u32[]{:S(2)}, u32[]{:S(2)}) collective-permute-start(f32[32,576]{1,0:T(8,128)S(1)} %get-tuple-element.97), channel_id=1, source_target_pairs={{0,24},{8,16},{16,8},{24,0},{1,25},{9,17},{17,9},{25,1},{2,26},{10... | collective-permute-start | bytes 221192 | tf_op jit(solution)/shard_map/ppermute | solution.py:359
  60.5 5.4 %collective-permute-start.14 = (f32[32,576]{1,0:T(8,128)S(1)}, f32[32,576]{1,0:T(8,128)S(1)}, u32[]{:S(2)}, u32[]{:S(2)}) collective-permute-start(f32[32,576]{1,0:T(8,128)S(1)} %get-tuple-element.98), channel_id=1, source_target_pairs={{0,16},{8,24},{16,0},{24,8},{1,17},{9,25},{17,1},{25,9},{2,18},{10... | collective-permute-start | bytes 221192 | tf_op jit(solution)/shard_map/ppermute | solution.py:359
  60.5 5.4 %collective-permute-start.15 = (f32[32,576]{1,0:T(8,128)S(1)}, f32[32,576]{1,0:T(8,128)S(1)}, u32[]{:S(2)}, u32[]{:S(2)}) collective-permute-start(f32[32,576]{1,0:T(8,128)S(1)} %get-tuple-element.99), channel_id=1, source_target_pairs={{0,8},{8,0},{16,24},{24,16},{1,9},{9,1},{17,25},{25,17},{2,10},{10... | collective-permute-start | bytes 221192 | tf_op jit(solution)/shard_map/ppermute | solution.py:359

commit v5 on v4

--- a/solution.py
+++ b/solution.py
@@ -55,13 +55,13 @@
     return sigma * (1.0 + value * (1.0 - sigma))
 
 
-def relative_blocks():
+def relative_blocks(flip):
     lat, y = lax.axis_index("lat"), lax.axis_index("rep")
     x, core = lat // 2, lat % 2
     order = []
     for r_core in range(2):
         c = core + r_core - 2 * core * r_core
-        y_first = c == 0
+        y_first = c == (1 if flip else 0)
         for r_first in range(2):
             for r_second in range(2):
                 move_y = jnp.where(y_first, r_first, r_second)
@@ -128,11 +128,11 @@
         high[tap * size : (tap + 1) * size, :], low[tap * size : (tap + 1) * size, :] = split(block)
 
 
-def turn(value, high, low, scratch):
+def turn(flip, value, high, low, scratch):
     channels = value.shape[1]
     each = channels // 8
     scratch[...] = value.T
-    for i, block in enumerate(relative_blocks()):
+    for i, block in enumerate(relative_blocks(flip)):
         part = scratch[pl.ds(pl.multiple_of(block * each, each), each), :]
         high[i * each : (i + 1) * each, :], low[i * each : (i + 1) * each, :] = split(part)
 
@@ -140,7 +140,7 @@
 def turn_grad(here, grad, act, high, low, scratch):
     cells = grad.shape[0] * grad.shape[1]
     act[...] = silu(here[...])
-    turn(grad[...].reshape(cells, grad.shape[2]), high, low, scratch)
+    turn(False, grad[...].reshape(cells, grad.shape[2]), high, low, scratch)
 
 
 def lay_taps(wide, x_high, x_low):
@@ -281,7 +281,7 @@
     main = jnp.where(inside(rows), main.reshape(rows + 2, cols, channels), 0.0)
     line = inside_line(rows)
     around = jnp.where(jnp.concatenate([line, line], axis=0), around, 0.0)
-    turn(main[1 : rows + 1].reshape(rows * cols, channels), t_high, t_low, turned)
+    turn(True, main[1 : rows + 1].reshape(rows * cols, channels), t_high, t_low, turned)
     spread_ext(main, around, wide2)
     lay_taps(wide2, x3_high, x3_low)
 
@@ -308,9 +308,9 @@
     return [(i, i ^ (odd if (i // 2) % 2 else even)) for i in range(count)]
 
 
-def plane_swap(away, second):
+def plane_swap(away, across):
     count = lax.axis_size("lat") * lax.axis_size("rep")
-    one, two = (4, 1) if second else (1, 4)
+    one, two = (4, 1) if across else (1, 4)
     return lax.ppermute(away, ("lat", "rep"), plane_perm(count, one, two))
 
 
@@ -328,8 +328,9 @@
 
 
 def cut_blocks(keep, got, *outs):
-    *blocks, token = outs
-    token[...] = jnp.zeros(token.shape, F32)
+    blocks = outs[:4]
+    for token in outs[4:]:
+        token[...] = jnp.zeros(token.shape, F32)
     total = keep[...] + got[...]
     count = len(blocks)
     size = total.shape[1] // count
@@ -346,20 +347,21 @@
     return lax.psum_scatter(keep + got, "lon", scatter_dimension=1, tiled=True).T
 
 
-def add_blocks(one, two, three, four, out):
-    out[...] = (one[...] + two[...] + three[...] + four[...]).T
-
-
-def send_blocks(keep, got, after=(), flops=0):
+def add_blocks(one, two, three, four, out, token):
+    token[...] = jnp.zeros(token.shape, F32)
+    out[...] = one[...] + two[...] + three[...] + four[...]
+
+
+def send_blocks(keep, got, after=(), flops=0, tokens=()):
     each, taps = keep.shape
     lon = lax.axis_size("lon")
-    outs = [((each, taps // lon), F32)] * lon + [((8, 128), F32)]
-    *blocks, token = call(cut_blocks, outs, [keep, got], after=after, flops=flops)
+    outs = [((each, taps // lon), F32)] * lon + list(tokens)
+    blocks = call(cut_blocks, outs, [keep, got], after=after, flops=flops)
     gots = [
         lax.ppermute(blocks[step], "lon", [(i, i ^ step) for i in range(lon)])
         for step in (3, 2, 1)
     ]
-    return [blocks[0], *gots], token
+    return [blocks[0], *gots], blocks[lon:]
 
 
 def local(inputs, cotangent, first_weight, second_weight):
@@ -441,18 +443,18 @@
     keep_2, away_2 = call(add_halves, halves_of(each), [keep_2, got_2], flops=LONG)
     got_2 = plane_swap(away_2, True)
     keep_1, away_1 = call(add_halves, halves_of(2 * each), [keep_1, got_1], after=[keep_2])
-    got_1 = plane_swap(away_1, False)
+    got_1 = plane_swap(away_1, True)
     outs = [((rows, cols, channels), F32), ((8, 128), F32)]
     output, token = call(
         output_kernel, outs, [here, x2_high, x2_low, w2_high, w2_low], after=[keep_1]
     )
     direct = lax.axis_size("lon") == 4
     if direct:
-        blocks, token = send_blocks(keep_2, got_2, [token], LONG)
+        blocks, (token,) = send_blocks(keep_2, got_2, [token], LONG, outs[1:])
     else:
         second_grad = wide_sum(keep_2, got_2)
     keep_1, away_1 = call(add_halves, halves_of(each), [keep_1, got_1], after=[token])
-    got_1 = plane_swap(away_1, True)
+    got_1 = plane_swap(away_1, False)
     input_grad, token = call(
         input_grad_kernel,
         outs,
@@ -460,9 +462,12 @@
         after=[keep_1],
     )
     if direct:
-        shape = (blocks[0].shape[1], each)
-        (second_grad,) = call(add_blocks, [(shape, F32)], blocks, after=[token], flops=LONG)
-        blocks, _ = send_blocks(keep_1, got_1, [second_grad])
+        shape = (each, blocks[0].shape[1])
+        summed, token = call(
+            add_blocks, [(shape, F32), outs[1]], blocks, after=[token], flops=LONG
+        )
+        second_grad = summed.T
+        blocks, _ = send_blocks(keep_1, got_1, [token])
         first_grad = sum(blocks[1:], blocks[0]).T
     else:
         first_grad = wide_sum(keep_1, got_1)

time: 66.9 us -> 64.4 us (0.963)
  starting transfers between devices: 26.5 us -> 24.3 us
    ppermute x4, starting transfers between devices: 7.92 us -> 5.73 us  [plane_swap(): return lax.ppermute(away, ('lat', 'rep'), plane_perm(count, one, two))]
    ppermute x4, waiting for transfers between devices: 6.48 us -> 4.98 us  [plane_swap(): return lax.ppermute(away, ('lat', 'rep'), plane_perm(count, one, two))]
    ppermute x6, waiting for transfers between devices: 2.84 us -> 4.01 us  [send_blocks(): lax.ppermute(blocks[step], 'lon', [(i, i ^ step) for i in range(lon)])]
    unnamed x13 -> x12, local copies, waits for them, and re-layouts: 2.87 us -> 2.91 us
  transfers between devices with their start and end apart: 16 -> 16, of which waited for: 7 -> 8; matrix products, arithmetic and copies ran while one was open for 1% -> 0% of each run, Pallas kernels for 23% -> 25%
where the time goes in v5:
time: 64.4 us; the launch traced here: 64.1 us
  starting transfers between devices  24.3 us (38%)
  Pallas kernels  21 us (33%)
  waiting for transfers between devices  13.4 us (21%)
  local copies, waits for them, and re-layouts  3.87 us (6%)
  between operations  0.83 us (1%)
  other arithmetic  0.66 us (1%)
    pallas_call x21, Pallas kernels, call(): pl.pallas_call(kernel, out_shape=[jax.ShapeDtypeStruct(shape, dtype) for...  21 us
    ppermute x6, starting transfers between devices, send_blocks(): lax.ppermute(blocks[step], 'lon', [(i, i ^ step) for i in range(lon)])  8.91 us
    ppermute x4, starting transfers between devices, pair_swap(): lax.ppermute(block, axis, who + [(b, a) for a, b in who])  6.31 us
    ppermute x4, starting transfers between devices, plane_swap(): return lax.ppermute(away, ('lat', 'rep'), plane_perm(count, one, two))  5.73 us
    ppermute x4, waiting for transfers between devices, plane_swap(): return lax.ppermute(away, ('lat', 'rep'), plane_perm(count, one, two))  4.98 us
    ppermute x6, waiting for transfers between devices, send_blocks(): lax.ppermute(blocks[step], 'lon', [(i, i ^ step) for i in range(lon)])  4.01 us
    ppermute x4, waiting for transfers between devices, pair_swap(): lax.ppermute(block, axis, who + [(b, a) for a, b in who])  3.69 us
    ppermute x2, starting transfers between devices, core_swap(): return lax.ppermute(away, ('lat', 'rep'), plane_perm(count, 2, 2))  3.4 us
  transfers between devices with their start and end apart: 16, of which 8 were waited for; matrix products, arithmetic and copies ran while one was open for 0% of the time, Pallas kernels for 25%

profile of v5, /device:TPU:0, one launch (start us, length us, event | category | flops | bytes accessed | tf_op | source)
XLA Modules:
  0.0 64.1 jit_solution(6127466569272916872)
XLA Ops:
  0.6 1.0 %slice_bitcast_fusion = (f32[2,32,256]{2,1,0:T(8,128)S(1)}, f32[2,32,256]{2,1,0:T(8,128)S(1)}, f32[2,32,256]{2,1,0:T(8,128)S(1)}, f32[2,32,256]{2,1,0:T(8,128)S(1)}) fusion(f32[1,16,32,256]{3,2,1,0:T(8,128)} %param.5, f32[1,16,32,256]{3,2,1,0:T(8,128)} %param.4), kind=kLoop, calls=%fused_computation.1 | loop fusion | bytes 524288 | tf_op jit(solution)/shard_map/slice | solution.py:376
  1.6 0.5 collective-permute-start
  2.2 0.7 %collective-permute-start.1 = (f32[2,2,32,256]{3,2,1,0:T(8,128)S(1)}, f32[2,2,32,256]{3,2,1,0:T(8,128)S(1)}, u32[]{:S(2)}, u32[]{:S(2)}) collective-permute-start(f32[2,2,32,256]{3,2,1,0:T(8,128)S(1)} %get-tuple-element.56), channel_id=1, source_target_pairs={{2,4},{4,2},{3,5},{5,3},{10,12},{12,10},{11,13},{13,11},{18,20},{2... | collective-permute-start | bytes 393224 | tf_op jit(solution)/shard_map/ppermute | solution.py:114
  2.8 0.0 copy-start
  2.8 1.0 %copy-done = f32[1,16,32,256]{3,2,1,0:T(8,128)S(1)} copy-done((f32[1,16,32,256]{3,2,1,0:T(8,128)S(1)}, f32[1,16,32,256]{3,2,1,0:T(8,128)}, u32[]{:S(2)}) %copy-start) | copy-done | bytes 524312
  3.9 0.0 copy-start.2
  3.9 1.0 %copy-done.2 = f32[1,16,32,256]{3,2,1,0:T(8,128)S(1)} copy-done((f32[1,16,32,256]{3,2,1,0:T(8,128)S(1)}, f32[1,16,32,256]{3,2,1,0:T(8,128)}, u32[]{:S(2)}) %copy-start.2) | copy-done | bytes 524312
  4.9 0.4 shard_map.75
  5.3 0.0 collective-permute-done.refs_2_.refs_1_
  5.3 0.0 collective-permute-done.1.refs_3_.refs_2_
  5.3 0.1 shard_map.77
  5.4 2.7 %collective-permute-start.2 = (f32[2,2,24,256]{3,2,1,0:T(8,128)S(1)}, f32[2,2,24,256]{3,2,1,0:T(8,128)S(1)}, u32[]{:S(2)}, u32[]{:S(2)}) collective-permute-start(f32[2,2,24,256]{3,2,1,0:T(8,128)S(1)} %get-tuple-element.58.refs_3_), channel_id=1, source_target_pairs={{0,8},{16,24},{8,0},{24,16},{1,9},{17,25},{9,1},{25,17},{2,10},{18... | collective-permute-start | bytes 294920 | tf_op jit(solution)/shard_map/ppermute | solution.py:114
  8.0 2.5 %collective-permute-start.3 = (f32[2,2,24,256]{3,2,1,0:T(8,128)S(1)}, f32[2,2,24,256]{3,2,1,0:T(8,128)S(1)}, u32[]{:S(2)}, u32[]{:S(2)}) collective-permute-start(f32[2,2,24,256]{3,2,1,0:T(8,128)S(1)} %get-tuple-element.59.refs_4_), channel_id=1, source_target_pairs={{8,16},{24,0},{16,8},{0,24},{9,17},{25,1},{17,9},{1,25},{10,18},{2... | collective-permute-start | bytes 294920 | tf_op jit(solution)/shard_map/ppermute | solution.py:114
  10.5 0.0 copy-done.5
  10.5 0.3 shard_map.78
  10.9 0.0 collective-permute-done.2.refs_5_
  10.9 3.7 %collective-permute-done.3.refs_6_ = f32[2,2,24,256]{3,2,1,0:T(8,128)S(1)} collective-permute-done((f32[2,2,24,256]{3,2,1,0:T(8,128)S(1)}, f32[2,2,24,256]{3,2,1,0:T(8,128)S(1)}, u32[]{:S(2)}, u32[]{:S(2)}) %collective-permute-start.3) | collective-permute-done | bytes 98336 | tf_op jit(solution)/shard_map/ppermute | solution.py:114
  14.6 3.2 %shard_map.79 = (f32[576,256]{1,0:T(8,128)S(1)}, f32[48,256]{1,0:T(8,128)S(1)}, bf16[640,768]{1,0:T(8,128)(2,1)S(1)}, bf16[640,768]{1,0:T(8,128)(2,1)S(1)}, bf16...) custom-call(f32[16,32,256]{2,1,0:T(8,128)S(1)} %get-tuple-element.54.refs_0_, ...), custom_call_target="tpu_custom_call" | custom-call | tf_op jit(solution)/shard_map/pallas_call | solution.py:25
  17.8 1.1 %shard_map.80.refs_1_.refs_4_ = f32[128,2304]{1,0:T(8,128)S(1)} custom-call(bf16[256,512]{1,0:T(8,128)(2,1)S(1)} %get-tuple-element.64.refs_0_, bf16[256,512]{1,0:T(8,128)(2,1)S(1)} %get-tuple-element.57.refs_4_.refs_1_, bf16[576,768]{1,0:T(8,128)(2,1)S(1)} %get-tuple-element.62.refs_2_.refs_1_, bf16[576,768]{1,0:T(8,128)(2,1)S(1)} %get-tuple-element.63.refs_3_.refs_2_), custom_call_target="tpu_custom_call" | custom-call | tf_op jit(solution)/shard_map/pallas_call | solution.py:25
  18.9 0.0 copy-start.4
  18.9 2.6 %collective-permute-start.4 = (f32[128,2304]{1,0:T(8,128)S(1)}, f32[128,2304]{1,0:T(8,128)S(1)}, u32[]{:S(2)}, u32[]{:S(2)}) collective-permute-start(f32[128,2304]{1,0:T(8,128)S(1)} %shard_map.80.refs_1_.refs_4_), channel_id=1, source_target_pairs={{0,2},{1,3},{2,0},{3,1},{4,6},{5,7},{6,4},{7,5},{8,10},{9,11},{10,... | collective-permute-start | bytes 3538952 | tf_op jit(solution)/shard_map/ppermute | solution.py:319
  21.5 1.1 %shard_map.83.refs_0_ = f32[128,2304]{1,0:T(8,128)S(1)} custom-call(bf16[256,512]{1,0:T(8,128)(2,1)S(1)} %get-tuple-element.64.refs_0_, bf16[256,512]{1,0:T(8,128)(2,1)S(1)} %get-tuple-element.57.refs_4_.refs_1_, bf16[576,768]{1,0:T(8,128)(2,1)S(1)} %get-tuple-element.62.refs_2_.refs_1_, bf16[576,768]{1,0:T(8,128)(2,1)S(1)} %get-tuple-element.63.refs_3_.refs_2_, ...), custom_call_target="tpu_custom_call" | custom-call | tf_op jit(solution)/shard_map/pallas_call | solution.py:25
  22.6 0.0 copy-done.4
  22.6 0.7 %shard_map.82 = (bf16[2304,256]{1,0:T(8,128)(2,1)S(1)}, bf16[2304,256]{1,0:T(8,128)(2,1)S(1)}) custom-call(f32[2304,256]{1,0:T(8,128)S(1)} %copy-done.4, f32[128,2304]{1,0:T(8,128)S(1)} %shard_map.80.refs_1_.refs_4_), custom_call_target="tpu_custom_call" | custom-call | tf_op jit(solution)/shard_map/pallas_call | solution.py:25
  23.2 0.7 %collective-permute-done.4.refs_1_ = f32[128,2304]{1,0:T(8,128)S(1)} collective-permute-done((f32[128,2304]{1,0:T(8,128)S(1)}, f32[128,2304]{1,0:T(8,128)S(1)}, u32[]{:S(2)}, u32[]{:S(2)}) %collective-permute-start.4) | collective-permute-done | bytes 1179680 | tf_op jit(solution)/shard_map/ppermute | solution.py:319
  23.9 0.1 shard_map.84
  24.1 1.6 %collective-permute-start.6 = (f32[64,2304]{1,0:T(8,128)S(1)}, f32[64,2304]{1,0:T(8,128)S(1)}, u32[]{:S(2)}, u32[]{:S(2)}) collective-permute-start(f32[64,2304]{1,0:T(8,128)S(1)} %get-tuple-element.78), channel_id=1, source_target_pairs={{0,1},{1,0},{2,6},{3,7},{4,5},{5,4},{6,2},{7,3},{8,9},{9,8},{10,14... | collective-permute-start | bytes 1769480 | tf_op jit(solution)/shard_map/ppermute | solution.py:314
  25.6 0.0 copy-done.3
  25.6 3.3 %shard_map.85 = (bf16[576,768]{1,0:T(8,128)(2,1)S(1)}, bf16[576,768]{1,0:T(8,128)(2,1)S(1)}, bf16[256,512]{1,0:T(8,128)(2,1)S(1)}, bf16[256,512]{1,0:T(8,128)(2,1)S(1)}) custom-call(f32[16,32,256]{2,1,0:T(8,128)S(1)} %bitcast.21, f32[2,2,32,256]{3,2,1,0:T(8,128)S(1)} %collective-permute-done.refs_2_.refs_1_, ...), custom_call_target="tpu_custom_call" | custom-call | tf_op jit(solution)/shard_map/pallas_call | solution.py:25
  29.0 2.0 %shard_map.86 = (f32[128,2304]{1,0:T(8,128)S(1)}, f32[128,2304]{1,0:T(8,128)S(1)}) custom-call(bf16[256,512]{1,0:T(8,128)(2,1)S(1)} %get-tuple-element.72.refs_0_, bf16[256,512]{1,0:T(8,128)(2,1)S(1)} %get-tuple-element.73.refs_1_, bf16[640,768]{1,0:T(8,128)(2,1)S(1)} %get-tuple-element.74.refs_2_, bf16[640,768]{1,0:T(8,128)(2,1)S(1)} %get-tuple-element.75.refs_3_), custom_call_target="tpu_custom_call" | custom-call | tf_op jit(solution)/shard_map/pallas_call | solution.py:25
  31.0 0.8 %collective-permute-start.5 = (f32[128,2304]{1,0:T(8,128)S(1)}, f32[128,2304]{1,0:T(8,128)S(1)}, u32[]{:S(2)}, u32[]{:S(2)}) collective-permute-start(f32[128,2304]{1,0:T(8,128)S(1)} %get-tuple-element.77), channel_id=1, source_target_pairs={{0,2},{1,3},{2,0},{3,1},{4,6},{5,7},{6,4},{7,5},{8,10},{9,11},{10,... | collective-permute-start | bytes 3538952 | tf_op jit(solution)/shard_map/ppermute | solution.py:319
  31.8 2.2 %collective-permute-done.6.refs_1_ = f32[64,2304]{1,0:T(8,128)S(1)} collective-permute-done((f32[64,2304]{1,0:T(8,128)S(1)}, f32[64,2304]{1,0:T(8,128)S(1)}, u32[]{:S(2)}, u32[]{:S(2)}) %collective-permute-start.6) | collective-permute-done | bytes 589856 | tf_op jit(solution)/shard_map/ppermute | solution.py:314
  34.0 0.1 shard_map.87
  34.1 2.5 %collective-permute-start.8 = (f32[32,2304]{1,0:T(8,128)S(1)}, f32[32,2304]{1,0:T(8,128)S(1)}, u32[]{:S(2)}, u32[]{:S(2)}) collective-permute-start(f32[32,2304]{1,0:T(8,128)S(1)} %get-tuple-element.87), channel_id=1, source_target_pairs={{0,4},{1,5},{2,3},{3,2},{4,0},{5,1},{6,7},{7,6},{8,12},{9,13},{10,... | collective-permute-start | bytes 884744 | tf_op jit(solution)/shard_map/ppermute | solution.py:314
  36.6 0.3 shard_map.81
  36.9 0.0 collective-permute-done.5.refs_1_
  36.9 0.0 copy-start.1
  36.9 0.1 shard_map.88
  37.1 0.1 collective-permute-start.7
  37.1 0.8 %copy-done.1 = f32[1,16,32,256]{3,2,1,0:T(8,128)S(1)} copy-done((f32[1,16,32,256]{3,2,1,0:T(8,128)S(1)}, f32[1,16,32,256]{3,2,1,0:T(8,128)}, u32[]{:S(2)}) %copy-start.1) | copy-done | bytes 524312
  38.0 3.0 %shard_map.89 = (f32[16,32,256]{2,1,0:T(8,128)}, f32[8,128]{1,0:T(8,128)S(1)}) custom-call(f32[16,32,256]{2,1,0:T(8,128)S(1)} %bitcast.17, bf16[576,768]{1,0:T(8,128)(2,1)S(1)} %get-tuple-element.62.refs_2_.refs_1_, bf16[576,768]{1,0:T(8,128)(2,1)S(1)} %get-tuple-element.63.refs_3_.refs_2_, bf16[2304,256]{1,0:T(8,128)(2,1)S(1)} %get-tuple-element.65.refs_3_, ...), custom_call_target="tpu_custom_call" | custom-call | tf_op jit(solution)/shard_map/pallas_call | solution.py:25
  40.9 0.3 collective-permute-done.8.refs_1_
  41.3 0.5 shard_map.91
  41.8 2.6 %collective-permute-start.10 = (f32[32,576]{1,0:T(8,128)S(1)}, f32[32,576]{1,0:T(8,128)S(1)}, u32[]{:S(2)}, u32[]{:S(2)}) collective-permute-start(f32[32,576]{1,0:T(8,128)S(1)} %get-tuple-element.94), channel_id=1, source_target_pairs={{0,24},{8,16},{16,8},{24,0},{1,25},{9,17},{17,9},{25,1},{2,26},{10... | collective-permute-start | bytes 221192 | tf_op jit(solution)/shard_map/ppermute | solution.py:361
  44.4 0.0 collective-permute-start.11
  44.4 1.8 %collective-permute-start.12 = (f32[32,576]{1,0:T(8,128)S(1)}, f32[32,576]{1,0:T(8,128)S(1)}, u32[]{:S(2)}, u32[]{:S(2)}) collective-permute-start(f32[32,576]{1,0:T(8,128)S(1)} %get-tuple-element.96), channel_id=1, source_target_pairs={{0,8},{8,0},{16,24},{24,16},{1,9},{9,1},{17,25},{25,17},{2,10},{10... | collective-permute-start | bytes 221192 | tf_op jit(solution)/shard_map/ppermute | solution.py:361
  46.2 0.7 %shard_map.90 = (bf16[2304,256]{1,0:T(8,128)(2,1)S(1)}, bf16[2304,256]{1,0:T(8,128)(2,1)S(1)}) custom-call(f32[2304,256]{1,0:T(8,128)S(1)} %copy-done.5, f32[128,2304]{1,0:T(8,128)S(1)} %shard_map.80.refs_1_.refs_4_), custom_call_target="tpu_custom_call" | custom-call | tf_op jit(solution)/shard_map/pallas_call | solution.py:25
  46.9 0.7 %collective-permute-done.7.refs_1_ = f32[64,2304]{1,0:T(8,128)S(1)} collective-permute-done((f32[64,2304]{1,0:T(8,128)S(1)}, f32[64,2304]{1,0:T(8,128)S(1)}, u32[]{:S(2)}, u32[]{:S(2)}) %collective-permute-start.7) | collective-permute-done | bytes 589856 | tf_op jit(solution)/shard_map/ppermute | solution.py:314
  47.6 0.1 shard_map.92
  47.7 1.6 %collective-permute-start.9 = (f32[32,2304]{1,0:T(8,128)S(1)}, f32[32,2304]{1,0:T(8,128)S(1)}, u32[]{:S(2)}, u32[]{:S(2)}) collective-permute-start(f32[32,2304]{1,0:T(8,128)S(1)} %get-tuple-element.92), channel_id=1, source_target_pairs={{0,1},{1,0},{2,6},{3,7},{4,5},{5,4},{6,2},{7,3},{8,9},{9,8},{10,14... | collective-permute-start | bytes 884744 | tf_op jit(solution)/shard_map/ppermute | solution.py:314
  49.2 2.8 %shard_map.93 = (f32[16,32,256]{2,1,0:T(8,128)}, f32[8,128]{1,0:T(8,128)S(1)}) custom-call(f32[16,32,256]{2,1,0:T(8,128)S(1)} %bitcast.18, f32[16,32,256]{2,1,0:T(8,128)S(1)} %bitcast.22, bf16[576,768]{1,0:T(8,128)(2,1)S(1)} %get-tuple-element.82.refs_2_, bf16[576,768]{1,0:T(8,128)(2,1)S(1)} %get-tuple-element.83.refs_3_, ...), custom_call_target="tpu_custom_call" | custom-call | tf_op jit(solution)/shard_map/pallas_call | solution.py:25
  52.0 0.0 collective-permute-done.10.refs_1_
  52.0 0.0 collective-permute-done.11.refs_2_
  52.0 0.0 collective-permute-done.12.refs_3_
  52.0 0.7 %shard_map.94 = (f32[32,576]{1,0:T(8,128)}, f32[8,128]{1,0:T(8,128)S(1)}) custom-call(f32[32,576]{1,0:T(8,128)S(1)} %get-tuple-element.93.refs_0_, f32[32,576]{1,0:T(8,128)S(1)} %collective-permute-done.10.refs_1_, f32[32,576]{1,0:T(8,128)S(1)} %collective-permute-done.11.refs_2_, f32[32,576]{1,0:T(8,128)S(1)} %collective-permute-done.12.refs_3_, ...), custom_call_target="tpu_custom_call" | custom-call | flops 10000000000 | tf_op jit(solution)/shard_map/pallas_call | solution.py:25
  52.7 1.8 %collective-permute-done.9.refs_1_ = f32[32,2304]{1,0:T(8,128)S(1)} collective-permute-done((f32[32,2304]{1,0:T(8,128)S(1)}, f32[32,2304]{1,0:T(8,128)S(1)}, u32[]{:S(2)}, u32[]{:S(2)}) %collective-permute-start.9) | collective-permute-done | bytes 294944 | tf_op jit(solution)/shard_map/ppermute | solution.py:314
  54.5 0.5 shard_map.95
  55.0 2.6 %collective-permute-start.13 = (f32[32,576]{1,0:T(8,128)S(1)}, f32[32,576]{1,0:T(8,128)S(1)}, u32[]{:S(2)}, u32[]{:S(2)}) collective-permute-start(f32[32,576]{1,0:T(8,128)S(1)} %get-tuple-element.100), channel_id=1, source_target_pairs={{0,24},{8,16},{16,8},{24,0},{1,25},{9,17},{17,9},{25,1},{2,26},{10... | collective-permute-start | bytes 221192 | tf_op jit(solution)/shard_map/ppermute | solution.py:361
  57.6 0.0 collective-permute-start.14
  57.6 1.8 %collective-permute-start.15 = (f32[32,576]{1,0:T(8,128)S(1)}, f32[32,576]{1,0:T(8,128)S(1)}, u32[]{:S(2)}, u32[]{:S(2)}) collective-permute-start(f32[32,576]{1,0:T(8,128)S(1)} %get-tuple-element.102), channel_id=1, source_target_pairs={{0,8},{8,0},{16,24},{24,16},{1,9},{9,1},{17,25},{25,17},{2,10},{10... | collective-permute-start | bytes 221192 | tf_op jit(solution)/shard_map/ppermute | solution.py:361
  59.4 2.2 %collective-permute-done.13 = f32[32,576]{1,0:T(8,128)S(1)} collective-permute-done((f32[32,576]{1,0:T(8,128)S(1)}, f32[32,576]{1,0:T(8,128)S(1)}, u32[]{:S(2)}, u32[]{:S(2)}) %collective-permute-start.13) | collective-permute-done | bytes 73760 | tf_op jit(solution)/shard_map/ppermute | solution.py:361
  61.7 1.8 %collective-permute-done.14 = f32[32,576]{1,0:T(8,128)S(1)} collective-permute-done((f32[32,576]{1,0:T(8,128)S(1)}, f32[32,576]{1,0:T(8,128)S(1)}, u32[]{:S(2)}, u32[]{:S(2)}) %collective-permute-start.14) | collective-permute-done | bytes 73760 | tf_op jit(solution)/shard_map/ppermute | solution.py:361
  63.4 0.0 collective-permute-done.15
  63.4 0.7 %add_bitcast_fusion = f32[576,32]{0,1:T(8,128)} fusion(f32[32,576]{1,0:T(8,128)S(1)} %collective-permute-done.15, f32[32,576]{1,0:T(8,128)S(1)} %collective-permute-done.14, f32[32,576]{1,0:T(8,128)S(1)} %get-tuple-element.99, f32[32,576]{1,0:T(8,128)S(1)} %collective-permute-done.13), kind=kLoop, calls=%fused_computation | loop fusion | flops 55296 | bytes 368640 | tf_op jit(solution)/shard_map/transpose | solution.py:471
  (3 shorter events, 0.0 us)
Async XLA Ops:
  1.6 3.6 %collective-permute-start = (f32[2,2,32,256]{3,2,1,0:T(8,128)S(1)}, f32[2,2,32,256]{3,2,1,0:T(8,128)S(1)}, u32[]{:S(2)}, u32[]{:S(2)}) collective-permute-start(f32[2,2,32,256]{3,2,1,0:T(8,128)S(1)} %get-tuple-element.55), channel_id=1, source_target_pairs={{0,2},{4,6},{2,0},{6,4},{1,3},{5,7},{3,1},{7,5},{8,10},{12,14},{10... | collective-permute-start | bytes 393224 | tf_op jit(solution)/shard_map/ppermute | solution.py:114
  2.2 3.1 %collective-permute-start.1 = (f32[2,2,32,256]{3,2,1,0:T(8,128)S(1)}, f32[2,2,32,256]{3,2,1,0:T(8,128)S(1)}, u32[]{:S(2)}, u32[]{:S(2)}) collective-permute-start(f32[2,2,32,256]{3,2,1,0:T(8,128)S(1)} %get-tuple-element.56), channel_id=1, source_target_pairs={{2,4},{4,2},{3,5},{5,3},{10,12},{12,10},{11,13},{13,11},{18,20},{2... | collective-permute-start | bytes 393224 | tf_op jit(solution)/shard_map/ppermute | solution.py:114
  2.8 1.0 %copy-start = (f32[1,16,32,256]{3,2,1,0:T(8,128)S(1)}, f32[1,16,32,256]{3,2,1,0:T(8,128)}, u32[]{:S(2)}) copy-start(f32[1,16,32,256]{3,2,1,0:T(8,128)} %param.4) | copy-start | bytes 1572868
  3.9 1.0 %copy-start.2 = (f32[1,16,32,256]{3,2,1,0:T(8,128)S(1)}, f32[1,16,32,256]{3,2,1,0:T(8,128)}, u32[]{:S(2)}) copy-start(f32[1,16,32,256]{3,2,1,0:T(8,128)} %param.5) | copy-start | bytes 1572868
  4.9 5.6 %copy-start.5 = (f32[2304,256]{1,0:T(8,128)S(1)}, f32[2304,256]{1,0:T(8,128)}, u32[]{:S(2)}) copy-start(f32[2304,256]{1,0:T(8,128)} %refs_0_.7) | copy-start | bytes 7077892
  5.4 5.5 %collective-permute-start.2 = (f32[2,2,24,256]{3,2,1,0:T(8,128)S(1)}, f32[2,2,24,256]{3,2,1,0:T(8,128)S(1)}, u32[]{:S(2)}, u32[]{:S(2)}) collective-permute-start(f32[2,2,24,256]{3,2,1,0:T(8,128)S(1)} %get-tuple-element.58.refs_3_), channel_id=1, source_target_pairs={{0,8},{16,24},{8,0},{24,16},{1,9},{17,25},{9,1},{25,17},{2,10},{18... | collective-permute-start | bytes 294920 | tf_op jit(solution)/shard_map/ppermute | solution.py:114
  8.0 6.5 %collective-permute-start.3 = (f32[2,2,24,256]{3,2,1,0:T(8,128)S(1)}, f32[2,2,24,256]{3,2,1,0:T(8,128)S(1)}, u32[]{:S(2)}, u32[]{:S(2)}) collective-permute-start(f32[2,2,24,256]{3,2,1,0:T(8,128)S(1)} %get-tuple-element.59.refs_4_), channel_id=1, source_target_pairs={{8,16},{24,0},{16,8},{0,24},{9,17},{25,1},{17,9},{1,25},{10,18},{2... | collective-permute-start | bytes 294920 | tf_op jit(solution)/shard_map/ppermute | solution.py:114
  18.9 3.7 %copy-start.4 = (f32[2304,256]{1,0:T(8,128)S(1)}, f32[2304,256]{1,0:T(8,128)}, u32[]{:S(2)}) copy-start(f32[2304,256]{1,0:T(8,128)} %refs_0_.6) | copy-start | bytes 7077892
  18.9 5.1 %collective-permute-start.4 = (f32[128,2304]{1,0:T(8,128)S(1)}, f32[128,2304]{1,0:T(8,128)S(1)}, u32[]{:S(2)}, u32[]{:S(2)}) collective-permute-start(f32[128,2304]{1,0:T(8,128)S(1)} %shard_map.80.refs_1_.refs_4_), channel_id=1, source_target_pairs={{0,2},{1,3},{2,0},{3,1},{4,6},{5,7},{6,4},{7,5},{8,10},{9,11},{10,... | collective-permute-start | bytes 3538952 | tf_op jit(solution)/shard_map/ppermute | solution.py:319
  23.9 1.7 %copy-start.3 = (f32[1,16,32,256]{3,2,1,0:T(8,128)S(1)}, f32[1,16,32,256]{3,2,1,0:T(8,128)}, u32[]{:S(2)}) copy-start(f32[1,16,32,256]{3,2,1,0:T(8,128)} %param.5) | copy-start | bytes 1572868
  24.1 9.9 %collective-permute-start.6 = (f32[64,2304]{1,0:T(8,128)S(1)}, f32[64,2304]{1,0:T(8,128)S(1)}, u32[]{:S(2)}, u32[]{:S(2)}) collective-permute-start(f32[64,2304]{1,0:T(8,128)S(1)} %get-tuple-element.78), channel_id=1, source_target_pairs={{0,1},{1,0},{2,6},{3,7},{4,5},{5,4},{6,2},{7,3},{8,9},{9,8},{10,14... | collective-permute-start | bytes 1769480 | tf_op jit(solution)/shard_map/ppermute | solution.py:314
  31.0 5.9 %collective-permute-start.5 = (f32[128,2304]{1,0:T(8,128)S(1)}, f32[128,2304]{1,0:T(8,128)S(1)}, u32[]{:S(2)}, u32[]{:S(2)}) collective-permute-start(f32[128,2304]{1,0:T(8,128)S(1)} %get-tuple-element.77), channel_id=1, source_target_pairs={{0,2},{1,3},{2,0},{3,1},{4,6},{5,7},{6,4},{7,5},{8,10},{9,11},{10,... | collective-permute-start | bytes 3538952 | tf_op jit(solution)/shard_map/ppermute | solution.py:319
  34.1 7.2 %collective-permute-start.8 = (f32[32,2304]{1,0:T(8,128)S(1)}, f32[32,2304]{1,0:T(8,128)S(1)}, u32[]{:S(2)}, u32[]{:S(2)}) collective-permute-start(f32[32,2304]{1,0:T(8,128)S(1)} %get-tuple-element.87), channel_id=1, source_target_pairs={{0,4},{1,5},{2,3},{3,2},{4,0},{5,1},{6,7},{7,6},{8,12},{9,13},{10,... | collective-permute-start | bytes 884744 | tf_op jit(solution)/shard_map/ppermute | solution.py:314
  36.9 1.0 %copy-start.1 = (f32[1,16,32,256]{3,2,1,0:T(8,128)S(1)}, f32[1,16,32,256]{3,2,1,0:T(8,128)}, u32[]{:S(2)}) copy-start(f32[1,16,32,256]{3,2,1,0:T(8,128)} %param.4) | copy-start | bytes 1572868
  37.1 10.5 %collective-permute-start.7 = (f32[64,2304]{1,0:T(8,128)S(1)}, f32[64,2304]{1,0:T(8,128)S(1)}, u32[]{:S(2)}, u32[]{:S(2)}) collective-permute-start(f32[64,2304]{1,0:T(8,128)S(1)} %get-tuple-element.86), channel_id=1, source_target_pairs={{0,4},{1,5},{2,3},{3,2},{4,0},{5,1},{6,7},{7,6},{8,12},{9,13},{10,... | collective-permute-start | bytes 1769480 | tf_op jit(solution)/shard_map/ppermute | solution.py:314
  41.8 10.3 %collective-permute-start.10 = (f32[32,576]{1,0:T(8,128)S(1)}, f32[32,576]{1,0:T(8,128)S(1)}, u32[]{:S(2)}, u32[]{:S(2)}) collective-permute-start(f32[32,576]{1,0:T(8,128)S(1)} %get-tuple-element.94), channel_id=1, source_target_pairs={{0,24},{8,16},{16,8},{24,0},{1,25},{9,17},{17,9},{25,1},{2,26},{10... | collective-permute-start | bytes 221192 | tf_op jit(solution)/shard_map/ppermute | solution.py:361
  44.4 7.6 %collective-permute-start.11 = (f32[32,576]{1,0:T(8,128)S(1)}, f32[32,576]{1,0:T(8,128)S(1)}, u32[]{:S(2)}, u32[]{:S(2)}) collective-permute-start(f32[32,576]{1,0:T(8,128)S(1)} %get-tuple-element.95), channel_id=1, source_target_pairs={{0,16},{8,24},{16,0},{24,8},{1,17},{9,25},{17,1},{25,9},{2,18},{10... | collective-permute-start | bytes 221192 | tf_op jit(solution)/shard_map/ppermute | solution.py:361
  44.4 7.6 %collective-permute-start.12 = (f32[32,576]{1,0:T(8,128)S(1)}, f32[32,576]{1,0:T(8,128)S(1)}, u32[]{:S(2)}, u32[]{:S(2)}) collective-permute-start(f32[32,576]{1,0:T(8,128)S(1)} %get-tuple-element.96), channel_id=1, source_target_pairs={{0,8},{8,0},{16,24},{24,16},{1,9},{9,1},{17,25},{25,17},{2,10},{10... | collective-permute-start | bytes 221192 | tf_op jit(solution)/shard_map/ppermute | solution.py:361
  47.7 6.8 %collective-permute-start.9 = (f32[32,2304]{1,0:T(8,128)S(1)}, f32[32,2304]{1,0:T(8,128)S(1)}, u32[]{:S(2)}, u32[]{:S(2)}) collective-permute-start(f32[32,2304]{1,0:T(8,128)S(1)} %get-tuple-element.92), channel_id=1, source_target_pairs={{0,1},{1,0},{2,6},{3,7},{4,5},{5,4},{6,2},{7,3},{8,9},{9,8},{10,14... | collective-permute-start | bytes 884744 | tf_op jit(solution)/shard_map/ppermute | solution.py:314
  55.0 6.7 %collective-permute-start.13 = (f32[32,576]{1,0:T(8,128)S(1)}, f32[32,576]{1,0:T(8,128)S(1)}, u32[]{:S(2)}, u32[]{:S(2)}) collective-permute-start(f32[32,576]{1,0:T(8,128)S(1)} %get-tuple-element.100), channel_id=1, source_target_pairs={{0,24},{8,16},{16,8},{24,0},{1,25},{9,17},{17,9},{25,1},{2,26},{10... | collective-permute-start | bytes 221192 | tf_op jit(solution)/shard_map/ppermute | solution.py:361
  57.6 5.8 %collective-permute-start.14 = (f32[32,576]{1,0:T(8,128)S(1)}, f32[32,576]{1,0:T(8,128)S(1)}, u32[]{:S(2)}, u32[]{:S(2)}) collective-permute-start(f32[32,576]{1,0:T(8,128)S(1)} %get-tuple-element.101), channel_id=1, source_target_pairs={{0,16},{8,24},{16,0},{24,8},{1,17},{9,25},{17,1},{25,9},{2,18},{10... | collective-permute-start | bytes 221192 | tf_op jit(solution)/shard_map/ppermute | solution.py:361
  57.6 5.8 %collective-permute-start.15 = (f32[32,576]{1,0:T(8,128)S(1)}, f32[32,576]{1,0:T(8,128)S(1)}, u32[]{:S(2)}, u32[]{:S(2)}) collective-permute-start(f32[32,576]{1,0:T(8,128)S(1)} %get-tuple-element.102), channel_id=1, source_target_pairs={{0,8},{8,0},{16,24},{24,16},{1,9},{9,1},{17,25},{25,17},{2,10},{10... | collective-permute-start | bytes 221192 | tf_op jit(solution)/shard_map/ppermute | solution.py:361

commit v6 on v5

--- a/solution.py
+++ b/solution.py
@@ -81,27 +81,20 @@
 
 def pack_cols(here, grad, one, two, first, second):
     rows, cols = here.shape[:2]
+    tall = rows + 4
     even_lat = lax.axis_index("lat") % 2 == 0
     even = lax.axis_index("lon") % 2 == 0
     for f, field in enumerate((here, grad)):
         low = jnp.where(even_lat, two[f], one[f])
         high = jnp.where(even_lat, one[f], two[f])
         for c in range(2):
-            edges = []
-            for col in (c, cols - 2 + c):
-                edges.append(
-                    jnp.concatenate(
-                        [
-                            low[:, col],
-                            field[:, col],
-                            high[:, col],
-                            jnp.zeros((LINE - rows - 4, field.shape[2]), F32),
-                        ],
-                        axis=0,
-                    )
-                )
-            first[f, c] = jnp.where(even, edges[1], edges[0])
-            second[f, c] = jnp.where(even, edges[0], edges[1])
+            edges = [
+                jnp.concatenate([low[:, col], field[:, col], high[:, col]], axis=0)
+                for col in (c, cols - 2 + c)
+            ]
+            place = slice((2 * f + c) * tall, (2 * f + c + 1) * tall)
+            first[place] = jnp.where(even, edges[1], edges[0])
+            second[place] = jnp.where(even, edges[0], edges[1])
 
 
 def pair_swap(one, two, axis, periodic):
@@ -167,14 +160,15 @@
 
 def side_columns(mine_one, mine_two, got_one, got_two, f):
     even = lax.axis_index("lon") % 2 == 0
-
-    def either(a, b):
-        return jnp.where(even, a, b)
-
-    left = [either(got_two[f, c], got_one[f, c]) for c in range(2)]
-    left.append(either(mine_two[f, 0], mine_one[f, 0]))
-    right = [either(mine_one[f, 1], mine_two[f, 1])]
-    right += [either(got_one[f, c], got_two[f, c]) for c in range(2)]
+    tall = mine_one.shape[0] // 4
+    rest = jnp.zeros((LINE - tall, mine_one.shape[1]), F32)
+
+    def either(a, b, c):
+        place = slice((2 * f + c) * tall, (2 * f + c + 1) * tall)
+        return jnp.concatenate([jnp.where(even, a[place], b[place]), rest], axis=0)
+
+    left = [either(got_two, got_one, c) for c in range(2)] + [either(mine_two, mine_one, 0)]
+    right = [either(mine_one, mine_two, 1)] + [either(got_one, got_two, c) for c in range(2)]
     return left, right
 
 
@@ -327,6 +321,16 @@
     next_away[...] = keep[half:] + got[half:]
 
 
+def add_up(keep, got, away):
+    away[...] = keep[...] + got[...]
+
+
+def add_three(keep_one, keep_two, core_one, core_two, got, next_keep, next_away):
+    half = keep_one.shape[0]
+    next_keep[...] = keep_one[...] + core_one[...] + got[:half]
+    next_away[...] = keep_two[...] + core_two[...] + got[half:]
+
+
 def cut_blocks(keep, got, *outs):
     blocks = outs[:4]
     for token in outs[4:]:
@@ -384,7 +388,7 @@
         [here, grad],
         scratch=[((channels, cells), F32)],
     )
-    line = ((2, 2, LINE, channels), F32)
+    line = ((4 * (rows + 4), channels), F32)
     m1, m2 = call(pack_cols, [line] * 2, [here, grad, r1, r2], after=[t_low])
     q1, q2 = pair_swap(m1, m2, "lon", True)
     lines = ((2 * LINE, channels), F32)
@@ -406,33 +410,38 @@
     def halves_of(count):
         return [((count, 9 * channels), F32)] * 2
 
-    def second_products(name, after):
-        part = slice(0, channels // 2) if name == "keep" else slice(channels // 2, channels)
+    quarter = ((2 * each, 9 * channels), F32)
+    eighth = ((each, 9 * channels), F32)
+
+    def second_products(first, outs, after):
+        def rows_of(ref):
+            starts = [first * 2 * each, (first + 2) * 2 * each]
+            return jnp.concatenate([ref[i : i + 2 * each] for i in starts], axis=0)
+
         return call(
             lambda high, low, *refs: products_kernel(
-                scale, cols, 0, high.at[part], low.at[part], *refs
+                scale, cols, 0, rows_of(high), rows_of(low), *refs
             ),
-            [half],
+            outs,
             [t_high, t_low, x2_high, x2_low],
             after=after,
-        )[0]
-
-    away_2 = second_products("away", [])
+        )
+
+    keep_2, away_2 = second_products(1, [quarter] * 2, [])
     got_2 = core_swap(away_2)
-    keep_2 = second_products("keep", [away_2])
     b2_high, b2_low = call(prepare_back, pair, [second_weight], after=[away_2])
     w2_high, w2_low = call(prepare, pair, [second_weight], after=[away_2])
     b1_high, b1_low = call(prepare_back, pair, [first_weight], after=[away_2])
-    keep_2, away_2 = call(
-        add_halves, halves_of(2 * each), [keep_2, got_2], after=[b2_low]
-    )
+    (away_2,) = call(add_up, [quarter], [keep_2, got_2], after=[b2_low])
     got_2 = plane_swap(away_2, False)
+    *keeps, away_one, away_two = second_products(0, [eighth] * 4, [away_2])
+    cores = [core_swap(away_one), core_swap(away_two)]
     x3_high, x3_low, t_high, t_low = call(
         inner_kernel,
         taps_2 + [((channels, cells), BF16)] * 2,
         [grad, r1, r2, m1, m2, q1, q2, b2_high, b2_low, hidden, side],
         scratch=[wide] + taps_1 + [wide2] + around + [((channels, cells), F32)],
-        after=[keep_2],
+        after=keeps[:1],
     )
     keep_1, away_1 = call(
         lambda *refs: products_kernel(scale, cols, 1, *refs),
@@ -440,7 +449,9 @@
         [t_high, t_low, x1_high, x1_low],
     )
     got_1 = core_swap(away_1)
-    keep_2, away_2 = call(add_halves, halves_of(each), [keep_2, got_2], flops=LONG)
+    keep_2, away_2 = call(
+        add_three, halves_of(each), [*keeps, *cores, got_2], flops=LONG
+    )
     got_2 = plane_swap(away_2, True)
     keep_1, away_1 = call(add_halves, halves_of(2 * each), [keep_1, got_1], after=[keep_2])
     got_1 = plane_swap(away_1, True)

time: 64.4 us -> 63.3 us (0.983)
  waiting for transfers between devices: 13.4 us -> 11.7 us
  starting transfers between devices: 24.3 us -> 25.9 us
  local copies, waits for them, and re-layouts: 3.87 us -> 3.06 us
    ppermute x4, waiting for transfers between devices: 4.98 us -> 3.2 us  [plane_swap(): return lax.ppermute(away, ('lat', 'rep'), plane_perm(count, one, two))]
    ppermute x4, starting transfers between devices: 5.73 us -> 6.73 us  [plane_swap(): return lax.ppermute(away, ('lat', 'rep'), plane_perm(count, one, two))]
    unnamed x12, local copies, waits for them, and re-layouts: 2.91 us -> 2.1 us
    ppermute x2 -> x4, starting transfers between devices: 3.4 us -> 3.94 us  [core_swap(): return lax.ppermute(away, ('lat', 'rep'), plane_perm(count, 2, 2))]
  transfers between devices with their start and end apart: 16 -> 18, of which waited for: 8 -> 8; matrix products, arithmetic and copies ran while one was open for 0% -> 0% of each run, Pallas kernels for 25% -> 25%
where the time goes in v6:
time: 63.3 us; the launch traced here: 63 us
  starting transfers between devices  25.9 us (41%)
  Pallas kernels  20.9 us (33%)
  waiting for transfers between devices  11.7 us (18%)
  local copies, waits for them, and re-layouts  3.06 us (5%)
  between operations  0.83 us (1%)
  other arithmetic  0.66 us (1%)
    pallas_call x21, Pallas kernels, call(): pl.pallas_call(kernel, out_shape=[jax.ShapeDtypeStruct(shape, dtype) for...  20.9 us
    ppermute x6, starting transfers between devices, send_blocks(): lax.ppermute(blocks[step], 'lon', [(i, i ^ step) for i in range(lon)])  8.91 us
    ppermute x4, starting transfers between devices, plane_swap(): return lax.ppermute(away, ('lat', 'rep'), plane_perm(count, one, two))  6.73 us
    ppermute x4, starting transfers between devices, pair_swap(): lax.ppermute(block, axis, who + [(b, a) for a, b in who])  6.31 us
    ppermute x6, waiting for transfers between devices, send_blocks(): lax.ppermute(blocks[step], 'lon', [(i, i ^ step) for i in range(lon)])  4.01 us
    ppermute x4, starting transfers between devices, core_swap(): return lax.ppermute(away, ('lat', 'rep'), plane_perm(count, 2, 2))  3.94 us
    ppermute x4, waiting for transfers between devices, pair_swap(): lax.ppermute(block, axis, who + [(b, a) for a, b in who])  3.52 us
    ppermute x4, waiting for transfers between devices, plane_swap(): return lax.ppermute(away, ('lat', 'rep'), plane_perm(count, one, two))  3.2 us
  transfers between devices with their start and end apart: 18, of which 8 were waited for; matrix products, arithmetic and copies ran while one was open for 0% of the time, Pallas kernels for 25%

profile of v6, /device:TPU:0, one launch (start us, length us, event | category | flops | bytes accessed | tf_op | source)
XLA Modules:
  0.0 63.0 jit_solution(16400999186837108587)
XLA Ops:
  0.6 1.0 %slice_bitcast_fusion = (f32[2,32,256]{2,1,0:T(8,128)S(1)}, f32[2,32,256]{2,1,0:T(8,128)S(1)}, f32[2,32,256]{2,1,0:T(8,128)S(1)}, f32[2,32,256]{2,1,0:T(8,128)S(1)}) fusion(f32[1,16,32,256]{3,2,1,0:T(8,128)} %param.5, f32[1,16,32,256]{3,2,1,0:T(8,128)} %param.4), kind=kLoop, calls=%fused_computation.1 | loop fusion | bytes 524288 | tf_op jit(solution)/shard_map/slice | solution.py:380
  1.6 0.5 collective-permute-start
  2.2 0.7 %collective-permute-start.1 = (f32[2,2,32,256]{3,2,1,0:T(8,128)S(1)}, f32[2,2,32,256]{3,2,1,0:T(8,128)S(1)}, u32[]{:S(2)}, u32[]{:S(2)}) collective-permute-start(f32[2,2,32,256]{3,2,1,0:T(8,128)S(1)} %get-tuple-element.60), channel_id=1, source_target_pairs={{2,4},{4,2},{3,5},{5,3},{10,12},{12,10},{11,13},{13,11},{18,20},{2... | collective-permute-start | bytes 393224 | tf_op jit(solution)/shard_map/ppermute | solution.py:107
  2.8 0.0 copy-start
  2.8 1.0 %copy-done = f32[1,16,32,256]{3,2,1,0:T(8,128)S(1)} copy-done((f32[1,16,32,256]{3,2,1,0:T(8,128)S(1)}, f32[1,16,32,256]{3,2,1,0:T(8,128)}, u32[]{:S(2)}) %copy-start) | copy-done | bytes 524312
  3.9 1.0 %copy-done.2 = f32[1,16,32,256]{3,2,1,0:T(8,128)S(1)} copy-done((f32[1,16,32,256]{3,2,1,0:T(8,128)S(1)}, f32[1,16,32,256]{3,2,1,0:T(8,128)}, u32[]{:S(2)}) %copy-start.2) | copy-done | bytes 524312
  4.9 0.4 shard_map.75
  5.3 0.0 collective-permute-done.refs_2_.refs_1_
  5.3 0.0 collective-permute-done.1.refs_3_.refs_2_
  5.3 0.1 shard_map.77
  5.4 2.7 %collective-permute-start.2 = (f32[80,256]{1,0:T(8,128)S(1)}, f32[80,256]{1,0:T(8,128)S(1)}, u32[]{:S(2)}, u32[]{:S(2)}) collective-permute-start(f32[80,256]{1,0:T(8,128)S(1)} %get-tuple-element.62.refs_3_), channel_id=1, source_target_pairs={{0,8},{16,24},{8,0},{24,16},{1,9},{17,25},{9,1},{25,17},{2,10},{18... | collective-permute-start | bytes 245768 | tf_op jit(solution)/shard_map/ppermute | solution.py:107
  8.0 2.5 %collective-permute-start.3 = (f32[80,256]{1,0:T(8,128)S(1)}, f32[80,256]{1,0:T(8,128)S(1)}, u32[]{:S(2)}, u32[]{:S(2)}) collective-permute-start(f32[80,256]{1,0:T(8,128)S(1)} %get-tuple-element.63.refs_4_), channel_id=1, source_target_pairs={{8,16},{24,0},{16,8},{0,24},{9,17},{25,1},{17,9},{1,25},{10,18},{2... | collective-permute-start | bytes 245768 | tf_op jit(solution)/shard_map/ppermute | solution.py:107
  10.5 0.0 copy-done.5
  10.5 0.3 shard_map.78
  10.9 0.0 collective-permute-done.2.refs_5_
  10.9 3.5 %collective-permute-done.3.refs_6_ = f32[80,256]{1,0:T(8,128)S(1)} collective-permute-done((f32[80,256]{1,0:T(8,128)S(1)}, f32[80,256]{1,0:T(8,128)S(1)}, u32[]{:S(2)}, u32[]{:S(2)}) %collective-permute-start.3) | collective-permute-done | bytes 81952 | tf_op jit(solution)/shard_map/ppermute | solution.py:107
  14.4 3.2 %shard_map.79 = (f32[576,256]{1,0:T(8,128)S(1)}, f32[48,256]{1,0:T(8,128)S(1)}, bf16[640,768]{1,0:T(8,128)(2,1)S(1)}, bf16[640,768]{1,0:T(8,128)(2,1)S(1)}, bf16...) custom-call(f32[16,32,256]{2,1,0:T(8,128)S(1)} %get-tuple-element.58.refs_0_, ...), custom_call_target="tpu_custom_call" | custom-call | tf_op jit(solution)/shard_map/pallas_call | solution.py:25
  17.6 1.1 %shard_map.80 = (f32[64,2304]{1,0:T(8,128)S(1)}, f32[64,2304]{1,0:T(8,128)S(1)}) custom-call(bf16[256,512]{1,0:T(8,128)(2,1)S(1)} %get-tuple-element.68.refs_0_, bf16[256,512]{1,0:T(8,128)(2,1)S(1)} %get-tuple-element.61.refs_4_.refs_1_, bf16[576,768]{1,0:T(8,128)(2,1)S(1)} %get-tuple-element.66.refs_2_.refs_1_, ...), custom_call_target="tpu_custom_call" | custom-call | tf_op jit(solution)/shard_map/pallas_call | solution.py:25
  18.7 2.5 %collective-permute-start.4 = (f32[64,2304]{1,0:T(8,128)S(1)}, f32[64,2304]{1,0:T(8,128)S(1)}, u32[]{:S(2)}, u32[]{:S(2)}) collective-permute-start(f32[64,2304]{1,0:T(8,128)S(1)} %get-tuple-element.69.refs_1_), channel_id=1, source_target_pairs={{0,2},{1,3},{2,0},{3,1},{4,6},{5,7},{6,4},{7,5},{8,10},{9,11},{10,... | collective-permute-start | bytes 1769480 | tf_op jit(solution)/shard_map/ppermute | solution.py:313
  21.2 0.7 %shard_map.82 = (bf16[2304,256]{1,0:T(8,128)(2,1)S(1)}, bf16[2304,256]{1,0:T(8,128)(2,1)S(1)}) custom-call(f32[2304,256]{1,0:T(8,128)S(1)} %copy-done.4, f32[64,2304]{1,0:T(8,128)S(1)} %get-tuple-element.69.refs_1_), custom_call_target="tpu_custom_call" | custom-call | tf_op jit(solution)/shard_map/pallas_call | solution.py:25
  21.9 0.9 %collective-permute-done.4.refs_1_ = f32[64,2304]{1,0:T(8,128)S(1)} collective-permute-done((f32[64,2304]{1,0:T(8,128)S(1)}, f32[64,2304]{1,0:T(8,128)S(1)}, u32[]{:S(2)}, u32[]{:S(2)}) %collective-permute-start.4) | collective-permute-done | bytes 589856 | tf_op jit(solution)/shard_map/ppermute | solution.py:313
  22.8 0.1 shard_map.83.refs_4_
  22.9 0.0 copy-start.3
  22.9 1.6 %collective-permute-start.8 = (f32[64,2304]{1,0:T(8,128)S(1)}, f32[64,2304]{1,0:T(8,128)S(1)}, u32[]{:S(2)}, u32[]{:S(2)}) collective-permute-start(f32[64,2304]{1,0:T(8,128)S(1)} %shard_map.83.refs_4_), channel_id=1, source_target_pairs={{0,1},{1,0},{2,6},{3,7},{4,5},{5,4},{6,2},{7,3},{8,9},{9,8},{10,14... | collective-permute-start | bytes 1769480 | tf_op jit(solution)/shard_map/ppermute | solution.py:308
  24.5 1.1 %shard_map.84 = (f32[32,2304]{1,0:T(8,128)S(1)}, f32[32,2304]{1,0:T(8,128)S(1)}, f32[32,2304]{1,0:T(8,128)S(1)}, f32[32,2304]{1,0:T(8,128)S(1)}) custom-call(bf16[256,512]{1,0:T(8,128)(2,1)S(1)} %get-tuple-element.68.refs_0_, bf16[256,512]{1,0:T(8,128)(2,1)S(1)} %get-tuple-element.61.refs_4_.refs_1_, bf16[576,768]{1,0:T(8,128)(2,1)S(1)} %get-tuple-element.66.refs_2_.refs_1_, ...), custom_call_target="tpu_custom_call" | custom-call | tf_op jit(solution)/shard_map/pallas_call | solution.py:25
  25.6 0.9 %collective-permute-start.6 = (f32[32,2304]{1,0:T(8,128)S(1)}, f32[32,2304]{1,0:T(8,128)S(1)}, u32[]{:S(2)}, u32[]{:S(2)}) collective-permute-start(f32[32,2304]{1,0:T(8,128)S(1)} %get-tuple-element.85), channel_id=1, source_target_pairs={{0,2},{1,3},{2,0},{3,1},{4,6},{5,7},{6,4},{7,5},{8,10},{9,11},{10,... | collective-permute-start | bytes 884744 | tf_op jit(solution)/shard_map/ppermute | solution.py:313
  26.5 0.1 collective-permute-start.7
  26.6 3.2 %shard_map.85 = (bf16[576,768]{1,0:T(8,128)(2,1)S(1)}, bf16[576,768]{1,0:T(8,128)(2,1)S(1)}, bf16[256,512]{1,0:T(8,128)(2,1)S(1)}, bf16[256,512]{1,0:T(8,128)(2,1)S(1)}) custom-call(f32[16,32,256]{2,1,0:T(8,128)S(1)} %bitcast.21, f32[2,2,32,256]{3,2,1,0:T(8,128)S(1)} %collective-permute-done.refs_2_.refs_1_, ...), custom_call_target="tpu_custom_call" | custom-call | tf_op jit(solution)/shard_map/pallas_call | solution.py:25
  29.8 2.0 %shard_map.86 = (f32[128,2304]{1,0:T(8,128)S(1)}, f32[128,2304]{1,0:T(8,128)S(1)}) custom-call(bf16[256,512]{1,0:T(8,128)(2,1)S(1)} %get-tuple-element.78.refs_0_, bf16[256,512]{1,0:T(8,128)(2,1)S(1)} %get-tuple-element.79.refs_1_, bf16[640,768]{1,0:T(8,128)(2,1)S(1)} %get-tuple-element.80.refs_2_, bf16[640,768]{1,0:T(8,128)(2,1)S(1)} %get-tuple-element.81.refs_3_), custom_call_target="tpu_custom_call" | custom-call | tf_op jit(solution)/shard_map/pallas_call | solution.py:25
  31.8 0.5 collective-permute-start.5
  32.3 0.0 collective-permute-done.6.refs_2_
  32.3 0.0 collective-permute-done.7.refs_3_
  32.3 0.5 collective-permute-done.8.refs_4_
  32.8 0.1 shard_map.87
  32.9 2.6 %collective-permute-start.10 = (f32[32,2304]{1,0:T(8,128)S(1)}, f32[32,2304]{1,0:T(8,128)S(1)}, u32[]{:S(2)}, u32[]{:S(2)}) collective-permute-start(f32[32,2304]{1,0:T(8,128)S(1)} %get-tuple-element.95), channel_id=1, source_target_pairs={{0,4},{1,5},{2,3},{3,2},{4,0},{5,1},{6,7},{7,6},{8,12},{9,13},{10,... | collective-permute-start | bytes 884744 | tf_op jit(solution)/shard_map/ppermute | solution.py:308
  35.5 0.3 shard_map.81
  35.9 0.0 collective-permute-done.5.refs_1_
  35.9 0.0 copy-start.1
  35.9 0.1 shard_map.88
  36.0 1.0 %collective-permute-start.9 = (f32[64,2304]{1,0:T(8,128)S(1)}, f32[64,2304]{1,0:T(8,128)S(1)}, u32[]{:S(2)}, u32[]{:S(2)}) collective-permute-start(f32[64,2304]{1,0:T(8,128)S(1)} %get-tuple-element.94), channel_id=1, source_target_pairs={{0,4},{1,5},{2,3},{3,2},{4,0},{5,1},{6,7},{7,6},{8,12},{9,13},{10,... | collective-permute-start | bytes 1769480 | tf_op jit(solution)/shard_map/ppermute | solution.py:308
  37.0 3.0 %shard_map.89 = (f32[16,32,256]{2,1,0:T(8,128)}, f32[8,128]{1,0:T(8,128)S(1)}) custom-call(f32[16,32,256]{2,1,0:T(8,128)S(1)} %bitcast.17, bf16[576,768]{1,0:T(8,128)(2,1)S(1)} %get-tuple-element.66.refs_2_.refs_1_, bf16[576,768]{1,0:T(8,128)(2,1)S(1)} %get-tuple-element.67.refs_3_.refs_2_, bf16[2304,256]{1,0:T(8,128)(2,1)S(1)} %get-tuple-element.70.refs_3_, ...), custom_call_target="tpu_custom_call" | custom-call | tf_op jit(solution)/shard_map/pallas_call | solution.py:25
  40.0 0.2 collective-permute-done.10.refs_1_
  40.2 0.5 shard_map.91
  40.7 2.6 %collective-permute-start.12 = (f32[32,576]{1,0:T(8,128)S(1)}, f32[32,576]{1,0:T(8,128)S(1)}, u32[]{:S(2)}, u32[]{:S(2)}) collective-permute-start(f32[32,576]{1,0:T(8,128)S(1)} %get-tuple-element.102), channel_id=1, source_target_pairs={{0,24},{8,16},{16,8},{24,0},{1,25},{9,17},{17,9},{25,1},{2,26},{10... | collective-permute-start | bytes 221192 | tf_op jit(solution)/shard_map/ppermute | solution.py:365
  43.4 0.0 collective-permute-start.13
  43.4 1.8 %collective-permute-start.14 = (f32[32,576]{1,0:T(8,128)S(1)}, f32[32,576]{1,0:T(8,128)S(1)}, u32[]{:S(2)}, u32[]{:S(2)}) collective-permute-start(f32[32,576]{1,0:T(8,128)S(1)} %get-tuple-element.104), channel_id=1, source_target_pairs={{0,8},{8,0},{16,24},{24,16},{1,9},{9,1},{17,25},{25,17},{2,10},{10... | collective-permute-start | bytes 221192 | tf_op jit(solution)/shard_map/ppermute | solution.py:365
  45.2 0.7 %shard_map.90 = (bf16[2304,256]{1,0:T(8,128)(2,1)S(1)}, bf16[2304,256]{1,0:T(8,128)(2,1)S(1)}) custom-call(f32[2304,256]{1,0:T(8,128)S(1)} %copy-done.5, f32[64,2304]{1,0:T(8,128)S(1)} %get-tuple-element.69.refs_1_), custom_call_target="tpu_custom_call" | custom-call | tf_op jit(solution)/shard_map/pallas_call | solution.py:25
  45.9 0.7 %collective-permute-done.9.refs_1_ = f32[64,2304]{1,0:T(8,128)S(1)} collective-permute-done((f32[64,2304]{1,0:T(8,128)S(1)}, f32[64,2304]{1,0:T(8,128)S(1)}, u32[]{:S(2)}, u32[]{:S(2)}) %collective-permute-start.9) | collective-permute-done | bytes 589856 | tf_op jit(solution)/shard_map/ppermute | solution.py:308
  46.5 0.1 shard_map.92
  46.6 1.6 %collective-permute-start.11 = (f32[32,2304]{1,0:T(8,128)S(1)}, f32[32,2304]{1,0:T(8,128)S(1)}, u32[]{:S(2)}, u32[]{:S(2)}) collective-permute-start(f32[32,2304]{1,0:T(8,128)S(1)} %get-tuple-element.100), channel_id=1, source_target_pairs={{0,1},{1,0},{2,6},{3,7},{4,5},{5,4},{6,2},{7,3},{8,9},{9,8},{10,14... | collective-permute-start | bytes 884744 | tf_op jit(solution)/shard_map/ppermute | solution.py:308
  48.2 2.8 %shard_map.93 = (f32[16,32,256]{2,1,0:T(8,128)}, f32[8,128]{1,0:T(8,128)S(1)}) custom-call(f32[16,32,256]{2,1,0:T(8,128)S(1)} %bitcast.18, f32[16,32,256]{2,1,0:T(8,128)S(1)} %bitcast.22, bf16[576,768]{1,0:T(8,128)(2,1)S(1)} %get-tuple-element.90.refs_2_, bf16[576,768]{1,0:T(8,128)(2,1)S(1)} %get-tuple-element.91.refs_3_, ...), custom_call_target="tpu_custom_call" | custom-call | tf_op jit(solution)/shard_map/pallas_call | solution.py:25
  51.0 0.0 collective-permute-done.12.refs_1_
  51.0 0.0 collective-permute-done.13.refs_2_
  51.0 0.0 collective-permute-done.14.refs_3_
  51.0 0.7 %shard_map.94 = (f32[32,576]{1,0:T(8,128)}, f32[8,128]{1,0:T(8,128)S(1)}) custom-call(f32[32,576]{1,0:T(8,128)S(1)} %get-tuple-element.101.refs_0_, f32[32,576]{1,0:T(8,128)S(1)} %collective-permute-done.12.refs_1_, f32[32,576]{1,0:T(8,128)S(1)} %collective-permute-done.13.refs_2_, f32[32,576]{1,0:T(8,128)S(1)} %collective-permute-done.14.refs_3_, ...), custom_call_target="tpu_custom_call" | custom-call | flops 10000000000 | tf_op jit(solution)/shard_map/pallas_call | solution.py:25
  51.7 1.7 %collective-permute-done.11.refs_1_ = f32[32,2304]{1,0:T(8,128)S(1)} collective-permute-done((f32[32,2304]{1,0:T(8,128)S(1)}, f32[32,2304]{1,0:T(8,128)S(1)}, u32[]{:S(2)}, u32[]{:S(2)}) %collective-permute-start.11) | collective-permute-done | bytes 294944 | tf_op jit(solution)/shard_map/ppermute | solution.py:308
  53.4 0.5 shard_map.95
  53.9 2.6 %collective-permute-start.15 = (f32[32,576]{1,0:T(8,128)S(1)}, f32[32,576]{1,0:T(8,128)S(1)}, u32[]{:S(2)}, u32[]{:S(2)}) collective-permute-start(f32[32,576]{1,0:T(8,128)S(1)} %get-tuple-element.108), channel_id=1, source_target_pairs={{0,24},{8,16},{16,8},{24,0},{1,25},{9,17},{17,9},{25,1},{2,26},{10... | collective-permute-start | bytes 221192 | tf_op jit(solution)/shard_map/ppermute | solution.py:365
  56.5 0.0 collective-permute-start.16
  56.5 1.8 %collective-permute-start.17 = (f32[32,576]{1,0:T(8,128)S(1)}, f32[32,576]{1,0:T(8,128)S(1)}, u32[]{:S(2)}, u32[]{:S(2)}) collective-permute-start(f32[32,576]{1,0:T(8,128)S(1)} %get-tuple-element.110), channel_id=1, source_target_pairs={{0,8},{8,0},{16,24},{24,16},{1,9},{9,1},{17,25},{25,17},{2,10},{10... | collective-permute-start | bytes 221192 | tf_op jit(solution)/shard_map/ppermute | solution.py:365
  58.4 2.2 %collective-permute-done.15 = f32[32,576]{1,0:T(8,128)S(1)} collective-permute-done((f32[32,576]{1,0:T(8,128)S(1)}, f32[32,576]{1,0:T(8,128)S(1)}, u32[]{:S(2)}, u32[]{:S(2)}) %collective-permute-start.15) | collective-permute-done | bytes 73760 | tf_op jit(solution)/shard_map/ppermute | solution.py:365
  60.6 1.8 %collective-permute-done.16 = f32[32,576]{1,0:T(8,128)S(1)} collective-permute-done((f32[32,576]{1,0:T(8,128)S(1)}, f32[32,576]{1,0:T(8,128)S(1)}, u32[]{:S(2)}, u32[]{:S(2)}) %collective-permute-start.16) | collective-permute-done | bytes 73760 | tf_op jit(solution)/shard_map/ppermute | solution.py:365
  62.4 0.0 collective-permute-done.17
  62.4 0.7 %add_bitcast_fusion = f32[576,32]{0,1:T(8,128)} fusion(f32[32,576]{1,0:T(8,128)S(1)} %collective-permute-done.17, f32[32,576]{1,0:T(8,128)S(1)} %collective-permute-done.16, f32[32,576]{1,0:T(8,128)S(1)} %get-tuple-element.107, f32[32,576]{1,0:T(8,128)S(1)} %collective-permute-done.15), kind=kLoop, calls=%fused_computation | loop fusion | flops 55296 | bytes 368640 | tf_op jit(solution)/shard_map/transpose | solution.py:482
  (7 shorter events, 0.0 us)
Async XLA Ops:
  1.6 3.6 %collective-permute-start = (f32[2,2,32,256]{3,2,1,0:T(8,128)S(1)}, f32[2,2,32,256]{3,2,1,0:T(8,128)S(1)}, u32[]{:S(2)}, u32[]{:S(2)}) collective-permute-start(f32[2,2,32,256]{3,2,1,0:T(8,128)S(1)} %get-tuple-element.59), channel_id=1, source_target_pairs={{0,2},{4,6},{2,0},{6,4},{1,3},{5,7},{3,1},{7,5},{8,10},{12,14},{10... | collective-permute-start | bytes 393224 | tf_op jit(solution)/shard_map/ppermute | solution.py:107
  2.2 3.1 %collective-permute-start.1 = (f32[2,2,32,256]{3,2,1,0:T(8,128)S(1)}, f32[2,2,32,256]{3,2,1,0:T(8,128)S(1)}, u32[]{:S(2)}, u32[]{:S(2)}) collective-permute-start(f32[2,2,32,256]{3,2,1,0:T(8,128)S(1)} %get-tuple-element.60), channel_id=1, source_target_pairs={{2,4},{4,2},{3,5},{5,3},{10,12},{12,10},{11,13},{13,11},{18,20},{2... | collective-permute-start | bytes 393224 | tf_op jit(solution)/shard_map/ppermute | solution.py:107
  2.8 1.0 %copy-start = (f32[1,16,32,256]{3,2,1,0:T(8,128)S(1)}, f32[1,16,32,256]{3,2,1,0:T(8,128)}, u32[]{:S(2)}) copy-start(f32[1,16,32,256]{3,2,1,0:T(8,128)} %param.4) | copy-start | bytes 1572868
  3.9 1.0 %copy-start.2 = (f32[1,16,32,256]{3,2,1,0:T(8,128)S(1)}, f32[1,16,32,256]{3,2,1,0:T(8,128)}, u32[]{:S(2)}) copy-start(f32[1,16,32,256]{3,2,1,0:T(8,128)} %param.5) | copy-start | bytes 1572868
  4.9 5.6 %copy-start.5 = (f32[2304,256]{1,0:T(8,128)S(1)}, f32[2304,256]{1,0:T(8,128)}, u32[]{:S(2)}) copy-start(f32[2304,256]{1,0:T(8,128)} %refs_0_.7) | copy-start | bytes 7077892
  5.4 5.5 %collective-permute-start.2 = (f32[80,256]{1,0:T(8,128)S(1)}, f32[80,256]{1,0:T(8,128)S(1)}, u32[]{:S(2)}, u32[]{:S(2)}) collective-permute-start(f32[80,256]{1,0:T(8,128)S(1)} %get-tuple-element.62.refs_3_), channel_id=1, source_target_pairs={{0,8},{16,24},{8,0},{24,16},{1,9},{17,25},{9,1},{25,17},{2,10},{18... | collective-permute-start | bytes 245768 | tf_op jit(solution)/shard_map/ppermute | solution.py:107
  8.0 6.3 %collective-permute-start.3 = (f32[80,256]{1,0:T(8,128)S(1)}, f32[80,256]{1,0:T(8,128)S(1)}, u32[]{:S(2)}, u32[]{:S(2)}) collective-permute-start(f32[80,256]{1,0:T(8,128)S(1)} %get-tuple-element.63.refs_4_), channel_id=1, source_target_pairs={{8,16},{24,0},{16,8},{0,24},{9,17},{25,1},{17,9},{1,25},{10,18},{2... | collective-permute-start | bytes 245768 | tf_op jit(solution)/shard_map/ppermute | solution.py:107
  14.4 6.8 %copy-start.4 = (f32[2304,256]{1,0:T(8,128)S(1)}, f32[2304,256]{1,0:T(8,128)}, u32[]{:S(2)}) copy-start(f32[2304,256]{1,0:T(8,128)} %refs_0_.6) | copy-start | bytes 7077892
  18.7 4.1 %collective-permute-start.4 = (f32[64,2304]{1,0:T(8,128)S(1)}, f32[64,2304]{1,0:T(8,128)S(1)}, u32[]{:S(2)}, u32[]{:S(2)}) collective-permute-start(f32[64,2304]{1,0:T(8,128)S(1)} %get-tuple-element.69.refs_1_), channel_id=1, source_target_pairs={{0,2},{1,3},{2,0},{3,1},{4,6},{5,7},{6,4},{7,5},{8,10},{9,11},{10,... | collective-permute-start | bytes 1769480 | tf_op jit(solution)/shard_map/ppermute | solution.py:313
  22.9 3.7 %copy-start.3 = (f32[1,16,32,256]{3,2,1,0:T(8,128)S(1)}, f32[1,16,32,256]{3,2,1,0:T(8,128)}, u32[]{:S(2)}) copy-start(f32[1,16,32,256]{3,2,1,0:T(8,128)} %param.5) | copy-start | bytes 1572868
  22.9 9.9 %collective-permute-start.8 = (f32[64,2304]{1,0:T(8,128)S(1)}, f32[64,2304]{1,0:T(8,128)S(1)}, u32[]{:S(2)}, u32[]{:S(2)}) collective-permute-start(f32[64,2304]{1,0:T(8,128)S(1)} %shard_map.83.refs_4_), channel_id=1, source_target_pairs={{0,1},{1,0},{2,6},{3,7},{4,5},{5,4},{6,2},{7,3},{8,9},{9,8},{10,14... | collective-permute-start | bytes 1769480 | tf_op jit(solution)/shard_map/ppermute | solution.py:308
  25.6 6.7 %collective-permute-start.6 = (f32[32,2304]{1,0:T(8,128)S(1)}, f32[32,2304]{1,0:T(8,128)S(1)}, u32[]{:S(2)}, u32[]{:S(2)}) collective-permute-start(f32[32,2304]{1,0:T(8,128)S(1)} %get-tuple-element.85), channel_id=1, source_target_pairs={{0,2},{1,3},{2,0},{3,1},{4,6},{5,7},{6,4},{7,5},{8,10},{9,11},{10,... | collective-permute-start | bytes 884744 | tf_op jit(solution)/shard_map/ppermute | solution.py:313
  26.5 5.8 %collective-permute-start.7 = (f32[32,2304]{1,0:T(8,128)S(1)}, f32[32,2304]{1,0:T(8,128)S(1)}, u32[]{:S(2)}, u32[]{:S(2)}) collective-permute-start(f32[32,2304]{1,0:T(8,128)S(1)} %get-tuple-element.86), channel_id=1, source_target_pairs={{0,2},{1,3},{2,0},{3,1},{4,6},{5,7},{6,4},{7,5},{8,10},{9,11},{10,... | collective-permute-start | bytes 884744 | tf_op jit(solution)/shard_map/ppermute | solution.py:313
  31.8 4.1 %collective-permute-start.5 = (f32[128,2304]{1,0:T(8,128)S(1)}, f32[128,2304]{1,0:T(8,128)S(1)}, u32[]{:S(2)}, u32[]{:S(2)}) collective-permute-start(f32[128,2304]{1,0:T(8,128)S(1)} %get-tuple-element.83), channel_id=1, source_target_pairs={{0,2},{1,3},{2,0},{3,1},{4,6},{5,7},{6,4},{7,5},{8,10},{9,11},{10,... | collective-permute-start | bytes 3538952 | tf_op jit(solution)/shard_map/ppermute | solution.py:313
  32.9 7.3 %collective-permute-start.10 = (f32[32,2304]{1,0:T(8,128)S(1)}, f32[32,2304]{1,0:T(8,128)S(1)}, u32[]{:S(2)}, u32[]{:S(2)}) collective-permute-start(f32[32,2304]{1,0:T(8,128)S(1)} %get-tuple-element.95), channel_id=1, source_target_pairs={{0,4},{1,5},{2,3},{3,2},{4,0},{5,1},{6,7},{7,6},{8,12},{9,13},{10,... | collective-permute-start | bytes 884744 | tf_op jit(solution)/shard_map/ppermute | solution.py:308
  35.9 1.1 %copy-start.1 = (f32[1,16,32,256]{3,2,1,0:T(8,128)S(1)}, f32[1,16,32,256]{3,2,1,0:T(8,128)}, u32[]{:S(2)}) copy-start(f32[1,16,32,256]{3,2,1,0:T(8,128)} %param.4) | copy-start | bytes 1572868
  36.0 10.5 %collective-permute-start.9 = (f32[64,2304]{1,0:T(8,128)S(1)}, f32[64,2304]{1,0:T(8,128)S(1)}, u32[]{:S(2)}, u32[]{:S(2)}) collective-permute-start(f32[64,2304]{1,0:T(8,128)S(1)} %get-tuple-element.94), channel_id=1, source_target_pairs={{0,4},{1,5},{2,3},{3,2},{4,0},{5,1},{6,7},{7,6},{8,12},{9,13},{10,... | collective-permute-start | bytes 1769480 | tf_op jit(solution)/shard_map/ppermute | solution.py:308
  40.7 10.3 %collective-permute-start.12 = (f32[32,576]{1,0:T(8,128)S(1)}, f32[32,576]{1,0:T(8,128)S(1)}, u32[]{:S(2)}, u32[]{:S(2)}) collective-permute-start(f32[32,576]{1,0:T(8,128)S(1)} %get-tuple-element.102), channel_id=1, source_target_pairs={{0,24},{8,16},{16,8},{24,0},{1,25},{9,17},{17,9},{25,1},{2,26},{10... | collective-permute-start | bytes 221192 | tf_op jit(solution)/shard_map/ppermute | solution.py:365
  43.4 7.6 %collective-permute-start.13 = (f32[32,576]{1,0:T(8,128)S(1)}, f32[32,576]{1,0:T(8,128)S(1)}, u32[]{:S(2)}, u32[]{:S(2)}) collective-permute-start(f32[32,576]{1,0:T(8,128)S(1)} %get-tuple-element.103), channel_id=1, source_target_pairs={{0,16},{8,24},{16,0},{24,8},{1,17},{9,25},{17,1},{25,9},{2,18},{10... | collective-permute-start | bytes 221192 | tf_op jit(solution)/shard_map/ppermute | solution.py:365
  43.4 7.6 %collective-permute-start.14 = (f32[32,576]{1,0:T(8,128)S(1)}, f32[32,576]{1,0:T(8,128)S(1)}, u32[]{:S(2)}, u32[]{:S(2)}) collective-permute-start(f32[32,576]{1,0:T(8,128)S(1)} %get-tuple-element.104), channel_id=1, source_target_pairs={{0,8},{8,0},{16,24},{24,16},{1,9},{9,1},{17,25},{25,17},{2,10},{10... | collective-permute-start | bytes 221192 | tf_op jit(solution)/shard_map/ppermute | solution.py:365
  46.6 6.8 %collective-permute-start.11 = (f32[32,2304]{1,0:T(8,128)S(1)}, f32[32,2304]{1,0:T(8,128)S(1)}, u32[]{:S(2)}, u32[]{:S(2)}) collective-permute-start(f32[32,2304]{1,0:T(8,128)S(1)} %get-tuple-element.100), channel_id=1, source_target_pairs={{0,1},{1,0},{2,6},{3,7},{4,5},{5,4},{6,2},{7,3},{8,9},{9,8},{10,14... | collective-permute-start | bytes 884744 | tf_op jit(solution)/shard_map/ppermute | solution.py:308
  53.9 6.7 %collective-permute-start.15 = (f32[32,576]{1,0:T(8,128)S(1)}, f32[32,576]{1,0:T(8,128)S(1)}, u32[]{:S(2)}, u32[]{:S(2)}) collective-permute-start(f32[32,576]{1,0:T(8,128)S(1)} %get-tuple-element.108), channel_id=1, source_target_pairs={{0,24},{8,16},{16,8},{24,0},{1,25},{9,17},{17,9},{25,1},{2,26},{10... | collective-permute-start | bytes 221192 | tf_op jit(solution)/shard_map/ppermute | solution.py:365
  56.5 5.8 %collective-permute-start.16 = (f32[32,576]{1,0:T(8,128)S(1)}, f32[32,576]{1,0:T(8,128)S(1)}, u32[]{:S(2)}, u32[]{:S(2)}) collective-permute-start(f32[32,576]{1,0:T(8,128)S(1)} %get-tuple-element.109), channel_id=1, source_target_pairs={{0,16},{8,24},{16,0},{24,8},{1,17},{9,25},{17,1},{25,9},{2,18},{10... | collective-permute-start | bytes 221192 | tf_op jit(solution)/shard_map/ppermute | solution.py:365
  56.5 5.8 %collective-permute-start.17 = (f32[32,576]{1,0:T(8,128)S(1)}, f32[32,576]{1,0:T(8,128)S(1)}, u32[]{:S(2)}, u32[]{:S(2)}) collective-permute-start(f32[32,576]{1,0:T(8,128)S(1)} %get-tuple-element.110), channel_id=1, source_target_pairs={{0,8},{8,0},{16,24},{24,16},{1,9},{9,1},{17,25},{25,17},{2,10},{10... | collective-permute-start | bytes 221192 | tf_op jit(solution)/shard_map/ppermute | solution.py:365

commit v7 on v6

--- a/solution.py
+++ b/solution.py
@@ -11,6 +11,7 @@
 BF16 = jnp.bfloat16
 VMEM = pl.BlockSpec(memory_space=pltpu.VMEM)
 LONG = 10**10
+LANES = 128
 LINE = 24
 EDGE = 8
 
@@ -331,6 +332,24 @@
     next_away[...] = keep_two[...] + core_two[...] + got[half:]
 
 
+def pack(block):
+    rows, width = block.shape
+    whole = width // LANES
+    pieces = [block[:, i * LANES : (i + 1) * LANES] for i in range(whole)]
+    rest = block[:, whole * LANES :]
+    pieces.append(jnp.concatenate([rest[: rows // 2], rest[rows // 2 :]], axis=1))
+    return jnp.concatenate(pieces, axis=0)
+
+
+def unpack(packed, rows):
+    whole = packed.shape[0] // rows
+    pieces = [packed[i * rows : (i + 1) * rows] for i in range(whole)]
+    rest = packed[whole * rows :]
+    half = LANES // 2
+    pieces.append(jnp.concatenate([rest[:, :half], rest[:, half:]], axis=0))
+    return jnp.concatenate(pieces, axis=1)
+
+
 def cut_blocks(keep, got, *outs):
     blocks = outs[:4]
     for token in outs[4:]:
@@ -344,22 +363,23 @@
         value = parts[step]
         for place in range(1, count):
             value = jnp.where(z == place, parts[place ^ step], value)
-        block[...] = value
+        block[...] = pack(value)
 
 
 def wide_sum(keep, got):
     return lax.psum_scatter(keep + got, "lon", scatter_dimension=1, tiled=True).T
 
 
-def add_blocks(one, two, three, four, out, token):
-    token[...] = jnp.zeros(token.shape, F32)
-    out[...] = one[...] + two[...] + three[...] + four[...]
+def add_blocks(one, two, three, four, out, *tokens):
+    for token in tokens:
+        token[...] = jnp.zeros(token.shape, F32)
+    out[...] = unpack(one[...] + two[...] + three[...] + four[...], out.shape[0])
 
 
 def send_blocks(keep, got, after=(), flops=0, tokens=()):
     each, taps = keep.shape
     lon = lax.axis_size("lon")
-    outs = [((each, taps // lon), F32)] * lon + list(tokens)
+    outs = [((each * taps // lon // LANES, LANES), F32)] * lon + list(tokens)
     blocks = call(cut_blocks, outs, [keep, got], after=after, flops=flops)
     gots = [
         lax.ppermute(blocks[step], "lon", [(i, i ^ step) for i in range(lon)])
@@ -473,13 +493,13 @@
         after=[keep_1],
     )
     if direct:
-        shape = (each, blocks[0].shape[1])
+        shape = (each, 9 * channels // 4)
         summed, token = call(
             add_blocks, [(shape, F32), outs[1]], blocks, after=[token], flops=LONG
         )
         second_grad = summed.T
         blocks, _ = send_blocks(keep_1, got_1, [token])
-        first_grad = sum(blocks[1:], blocks[0]).T
+        first_grad = call(add_blocks, [(shape, F32)], blocks)[0].T
     else:
         first_grad = wide_sum(keep_1, got_1)
     return (output[None], input_grad[None], first_grad, second_grad)

time: 63.3 us -> 63 us (level)
  Pallas kernels: 20.9 us -> 21.8 us
  other arithmetic: 0.66 us -> 0 us
    pallas_call x21 -> x22, Pallas kernels: 20.9 us -> 21.8 us  [call(): pl.pallas_call(kernel, out_shape=[jax.ShapeDtypeStruct(shape, dtype) for...]
    transpose x1 -> x0, other arithmetic: 0.66 us -> none  [local(): first_grad = sum(blocks[1:], blocks[0]).T]
  transfers between devices with their start and end apart: 18 -> 18, of which waited for: 8 -> 8; matrix products, arithmetic and copies ran while one was open for 0% -> 0% of each run, Pallas kernels for 25% -> 26%
where the time goes in v7:
time: 63 us; the launch traced here: 62.7 us
  starting transfers between devices  25.8 us (41%)
  Pallas kernels  21.8 us (35%)
  waiting for transfers between devices  11.2 us (18%)
  local copies, waits for them, and re-layouts  3.06 us (5%)
  between operations  0.82 us (1%)
    pallas_call x22, Pallas kernels, call(): pl.pallas_call(kernel, out_shape=[jax.ShapeDtypeStruct(shape, dtype) for...  21.8 us
    ppermute x6, starting transfers between devices, send_blocks(): lax.ppermute(blocks[step], 'lon', [(i, i ^ step) for i in range(lon)])  8.85 us
    ppermute x4, starting transfers between devices, plane_swap(): return lax.ppermute(away, ('lat', 'rep'), plane_perm(count, one, two))  6.73 us
    ppermute x4, starting transfers between devices, pair_swap(): lax.ppermute(block, axis, who + [(b, a) for a, b in who])  6.31 us
    ppermute x4, starting transfers between devices, core_swap(): return lax.ppermute(away, ('lat', 'rep'), plane_perm(count, 2, 2))  3.94 us
    ppermute x6, waiting for transfers between devices, send_blocks(): lax.ppermute(blocks[step], 'lon', [(i, i ^ step) for i in range(lon)])  3.59 us
    ppermute x4, waiting for transfers between devices, pair_swap(): lax.ppermute(block, axis, who + [(b, a) for a, b in who])  3.52 us
    ppermute x4, waiting for transfers between devices, plane_swap(): return lax.ppermute(away, ('lat', 'rep'), plane_perm(count, one, two))  3.11 us
  transfers between devices with their start and end apart: 18, of which 8 were waited for; matrix products, arithmetic and copies ran while one was open for 0% of the time, Pallas kernels for 26%

profile of v7, /device:TPU:0, one launch (start us, length us, event | category | flops | bytes accessed | tf_op | source)
XLA Modules:
  0.0 62.7 jit_solution(15131943894869648258)
XLA Ops:
  0.6 1.0 %slice_bitcast_fusion = (f32[2,32,256]{2,1,0:T(8,128)S(1)}, f32[2,32,256]{2,1,0:T(8,128)S(1)}, f32[2,32,256]{2,1,0:T(8,128)S(1)}, f32[2,32,256]{2,1,0:T(8,128)S(1)}) fusion(f32[1,16,32,256]{3,2,1,0:T(8,128)} %param.5, f32[1,16,32,256]{3,2,1,0:T(8,128)} %param.4), kind=kLoop, calls=%fused_computation | loop fusion | bytes 524288 | tf_op jit(solution)/shard_map/slice | solution.py:400
  1.6 0.5 collective-permute-start
  2.2 0.7 %collective-permute-start.1 = (f32[2,2,32,256]{3,2,1,0:T(8,128)S(1)}, f32[2,2,32,256]{3,2,1,0:T(8,128)S(1)}, u32[]{:S(2)}, u32[]{:S(2)}) collective-permute-start(f32[2,2,32,256]{3,2,1,0:T(8,128)S(1)} %get-tuple-element.60), channel_id=1, source_target_pairs={{2,4},{4,2},{3,5},{5,3},{10,12},{12,10},{11,13},{13,11},{18,20},{2... | collective-permute-start | bytes 393224 | tf_op jit(solution)/shard_map/ppermute | solution.py:108
  2.8 0.0 copy-start
  2.8 1.0 %copy-done = f32[1,16,32,256]{3,2,1,0:T(8,128)S(1)} copy-done((f32[1,16,32,256]{3,2,1,0:T(8,128)S(1)}, f32[1,16,32,256]{3,2,1,0:T(8,128)}, u32[]{:S(2)}) %copy-start) | copy-done | bytes 524312
  3.9 1.0 %copy-done.2 = f32[1,16,32,256]{3,2,1,0:T(8,128)S(1)} copy-done((f32[1,16,32,256]{3,2,1,0:T(8,128)S(1)}, f32[1,16,32,256]{3,2,1,0:T(8,128)}, u32[]{:S(2)}) %copy-start.2) | copy-done | bytes 524312
  4.9 0.4 shard_map.75
  5.3 0.0 collective-permute-done.refs_2_.refs_1_
  5.3 0.0 collective-permute-done.1.refs_3_.refs_2_
  5.3 0.1 shard_map.77
  5.4 2.7 %collective-permute-start.2 = (f32[80,256]{1,0:T(8,128)S(1)}, f32[80,256]{1,0:T(8,128)S(1)}, u32[]{:S(2)}, u32[]{:S(2)}) collective-permute-start(f32[80,256]{1,0:T(8,128)S(1)} %get-tuple-element.62.refs_3_), channel_id=1, source_target_pairs={{0,8},{16,24},{8,0},{24,16},{1,9},{17,25},{9,1},{25,17},{2,10},{18... | collective-permute-start | bytes 245768 | tf_op jit(solution)/shard_map/ppermute | solution.py:108
  8.0 2.5 %collective-permute-start.3 = (f32[80,256]{1,0:T(8,128)S(1)}, f32[80,256]{1,0:T(8,128)S(1)}, u32[]{:S(2)}, u32[]{:S(2)}) collective-permute-start(f32[80,256]{1,0:T(8,128)S(1)} %get-tuple-element.63.refs_4_), channel_id=1, source_target_pairs={{8,16},{24,0},{16,8},{0,24},{9,17},{25,1},{17,9},{1,25},{10,18},{2... | collective-permute-start | bytes 245768 | tf_op jit(solution)/shard_map/ppermute | solution.py:108
  10.5 0.0 copy-done.5
  10.5 0.3 shard_map.78
  10.9 0.0 collective-permute-done.2.refs_5_
  10.9 3.5 %collective-permute-done.3.refs_6_ = f32[80,256]{1,0:T(8,128)S(1)} collective-permute-done((f32[80,256]{1,0:T(8,128)S(1)}, f32[80,256]{1,0:T(8,128)S(1)}, u32[]{:S(2)}, u32[]{:S(2)}) %collective-permute-start.3) | collective-permute-done | bytes 81952 | tf_op jit(solution)/shard_map/ppermute | solution.py:108
  14.4 3.2 %shard_map.79 = (f32[576,256]{1,0:T(8,128)S(1)}, f32[48,256]{1,0:T(8,128)S(1)}, bf16[640,768]{1,0:T(8,128)(2,1)S(1)}, bf16[640,768]{1,0:T(8,128)(2,1)S(1)}, bf16...) custom-call(f32[16,32,256]{2,1,0:T(8,128)S(1)} %get-tuple-element.58.refs_0_, ...), custom_call_target="tpu_custom_call" | custom-call | tf_op jit(solution)/shard_map/pallas_call | solution.py:26
  17.6 1.1 %shard_map.80 = (f32[64,2304]{1,0:T(8,128)S(1)}, f32[64,2304]{1,0:T(8,128)S(1)}) custom-call(bf16[256,512]{1,0:T(8,128)(2,1)S(1)} %get-tuple-element.68.refs_0_, bf16[256,512]{1,0:T(8,128)(2,1)S(1)} %get-tuple-element.61.refs_4_.refs_1_, bf16[576,768]{1,0:T(8,128)(2,1)S(1)} %get-tuple-element.66.refs_2_.refs_1_, ...), custom_call_target="tpu_custom_call" | custom-call | tf_op jit(solution)/shard_map/pallas_call | solution.py:26
  18.7 2.5 %collective-permute-start.4 = (f32[64,2304]{1,0:T(8,128)S(1)}, f32[64,2304]{1,0:T(8,128)S(1)}, u32[]{:S(2)}, u32[]{:S(2)}) collective-permute-start(f32[64,2304]{1,0:T(8,128)S(1)} %get-tuple-element.69.refs_1_), channel_id=1, source_target_pairs={{0,2},{1,3},{2,0},{3,1},{4,6},{5,7},{6,4},{7,5},{8,10},{9,11},{10,... | collective-permute-start | bytes 1769480 | tf_op jit(solution)/shard_map/ppermute | solution.py:314
  21.2 0.7 %shard_map.82 = (bf16[2304,256]{1,0:T(8,128)(2,1)S(1)}, bf16[2304,256]{1,0:T(8,128)(2,1)S(1)}) custom-call(f32[2304,256]{1,0:T(8,128)S(1)} %copy-done.4, f32[64,2304]{1,0:T(8,128)S(1)} %get-tuple-element.69.refs_1_), custom_call_target="tpu_custom_call" | custom-call | tf_op jit(solution)/shard_map/pallas_call | solution.py:26
  21.9 0.9 %collective-permute-done.4.refs_1_ = f32[64,2304]{1,0:T(8,128)S(1)} collective-permute-done((f32[64,2304]{1,0:T(8,128)S(1)}, f32[64,2304]{1,0:T(8,128)S(1)}, u32[]{:S(2)}, u32[]{:S(2)}) %collective-permute-start.4) | collective-permute-done | bytes 589856 | tf_op jit(solution)/shard_map/ppermute | solution.py:314
  22.8 0.1 shard_map.83.refs_4_
  22.9 0.0 copy-start.3
  22.9 1.6 %collective-permute-start.8 = (f32[64,2304]{1,0:T(8,128)S(1)}, f32[64,2304]{1,0:T(8,128)S(1)}, u32[]{:S(2)}, u32[]{:S(2)}) collective-permute-start(f32[64,2304]{1,0:T(8,128)S(1)} %shard_map.83.refs_4_), channel_id=1, source_target_pairs={{0,1},{1,0},{2,6},{3,7},{4,5},{5,4},{6,2},{7,3},{8,9},{9,8},{10,14... | collective-permute-start | bytes 1769480 | tf_op jit(solution)/shard_map/ppermute | solution.py:309
  24.5 1.1 %shard_map.84 = (f32[32,2304]{1,0:T(8,128)S(1)}, f32[32,2304]{1,0:T(8,128)S(1)}, f32[32,2304]{1,0:T(8,128)S(1)}, f32[32,2304]{1,0:T(8,128)S(1)}) custom-call(bf16[256,512]{1,0:T(8,128)(2,1)S(1)} %get-tuple-element.68.refs_0_, bf16[256,512]{1,0:T(8,128)(2,1)S(1)} %get-tuple-element.61.refs_4_.refs_1_, bf16[576,768]{1,0:T(8,128)(2,1)S(1)} %get-tuple-element.66.refs_2_.refs_1_, ...), custom_call_target="tpu_custom_call" | custom-call | tf_op jit(solution)/shard_map/pallas_call | solution.py:26
  25.6 0.9 %collective-permute-start.6 = (f32[32,2304]{1,0:T(8,128)S(1)}, f32[32,2304]{1,0:T(8,128)S(1)}, u32[]{:S(2)}, u32[]{:S(2)}) collective-permute-start(f32[32,2304]{1,0:T(8,128)S(1)} %get-tuple-element.85), channel_id=1, source_target_pairs={{0,2},{1,3},{2,0},{3,1},{4,6},{5,7},{6,4},{7,5},{8,10},{9,11},{10,... | collective-permute-start | bytes 884744 | tf_op jit(solution)/shard_map/ppermute | solution.py:314
  26.5 0.1 collective-permute-start.7
  26.6 3.2 %shard_map.85 = (bf16[576,768]{1,0:T(8,128)(2,1)S(1)}, bf16[576,768]{1,0:T(8,128)(2,1)S(1)}, bf16[256,512]{1,0:T(8,128)(2,1)S(1)}, bf16[256,512]{1,0:T(8,128)(2,1)S(1)}) custom-call(f32[16,32,256]{2,1,0:T(8,128)S(1)} %bitcast.20, f32[2,2,32,256]{3,2,1,0:T(8,128)S(1)} %collective-permute-done.refs_2_.refs_1_, ...), custom_call_target="tpu_custom_call" | custom-call | tf_op jit(solution)/shard_map/pallas_call | solution.py:26
  29.8 2.0 %shard_map.86 = (f32[128,2304]{1,0:T(8,128)S(1)}, f32[128,2304]{1,0:T(8,128)S(1)}) custom-call(bf16[256,512]{1,0:T(8,128)(2,1)S(1)} %get-tuple-element.78.refs_0_, bf16[256,512]{1,0:T(8,128)(2,1)S(1)} %get-tuple-element.79.refs_1_, bf16[640,768]{1,0:T(8,128)(2,1)S(1)} %get-tuple-element.80.refs_2_, bf16[640,768]{1,0:T(8,128)(2,1)S(1)} %get-tuple-element.81.refs_3_), custom_call_target="tpu_custom_call" | custom-call | tf_op jit(solution)/shard_map/pallas_call | solution.py:26
  31.8 0.5 collective-permute-start.5
  32.3 0.0 collective-permute-done.6.refs_2_
  32.3 0.0 collective-permute-done.7.refs_3_
  32.3 0.5 collective-permute-done.8.refs_4_
  32.8 0.1 shard_map.87
  32.9 2.6 %collective-permute-start.10 = (f32[32,2304]{1,0:T(8,128)S(1)}, f32[32,2304]{1,0:T(8,128)S(1)}, u32[]{:S(2)}, u32[]{:S(2)}) collective-permute-start(f32[32,2304]{1,0:T(8,128)S(1)} %get-tuple-element.95), channel_id=1, source_target_pairs={{0,4},{1,5},{2,3},{3,2},{4,0},{5,1},{6,7},{7,6},{8,12},{9,13},{10,... | collective-permute-start | bytes 884744 | tf_op jit(solution)/shard_map/ppermute | solution.py:309
  35.5 0.3 shard_map.81
  35.9 0.0 collective-permute-done.5.refs_1_
  35.9 0.0 copy-start.1
  35.9 0.1 shard_map.88
  36.0 1.0 %collective-permute-start.9 = (f32[64,2304]{1,0:T(8,128)S(1)}, f32[64,2304]{1,0:T(8,128)S(1)}, u32[]{:S(2)}, u32[]{:S(2)}) collective-permute-start(f32[64,2304]{1,0:T(8,128)S(1)} %get-tuple-element.94), channel_id=1, source_target_pairs={{0,4},{1,5},{2,3},{3,2},{4,0},{5,1},{6,7},{7,6},{8,12},{9,13},{10,... | collective-permute-start | bytes 1769480 | tf_op jit(solution)/shard_map/ppermute | solution.py:309
  37.0 3.0 %shard_map.89 = (f32[16,32,256]{2,1,0:T(8,128)}, f32[8,128]{1,0:T(8,128)S(1)}) custom-call(f32[16,32,256]{2,1,0:T(8,128)S(1)} %bitcast.16, bf16[576,768]{1,0:T(8,128)(2,1)S(1)} %get-tuple-element.66.refs_2_.refs_1_, bf16[576,768]{1,0:T(8,128)(2,1)S(1)} %get-tuple-element.67.refs_3_.refs_2_, bf16[2304,256]{1,0:T(8,128)(2,1)S(1)} %get-tuple-element.70.refs_3_, ...), custom_call_target="tpu_custom_call" | custom-call | tf_op jit(solution)/shard_map/pallas_call | solution.py:26
  40.0 0.2 collective-permute-done.10.refs_1_
  40.2 0.6 shard_map.91
  40.8 2.6 %collective-permute-start.12 = (f32[144,128]{1,0:T(8,128)S(1)}, f32[144,128]{1,0:T(8,128)S(1)}, u32[]{:S(2)}, u32[]{:S(2)}) collective-permute-start(f32[144,128]{1,0:T(8,128)S(1)} %get-tuple-element.102), channel_id=1, source_target_pairs={{0,24},{8,16},{16,8},{24,0},{1,25},{9,17},{17,9},{25,1},{2,26},{10... | collective-permute-start | bytes 221192 | tf_op jit(solution)/shard_map/ppermute | solution.py:385
  43.4 0.0 collective-permute-start.13
  43.4 1.8 %collective-permute-start.14 = (f32[144,128]{1,0:T(8,128)S(1)}, f32[144,128]{1,0:T(8,128)S(1)}, u32[]{:S(2)}, u32[]{:S(2)}) collective-permute-start(f32[144,128]{1,0:T(8,128)S(1)} %get-tuple-element.104), channel_id=1, source_target_pairs={{0,8},{8,0},{16,24},{24,16},{1,9},{9,1},{17,25},{25,17},{2,10},{10... | collective-permute-start | bytes 221192 | tf_op jit(solution)/shard_map/ppermute | solution.py:385
  45.2 0.7 %shard_map.90 = (bf16[2304,256]{1,0:T(8,128)(2,1)S(1)}, bf16[2304,256]{1,0:T(8,128)(2,1)S(1)}) custom-call(f32[2304,256]{1,0:T(8,128)S(1)} %copy-done.5, f32[64,2304]{1,0:T(8,128)S(1)} %get-tuple-element.69.refs_1_), custom_call_target="tpu_custom_call" | custom-call | tf_op jit(solution)/shard_map/pallas_call | solution.py:26
  45.9 0.6 %collective-permute-done.9.refs_1_ = f32[64,2304]{1,0:T(8,128)S(1)} collective-permute-done((f32[64,2304]{1,0:T(8,128)S(1)}, f32[64,2304]{1,0:T(8,128)S(1)}, u32[]{:S(2)}, u32[]{:S(2)}) %collective-permute-start.9) | collective-permute-done | bytes 589856 | tf_op jit(solution)/shard_map/ppermute | solution.py:309
  46.5 0.1 shard_map.92
  46.6 1.6 %collective-permute-start.11 = (f32[32,2304]{1,0:T(8,128)S(1)}, f32[32,2304]{1,0:T(8,128)S(1)}, u32[]{:S(2)}, u32[]{:S(2)}) collective-permute-start(f32[32,2304]{1,0:T(8,128)S(1)} %get-tuple-element.100), channel_id=1, source_target_pairs={{0,1},{1,0},{2,6},{3,7},{4,5},{5,4},{6,2},{7,3},{8,9},{9,8},{10,14... | collective-permute-start | bytes 884744 | tf_op jit(solution)/shard_map/ppermute | solution.py:309
  48.2 2.8 %shard_map.93 = (f32[16,32,256]{2,1,0:T(8,128)}, f32[8,128]{1,0:T(8,128)S(1)}) custom-call(f32[16,32,256]{2,1,0:T(8,128)S(1)} %bitcast.17, f32[16,32,256]{2,1,0:T(8,128)S(1)} %bitcast.21, bf16[576,768]{1,0:T(8,128)(2,1)S(1)} %get-tuple-element.90.refs_2_, bf16[576,768]{1,0:T(8,128)(2,1)S(1)} %get-tuple-element.91.refs_3_, ...), custom_call_target="tpu_custom_call" | custom-call | tf_op jit(solution)/shard_map/pallas_call | solution.py:26
  51.0 0.0 collective-permute-done.12.refs_1_
  51.0 0.0 collective-permute-done.13.refs_2_
  51.0 0.0 collective-permute-done.14.refs_3_
  51.0 0.7 %shard_map.94 = (f32[32,576]{1,0:T(8,128)}, f32[8,128]{1,0:T(8,128)S(1)}) custom-call(f32[144,128]{1,0:T(8,128)S(1)} %get-tuple-element.101.refs_0_, f32[144,128]{1,0:T(8,128)S(1)} %collective-permute-done.12.refs_1_, f32[144,128]{1,0:T(8,128)S(1)} %collective-permute-done.13.refs_2_, f32[144,128]{1,0:T(8,128)S(1)} %collective-permute-done.14.refs_3_, ...), custom_call_target="tpu_custom_call" | custom-call | flops 10000000000 | tf_op jit(solution)/shard_map/pallas_call | solution.py:26
  51.7 1.7 %collective-permute-done.11.refs_1_ = f32[32,2304]{1,0:T(8,128)S(1)} collective-permute-done((f32[32,2304]{1,0:T(8,128)S(1)}, f32[32,2304]{1,0:T(8,128)S(1)}, u32[]{:S(2)}, u32[]{:S(2)}) %collective-permute-start.11) | collective-permute-done | bytes 294944 | tf_op jit(solution)/shard_map/ppermute | solution.py:309
  53.4 0.6 shard_map.95
  54.0 2.6 %collective-permute-start.15 = (f32[144,128]{1,0:T(8,128)S(1)}, f32[144,128]{1,0:T(8,128)S(1)}, u32[]{:S(2)}, u32[]{:S(2)}) collective-permute-start(f32[144,128]{1,0:T(8,128)S(1)} %get-tuple-element.108), channel_id=1, source_target_pairs={{0,24},{8,16},{16,8},{24,0},{1,25},{9,17},{17,9},{25,1},{2,26},{10... | collective-permute-start | bytes 221192 | tf_op jit(solution)/shard_map/ppermute | solution.py:385
  56.6 0.0 collective-permute-start.16
  56.6 1.8 %collective-permute-start.17 = (f32[144,128]{1,0:T(8,128)S(1)}, f32[144,128]{1,0:T(8,128)S(1)}, u32[]{:S(2)}, u32[]{:S(2)}) collective-permute-start(f32[144,128]{1,0:T(8,128)S(1)} %get-tuple-element.110), channel_id=1, source_target_pairs={{0,8},{8,0},{16,24},{24,16},{1,9},{9,1},{17,25},{25,17},{2,10},{10... | collective-permute-start | bytes 221192 | tf_op jit(solution)/shard_map/ppermute | solution.py:385
  58.4 2.0 %collective-permute-done.15.refs_1_ = f32[144,128]{1,0:T(8,128)S(1)} collective-permute-done((f32[144,128]{1,0:T(8,128)S(1)}, f32[144,128]{1,0:T(8,128)S(1)}, u32[]{:S(2)}, u32[]{:S(2)}) %collective-permute-start.15) | collective-permute-done | bytes 73760 | tf_op jit(solution)/shard_map/ppermute | solution.py:385
  60.4 1.6 %collective-permute-done.16.refs_2_ = f32[144,128]{1,0:T(8,128)S(1)} collective-permute-done((f32[144,128]{1,0:T(8,128)S(1)}, f32[144,128]{1,0:T(8,128)S(1)}, u32[]{:S(2)}, u32[]{:S(2)}) %collective-permute-start.16) | collective-permute-done | bytes 73760 | tf_op jit(solution)/shard_map/ppermute | solution.py:385
  62.0 0.0 collective-permute-done.17.refs_3_
  62.0 0.7 %shard_map.96 = f32[32,576]{1,0:T(8,128)} custom-call(f32[144,128]{1,0:T(8,128)S(1)} %get-tuple-element.107.refs_0_, f32[144,128]{1,0:T(8,128)S(1)} %collective-permute-done.15.refs_1_, f32[144,128]{1,0:T(8,128)S(1)} %collective-permute-done.16.refs_2_, f32[144,128]{1,0:T(8,128)S(1)} %collective-permute-done.17.refs_3_), custom_call_target="tpu_custom_call" | custom-call | tf_op jit(solution)/shard_map/pallas_call | solution.py:26
  (7 shorter events, 0.0 us)
Async XLA Ops:
  1.6 3.6 %collective-permute-start = (f32[2,2,32,256]{3,2,1,0:T(8,128)S(1)}, f32[2,2,32,256]{3,2,1,0:T(8,128)S(1)}, u32[]{:S(2)}, u32[]{:S(2)}) collective-permute-start(f32[2,2,32,256]{3,2,1,0:T(8,128)S(1)} %get-tuple-element.59), channel_id=1, source_target_pairs={{0,2},{4,6},{2,0},{6,4},{1,3},{5,7},{3,1},{7,5},{8,10},{12,14},{10... | collective-permute-start | bytes 393224 | tf_op jit(solution)/shard_map/ppermute | solution.py:108
  2.2 3.1 %collective-permute-start.1 = (f32[2,2,32,256]{3,2,1,0:T(8,128)S(1)}, f32[2,2,32,256]{3,2,1,0:T(8,128)S(1)}, u32[]{:S(2)}, u32[]{:S(2)}) collective-permute-start(f32[2,2,32,256]{3,2,1,0:T(8,128)S(1)} %get-tuple-element.60), channel_id=1, source_target_pairs={{2,4},{4,2},{3,5},{5,3},{10,12},{12,10},{11,13},{13,11},{18,20},{2... | collective-permute-start | bytes 393224 | tf_op jit(solution)/shard_map/ppermute | solution.py:108
  2.8 1.0 %copy-start = (f32[1,16,32,256]{3,2,1,0:T(8,128)S(1)}, f32[1,16,32,256]{3,2,1,0:T(8,128)}, u32[]{:S(2)}) copy-start(f32[1,16,32,256]{3,2,1,0:T(8,128)} %param.4) | copy-start | bytes 1572868
  3.9 1.0 %copy-start.2 = (f32[1,16,32,256]{3,2,1,0:T(8,128)S(1)}, f32[1,16,32,256]{3,2,1,0:T(8,128)}, u32[]{:S(2)}) copy-start(f32[1,16,32,256]{3,2,1,0:T(8,128)} %param.5) | copy-start | bytes 1572868
  4.9 5.6 %copy-start.5 = (f32[2304,256]{1,0:T(8,128)S(1)}, f32[2304,256]{1,0:T(8,128)}, u32[]{:S(2)}) copy-start(f32[2304,256]{1,0:T(8,128)} %refs_0_.7) | copy-start | bytes 7077892
  5.4 5.5 %collective-permute-start.2 = (f32[80,256]{1,0:T(8,128)S(1)}, f32[80,256]{1,0:T(8,128)S(1)}, u32[]{:S(2)}, u32[]{:S(2)}) collective-permute-start(f32[80,256]{1,0:T(8,128)S(1)} %get-tuple-element.62.refs_3_), channel_id=1, source_target_pairs={{0,8},{16,24},{8,0},{24,16},{1,9},{17,25},{9,1},{25,17},{2,10},{18... | collective-permute-start | bytes 245768 | tf_op jit(solution)/shard_map/ppermute | solution.py:108
  8.0 6.3 %collective-permute-start.3 = (f32[80,256]{1,0:T(8,128)S(1)}, f32[80,256]{1,0:T(8,128)S(1)}, u32[]{:S(2)}, u32[]{:S(2)}) collective-permute-start(f32[80,256]{1,0:T(8,128)S(1)} %get-tuple-element.63.refs_4_), channel_id=1, source_target_pairs={{8,16},{24,0},{16,8},{0,24},{9,17},{25,1},{17,9},{1,25},{10,18},{2... | collective-permute-start | bytes 245768 | tf_op jit(solution)/shard_map/ppermute | solution.py:108
  14.4 6.8 %copy-start.4 = (f32[2304,256]{1,0:T(8,128)S(1)}, f32[2304,256]{1,0:T(8,128)}, u32[]{:S(2)}) copy-start(f32[2304,256]{1,0:T(8,128)} %refs_0_.6) | copy-start | bytes 7077892
  18.7 4.1 %collective-permute-start.4 = (f32[64,2304]{1,0:T(8,128)S(1)}, f32[64,2304]{1,0:T(8,128)S(1)}, u32[]{:S(2)}, u32[]{:S(2)}) collective-permute-start(f32[64,2304]{1,0:T(8,128)S(1)} %get-tuple-element.69.refs_1_), channel_id=1, source_target_pairs={{0,2},{1,3},{2,0},{3,1},{4,6},{5,7},{6,4},{7,5},{8,10},{9,11},{10,... | collective-permute-start | bytes 1769480 | tf_op jit(solution)/shard_map/ppermute | solution.py:314
  22.9 3.7 %copy-start.3 = (f32[1,16,32,256]{3,2,1,0:T(8,128)S(1)}, f32[1,16,32,256]{3,2,1,0:T(8,128)}, u32[]{:S(2)}) copy-start(f32[1,16,32,256]{3,2,1,0:T(8,128)} %param.5) | copy-start | bytes 1572868
  22.9 9.9 %collective-permute-start.8 = (f32[64,2304]{1,0:T(8,128)S(1)}, f32[64,2304]{1,0:T(8,128)S(1)}, u32[]{:S(2)}, u32[]{:S(2)}) collective-permute-start(f32[64,2304]{1,0:T(8,128)S(1)} %shard_map.83.refs_4_), channel_id=1, source_target_pairs={{0,1},{1,0},{2,6},{3,7},{4,5},{5,4},{6,2},{7,3},{8,9},{9,8},{10,14... | collective-permute-start | bytes 1769480 | tf_op jit(solution)/shard_map/ppermute | solution.py:309
  25.6 6.7 %collective-permute-start.6 = (f32[32,2304]{1,0:T(8,128)S(1)}, f32[32,2304]{1,0:T(8,128)S(1)}, u32[]{:S(2)}, u32[]{:S(2)}) collective-permute-start(f32[32,2304]{1,0:T(8,128)S(1)} %get-tuple-element.85), channel_id=1, source_target_pairs={{0,2},{1,3},{2,0},{3,1},{4,6},{5,7},{6,4},{7,5},{8,10},{9,11},{10,... | collective-permute-start | bytes 884744 | tf_op jit(solution)/shard_map/ppermute | solution.py:314
  26.5 5.8 %collective-permute-start.7 = (f32[32,2304]{1,0:T(8,128)S(1)}, f32[32,2304]{1,0:T(8,128)S(1)}, u32[]{:S(2)}, u32[]{:S(2)}) collective-permute-start(f32[32,2304]{1,0:T(8,128)S(1)} %get-tuple-element.86), channel_id=1, source_target_pairs={{0,2},{1,3},{2,0},{3,1},{4,6},{5,7},{6,4},{7,5},{8,10},{9,11},{10,... | collective-permute-start | bytes 884744 | tf_op jit(solution)/shard_map/ppermute | solution.py:314
  31.8 4.1 %collective-permute-start.5 = (f32[128,2304]{1,0:T(8,128)S(1)}, f32[128,2304]{1,0:T(8,128)S(1)}, u32[]{:S(2)}, u32[]{:S(2)}) collective-permute-start(f32[128,2304]{1,0:T(8,128)S(1)} %get-tuple-element.83), channel_id=1, source_target_pairs={{0,2},{1,3},{2,0},{3,1},{4,6},{5,7},{6,4},{7,5},{8,10},{9,11},{10,... | collective-permute-start | bytes 3538952 | tf_op jit(solution)/shard_map/ppermute | solution.py:314
  32.9 7.3 %collective-permute-start.10 = (f32[32,2304]{1,0:T(8,128)S(1)}, f32[32,2304]{1,0:T(8,128)S(1)}, u32[]{:S(2)}, u32[]{:S(2)}) collective-permute-start(f32[32,2304]{1,0:T(8,128)S(1)} %get-tuple-element.95), channel_id=1, source_target_pairs={{0,4},{1,5},{2,3},{3,2},{4,0},{5,1},{6,7},{7,6},{8,12},{9,13},{10,... | collective-permute-start | bytes 884744 | tf_op jit(solution)/shard_map/ppermute | solution.py:309
  35.9 1.1 %copy-start.1 = (f32[1,16,32,256]{3,2,1,0:T(8,128)S(1)}, f32[1,16,32,256]{3,2,1,0:T(8,128)}, u32[]{:S(2)}) copy-start(f32[1,16,32,256]{3,2,1,0:T(8,128)} %param.4) | copy-start | bytes 1572868
  36.0 10.5 %collective-permute-start.9 = (f32[64,2304]{1,0:T(8,128)S(1)}, f32[64,2304]{1,0:T(8,128)S(1)}, u32[]{:S(2)}, u32[]{:S(2)}) collective-permute-start(f32[64,2304]{1,0:T(8,128)S(1)} %get-tuple-element.94), channel_id=1, source_target_pairs={{0,4},{1,5},{2,3},{3,2},{4,0},{5,1},{6,7},{7,6},{8,12},{9,13},{10,... | collective-permute-start | bytes 1769480 | tf_op jit(solution)/shard_map/ppermute | solution.py:309
  40.8 10.2 %collective-permute-start.12 = (f32[144,128]{1,0:T(8,128)S(1)}, f32[144,128]{1,0:T(8,128)S(1)}, u32[]{:S(2)}, u32[]{:S(2)}) collective-permute-start(f32[144,128]{1,0:T(8,128)S(1)} %get-tuple-element.102), channel_id=1, source_target_pairs={{0,24},{8,16},{16,8},{24,0},{1,25},{9,17},{17,9},{25,1},{2,26},{10... | collective-permute-start | bytes 221192 | tf_op jit(solution)/shard_map/ppermute | solution.py:385
  43.4 7.6 %collective-permute-start.13 = (f32[144,128]{1,0:T(8,128)S(1)}, f32[144,128]{1,0:T(8,128)S(1)}, u32[]{:S(2)}, u32[]{:S(2)}) collective-permute-start(f32[144,128]{1,0:T(8,128)S(1)} %get-tuple-element.103), channel_id=1, source_target_pairs={{0,16},{8,24},{16,0},{24,8},{1,17},{9,25},{17,1},{25,9},{2,18},{10... | collective-permute-start | bytes 221192 | tf_op jit(solution)/shard_map/ppermute | solution.py:385
  43.4 7.6 %collective-permute-start.14 = (f32[144,128]{1,0:T(8,128)S(1)}, f32[144,128]{1,0:T(8,128)S(1)}, u32[]{:S(2)}, u32[]{:S(2)}) collective-permute-start(f32[144,128]{1,0:T(8,128)S(1)} %get-tuple-element.104), channel_id=1, source_target_pairs={{0,8},{8,0},{16,24},{24,16},{1,9},{9,1},{17,25},{25,17},{2,10},{10... | collective-permute-start | bytes 221192 | tf_op jit(solution)/shard_map/ppermute | solution.py:385
  46.6 6.8 %collective-permute-start.11 = (f32[32,2304]{1,0:T(8,128)S(1)}, f32[32,2304]{1,0:T(8,128)S(1)}, u32[]{:S(2)}, u32[]{:S(2)}) collective-permute-start(f32[32,2304]{1,0:T(8,128)S(1)} %get-tuple-element.100), channel_id=1, source_target_pairs={{0,1},{1,0},{2,6},{3,7},{4,5},{5,4},{6,2},{7,3},{8,9},{9,8},{10,14... | collective-permute-start | bytes 884744 | tf_op jit(solution)/shard_map/ppermute | solution.py:309
  54.0 6.5 %collective-permute-start.15 = (f32[144,128]{1,0:T(8,128)S(1)}, f32[144,128]{1,0:T(8,128)S(1)}, u32[]{:S(2)}, u32[]{:S(2)}) collective-permute-start(f32[144,128]{1,0:T(8,128)S(1)} %get-tuple-element.108), channel_id=1, source_target_pairs={{0,24},{8,16},{16,8},{24,0},{1,25},{9,17},{17,9},{25,1},{2,26},{10... | collective-permute-start | bytes 221192 | tf_op jit(solution)/shard_map/ppermute | solution.py:385
  56.6 5.4 %collective-permute-start.16 = (f32[144,128]{1,0:T(8,128)S(1)}, f32[144,128]{1,0:T(8,128)S(1)}, u32[]{:S(2)}, u32[]{:S(2)}) collective-permute-start(f32[144,128]{1,0:T(8,128)S(1)} %get-tuple-element.109), channel_id=1, source_target_pairs={{0,16},{8,24},{16,0},{24,8},{1,17},{9,25},{17,1},{25,9},{2,18},{10... | collective-permute-start | bytes 221192 | tf_op jit(solution)/shard_map/ppermute | solution.py:385
  56.6 5.4 %collective-permute-start.17 = (f32[144,128]{1,0:T(8,128)S(1)}, f32[144,128]{1,0:T(8,128)S(1)}, u32[]{:S(2)}, u32[]{:S(2)}) collective-permute-start(f32[144,128]{1,0:T(8,128)S(1)} %get-tuple-element.110), channel_id=1, source_target_pairs={{0,8},{8,0},{16,24},{24,16},{1,9},{9,1},{17,25},{25,17},{2,10},{10... | collective-permute-start | bytes 221192 | tf_op jit(solution)/shard_map/ppermute | solution.py:385

commit v8 on v7

--- a/solution.py
+++ b/solution.py
@@ -332,11 +332,15 @@
     next_away[...] = keep_two[...] + core_two[...] + got[half:]
 
 
-def pack(block):
-    rows, width = block.shape
-    whole = width // LANES
-    pieces = [block[:, i * LANES : (i + 1) * LANES] for i in range(whole)]
-    rest = block[:, whole * LANES :]
+def pack(total, place):
+    rows, width = total.shape
+    tiles = width // LANES // 4
+    start = (place // 2) * (2 * tiles + 1)
+    whole = start + (place % 2) * (tiles + 1)
+    pieces = [total[:, i * LANES : (i + 1) * LANES] for i in range(whole, whole + tiles)]
+    half = LANES // 2
+    left = (start + tiles) * LANES + (place % 2) * half
+    rest = total[:, left : left + half]
     pieces.append(jnp.concatenate([rest[: rows // 2], rest[rows // 2 :]], axis=1))
     return jnp.concatenate(pieces, axis=0)
 
@@ -346,8 +350,13 @@
     pieces = [packed[i * rows : (i + 1) * rows] for i in range(whole)]
     rest = packed[whole * rows :]
     half = LANES // 2
-    pieces.append(jnp.concatenate([rest[:, :half], rest[:, half:]], axis=0))
-    return jnp.concatenate(pieces, axis=1)
+    rest = jnp.concatenate([rest[:, :half], rest[:, half:]], axis=0)
+    odd = lax.axis_index("lon") % 2 == 1
+    return jnp.where(
+        odd,
+        jnp.concatenate([rest, *pieces], axis=1),
+        jnp.concatenate([*pieces, rest], axis=1),
+    )
 
 
 def cut_blocks(keep, got, *outs):
@@ -356,14 +365,13 @@
         token[...] = jnp.zeros(token.shape, F32)
     total = keep[...] + got[...]
     count = len(blocks)
-    size = total.shape[1] // count
-    parts = [total[:, i * size : (i + 1) * size] for i in range(count)]
+    parts = [pack(total, place) for place in range(count)]
     z = lax.axis_index("lon")
     for step, block in enumerate(blocks):
         value = parts[step]
         for place in range(1, count):
             value = jnp.where(z == place, parts[place ^ step], value)
-        block[...] = pack(value)
+        block[...] = value
 
 
 def wide_sum(keep, got):

time: 63 us -> 62.5 us (level)
  Pallas kernels: 21.8 us -> 20.9 us
    pallas_call x22, Pallas kernels: 21.8 us -> 20.9 us  [call(): pl.pallas_call(kernel, out_shape=[jax.ShapeDtypeStruct(shape, dtype) for...]
  transfers between devices with their start and end apart: 18 -> 18, of which waited for: 8 -> 8; matrix products, arithmetic and copies ran while one was open for 0% -> 0% of each run, Pallas kernels for 26% -> 25%
where the time goes in v8:
time: 62.5 us; the launch traced here: 62.2 us
  starting transfers between devices  25.9 us (41%)
  Pallas kernels  20.9 us (33%)
  waiting for transfers between devices  11.6 us (19%)
  local copies, waits for them, and re-layouts  3.06 us (5%)
  between operations  0.83 us (1%)
    pallas_call x22, Pallas kernels, call(): pl.pallas_call(kernel, out_shape=[jax.ShapeDtypeStruct(shape, dtype) for...  20.9 us
    ppermute x6, starting transfers between devices, send_blocks(): lax.ppermute(blocks[step], 'lon', [(i, i ^ step) for i in range(lon)])  8.91 us
    ppermute x4, starting transfers between devices, plane_swap(): return lax.ppermute(away, ('lat', 'rep'), plane_perm(count, one, two))  6.73 us
    ppermute x4, starting transfers between devices, pair_swap(): lax.ppermute(block, axis, who + [(b, a) for a, b in who])  6.31 us
    ppermute x4, starting transfers between devices, core_swap(): return lax.ppermute(away, ('lat', 'rep'), plane_perm(count, 2, 2))  3.94 us
    ppermute x6, waiting for transfers between devices, send_blocks(): lax.ppermute(blocks[step], 'lon', [(i, i ^ step) for i in range(lon)])  3.59 us
    ppermute x4, waiting for transfers between devices, plane_swap(): return lax.ppermute(away, ('lat', 'rep'), plane_perm(count, one, two))  3.55 us
    ppermute x4, waiting for transfers between devices, pair_swap(): lax.ppermute(block, axis, who + [(b, a) for a, b in who])  3.52 us
  transfers between devices with their start and end apart: 18, of which 8 were waited for; matrix products, arithmetic and copies ran while one was open for 0% of the time, Pallas kernels for 25%

profile of v8, /device:TPU:0, one launch (start us, length us, event | category | flops | bytes accessed | tf_op | source)
XLA Modules:
  0.0 62.2 jit_solution(7999826022874185481)
XLA Ops:
  0.6 1.0 %slice_bitcast_fusion = (f32[2,32,256]{2,1,0:T(8,128)S(1)}, f32[2,32,256]{2,1,0:T(8,128)S(1)}, f32[2,32,256]{2,1,0:T(8,128)S(1)}, f32[2,32,256]{2,1,0:T(8,128)S(1)}) fusion(f32[1,16,32,256]{3,2,1,0:T(8,128)} %param.5, f32[1,16,32,256]{3,2,1,0:T(8,128)} %param.4), kind=kLoop, calls=%fused_computation | loop fusion | bytes 524288 | tf_op jit(solution)/shard_map/slice | solution.py:408
  1.6 0.5 collective-permute-start
  2.2 0.7 %collective-permute-start.1 = (f32[2,2,32,256]{3,2,1,0:T(8,128)S(1)}, f32[2,2,32,256]{3,2,1,0:T(8,128)S(1)}, u32[]{:S(2)}, u32[]{:S(2)}) collective-permute-start(f32[2,2,32,256]{3,2,1,0:T(8,128)S(1)} %get-tuple-element.60), channel_id=1, source_target_pairs={{2,4},{4,2},{3,5},{5,3},{10,12},{12,10},{11,13},{13,11},{18,20},{2... | collective-permute-start | bytes 393224 | tf_op jit(solution)/shard_map/ppermute | solution.py:108
  2.8 0.0 copy-start
  2.8 1.0 %copy-done = f32[1,16,32,256]{3,2,1,0:T(8,128)S(1)} copy-done((f32[1,16,32,256]{3,2,1,0:T(8,128)S(1)}, f32[1,16,32,256]{3,2,1,0:T(8,128)}, u32[]{:S(2)}) %copy-start) | copy-done | bytes 524312
  3.9 1.0 %copy-done.2 = f32[1,16,32,256]{3,2,1,0:T(8,128)S(1)} copy-done((f32[1,16,32,256]{3,2,1,0:T(8,128)S(1)}, f32[1,16,32,256]{3,2,1,0:T(8,128)}, u32[]{:S(2)}) %copy-start.2) | copy-done | bytes 524312
  4.9 0.4 shard_map.75
  5.3 0.0 collective-permute-done.refs_2_.refs_1_
  5.3 0.0 collective-permute-done.1.refs_3_.refs_2_
  5.3 0.1 shard_map.77
  5.4 2.7 %collective-permute-start.2 = (f32[80,256]{1,0:T(8,128)S(1)}, f32[80,256]{1,0:T(8,128)S(1)}, u32[]{:S(2)}, u32[]{:S(2)}) collective-permute-start(f32[80,256]{1,0:T(8,128)S(1)} %get-tuple-element.62.refs_3_), channel_id=1, source_target_pairs={{0,8},{16,24},{8,0},{24,16},{1,9},{17,25},{9,1},{25,17},{2,10},{18... | collective-permute-start | bytes 245768 | tf_op jit(solution)/shard_map/ppermute | solution.py:108
  8.0 2.5 %collective-permute-start.3 = (f32[80,256]{1,0:T(8,128)S(1)}, f32[80,256]{1,0:T(8,128)S(1)}, u32[]{:S(2)}, u32[]{:S(2)}) collective-permute-start(f32[80,256]{1,0:T(8,128)S(1)} %get-tuple-element.63.refs_4_), channel_id=1, source_target_pairs={{8,16},{24,0},{16,8},{0,24},{9,17},{25,1},{17,9},{1,25},{10,18},{2... | collective-permute-start | bytes 245768 | tf_op jit(solution)/shard_map/ppermute | solution.py:108
  10.5 0.0 copy-done.5
  10.5 0.3 shard_map.78
  10.9 0.0 collective-permute-done.2.refs_5_
  10.9 3.5 %collective-permute-done.3.refs_6_ = f32[80,256]{1,0:T(8,128)S(1)} collective-permute-done((f32[80,256]{1,0:T(8,128)S(1)}, f32[80,256]{1,0:T(8,128)S(1)}, u32[]{:S(2)}, u32[]{:S(2)}) %collective-permute-start.3) | collective-permute-done | bytes 81952 | tf_op jit(solution)/shard_map/ppermute | solution.py:108
  14.4 3.2 %shard_map.79 = (f32[576,256]{1,0:T(8,128)S(1)}, f32[48,256]{1,0:T(8,128)S(1)}, bf16[640,768]{1,0:T(8,128)(2,1)S(1)}, bf16[640,768]{1,0:T(8,128)(2,1)S(1)}, bf16...) custom-call(f32[16,32,256]{2,1,0:T(8,128)S(1)} %get-tuple-element.58.refs_0_, ...), custom_call_target="tpu_custom_call" | custom-call | tf_op jit(solution)/shard_map/pallas_call | solution.py:26
  17.6 1.1 %shard_map.80 = (f32[64,2304]{1,0:T(8,128)S(1)}, f32[64,2304]{1,0:T(8,128)S(1)}) custom-call(bf16[256,512]{1,0:T(8,128)(2,1)S(1)} %get-tuple-element.68.refs_0_, bf16[256,512]{1,0:T(8,128)(2,1)S(1)} %get-tuple-element.61.refs_4_.refs_1_, bf16[576,768]{1,0:T(8,128)(2,1)S(1)} %get-tuple-element.66.refs_2_.refs_1_, ...), custom_call_target="tpu_custom_call" | custom-call | tf_op jit(solution)/shard_map/pallas_call | solution.py:26
  18.7 2.5 %collective-permute-start.4 = (f32[64,2304]{1,0:T(8,128)S(1)}, f32[64,2304]{1,0:T(8,128)S(1)}, u32[]{:S(2)}, u32[]{:S(2)}) collective-permute-start(f32[64,2304]{1,0:T(8,128)S(1)} %get-tuple-element.69.refs_1_), channel_id=1, source_target_pairs={{0,2},{1,3},{2,0},{3,1},{4,6},{5,7},{6,4},{7,5},{8,10},{9,11},{10,... | collective-permute-start | bytes 1769480 | tf_op jit(solution)/shard_map/ppermute | solution.py:314
  21.2 0.7 %shard_map.82 = (bf16[2304,256]{1,0:T(8,128)(2,1)S(1)}, bf16[2304,256]{1,0:T(8,128)(2,1)S(1)}) custom-call(f32[2304,256]{1,0:T(8,128)S(1)} %copy-done.4, f32[64,2304]{1,0:T(8,128)S(1)} %get-tuple-element.69.refs_1_), custom_call_target="tpu_custom_call" | custom-call | tf_op jit(solution)/shard_map/pallas_call | solution.py:26
  21.9 0.9 %collective-permute-done.4.refs_1_ = f32[64,2304]{1,0:T(8,128)S(1)} collective-permute-done((f32[64,2304]{1,0:T(8,128)S(1)}, f32[64,2304]{1,0:T(8,128)S(1)}, u32[]{:S(2)}, u32[]{:S(2)}) %collective-permute-start.4) | collective-permute-done | bytes 589856 | tf_op jit(solution)/shard_map/ppermute | solution.py:314
  22.8 0.1 shard_map.83.refs_4_
  22.9 0.0 copy-start.3
  22.9 1.6 %collective-permute-start.8 = (f32[64,2304]{1,0:T(8,128)S(1)}, f32[64,2304]{1,0:T(8,128)S(1)}, u32[]{:S(2)}, u32[]{:S(2)}) collective-permute-start(f32[64,2304]{1,0:T(8,128)S(1)} %shard_map.83.refs_4_), channel_id=1, source_target_pairs={{0,1},{1,0},{2,6},{3,7},{4,5},{5,4},{6,2},{7,3},{8,9},{9,8},{10,14... | collective-permute-start | bytes 1769480 | tf_op jit(solution)/shard_map/ppermute | solution.py:309
  24.5 1.1 %shard_map.84 = (f32[32,2304]{1,0:T(8,128)S(1)}, f32[32,2304]{1,0:T(8,128)S(1)}, f32[32,2304]{1,0:T(8,128)S(1)}, f32[32,2304]{1,0:T(8,128)S(1)}) custom-call(bf16[256,512]{1,0:T(8,128)(2,1)S(1)} %get-tuple-element.68.refs_0_, bf16[256,512]{1,0:T(8,128)(2,1)S(1)} %get-tuple-element.61.refs_4_.refs_1_, bf16[576,768]{1,0:T(8,128)(2,1)S(1)} %get-tuple-element.66.refs_2_.refs_1_, ...), custom_call_target="tpu_custom_call" | custom-call | tf_op jit(solution)/shard_map/pallas_call | solution.py:26
  25.6 0.9 %collective-permute-start.6 = (f32[32,2304]{1,0:T(8,128)S(1)}, f32[32,2304]{1,0:T(8,128)S(1)}, u32[]{:S(2)}, u32[]{:S(2)}) collective-permute-start(f32[32,2304]{1,0:T(8,128)S(1)} %get-tuple-element.85), channel_id=1, source_target_pairs={{0,2},{1,3},{2,0},{3,1},{4,6},{5,7},{6,4},{7,5},{8,10},{9,11},{10,... | collective-permute-start | bytes 884744 | tf_op jit(solution)/shard_map/ppermute | solution.py:314
  26.5 0.1 collective-permute-start.7
  26.6 3.2 %shard_map.85 = (bf16[576,768]{1,0:T(8,128)(2,1)S(1)}, bf16[576,768]{1,0:T(8,128)(2,1)S(1)}, bf16[256,512]{1,0:T(8,128)(2,1)S(1)}, bf16[256,512]{1,0:T(8,128)(2,1)S(1)}) custom-call(f32[16,32,256]{2,1,0:T(8,128)S(1)} %bitcast.20, f32[2,2,32,256]{3,2,1,0:T(8,128)S(1)} %collective-permute-done.refs_2_.refs_1_, ...), custom_call_target="tpu_custom_call" | custom-call | tf_op jit(solution)/shard_map/pallas_call | solution.py:26
  29.8 2.0 %shard_map.86 = (f32[128,2304]{1,0:T(8,128)S(1)}, f32[128,2304]{1,0:T(8,128)S(1)}) custom-call(bf16[256,512]{1,0:T(8,128)(2,1)S(1)} %get-tuple-element.78.refs_0_, bf16[256,512]{1,0:T(8,128)(2,1)S(1)} %get-tuple-element.79.refs_1_, bf16[640,768]{1,0:T(8,128)(2,1)S(1)} %get-tuple-element.80.refs_2_, bf16[640,768]{1,0:T(8,128)(2,1)S(1)} %get-tuple-element.81.refs_3_), custom_call_target="tpu_custom_call" | custom-call | tf_op jit(solution)/shard_map/pallas_call | solution.py:26
  31.8 0.5 collective-permute-start.5
  32.3 0.0 collective-permute-done.6.refs_2_
  32.3 0.0 collective-permute-done.7.refs_3_
  32.3 0.5 collective-permute-done.8.refs_4_
  32.8 0.1 shard_map.87
  32.9 2.6 %collective-permute-start.10 = (f32[32,2304]{1,0:T(8,128)S(1)}, f32[32,2304]{1,0:T(8,128)S(1)}, u32[]{:S(2)}, u32[]{:S(2)}) collective-permute-start(f32[32,2304]{1,0:T(8,128)S(1)} %get-tuple-element.95), channel_id=1, source_target_pairs={{0,4},{1,5},{2,3},{3,2},{4,0},{5,1},{6,7},{7,6},{8,12},{9,13},{10,... | collective-permute-start | bytes 884744 | tf_op jit(solution)/shard_map/ppermute | solution.py:309
  35.5 0.3 shard_map.81
  35.9 0.0 collective-permute-done.5.refs_1_
  35.9 0.0 copy-start.1
  35.9 0.1 shard_map.88
  36.0 1.0 %collective-permute-start.9 = (f32[64,2304]{1,0:T(8,128)S(1)}, f32[64,2304]{1,0:T(8,128)S(1)}, u32[]{:S(2)}, u32[]{:S(2)}) collective-permute-start(f32[64,2304]{1,0:T(8,128)S(1)} %get-tuple-element.94), channel_id=1, source_target_pairs={{0,4},{1,5},{2,3},{3,2},{4,0},{5,1},{6,7},{7,6},{8,12},{9,13},{10,... | collective-permute-start | bytes 1769480 | tf_op jit(solution)/shard_map/ppermute | solution.py:309
  37.0 3.0 %shard_map.89 = (f32[16,32,256]{2,1,0:T(8,128)}, f32[8,128]{1,0:T(8,128)S(1)}) custom-call(f32[16,32,256]{2,1,0:T(8,128)S(1)} %bitcast.16, bf16[576,768]{1,0:T(8,128)(2,1)S(1)} %get-tuple-element.66.refs_2_.refs_1_, bf16[576,768]{1,0:T(8,128)(2,1)S(1)} %get-tuple-element.67.refs_3_.refs_2_, bf16[2304,256]{1,0:T(8,128)(2,1)S(1)} %get-tuple-element.70.refs_3_, ...), custom_call_target="tpu_custom_call" | custom-call | tf_op jit(solution)/shard_map/pallas_call | solution.py:26
  40.0 0.2 collective-permute-done.10.refs_1_
  40.2 0.1 shard_map.91
  40.3 2.6 %collective-permute-start.12 = (f32[144,128]{1,0:T(8,128)S(1)}, f32[144,128]{1,0:T(8,128)S(1)}, u32[]{:S(2)}, u32[]{:S(2)}) collective-permute-start(f32[144,128]{1,0:T(8,128)S(1)} %get-tuple-element.102), channel_id=1, source_target_pairs={{0,24},{8,16},{16,8},{24,0},{1,25},{9,17},{17,9},{25,1},{2,26},{10... | collective-permute-start | bytes 221192 | tf_op jit(solution)/shard_map/ppermute | solution.py:393
  42.9 0.0 collective-permute-start.13
  42.9 1.8 %collective-permute-start.14 = (f32[144,128]{1,0:T(8,128)S(1)}, f32[144,128]{1,0:T(8,128)S(1)}, u32[]{:S(2)}, u32[]{:S(2)}) collective-permute-start(f32[144,128]{1,0:T(8,128)S(1)} %get-tuple-element.104), channel_id=1, source_target_pairs={{0,8},{8,0},{16,24},{24,16},{1,9},{9,1},{17,25},{25,17},{2,10},{10... | collective-permute-start | bytes 221192 | tf_op jit(solution)/shard_map/ppermute | solution.py:393
  44.8 0.7 %shard_map.90 = (bf16[2304,256]{1,0:T(8,128)(2,1)S(1)}, bf16[2304,256]{1,0:T(8,128)(2,1)S(1)}) custom-call(f32[2304,256]{1,0:T(8,128)S(1)} %copy-done.5, f32[64,2304]{1,0:T(8,128)S(1)} %get-tuple-element.69.refs_1_), custom_call_target="tpu_custom_call" | custom-call | tf_op jit(solution)/shard_map/pallas_call | solution.py:26
  45.4 1.1 %collective-permute-done.9.refs_1_ = f32[64,2304]{1,0:T(8,128)S(1)} collective-permute-done((f32[64,2304]{1,0:T(8,128)S(1)}, f32[64,2304]{1,0:T(8,128)S(1)}, u32[]{:S(2)}, u32[]{:S(2)}) %collective-permute-start.9) | collective-permute-done | bytes 589856 | tf_op jit(solution)/shard_map/ppermute | solution.py:309
  46.5 0.1 shard_map.92
  46.6 1.6 %collective-permute-start.11 = (f32[32,2304]{1,0:T(8,128)S(1)}, f32[32,2304]{1,0:T(8,128)S(1)}, u32[]{:S(2)}, u32[]{:S(2)}) collective-permute-start(f32[32,2304]{1,0:T(8,128)S(1)} %get-tuple-element.100), channel_id=1, source_target_pairs={{0,1},{1,0},{2,6},{3,7},{4,5},{5,4},{6,2},{7,3},{8,9},{9,8},{10,14... | collective-permute-start | bytes 884744 | tf_op jit(solution)/shard_map/ppermute | solution.py:309
  48.2 2.8 %shard_map.93 = (f32[16,32,256]{2,1,0:T(8,128)}, f32[8,128]{1,0:T(8,128)S(1)}) custom-call(f32[16,32,256]{2,1,0:T(8,128)S(1)} %bitcast.17, f32[16,32,256]{2,1,0:T(8,128)S(1)} %bitcast.21, bf16[576,768]{1,0:T(8,128)(2,1)S(1)} %get-tuple-element.90.refs_2_, bf16[576,768]{1,0:T(8,128)(2,1)S(1)} %get-tuple-element.91.refs_3_, ...), custom_call_target="tpu_custom_call" | custom-call | tf_op jit(solution)/shard_map/pallas_call | solution.py:26
  51.0 0.0 collective-permute-done.12.refs_1_
  51.0 0.0 collective-permute-done.13.refs_2_
  51.0 0.0 collective-permute-done.14.refs_3_
  51.0 0.7 %shard_map.94 = (f32[32,576]{1,0:T(8,128)}, f32[8,128]{1,0:T(8,128)S(1)}) custom-call(f32[144,128]{1,0:T(8,128)S(1)} %get-tuple-element.101.refs_0_, f32[144,128]{1,0:T(8,128)S(1)} %collective-permute-done.12.refs_1_, f32[144,128]{1,0:T(8,128)S(1)} %collective-permute-done.13.refs_2_, f32[144,128]{1,0:T(8,128)S(1)} %collective-permute-done.14.refs_3_, ...), custom_call_target="tpu_custom_call" | custom-call | flops 10000000000 | tf_op jit(solution)/shard_map/pallas_call | solution.py:26
  51.7 1.7 %collective-permute-done.11.refs_1_ = f32[32,2304]{1,0:T(8,128)S(1)} collective-permute-done((f32[32,2304]{1,0:T(8,128)S(1)}, f32[32,2304]{1,0:T(8,128)S(1)}, u32[]{:S(2)}, u32[]{:S(2)}) %collective-permute-start.11) | collective-permute-done | bytes 294944 | tf_op jit(solution)/shard_map/ppermute | solution.py:309
  53.4 0.1 shard_map.95
  53.5 2.6 %collective-permute-start.15 = (f32[144,128]{1,0:T(8,128)S(1)}, f32[144,128]{1,0:T(8,128)S(1)}, u32[]{:S(2)}, u32[]{:S(2)}) collective-permute-start(f32[144,128]{1,0:T(8,128)S(1)} %get-tuple-element.108), channel_id=1, source_target_pairs={{0,24},{8,16},{16,8},{24,0},{1,25},{9,17},{17,9},{25,1},{2,26},{10... | collective-permute-start | bytes 221192 | tf_op jit(solution)/shard_map/ppermute | solution.py:393
  56.1 0.0 collective-permute-start.16
  56.1 1.8 %collective-permute-start.17 = (f32[144,128]{1,0:T(8,128)S(1)}, f32[144,128]{1,0:T(8,128)S(1)}, u32[]{:S(2)}, u32[]{:S(2)}) collective-permute-start(f32[144,128]{1,0:T(8,128)S(1)} %get-tuple-element.110), channel_id=1, source_target_pairs={{0,8},{8,0},{16,24},{24,16},{1,9},{9,1},{17,25},{25,17},{2,10},{10... | collective-permute-start | bytes 221192 | tf_op jit(solution)/shard_map/ppermute | solution.py:393
  57.9 2.0 %collective-permute-done.15.refs_1_ = f32[144,128]{1,0:T(8,128)S(1)} collective-permute-done((f32[144,128]{1,0:T(8,128)S(1)}, f32[144,128]{1,0:T(8,128)S(1)}, u32[]{:S(2)}, u32[]{:S(2)}) %collective-permute-start.15) | collective-permute-done | bytes 73760 | tf_op jit(solution)/shard_map/ppermute | solution.py:393
  60.0 1.6 %collective-permute-done.16.refs_2_ = f32[144,128]{1,0:T(8,128)S(1)} collective-permute-done((f32[144,128]{1,0:T(8,128)S(1)}, f32[144,128]{1,0:T(8,128)S(1)}, u32[]{:S(2)}, u32[]{:S(2)}) %collective-permute-start.16) | collective-permute-done | bytes 73760 | tf_op jit(solution)/shard_map/ppermute | solution.py:393
  61.5 0.0 collective-permute-done.17.refs_3_
  61.5 0.7 %shard_map.96 = f32[32,576]{1,0:T(8,128)} custom-call(f32[144,128]{1,0:T(8,128)S(1)} %get-tuple-element.107.refs_0_, f32[144,128]{1,0:T(8,128)S(1)} %collective-permute-done.15.refs_1_, f32[144,128]{1,0:T(8,128)S(1)} %collective-permute-done.16.refs_2_, f32[144,128]{1,0:T(8,128)S(1)} %collective-permute-done.17.refs_3_), custom_call_target="tpu_custom_call" | custom-call | tf_op jit(solution)/shard_map/pallas_call | solution.py:26
  (7 shorter events, 0.0 us)
Async XLA Ops:
  1.6 3.6 %collective-permute-start = (f32[2,2,32,256]{3,2,1,0:T(8,128)S(1)}, f32[2,2,32,256]{3,2,1,0:T(8,128)S(1)}, u32[]{:S(2)}, u32[]{:S(2)}) collective-permute-start(f32[2,2,32,256]{3,2,1,0:T(8,128)S(1)} %get-tuple-element.59), channel_id=1, source_target_pairs={{0,2},{4,6},{2,0},{6,4},{1,3},{5,7},{3,1},{7,5},{8,10},{12,14},{10... | collective-permute-start | bytes 393224 | tf_op jit(solution)/shard_map/ppermute | solution.py:108
  2.2 3.1 %collective-permute-start.1 = (f32[2,2,32,256]{3,2,1,0:T(8,128)S(1)}, f32[2,2,32,256]{3,2,1,0:T(8,128)S(1)}, u32[]{:S(2)}, u32[]{:S(2)}) collective-permute-start(f32[2,2,32,256]{3,2,1,0:T(8,128)S(1)} %get-tuple-element.60), channel_id=1, source_target_pairs={{2,4},{4,2},{3,5},{5,3},{10,12},{12,10},{11,13},{13,11},{18,20},{2... | collective-permute-start | bytes 393224 | tf_op jit(solution)/shard_map/ppermute | solution.py:108
  2.8 1.0 %copy-start = (f32[1,16,32,256]{3,2,1,0:T(8,128)S(1)}, f32[1,16,32,256]{3,2,1,0:T(8,128)}, u32[]{:S(2)}) copy-start(f32[1,16,32,256]{3,2,1,0:T(8,128)} %param.4) | copy-start | bytes 1572868
  3.9 1.0 %copy-start.2 = (f32[1,16,32,256]{3,2,1,0:T(8,128)S(1)}, f32[1,16,32,256]{3,2,1,0:T(8,128)}, u32[]{:S(2)}) copy-start(f32[1,16,32,256]{3,2,1,0:T(8,128)} %param.5) | copy-start | bytes 1572868
  4.9 5.6 %copy-start.5 = (f32[2304,256]{1,0:T(8,128)S(1)}, f32[2304,256]{1,0:T(8,128)}, u32[]{:S(2)}) copy-start(f32[2304,256]{1,0:T(8,128)} %refs_0_.7) | copy-start | bytes 7077892
  5.4 5.5 %collective-permute-start.2 = (f32[80,256]{1,0:T(8,128)S(1)}, f32[80,256]{1,0:T(8,128)S(1)}, u32[]{:S(2)}, u32[]{:S(2)}) collective-permute-start(f32[80,256]{1,0:T(8,128)S(1)} %get-tuple-element.62.refs_3_), channel_id=1, source_target_pairs={{0,8},{16,24},{8,0},{24,16},{1,9},{17,25},{9,1},{25,17},{2,10},{18... | collective-permute-start | bytes 245768 | tf_op jit(solution)/shard_map/ppermute | solution.py:108
  8.0 6.3 %collective-permute-start.3 = (f32[80,256]{1,0:T(8,128)S(1)}, f32[80,256]{1,0:T(8,128)S(1)}, u32[]{:S(2)}, u32[]{:S(2)}) collective-permute-start(f32[80,256]{1,0:T(8,128)S(1)} %get-tuple-element.63.refs_4_), channel_id=1, source_target_pairs={{8,16},{24,0},{16,8},{0,24},{9,17},{25,1},{17,9},{1,25},{10,18},{2... | collective-permute-start | bytes 245768 | tf_op jit(solution)/shard_map/ppermute | solution.py:108
  14.4 6.8 %copy-start.4 = (f32[2304,256]{1,0:T(8,128)S(1)}, f32[2304,256]{1,0:T(8,128)}, u32[]{:S(2)}) copy-start(f32[2304,256]{1,0:T(8,128)} %refs_0_.6) | copy-start | bytes 7077892
  18.7 4.1 %collective-permute-start.4 = (f32[64,2304]{1,0:T(8,128)S(1)}, f32[64,2304]{1,0:T(8,128)S(1)}, u32[]{:S(2)}, u32[]{:S(2)}) collective-permute-start(f32[64,2304]{1,0:T(8,128)S(1)} %get-tuple-element.69.refs_1_), channel_id=1, source_target_pairs={{0,2},{1,3},{2,0},{3,1},{4,6},{5,7},{6,4},{7,5},{8,10},{9,11},{10,... | collective-permute-start | bytes 1769480 | tf_op jit(solution)/shard_map/ppermute | solution.py:314
  22.9 3.7 %copy-start.3 = (f32[1,16,32,256]{3,2,1,0:T(8,128)S(1)}, f32[1,16,32,256]{3,2,1,0:T(8,128)}, u32[]{:S(2)}) copy-start(f32[1,16,32,256]{3,2,1,0:T(8,128)} %param.5) | copy-start | bytes 1572868
  22.9 9.9 %collective-permute-start.8 = (f32[64,2304]{1,0:T(8,128)S(1)}, f32[64,2304]{1,0:T(8,128)S(1)}, u32[]{:S(2)}, u32[]{:S(2)}) collective-permute-start(f32[64,2304]{1,0:T(8,128)S(1)} %shard_map.83.refs_4_), channel_id=1, source_target_pairs={{0,1},{1,0},{2,6},{3,7},{4,5},{5,4},{6,2},{7,3},{8,9},{9,8},{10,14... | collective-permute-start | bytes 1769480 | tf_op jit(solution)/shard_map/ppermute | solution.py:309
  25.6 6.7 %collective-permute-start.6 = (f32[32,2304]{1,0:T(8,128)S(1)}, f32[32,2304]{1,0:T(8,128)S(1)}, u32[]{:S(2)}, u32[]{:S(2)}) collective-permute-start(f32[32,2304]{1,0:T(8,128)S(1)} %get-tuple-element.85), channel_id=1, source_target_pairs={{0,2},{1,3},{2,0},{3,1},{4,6},{5,7},{6,4},{7,5},{8,10},{9,11},{10,... | collective-permute-start | bytes 884744 | tf_op jit(solution)/shard_map/ppermute | solution.py:314
  26.5 5.8 %collective-permute-start.7 = (f32[32,2304]{1,0:T(8,128)S(1)}, f32[32,2304]{1,0:T(8,128)S(1)}, u32[]{:S(2)}, u32[]{:S(2)}) collective-permute-start(f32[32,2304]{1,0:T(8,128)S(1)} %get-tuple-element.86), channel_id=1, source_target_pairs={{0,2},{1,3},{2,0},{3,1},{4,6},{5,7},{6,4},{7,5},{8,10},{9,11},{10,... | collective-permute-start | bytes 884744 | tf_op jit(solution)/shard_map/ppermute | solution.py:314
  31.8 4.1 %collective-permute-start.5 = (f32[128,2304]{1,0:T(8,128)S(1)}, f32[128,2304]{1,0:T(8,128)S(1)}, u32[]{:S(2)}, u32[]{:S(2)}) collective-permute-start(f32[128,2304]{1,0:T(8,128)S(1)} %get-tuple-element.83), channel_id=1, source_target_pairs={{0,2},{1,3},{2,0},{3,1},{4,6},{5,7},{6,4},{7,5},{8,10},{9,11},{10,... | collective-permute-start | bytes 3538952 | tf_op jit(solution)/shard_map/ppermute | solution.py:314
  32.9 7.3 %collective-permute-start.10 = (f32[32,2304]{1,0:T(8,128)S(1)}, f32[32,2304]{1,0:T(8,128)S(1)}, u32[]{:S(2)}, u32[]{:S(2)}) collective-permute-start(f32[32,2304]{1,0:T(8,128)S(1)} %get-tuple-element.95), channel_id=1, source_target_pairs={{0,4},{1,5},{2,3},{3,2},{4,0},{5,1},{6,7},{7,6},{8,12},{9,13},{10,... | collective-permute-start | bytes 884744 | tf_op jit(solution)/shard_map/ppermute | solution.py:309
  35.9 1.1 %copy-start.1 = (f32[1,16,32,256]{3,2,1,0:T(8,128)S(1)}, f32[1,16,32,256]{3,2,1,0:T(8,128)}, u32[]{:S(2)}) copy-start(f32[1,16,32,256]{3,2,1,0:T(8,128)} %param.4) | copy-start | bytes 1572868
  36.0 10.5 %collective-permute-start.9 = (f32[64,2304]{1,0:T(8,128)S(1)}, f32[64,2304]{1,0:T(8,128)S(1)}, u32[]{:S(2)}, u32[]{:S(2)}) collective-permute-start(f32[64,2304]{1,0:T(8,128)S(1)} %get-tuple-element.94), channel_id=1, source_target_pairs={{0,4},{1,5},{2,3},{3,2},{4,0},{5,1},{6,7},{7,6},{8,12},{9,13},{10,... | collective-permute-start | bytes 1769480 | tf_op jit(solution)/shard_map/ppermute | solution.py:309
  40.3 10.7 %collective-permute-start.12 = (f32[144,128]{1,0:T(8,128)S(1)}, f32[144,128]{1,0:T(8,128)S(1)}, u32[]{:S(2)}, u32[]{:S(2)}) collective-permute-start(f32[144,128]{1,0:T(8,128)S(1)} %get-tuple-element.102), channel_id=1, source_target_pairs={{0,24},{8,16},{16,8},{24,0},{1,25},{9,17},{17,9},{25,1},{2,26},{10... | collective-permute-start | bytes 221192 | tf_op jit(solution)/shard_map/ppermute | solution.py:393
  42.9 8.1 %collective-permute-start.13 = (f32[144,128]{1,0:T(8,128)S(1)}, f32[144,128]{1,0:T(8,128)S(1)}, u32[]{:S(2)}, u32[]{:S(2)}) collective-permute-start(f32[144,128]{1,0:T(8,128)S(1)} %get-tuple-element.103), channel_id=1, source_target_pairs={{0,16},{8,24},{16,0},{24,8},{1,17},{9,25},{17,1},{25,9},{2,18},{10... | collective-permute-start | bytes 221192 | tf_op jit(solution)/shard_map/ppermute | solution.py:393
  42.9 8.1 %collective-permute-start.14 = (f32[144,128]{1,0:T(8,128)S(1)}, f32[144,128]{1,0:T(8,128)S(1)}, u32[]{:S(2)}, u32[]{:S(2)}) collective-permute-start(f32[144,128]{1,0:T(8,128)S(1)} %get-tuple-element.104), channel_id=1, source_target_pairs={{0,8},{8,0},{16,24},{24,16},{1,9},{9,1},{17,25},{25,17},{2,10},{10... | collective-permute-start | bytes 221192 | tf_op jit(solution)/shard_map/ppermute | solution.py:393
  46.6 6.8 %collective-permute-start.11 = (f32[32,2304]{1,0:T(8,128)S(1)}, f32[32,2304]{1,0:T(8,128)S(1)}, u32[]{:S(2)}, u32[]{:S(2)}) collective-permute-start(f32[32,2304]{1,0:T(8,128)S(1)} %get-tuple-element.100), channel_id=1, source_target_pairs={{0,1},{1,0},{2,6},{3,7},{4,5},{5,4},{6,2},{7,3},{8,9},{9,8},{10,14... | collective-permute-start | bytes 884744 | tf_op jit(solution)/shard_map/ppermute | solution.py:309
  53.5 6.5 %collective-permute-start.15 = (f32[144,128]{1,0:T(8,128)S(1)}, f32[144,128]{1,0:T(8,128)S(1)}, u32[]{:S(2)}, u32[]{:S(2)}) collective-permute-start(f32[144,128]{1,0:T(8,128)S(1)} %get-tuple-element.108), channel_id=1, source_target_pairs={{0,24},{8,16},{16,8},{24,0},{1,25},{9,17},{17,9},{25,1},{2,26},{10... | collective-permute-start | bytes 221192 | tf_op jit(solution)/shard_map/ppermute | solution.py:393
  56.1 5.4 %collective-permute-start.16 = (f32[144,128]{1,0:T(8,128)S(1)}, f32[144,128]{1,0:T(8,128)S(1)}, u32[]{:S(2)}, u32[]{:S(2)}) collective-permute-start(f32[144,128]{1,0:T(8,128)S(1)} %get-tuple-element.109), channel_id=1, source_target_pairs={{0,16},{8,24},{16,0},{24,8},{1,17},{9,25},{17,1},{25,9},{2,18},{10... | collective-permute-start | bytes 221192 | tf_op jit(solution)/shard_map/ppermute | solution.py:393
  56.1 5.4 %collective-permute-start.17 = (f32[144,128]{1,0:T(8,128)S(1)}, f32[144,128]{1,0:T(8,128)S(1)}, u32[]{:S(2)}, u32[]{:S(2)}) collective-permute-start(f32[144,128]{1,0:T(8,128)S(1)} %get-tuple-element.110), channel_id=1, source_target_pairs={{0,8},{8,0},{16,24},{24,16},{1,9},{9,1},{17,25},{25,17},{2,10},{10... | collective-permute-start | bytes 221192 | tf_op jit(solution)/shard_map/ppermute | solution.py:393

commit v9 on v8

--- a/solution.py
+++ b/solution.py
@@ -458,8 +458,6 @@
     keep_2, away_2 = second_products(1, [quarter] * 2, [])
     got_2 = core_swap(away_2)
     b2_high, b2_low = call(prepare_back, pair, [second_weight], after=[away_2])
-    w2_high, w2_low = call(prepare, pair, [second_weight], after=[away_2])
-    b1_high, b1_low = call(prepare_back, pair, [first_weight], after=[away_2])
     (away_2,) = call(add_up, [quarter], [keep_2, got_2], after=[b2_low])
     got_2 = plane_swap(away_2, False)
     *keeps, away_one, away_two = second_products(0, [eighth] * 4, [away_2])
@@ -483,6 +481,7 @@
     got_2 = plane_swap(away_2, True)
     keep_1, away_1 = call(add_halves, halves_of(2 * each), [keep_1, got_1], after=[keep_2])
     got_1 = plane_swap(away_1, True)
+    w2_high, w2_low = call(prepare, pair, [second_weight], after=[keep_1])
     outs = [((rows, cols, channels), F32), ((8, 128), F32)]
     output, token = call(
         output_kernel, outs, [here, x2_high, x2_low, w2_high, w2_low], after=[keep_1]
@@ -494,6 +493,7 @@
         second_grad = wide_sum(keep_2, got_2)
     keep_1, away_1 = call(add_halves, halves_of(each), [keep_1, got_1], after=[token])
     got_1 = plane_swap(away_1, False)
+    b1_high, b1_low = call(prepare_back, pair, [first_weight], after=[keep_1])
     input_grad, token = call(
         input_grad_kernel,
         outs,

time: 62.5 us -> 63.2 us (1.011)
  transfers between devices with their start and end apart: 18 -> 18, of which waited for: 8 -> 7; matrix products, arithmetic and copies ran while one was open for 0% -> 0% of each run, Pallas kernels for 25% -> 25%
where the time goes in v9:
time: 63.2 us; the launch traced here: 62.9 us
  starting transfers between devices  26.3 us (42%)
  Pallas kernels  20.9 us (33%)
  waiting for transfers between devices  11.9 us (19%)
  local copies, waits for them, and re-layouts  3.06 us (5%)
  between operations  0.82 us (1%)
    pallas_call x22, Pallas kernels, call(): pl.pallas_call(kernel, out_shape=[jax.ShapeDtypeStruct(shape, dtype) for...  20.9 us
    ppermute x6, starting transfers between devices, send_blocks(): lax.ppermute(blocks[step], 'lon', [(i, i ^ step) for i in range(lon)])  8.91 us
    ppermute x4, starting transfers between devices, plane_swap(): return lax.ppermute(away, ('lat', 'rep'), plane_perm(count, one, two))  7.1 us
    ppermute x4, starting transfers between devices, pair_swap(): lax.ppermute(block, axis, who + [(b, a) for a, b in who])  6.31 us
    ppermute x4, starting transfers between devices, core_swap(): return lax.ppermute(away, ('lat', 'rep'), plane_perm(count, 2, 2))  3.94 us
    ppermute x4, waiting for transfers between devices, plane_swap(): return lax.ppermute(away, ('lat', 'rep'), plane_perm(count, one, two))  3.87 us
    ppermute x6, waiting for transfers between devices, send_blocks(): lax.ppermute(blocks[step], 'lon', [(i, i ^ step) for i in range(lon)])  3.59 us
    ppermute x4, waiting for transfers between devices, pair_swap(): lax.ppermute(block, axis, who + [(b, a) for a, b in who])  3.52 us
  transfers between devices with their start and end apart: 18, of which 7 were waited for; matrix products, arithmetic and copies ran while one was open for 0% of the time, Pallas kernels for 25%

profile of v9, /device:TPU:0, one launch (start us, length us, event | category | flops | bytes accessed | tf_op | source)
XLA Modules:
  0.0 62.9 jit_solution(13570152471847292058)
XLA Ops:
  0.6 1.0 %slice_bitcast_fusion = (f32[2,32,256]{2,1,0:T(8,128)S(1)}, f32[2,32,256]{2,1,0:T(8,128)S(1)}, f32[2,32,256]{2,1,0:T(8,128)S(1)}, f32[2,32,256]{2,1,0:T(8,128)S(1)}) fusion(f32[1,16,32,256]{3,2,1,0:T(8,128)} %param.5, f32[1,16,32,256]{3,2,1,0:T(8,128)} %param.4), kind=kLoop, calls=%fused_computation | loop fusion | bytes 524288 | tf_op jit(solution)/shard_map/slice | solution.py:408
  1.6 0.5 collective-permute-start
  2.2 0.7 %collective-permute-start.1 = (f32[2,2,32,256]{3,2,1,0:T(8,128)S(1)}, f32[2,2,32,256]{3,2,1,0:T(8,128)S(1)}, u32[]{:S(2)}, u32[]{:S(2)}) collective-permute-start(f32[2,2,32,256]{3,2,1,0:T(8,128)S(1)} %get-tuple-element.60), channel_id=1, source_target_pairs={{2,4},{4,2},{3,5},{5,3},{10,12},{12,10},{11,13},{13,11},{18,20},{2... | collective-permute-start | bytes 393224 | tf_op jit(solution)/shard_map/ppermute | solution.py:108
  2.8 0.0 copy-start
  2.8 1.0 %copy-done = f32[1,16,32,256]{3,2,1,0:T(8,128)S(1)} copy-done((f32[1,16,32,256]{3,2,1,0:T(8,128)S(1)}, f32[1,16,32,256]{3,2,1,0:T(8,128)}, u32[]{:S(2)}) %copy-start) | copy-done | bytes 524312
  3.9 1.0 %copy-done.2 = f32[1,16,32,256]{3,2,1,0:T(8,128)S(1)} copy-done((f32[1,16,32,256]{3,2,1,0:T(8,128)S(1)}, f32[1,16,32,256]{3,2,1,0:T(8,128)}, u32[]{:S(2)}) %copy-start.2) | copy-done | bytes 524312
  4.9 0.4 shard_map.75
  5.3 0.0 collective-permute-done.refs_2_.refs_1_
  5.3 0.0 collective-permute-done.1.refs_3_.refs_2_
  5.3 0.1 shard_map.77
  5.4 2.7 %collective-permute-start.2 = (f32[80,256]{1,0:T(8,128)S(1)}, f32[80,256]{1,0:T(8,128)S(1)}, u32[]{:S(2)}, u32[]{:S(2)}) collective-permute-start(f32[80,256]{1,0:T(8,128)S(1)} %get-tuple-element.62.refs_3_), channel_id=1, source_target_pairs={{0,8},{16,24},{8,0},{24,16},{1,9},{17,25},{9,1},{25,17},{2,10},{18... | collective-permute-start | bytes 245768 | tf_op jit(solution)/shard_map/ppermute | solution.py:108
  8.0 2.5 %collective-permute-start.3 = (f32[80,256]{1,0:T(8,128)S(1)}, f32[80,256]{1,0:T(8,128)S(1)}, u32[]{:S(2)}, u32[]{:S(2)}) collective-permute-start(f32[80,256]{1,0:T(8,128)S(1)} %get-tuple-element.63.refs_4_), channel_id=1, source_target_pairs={{8,16},{24,0},{16,8},{0,24},{9,17},{25,1},{17,9},{1,25},{10,18},{2... | collective-permute-start | bytes 245768 | tf_op jit(solution)/shard_map/ppermute | solution.py:108
  10.5 0.0 copy-done.5
  10.5 0.3 shard_map.78
  10.9 0.0 collective-permute-done.2.refs_5_
  10.9 3.5 %collective-permute-done.3.refs_6_ = f32[80,256]{1,0:T(8,128)S(1)} collective-permute-done((f32[80,256]{1,0:T(8,128)S(1)}, f32[80,256]{1,0:T(8,128)S(1)}, u32[]{:S(2)}, u32[]{:S(2)}) %collective-permute-start.3) | collective-permute-done | bytes 81952 | tf_op jit(solution)/shard_map/ppermute | solution.py:108
  14.4 3.2 %shard_map.79 = (f32[576,256]{1,0:T(8,128)S(1)}, f32[48,256]{1,0:T(8,128)S(1)}, bf16[640,768]{1,0:T(8,128)(2,1)S(1)}, bf16[640,768]{1,0:T(8,128)(2,1)S(1)}, bf16...) custom-call(f32[16,32,256]{2,1,0:T(8,128)S(1)} %get-tuple-element.58.refs_0_, ...), custom_call_target="tpu_custom_call" | custom-call | tf_op jit(solution)/shard_map/pallas_call | solution.py:26
  17.6 1.1 %shard_map.80 = (f32[64,2304]{1,0:T(8,128)S(1)}, f32[64,2304]{1,0:T(8,128)S(1)}) custom-call(bf16[256,512]{1,0:T(8,128)(2,1)S(1)} %get-tuple-element.68.refs_0_, bf16[256,512]{1,0:T(8,128)(2,1)S(1)} %get-tuple-element.61.refs_4_.refs_1_, bf16[576,768]{1,0:T(8,128)(2,1)S(1)} %get-tuple-element.66.refs_2_.refs_1_, ...), custom_call_target="tpu_custom_call" | custom-call | tf_op jit(solution)/shard_map/pallas_call | solution.py:26
  18.7 2.5 %collective-permute-start.4 = (f32[64,2304]{1,0:T(8,128)S(1)}, f32[64,2304]{1,0:T(8,128)S(1)}, u32[]{:S(2)}, u32[]{:S(2)}) collective-permute-start(f32[64,2304]{1,0:T(8,128)S(1)} %get-tuple-element.69.refs_1_), channel_id=1, source_target_pairs={{0,2},{1,3},{2,0},{3,1},{4,6},{5,7},{6,4},{7,5},{8,10},{9,11},{10,... | collective-permute-start | bytes 1769480 | tf_op jit(solution)/shard_map/ppermute | solution.py:314
  21.2 0.7 %shard_map.81 = (bf16[2304,256]{1,0:T(8,128)(2,1)S(1)}, bf16[2304,256]{1,0:T(8,128)(2,1)S(1)}) custom-call(f32[2304,256]{1,0:T(8,128)S(1)} %copy-done.4, f32[64,2304]{1,0:T(8,128)S(1)} %get-tuple-element.69.refs_1_), custom_call_target="tpu_custom_call" | custom-call | tf_op jit(solution)/shard_map/pallas_call | solution.py:26
  21.9 0.9 %collective-permute-done.4.refs_1_ = f32[64,2304]{1,0:T(8,128)S(1)} collective-permute-done((f32[64,2304]{1,0:T(8,128)S(1)}, f32[64,2304]{1,0:T(8,128)S(1)}, u32[]{:S(2)}, u32[]{:S(2)}) %collective-permute-start.4) | collective-permute-done | bytes 589856 | tf_op jit(solution)/shard_map/ppermute | solution.py:314
  22.8 0.1 shard_map.82.refs_4_
  22.9 0.0 copy-start.3
  22.9 1.6 %collective-permute-start.8 = (f32[64,2304]{1,0:T(8,128)S(1)}, f32[64,2304]{1,0:T(8,128)S(1)}, u32[]{:S(2)}, u32[]{:S(2)}) collective-permute-start(f32[64,2304]{1,0:T(8,128)S(1)} %shard_map.82.refs_4_), channel_id=1, source_target_pairs={{0,1},{1,0},{2,6},{3,7},{4,5},{5,4},{6,2},{7,3},{8,9},{9,8},{10,14... | collective-permute-start | bytes 1769480 | tf_op jit(solution)/shard_map/ppermute | solution.py:309
  24.5 1.1 %shard_map.83 = (f32[32,2304]{1,0:T(8,128)S(1)}, f32[32,2304]{1,0:T(8,128)S(1)}, f32[32,2304]{1,0:T(8,128)S(1)}, f32[32,2304]{1,0:T(8,128)S(1)}) custom-call(bf16[256,512]{1,0:T(8,128)(2,1)S(1)} %get-tuple-element.68.refs_0_, bf16[256,512]{1,0:T(8,128)(2,1)S(1)} %get-tuple-element.61.refs_4_.refs_1_, bf16[576,768]{1,0:T(8,128)(2,1)S(1)} %get-tuple-element.66.refs_2_.refs_1_, ...), custom_call_target="tpu_custom_call" | custom-call | tf_op jit(solution)/shard_map/pallas_call | solution.py:26
  25.6 0.9 %collective-permute-start.6 = (f32[32,2304]{1,0:T(8,128)S(1)}, f32[32,2304]{1,0:T(8,128)S(1)}, u32[]{:S(2)}, u32[]{:S(2)}) collective-permute-start(f32[32,2304]{1,0:T(8,128)S(1)} %get-tuple-element.83), channel_id=1, source_target_pairs={{0,2},{1,3},{2,0},{3,1},{4,6},{5,7},{6,4},{7,5},{8,10},{9,11},{10,... | collective-permute-start | bytes 884744 | tf_op jit(solution)/shard_map/ppermute | solution.py:314
  26.5 0.1 collective-permute-start.7
  26.6 3.2 %shard_map.84 = (bf16[576,768]{1,0:T(8,128)(2,1)S(1)}, bf16[576,768]{1,0:T(8,128)(2,1)S(1)}, bf16[256,512]{1,0:T(8,128)(2,1)S(1)}, bf16[256,512]{1,0:T(8,128)(2,1)S(1)}) custom-call(f32[16,32,256]{2,1,0:T(8,128)S(1)} %bitcast.20, f32[2,2,32,256]{3,2,1,0:T(8,128)S(1)} %collective-permute-done.refs_2_.refs_1_, ...), custom_call_target="tpu_custom_call" | custom-call | tf_op jit(solution)/shard_map/pallas_call | solution.py:26
  29.8 2.0 %shard_map.85 = (f32[128,2304]{1,0:T(8,128)S(1)}, f32[128,2304]{1,0:T(8,128)S(1)}) custom-call(bf16[256,512]{1,0:T(8,128)(2,1)S(1)} %get-tuple-element.76.refs_0_, bf16[256,512]{1,0:T(8,128)(2,1)S(1)} %get-tuple-element.77.refs_1_, bf16[640,768]{1,0:T(8,128)(2,1)S(1)} %get-tuple-element.78.refs_2_, bf16[640,768]{1,0:T(8,128)(2,1)S(1)} %get-tuple-element.79.refs_3_), custom_call_target="tpu_custom_call" | custom-call | tf_op jit(solution)/shard_map/pallas_call | solution.py:26
  31.8 0.5 collective-permute-start.5
  32.3 0.0 collective-permute-done.6.refs_2_
  32.3 0.0 collective-permute-done.7.refs_3_
  32.3 0.5 collective-permute-done.8.refs_4_
  32.8 0.1 shard_map.86
  32.9 2.6 %collective-permute-start.10 = (f32[32,2304]{1,0:T(8,128)S(1)}, f32[32,2304]{1,0:T(8,128)S(1)}, u32[]{:S(2)}, u32[]{:S(2)}) collective-permute-start(f32[32,2304]{1,0:T(8,128)S(1)} %get-tuple-element.93), channel_id=1, source_target_pairs={{0,4},{1,5},{2,3},{3,2},{4,0},{5,1},{6,7},{7,6},{8,12},{9,13},{10,... | collective-permute-start | bytes 884744 | tf_op jit(solution)/shard_map/ppermute | solution.py:309
  35.5 0.0 collective-permute-done.5.refs_1_
  35.5 0.1 shard_map.87
  35.6 0.0 copy-start.1
  35.7 0.3 shard_map.88
  36.0 1.4 %collective-permute-start.9 = (f32[64,2304]{1,0:T(8,128)S(1)}, f32[64,2304]{1,0:T(8,128)S(1)}, u32[]{:S(2)}, u32[]{:S(2)}) collective-permute-start(f32[64,2304]{1,0:T(8,128)S(1)} %get-tuple-element.92), channel_id=1, source_target_pairs={{0,4},{1,5},{2,3},{3,2},{4,0},{5,1},{6,7},{7,6},{8,12},{9,13},{10,... | collective-permute-start | bytes 1769480 | tf_op jit(solution)/shard_map/ppermute | solution.py:309
  37.4 3.0 %shard_map.89 = (f32[16,32,256]{2,1,0:T(8,128)}, f32[8,128]{1,0:T(8,128)S(1)}) custom-call(f32[16,32,256]{2,1,0:T(8,128)S(1)} %bitcast.16, bf16[576,768]{1,0:T(8,128)(2,1)S(1)} %get-tuple-element.66.refs_2_.refs_1_, bf16[576,768]{1,0:T(8,128)(2,1)S(1)} %get-tuple-element.67.refs_3_.refs_2_, bf16[2304,256]{1,0:T(8,128)(2,1)S(1)} %get-tuple-element.87.refs_3_, ...), custom_call_target="tpu_custom_call" | custom-call | tf_op jit(solution)/shard_map/pallas_call | solution.py:26
  40.3 0.0 collective-permute-done.10.refs_1_
  40.3 0.1 shard_map.90
  40.4 2.6 %collective-permute-start.12 = (f32[144,128]{1,0:T(8,128)S(1)}, f32[144,128]{1,0:T(8,128)S(1)}, u32[]{:S(2)}, u32[]{:S(2)}) collective-permute-start(f32[144,128]{1,0:T(8,128)S(1)} %get-tuple-element.102), channel_id=1, source_target_pairs={{0,24},{8,16},{16,8},{24,0},{1,25},{9,17},{17,9},{25,1},{2,26},{10... | collective-permute-start | bytes 221192 | tf_op jit(solution)/shard_map/ppermute | solution.py:393
  43.1 0.0 collective-permute-start.13
  43.1 1.8 %collective-permute-start.14 = (f32[144,128]{1,0:T(8,128)S(1)}, f32[144,128]{1,0:T(8,128)S(1)}, u32[]{:S(2)}, u32[]{:S(2)}) collective-permute-start(f32[144,128]{1,0:T(8,128)S(1)} %get-tuple-element.104), channel_id=1, source_target_pairs={{0,8},{8,0},{16,24},{24,16},{1,9},{9,1},{17,25},{25,17},{2,10},{10... | collective-permute-start | bytes 221192 | tf_op jit(solution)/shard_map/ppermute | solution.py:393
  44.9 1.7 %collective-permute-done.9.refs_1_ = f32[64,2304]{1,0:T(8,128)S(1)} collective-permute-done((f32[64,2304]{1,0:T(8,128)S(1)}, f32[64,2304]{1,0:T(8,128)S(1)}, u32[]{:S(2)}, u32[]{:S(2)}) %collective-permute-start.9) | collective-permute-done | bytes 589856 | tf_op jit(solution)/shard_map/ppermute | solution.py:309
  46.5 0.1 shard_map.91
  46.6 0.7 %shard_map.92 = (bf16[2304,256]{1,0:T(8,128)(2,1)S(1)}, bf16[2304,256]{1,0:T(8,128)(2,1)S(1)}) custom-call(f32[2304,256]{1,0:T(8,128)S(1)} %copy-done.5, f32[32,2304]{1,0:T(8,128)S(1)} %get-tuple-element.96.refs_1_.refs_6_.refs_0_), custom_call_target="tpu_custom_call" | custom-call | tf_op jit(solution)/shard_map/pallas_call | solution.py:26
  47.3 1.6 %collective-permute-start.11 = (f32[32,2304]{1,0:T(8,128)S(1)}, f32[32,2304]{1,0:T(8,128)S(1)}, u32[]{:S(2)}, u32[]{:S(2)}) collective-permute-start(f32[32,2304]{1,0:T(8,128)S(1)} %get-tuple-element.100), channel_id=1, source_target_pairs={{0,1},{1,0},{2,6},{3,7},{4,5},{5,4},{6,2},{7,3},{8,9},{9,8},{10,14... | collective-permute-start | bytes 884744 | tf_op jit(solution)/shard_map/ppermute | solution.py:309
  48.9 2.8 %shard_map.93 = (f32[16,32,256]{2,1,0:T(8,128)}, f32[8,128]{1,0:T(8,128)S(1)}) custom-call(f32[16,32,256]{2,1,0:T(8,128)S(1)} %bitcast.17, f32[16,32,256]{2,1,0:T(8,128)S(1)} %bitcast.21, bf16[576,768]{1,0:T(8,128)(2,1)S(1)} %get-tuple-element.90.refs_2_, bf16[576,768]{1,0:T(8,128)(2,1)S(1)} %get-tuple-element.91.refs_3_, ...), custom_call_target="tpu_custom_call" | custom-call | tf_op jit(solution)/shard_map/pallas_call | solution.py:26
  51.7 0.0 collective-permute-done.12.refs_1_
  51.7 0.0 collective-permute-done.13.refs_2_
  51.7 0.0 collective-permute-done.14.refs_3_
  51.7 0.7 %shard_map.94 = (f32[32,576]{1,0:T(8,128)}, f32[8,128]{1,0:T(8,128)S(1)}) custom-call(f32[144,128]{1,0:T(8,128)S(1)} %get-tuple-element.101.refs_0_, f32[144,128]{1,0:T(8,128)S(1)} %collective-permute-done.12.refs_1_, f32[144,128]{1,0:T(8,128)S(1)} %collective-permute-done.13.refs_2_, f32[144,128]{1,0:T(8,128)S(1)} %collective-permute-done.14.refs_3_, ...), custom_call_target="tpu_custom_call" | custom-call | flops 10000000000 | tf_op jit(solution)/shard_map/pallas_call | solution.py:26
  52.4 1.7 %collective-permute-done.11.refs_1_ = f32[32,2304]{1,0:T(8,128)S(1)} collective-permute-done((f32[32,2304]{1,0:T(8,128)S(1)}, f32[32,2304]{1,0:T(8,128)S(1)}, u32[]{:S(2)}, u32[]{:S(2)}) %collective-permute-start.11) | collective-permute-done | bytes 294944 | tf_op jit(solution)/shard_map/ppermute | solution.py:309
  54.1 0.1 shard_map.95
  54.2 2.6 %collective-permute-start.15 = (f32[144,128]{1,0:T(8,128)S(1)}, f32[144,128]{1,0:T(8,128)S(1)}, u32[]{:S(2)}, u32[]{:S(2)}) collective-permute-start(f32[144,128]{1,0:T(8,128)S(1)} %get-tuple-element.108), channel_id=1, source_target_pairs={{0,24},{8,16},{16,8},{24,0},{1,25},{9,17},{17,9},{25,1},{2,26},{10... | collective-permute-start | bytes 221192 | tf_op jit(solution)/shard_map/ppermute | solution.py:393
  56.8 0.0 collective-permute-start.16
  56.8 1.8 %collective-permute-start.17 = (f32[144,128]{1,0:T(8,128)S(1)}, f32[144,128]{1,0:T(8,128)S(1)}, u32[]{:S(2)}, u32[]{:S(2)}) collective-permute-start(f32[144,128]{1,0:T(8,128)S(1)} %get-tuple-element.110), channel_id=1, source_target_pairs={{0,8},{8,0},{16,24},{24,16},{1,9},{9,1},{17,25},{25,17},{2,10},{10... | collective-permute-start | bytes 221192 | tf_op jit(solution)/shard_map/ppermute | solution.py:393
  58.6 2.0 %collective-permute-done.15.refs_1_ = f32[144,128]{1,0:T(8,128)S(1)} collective-permute-done((f32[144,128]{1,0:T(8,128)S(1)}, f32[144,128]{1,0:T(8,128)S(1)}, u32[]{:S(2)}, u32[]{:S(2)}) %collective-permute-start.15) | collective-permute-done | bytes 73760 | tf_op jit(solution)/shard_map/ppermute | solution.py:393
  60.6 1.6 %collective-permute-done.16.refs_2_ = f32[144,128]{1,0:T(8,128)S(1)} collective-permute-done((f32[144,128]{1,0:T(8,128)S(1)}, f32[144,128]{1,0:T(8,128)S(1)}, u32[]{:S(2)}, u32[]{:S(2)}) %collective-permute-start.16) | collective-permute-done | bytes 73760 | tf_op jit(solution)/shard_map/ppermute | solution.py:393
  62.2 0.0 collective-permute-done.17.refs_3_
  62.2 0.7 %shard_map.96 = f32[32,576]{1,0:T(8,128)} custom-call(f32[144,128]{1,0:T(8,128)S(1)} %get-tuple-element.107.refs_0_, f32[144,128]{1,0:T(8,128)S(1)} %collective-permute-done.15.refs_1_, f32[144,128]{1,0:T(8,128)S(1)} %collective-permute-done.16.refs_2_, f32[144,128]{1,0:T(8,128)S(1)} %collective-permute-done.17.refs_3_), custom_call_target="tpu_custom_call" | custom-call | tf_op jit(solution)/shard_map/pallas_call | solution.py:26
  (7 shorter events, 0.0 us)
Async XLA Ops:
  1.6 3.6 %collective-permute-start = (f32[2,2,32,256]{3,2,1,0:T(8,128)S(1)}, f32[2,2,32,256]{3,2,1,0:T(8,128)S(1)}, u32[]{:S(2)}, u32[]{:S(2)}) collective-permute-start(f32[2,2,32,256]{3,2,1,0:T(8,128)S(1)} %get-tuple-element.59), channel_id=1, source_target_pairs={{0,2},{4,6},{2,0},{6,4},{1,3},{5,7},{3,1},{7,5},{8,10},{12,14},{10... | collective-permute-start | bytes 393224 | tf_op jit(solution)/shard_map/ppermute | solution.py:108
  2.2 3.1 %collective-permute-start.1 = (f32[2,2,32,256]{3,2,1,0:T(8,128)S(1)}, f32[2,2,32,256]{3,2,1,0:T(8,128)S(1)}, u32[]{:S(2)}, u32[]{:S(2)}) collective-permute-start(f32[2,2,32,256]{3,2,1,0:T(8,128)S(1)} %get-tuple-element.60), channel_id=1, source_target_pairs={{2,4},{4,2},{3,5},{5,3},{10,12},{12,10},{11,13},{13,11},{18,20},{2... | collective-permute-start | bytes 393224 | tf_op jit(solution)/shard_map/ppermute | solution.py:108
  2.8 1.0 %copy-start = (f32[1,16,32,256]{3,2,1,0:T(8,128)S(1)}, f32[1,16,32,256]{3,2,1,0:T(8,128)}, u32[]{:S(2)}) copy-start(f32[1,16,32,256]{3,2,1,0:T(8,128)} %param.4) | copy-start | bytes 1572868
  3.9 1.0 %copy-start.2 = (f32[1,16,32,256]{3,2,1,0:T(8,128)S(1)}, f32[1,16,32,256]{3,2,1,0:T(8,128)}, u32[]{:S(2)}) copy-start(f32[1,16,32,256]{3,2,1,0:T(8,128)} %param.5) | copy-start | bytes 1572868
  4.9 5.6 %copy-start.5 = (f32[2304,256]{1,0:T(8,128)S(1)}, f32[2304,256]{1,0:T(8,128)}, u32[]{:S(2)}) copy-start(f32[2304,256]{1,0:T(8,128)} %refs_0_.7) | copy-start | bytes 7077892
  5.4 5.5 %collective-permute-start.2 = (f32[80,256]{1,0:T(8,128)S(1)}, f32[80,256]{1,0:T(8,128)S(1)}, u32[]{:S(2)}, u32[]{:S(2)}) collective-permute-start(f32[80,256]{1,0:T(8,128)S(1)} %get-tuple-element.62.refs_3_), channel_id=1, source_target_pairs={{0,8},{16,24},{8,0},{24,16},{1,9},{17,25},{9,1},{25,17},{2,10},{18... | collective-permute-start | bytes 245768 | tf_op jit(solution)/shard_map/ppermute | solution.py:108
  8.0 6.3 %collective-permute-start.3 = (f32[80,256]{1,0:T(8,128)S(1)}, f32[80,256]{1,0:T(8,128)S(1)}, u32[]{:S(2)}, u32[]{:S(2)}) collective-permute-start(f32[80,256]{1,0:T(8,128)S(1)} %get-tuple-element.63.refs_4_), channel_id=1, source_target_pairs={{8,16},{24,0},{16,8},{0,24},{9,17},{25,1},{17,9},{1,25},{10,18},{2... | collective-permute-start | bytes 245768 | tf_op jit(solution)/shard_map/ppermute | solution.py:108
  14.4 6.8 %copy-start.4 = (f32[2304,256]{1,0:T(8,128)S(1)}, f32[2304,256]{1,0:T(8,128)}, u32[]{:S(2)}) copy-start(f32[2304,256]{1,0:T(8,128)} %refs_0_.6) | copy-start | bytes 7077892
  18.7 4.1 %collective-permute-start.4 = (f32[64,2304]{1,0:T(8,128)S(1)}, f32[64,2304]{1,0:T(8,128)S(1)}, u32[]{:S(2)}, u32[]{:S(2)}) collective-permute-start(f32[64,2304]{1,0:T(8,128)S(1)} %get-tuple-element.69.refs_1_), channel_id=1, source_target_pairs={{0,2},{1,3},{2,0},{3,1},{4,6},{5,7},{6,4},{7,5},{8,10},{9,11},{10,... | collective-permute-start | bytes 1769480 | tf_op jit(solution)/shard_map/ppermute | solution.py:314
  22.9 3.7 %copy-start.3 = (f32[1,16,32,256]{3,2,1,0:T(8,128)S(1)}, f32[1,16,32,256]{3,2,1,0:T(8,128)}, u32[]{:S(2)}) copy-start(f32[1,16,32,256]{3,2,1,0:T(8,128)} %param.5) | copy-start | bytes 1572868
  22.9 9.9 %collective-permute-start.8 = (f32[64,2304]{1,0:T(8,128)S(1)}, f32[64,2304]{1,0:T(8,128)S(1)}, u32[]{:S(2)}, u32[]{:S(2)}) collective-permute-start(f32[64,2304]{1,0:T(8,128)S(1)} %shard_map.82.refs_4_), channel_id=1, source_target_pairs={{0,1},{1,0},{2,6},{3,7},{4,5},{5,4},{6,2},{7,3},{8,9},{9,8},{10,14... | collective-permute-start | bytes 1769480 | tf_op jit(solution)/shard_map/ppermute | solution.py:309
  25.6 6.7 %collective-permute-start.6 = (f32[32,2304]{1,0:T(8,128)S(1)}, f32[32,2304]{1,0:T(8,128)S(1)}, u32[]{:S(2)}, u32[]{:S(2)}) collective-permute-start(f32[32,2304]{1,0:T(8,128)S(1)} %get-tuple-element.83), channel_id=1, source_target_pairs={{0,2},{1,3},{2,0},{3,1},{4,6},{5,7},{6,4},{7,5},{8,10},{9,11},{10,... | collective-permute-start | bytes 884744 | tf_op jit(solution)/shard_map/ppermute | solution.py:314
  26.5 5.8 %collective-permute-start.7 = (f32[32,2304]{1,0:T(8,128)S(1)}, f32[32,2304]{1,0:T(8,128)S(1)}, u32[]{:S(2)}, u32[]{:S(2)}) collective-permute-start(f32[32,2304]{1,0:T(8,128)S(1)} %get-tuple-element.84), channel_id=1, source_target_pairs={{0,2},{1,3},{2,0},{3,1},{4,6},{5,7},{6,4},{7,5},{8,10},{9,11},{10,... | collective-permute-start | bytes 884744 | tf_op jit(solution)/shard_map/ppermute | solution.py:314
  31.8 3.7 %collective-permute-start.5 = (f32[128,2304]{1,0:T(8,128)S(1)}, f32[128,2304]{1,0:T(8,128)S(1)}, u32[]{:S(2)}, u32[]{:S(2)}) collective-permute-start(f32[128,2304]{1,0:T(8,128)S(1)} %get-tuple-element.81), channel_id=1, source_target_pairs={{0,2},{1,3},{2,0},{3,1},{4,6},{5,7},{6,4},{7,5},{8,10},{9,11},{10,... | collective-permute-start | bytes 3538952 | tf_op jit(solution)/shard_map/ppermute | solution.py:314
  32.9 7.4 %collective-permute-start.10 = (f32[32,2304]{1,0:T(8,128)S(1)}, f32[32,2304]{1,0:T(8,128)S(1)}, u32[]{:S(2)}, u32[]{:S(2)}) collective-permute-start(f32[32,2304]{1,0:T(8,128)S(1)} %get-tuple-element.93), channel_id=1, source_target_pairs={{0,4},{1,5},{2,3},{3,2},{4,0},{5,1},{6,7},{7,6},{8,12},{9,13},{10,... | collective-permute-start | bytes 884744 | tf_op jit(solution)/shard_map/ppermute | solution.py:309
  35.6 1.7 %copy-start.1 = (f32[1,16,32,256]{3,2,1,0:T(8,128)S(1)}, f32[1,16,32,256]{3,2,1,0:T(8,128)}, u32[]{:S(2)}) copy-start(f32[1,16,32,256]{3,2,1,0:T(8,128)} %param.4) | copy-start | bytes 1572868
  36.0 10.5 %collective-permute-start.9 = (f32[64,2304]{1,0:T(8,128)S(1)}, f32[64,2304]{1,0:T(8,128)S(1)}, u32[]{:S(2)}, u32[]{:S(2)}) collective-permute-start(f32[64,2304]{1,0:T(8,128)S(1)} %get-tuple-element.92), channel_id=1, source_target_pairs={{0,4},{1,5},{2,3},{3,2},{4,0},{5,1},{6,7},{7,6},{8,12},{9,13},{10,... | collective-permute-start | bytes 1769480 | tf_op jit(solution)/shard_map/ppermute | solution.py:309
  40.4 11.2 %collective-permute-start.12 = (f32[144,128]{1,0:T(8,128)S(1)}, f32[144,128]{1,0:T(8,128)S(1)}, u32[]{:S(2)}, u32[]{:S(2)}) collective-permute-start(f32[144,128]{1,0:T(8,128)S(1)} %get-tuple-element.102), channel_id=1, source_target_pairs={{0,24},{8,16},{16,8},{24,0},{1,25},{9,17},{17,9},{25,1},{2,26},{10... | collective-permute-start | bytes 221192 | tf_op jit(solution)/shard_map/ppermute | solution.py:393
  43.1 8.6 %collective-permute-start.13 = (f32[144,128]{1,0:T(8,128)S(1)}, f32[144,128]{1,0:T(8,128)S(1)}, u32[]{:S(2)}, u32[]{:S(2)}) collective-permute-start(f32[144,128]{1,0:T(8,128)S(1)} %get-tuple-element.103), channel_id=1, source_target_pairs={{0,16},{8,24},{16,0},{24,8},{1,17},{9,25},{17,1},{25,9},{2,18},{10... | collective-permute-start | bytes 221192 | tf_op jit(solution)/shard_map/ppermute | solution.py:393
  43.1 8.6 %collective-permute-start.14 = (f32[144,128]{1,0:T(8,128)S(1)}, f32[144,128]{1,0:T(8,128)S(1)}, u32[]{:S(2)}, u32[]{:S(2)}) collective-permute-start(f32[144,128]{1,0:T(8,128)S(1)} %get-tuple-element.104), channel_id=1, source_target_pairs={{0,8},{8,0},{16,24},{24,16},{1,9},{9,1},{17,25},{25,17},{2,10},{10... | collective-permute-start | bytes 221192 | tf_op jit(solution)/shard_map/ppermute | solution.py:393
  47.3 6.8 %collective-permute-start.11 = (f32[32,2304]{1,0:T(8,128)S(1)}, f32[32,2304]{1,0:T(8,128)S(1)}, u32[]{:S(2)}, u32[]{:S(2)}) collective-permute-start(f32[32,2304]{1,0:T(8,128)S(1)} %get-tuple-element.100), channel_id=1, source_target_pairs={{0,1},{1,0},{2,6},{3,7},{4,5},{5,4},{6,2},{7,3},{8,9},{9,8},{10,14... | collective-permute-start | bytes 884744 | tf_op jit(solution)/shard_map/ppermute | solution.py:309
  54.2 6.5 %collective-permute-start.15 = (f32[144,128]{1,0:T(8,128)S(1)}, f32[144,128]{1,0:T(8,128)S(1)}, u32[]{:S(2)}, u32[]{:S(2)}) collective-permute-start(f32[144,128]{1,0:T(8,128)S(1)} %get-tuple-element.108), channel_id=1, source_target_pairs={{0,24},{8,16},{16,8},{24,0},{1,25},{9,17},{17,9},{25,1},{2,26},{10... | collective-permute-start | bytes 221192 | tf_op jit(solution)/shard_map/ppermute | solution.py:393
  56.8 5.4 %collective-permute-start.16 = (f32[144,128]{1,0:T(8,128)S(1)}, f32[144,128]{1,0:T(8,128)S(1)}, u32[]{:S(2)}, u32[]{:S(2)}) collective-permute-start(f32[144,128]{1,0:T(8,128)S(1)} %get-tuple-element.109), channel_id=1, source_target_pairs={{0,16},{8,24},{16,0},{24,8},{1,17},{9,25},{17,1},{25,9},{2,18},{10... | collective-permute-start | bytes 221192 | tf_op jit(solution)/shard_map/ppermute | solution.py:393
  56.8 5.4 %collective-permute-start.17 = (f32[144,128]{1,0:T(8,128)S(1)}, f32[144,128]{1,0:T(8,128)S(1)}, u32[]{:S(2)}, u32[]{:S(2)}) collective-permute-start(f32[144,128]{1,0:T(8,128)S(1)} %get-tuple-element.110), channel_id=1, source_target_pairs={{0,8},{8,0},{16,24},{24,16},{1,9},{9,1},{17,25},{25,17},{2,10},{10... | collective-permute-start | bytes 221192 | tf_op jit(solution)/shard_map/ppermute | solution.py:393
